TPU v7x, 512 devices: a whole 4x8x8 slice. The times are simulated.
512 devices in a mesh: tm: 64 (over y_lo, z, x), head: 8 (over y_hi, core).
Axes of the slice: x: 4, y: 8 (y_hi: 4, y_lo: 2; y = y_hi * 2 + y_lo), z: 8, core: 2. Of those that a mesh axis runs over, the one named last changes fastest.
Arguments:
- frames: bfloat16 [8192, 1920], P('tm', 'head'), may hold values from -6 to 6
- conv_weight: bfloat16 [64, 16, 120, 120], P('tm', 'head'), may hold values from -0.0625 to 0.0625
- w_qkv: bfloat16 [1920, 2880], P(None, 'head'), may hold values from -0.5 to 0.5
- lengths: int32 [4], replicated, may hold values from 1 to 4096, 8192 in all
- grad_out: bfloat16 [8192, 960], P('tm', 'head'), may hold values from -6 to 6
Outputs:
- attn_out: bfloat16 [8192, 960], P('tm', 'head')
- frame_grad: bfloat16 [8192, 1920], P('tm', 'head')
- weight_grad: float32 [1920, 2880], P('tm', 'head')
Inputs may be any that keep to these rules, and one draw needn't show every extreme that they name: 4 positive lengths summing to 8192; the longest is exactly 4096.
All inputs are finite; a program needn't handle non-finite values.
Results may differ from a plain program's by a relative error of at most 0.022.
Values may be sent and summed in bfloat16 or wider, within the bound.
No kernel may reach another device: no remote copies, remote signals or barrier semaphores. Data moves between devices by JAX's collectives and lax.ppermute only.
A program may use at most 64 MiB of HBM per device.

v0:
```python
import jax
import jax.numpy as jnp
from jax import lax
from jax.sharding import PartitionSpec as P

HD = 120
KERNEL = 64


inv_root_two = 0.7071067811865476
inv_root_tau = 0.3989422804014327
epsilon = 1e-05


def padded_2(shard, sides, width):
    for axis, dim in sides:
        devices, length = (lax.axis_size(axis), shard.shape[dim])
        up = [(i, (i + 1) % devices) for i in range(devices - 1)]
        down = [(j, i) for i, j in up]
        last = lax.slice_in_dim(shard, length - width, length, axis=dim)
        first = lax.slice_in_dim(shard, 0, width, axis=dim)
        before = lax.ppermute(last, axis, up)
        after = lax.ppermute(first, axis, down)
        shard = jnp.concatenate([before, shard, after], axis=dim)
    return shard


def segment_of(positions, lengths):
    boundary = jnp.cumsum(lengths)
    return jnp.sum((positions[:, None] >= boundary[None, :]).astype(jnp.int32), axis=1)


def gelu_parts(inputs):
    normal_cdf = 0.5 * (1.0 + lax.erf(inputs * inv_root_two))
    density = jnp.exp(-0.5 * inputs * inputs) * inv_root_tau
    return (inputs * normal_cdf, normal_cdf + inputs * density)


def shifted_stack(padded, first, stride, row_count, seg_pad, seg_rows):
    columns = []
    labels = []
    for offset in range(KERNEL):
        start = first + stride * offset
        columns.append(padded[start : start + row_count])
        labels.append(seg_pad[start : start + row_count])
    stacked = jnp.stack(columns, axis=1)
    keep = (jnp.stack(labels, axis=1) == seg_rows[:, None]).astype(stacked.dtype)
    return stacked * keep[:, :, None]


def masked_scores(query_rows, key_rows, same_mask, score_scale):
    scores = (
        jnp.einsum("qhd,khd->hqk", query_rows, key_rows, preferred_element_type=jnp.float32)
        * score_scale
    )
    return jnp.where(same_mask[None], scores, -jnp.inf)


def on_device(frames, conv_weight, w_qkv, lengths, grad_out):
    row_count, local_width = frames.shape
    time_shards = lax.axis_size("tm")
    shard_index = lax.axis_index("tm")
    half_kernel = KERNEL // 2
    group_count = conv_weight.shape[1]
    group_width = conv_weight.shape[2]
    head_count = grad_out.shape[1] // HD
    all_rows = row_count * time_shards
    model_width = w_qkv.shape[0]
    score_scale = HD ** (-0.5)
    positions = (
        shard_index * row_count - half_kernel + jnp.arange(row_count + KERNEL, dtype=jnp.int32)
    )
    seg_pad = segment_of(positions, lengths)
    seg_rows = seg_pad[half_kernel : half_kernel + row_count]
    seg_all = segment_of(jnp.arange(all_rows, dtype=jnp.int32), lengths)
    gathered_taps = lax.all_gather(conv_weight, "tm", axis=0, tiled=True)
    frames_pad = padded_2(frames, (("tm", 0),), half_kernel)
    patches = shifted_stack(frames_pad, 0, 1, row_count, seg_pad, seg_rows)
    patches = patches.reshape(row_count, KERNEL, group_count, group_width)
    conv_out = jnp.einsum(
        "tkgi,kgio->tgo", patches, gathered_taps, preferred_element_type=jnp.float32
    )
    conv_out = conv_out.reshape(row_count, local_width)
    activated, slope = gelu_parts(conv_out)
    hidden = frames.astype(jnp.float32) + activated
    row_sum, row_square = lax.psum(
        (jnp.sum(hidden, axis=1), jnp.sum(hidden * hidden, axis=1)), "head"
    )
    center = row_sum / model_width
    inv_std = lax.rsqrt(row_square / model_width - center * center + epsilon)
    unit_rows = (hidden - center[:, None]) * inv_std[:, None]
    normed = lax.all_gather(unit_rows.astype(jnp.bfloat16), "head", axis=1, tiled=True)
    projected = jnp.dot(normed, w_qkv, preferred_element_type=jnp.float32).astype(jnp.bfloat16)
    projected = projected.reshape(row_count, head_count, 3, HD)
    query_rows = projected[:, :, 0]
    key_rows = projected[:, :, 1]
    value_rows = projected[:, :, 2]
    upstream = grad_out.reshape(row_count, head_count, HD)
    keys_all, values_all = (
        lax.all_gather(key_rows, "tm", axis=0, tiled=True),
        lax.all_gather(value_rows, "tm", axis=0, tiled=True),
    )
    same_rows = seg_rows[:, None] == seg_all[None, :]
    scores = masked_scores(query_rows, keys_all, same_rows, score_scale)
    peak = jnp.max(scores, axis=2, keepdims=True)
    denominator = jnp.sum(jnp.exp(scores - peak), axis=2, keepdims=True)
    log_total = peak + jnp.log(denominator)
    attention = jnp.exp(scores - log_total)
    attended = jnp.einsum(
        "hqk,khd->qhd",
        attention.astype(jnp.bfloat16),
        values_all,
        preferred_element_type=jnp.float32,
    ).astype(jnp.bfloat16)
    delta = jnp.sum(upstream.astype(jnp.float32) * attended.astype(jnp.float32), axis=2)
    dprobs = jnp.einsum("qhd,khd->hqk", upstream, values_all, preferred_element_type=jnp.float32)
    dscores = (attention * (dprobs - delta.T[:, :, None]) * score_scale).astype(jnp.bfloat16)
    grad_q = jnp.einsum(
        "hqk,khd->qhd", dscores, keys_all, preferred_element_type=jnp.float32
    ).astype(jnp.bfloat16)
    query_all, upstream_all = (
        lax.all_gather(query_rows, "tm", axis=0, tiled=True),
        lax.all_gather(upstream, "tm", axis=0, tiled=True),
    )
    log_all, delta_all = (
        lax.all_gather(log_total[:, :, 0].T, "tm", axis=0, tiled=True),
        lax.all_gather(delta, "tm", axis=0, tiled=True),
    )
    same_cols = seg_all[:, None] == seg_rows[None, :]
    scores_t = masked_scores(query_all, key_rows, same_cols, score_scale)
    attention_t = jnp.exp(scores_t - log_all.T[:, :, None])
    grad_v = jnp.einsum(
        "hqk,qhd->khd",
        attention_t.astype(jnp.bfloat16),
        upstream_all,
        preferred_element_type=jnp.float32,
    ).astype(jnp.bfloat16)
    dprobs_t = jnp.einsum(
        "qhd,khd->hqk", upstream_all, value_rows, preferred_element_type=jnp.float32
    )
    dscores_t = (attention_t * (dprobs_t - delta_all.T[:, :, None]) * score_scale).astype(
        jnp.bfloat16
    )
    grad_k = jnp.einsum(
        "hqk,qhd->khd", dscores_t, query_all, preferred_element_type=jnp.float32
    ).astype(jnp.bfloat16)
    grad_joined = jnp.stack([grad_q, grad_k, grad_v], axis=2).reshape(
        row_count, head_count * 3 * HD
    )
    weight_grad = lax.psum_scatter(
        jnp.einsum("tc,tj->cj", normed, grad_joined, preferred_element_type=jnp.float32),
        "tm",
        scatter_dimension=0,
        tiled=True,
    )
    feature_grad = jnp.einsum("tj,cj->tc", grad_joined, w_qkv, preferred_element_type=jnp.float32)
    feature_share = lax.psum_scatter(
        feature_grad.astype(jnp.bfloat16), "head", scatter_dimension=1, tiled=True
    ).astype(jnp.float32)
    plain_sum, unit_sum = lax.psum(
        (jnp.sum(feature_share, axis=1), jnp.sum(feature_share * unit_rows, axis=1)), "head"
    )
    hidden_grad = inv_std[:, None] * (
        feature_share
        - plain_sum[:, None] / model_width
        - unit_rows * unit_sum[:, None] / model_width
    )
    error_rows = (slope * hidden_grad).astype(jnp.bfloat16)
    error_pad = padded_2(error_rows, (("tm", 0),), half_kernel)
    back_patches = shifted_stack(error_pad, KERNEL, -1, row_count, seg_pad, seg_rows)
    back_patches = back_patches.reshape(row_count, KERNEL, group_count, group_width)
    conv_back = jnp.einsum(
        "skgo,kgio->sgi", back_patches, gathered_taps, preferred_element_type=jnp.float32
    )
    frame_grad = (hidden_grad + conv_back.reshape(row_count, local_width)).astype(jnp.bfloat16)
    return (attended.reshape(row_count, head_count * HD), frame_grad, weight_grad)


def solution(mesh):
    return jax.shard_map(
        on_device,
        mesh=mesh,
        in_specs=(
            P("tm", "head"),
            P("tm", "head", None, None),
            P(None, "head"),
            P(),
            P("tm", "head"),
        ),
        out_specs=(P("tm", "head"), P("tm", "head"), P("tm", "head")),
        check_vma=False,
    )
```

profile of v0, /device:TPU:40, one launch (start us, length us, event | category | flops | bytes accessed | tf_op | source)
XLA Modules:
  0.0 1560.0 jit_solution(2119599993658146957)
XLA Ops:
  7.2 1.0 fusion.186
  8.3 3.4 collective-permute-start
  11.7 12.4 collective-permute-start.1
  24.1 1.6 copy.332
  25.8 0.8 reduce-window.8
  27.5 1.7 pad_maximum_fusion.3
  33.5 1.7 fusion.138
  36.4 0.6 constant_dynamic-update-slice_fusion.56
  37.1 0.7 constant_dynamic-update-slice_fusion.55
  38.4 0.6 constant_dynamic-update-slice_fusion.53
  41.9 0.6 constant_dynamic-update-slice_fusion.48
  42.5 0.6 constant_dynamic-update-slice_fusion.47
  43.8 0.6 constant_dynamic-update-slice_fusion.45
  44.4 0.6 constant_dynamic-update-slice_fusion.44
  45.7 0.6 constant_dynamic-update-slice_fusion.42
  46.6 0.7 constant_dynamic-update-slice_fusion.41
  48.5 0.6 constant_dynamic-update-slice_fusion.38
  49.1 0.6 constant_dynamic-update-slice_fusion.37
  56.3 0.7 constant_dynamic-update-slice_fusion.26
  57.0 0.7 constant_dynamic-update-slice_fusion.25
  58.2 0.6 constant_dynamic-update-slice_fusion.23
  58.9 0.6 constant_dynamic-update-slice_fusion.22
  63.6 0.6 constant_dynamic-update-slice_fusion.15
  65.6 0.6 constant_dynamic-update-slice_fusion.12
  67.4 0.7 constant_dynamic-update-slice_fusion.9
  72.5 255.5 %all-gather.14.cloned.1.call-done = bf16[64,2,120,120]{2,3,0,1:T(8,128)(2,1)} async-done(((bf16[1,2,120,120]{2,3,0,1:T(8,128)(2,1)}), bf16[64,2,120,120]{2,3,0,1:T(8,128)(2,1)}) %all-gather.14.cloned.1.call-update) | async-done | bytes 3686416 | tf_op jit(solution)/shard_map/all_gather | solution.py:76
  328.0 5.1 fusion.15
  333.2 14.2 all-reduce.3
  347.4 15.7 %all_gather.25 = bf16[128,1920]{0,1:T(8,128)(2,1)S(1)} all-gather(bf16[128,240]{0,1:T(8,128)(2,1)S(1)} %fusion.76), channel_id=1, replica_groups=mesh['tm'=64,'head'=8] {'head'}, dimensions={1}, use_global_device_ids=true | all-gather | bytes 552960 | tf_op jit(solution)/shard_map/all_gather | solution.py:92
  363.1 0.8 copy-done.3
  364.5 0.7 fusion.184
  365.2 0.7 all-gather.16.cloned.1.call-update
  367.3 232.0 %all-gather.18.cloned.1.call-done = bf16[8192,1,1,120]{0,3,2,1:T(8,128)(2,1)} async-done(((bf16[128,1,1,120]{0,3,2,1:T(8,128)(2,1)}), bf16[8192,1,1,120]{0,3,2,1:T(8,128)(2,1)}) %all-gather.18.cloned.1.call-update) | async-done | bytes 1966096 | tf_op jit(solution)/shard_map/all_gather | solution.py:100
  599.3 2.5 fusion.187
  601.8 2.0 copy-done.1
  603.8 0.8 exponential_reduce_fusion
  604.6 159.6 %all-gather.6 = f32[64,1,128]{2,1,0:T(1,128)} all-gather(f32[1,1,128]{2,1,0:T(1,128)S(1)} %bitcast.808), channel_id=5, replica_groups=mesh['tm'=64,'head'=8] {'tm'}, dimensions={0}, use_global_device_ids=true | all-gather | bytes 33280 | tf_op jit(solution)/shard_map/all_gather | solution.py:126
  764.3 72.0 %all-gather.16.cloned.1.call-done = bf16[8192,1,1,120]{0,3,2,1:T(8,128)(2,1)} async-done(((bf16[128,1,1,120]{0,3,2,1:T(8,128)(2,1)}), bf16[8192,1,1,120]{0,3,2,1:T(8,128)(2,1)}) %all-gather.16.cloned.1.call-update) | async-done | bytes 1966096 | tf_op jit(solution)/shard_map/all_gather | solution.py:101
  836.3 4.3 fusion.169
  840.5 153.9 %all-gather.7 = f32[64,1,128]{2,1,0:T(1,128)S(1)} all-gather(f32[1,1,128]{2,1,0:T(1,128)S(1)} %bitcast.809), channel_id=7, replica_groups=mesh['tm'=64,'head'=8] {'tm'}, dimensions={0}, use_global_device_ids=true | all-gather | bytes 33280 | tf_op jit(solution)/shard_map/all_gather | solution.py:127
  994.5 78.3 %all-gather.20.cloned.1.call-done = bf16[8192,1,1,120]{0,3,2,1:T(8,128)(2,1)} async-done(((bf16[128,1,1,120]{0,3,2,1:T(8,128)(2,1)}), bf16[8192,1,1,120]{0,3,2,1:T(8,128)(2,1)}) %all-gather.20.cloned.1.call-update) | async-done | bytes 1966096 | tf_op jit(solution)/shard_map/all_gather | solution.py:122
  1072.7 5.9 fusion.6
  1078.7 5.1 fusion.57
  1083.7 224.9 %all-gather.22.cloned.1.call-done = bf16[8192,120]{0,1:T(8,128)(2,1)} async-done(((bf16[128,120]{0,1:T(8,128)(2,1)}), bf16[8192,120]{0,1:T(8,128)(2,1)}) %all-gather.22.cloned.1.call-update) | async-done | bytes 1966096 | tf_op jit(solution)/shard_map/all_gather | solution.py:123
  1308.6 3.6 fusion.51
  1312.2 5.4 fusion.54
  1317.6 0.8 pad_maximum_fusion
  1318.4 3.2 fusion.188
  1321.6 1.5 convolution_convert_fusion
  1323.1 177.7 %fusion = f32[32,360]{1,0:T(8,128)S(1)} fusion(f32[1920,360]{1,0:T(8,128)} %fusion.188), kind=kCustom, calls=%all-reduce-scatter | all-reduce-scatter fusion | flops 737281 | bytes 2812928
  1500.8 1.9 collective-permute-start.4
  1502.7 1.9 collective-permute-start.5
  1504.6 1.9 collective-permute-start.6
  1506.6 1.9 collective-permute-start.7
  1508.5 1.3 dynamic-slice.4
  1510.4 6.9 collective-permute-done.7
  1518.0 0.9 convert_reduce_fusion
  1518.9 14.2 all-reduce.2
  1533.1 0.9 fusion.70
  1534.1 3.7 collective-permute-start.2
  1538.5 2.4 collective-permute-start.3
  1542.5 6.2 collective-permute-done.3
  1551.0 1.4 fusion.13
  1552.5 0.7 fusion.71
  (196 shorter events, 38.0 us)
Async XLA Ops:
  7.2 356.7 %copy-start = (bf16[1920,360]{0,1:T(8,128)(2,1)S(1)}, bf16[1920,360]{0,1:T(8,128)(2,1)}, u32[]{:S(2)}) copy-start(bf16[1920,360]{0,1:T(8,128)(2,1)} %param.7) | copy-start | bytes 4147204
  7.2 33.7 %copy-start.5 = (bf16[128,240]{0,1:T(8,128)(2,1)S(1)}, bf16[128,240]{0,1:T(8,128)(2,1)}, u32[]{:S(2)}) copy-start(bf16[128,240]{0,1:T(8,128)(2,1)} %param.5) | copy-start | bytes 184324
  7.2 320.8 %all-gather.14.cloned.1.call-start = ((), (), s32[]{:S(2)}) async-start(), calls=%async_computation.1 | async-start | bytes 3993600 | tf_op jit(solution)/shard_map/all_gather | solution.py:76
  8.3 19.2 %collective-permute-start = (bf16[32,240]{0,1:T(8,128)(2,1)S(1)}, bf16[32,240]{0,1:T(8,128)(2,1)S(1)}, u32[]{:S(2)}, u32[]{:S(2)}) collective-permute-start(bf16[32,240]{0,1:T(8,128)(2,1)S(1)} %get-tuple-element.149), channel_id=1, source_target_pairs={{0,8},{8,16},{16,24},{24,32},{32,40},{40,48},{48,56},{56,64},{64,7... | collective-permute-start | bytes 46088 | tf_op jit(solution)/shard_map/ppermute | solution.py:22
  11.7 40.6 %collective-permute-start.1 = (bf16[32,240]{0,1:T(8,128)(2,1)S(1)}, bf16[32,240]{0,1:T(8,128)(2,1)S(1)}, u32[]{:S(2)}, u32[]{:S(2)}) collective-permute-start(bf16[32,240]{0,1:T(8,128)(2,1)S(1)} %get-tuple-element.148), channel_id=1, source_target_pairs={{8,0},{16,8},{24,16},{32,24},{40,32},{48,40},{56,48},{64,56},{72,6... | collective-permute-start | bytes 46088 | tf_op jit(solution)/shard_map/ppermute | solution.py:23
  25.7 573.6 %all-gather.18.cloned.1.call-start = ((), (), s32[]{:S(2)}) async-start(), calls=%async_computation.4 | async-start | bytes 1996800 | tf_op jit(solution)/shard_map/all_gather | solution.py:100
  26.9 572.4 %copy-start.16 = (s32[128]{0:T(128)}, s32[128]{0:T(128)S(1)}, u32[]{:S(2)}) copy-start(s32[128]{0:T(128)S(1)} %get-tuple-element.184) | copy-start | bytes 1540
  333.1 268.7 %copy-start.7 = (f32[2,128,120,1]{1,2,3,0:T(8,128)}, f32[2,128,120,1]{1,2,3,0:T(8,128)S(1)}, u32[]{:S(2)}) copy-start(f32[2,128,120,1]{1,2,3,0:T(8,128)S(1)} %fusion.15) | copy-start | bytes 368644
  347.4 19.6 %copy-start.12 = (f32[128]{0:T(128)}, f32[128]{0:T(128)S(1)}, u32[]{:S(2)}) copy-start(f32[128]{0:T(128)S(1)} %get-tuple-element.219) | copy-start | bytes 1540
  347.4 19.7 %copy-start.14 = (f32[128]{0:T(128)}, f32[128]{0:T(128)S(1)}, u32[]{:S(2)}) copy-start(f32[128]{0:T(128)S(1)} %get-tuple-element.220) | copy-start | bytes 1540
  363.1 0.8 copy-start.3
  364.5 240.1 %copy-start.9 = (bf16[128,360]{0,1:T(8,128)(2,1)}, bf16[128,360]{0,1:T(8,128)(2,1)S(1)}, u32[]{:S(2)}) copy-start(bf16[128,360]{0,1:T(8,128)(2,1)S(1)} %convolution_convert_fusion.1) | copy-start | bytes 276484
  365.2 471.1 %all-gather.16.cloned.1.call-start = ((), (), s32[]{:S(2)}) async-start(), calls=%async_computation.3 | async-start | bytes 1996800 | tf_op jit(solution)/shard_map/all_gather | solution.py:101
  365.9 706.8 %all-gather.20.cloned.1.call-start = ((), (), s32[]{:S(2)}) async-start(), calls=%async_computation.5 | async-start | bytes 1996800 | tf_op jit(solution)/shard_map/all_gather | solution.py:122
  366.5 942.1 %all-gather.22.cloned.1.call-start = ((), (), s32[]{:S(2)}) async-start(), calls=%async_computation.6 | async-start | bytes 1996800 | tf_op jit(solution)/shard_map/all_gather | solution.py:123
  367.1 1150.9 %reduce-scatter.4.cloned.1.call-start = ((), (), s32[]{:S(2)}) async-start(), calls=%async_computation.2 | async-start | bytes 552960 | tf_op jit(solution)/shard_map/reduce_scatter | solution.py:157
  367.3 469.0 %copy-start.11 = (bf16[128,120]{0,1:T(8,128)(2,1)S(1)}, bf16[128,120]{0,1:T(8,128)(2,1)}, u32[]{:S(2)}) copy-start(bf16[128,120]{0,1:T(8,128)(2,1)} %param.9) | copy-start | bytes 92164
  601.8 2.0 copy-start.1
  604.6 235.9 %copy-start.17 = (f32[128]{0:T(128)}, f32[128]{0:T(128)S(1)}, u32[]{:S(2)}) copy-start(f32[128]{0:T(128)S(1)} %log_add_fusion) | copy-start | bytes 1540
  840.5 232.2 %copy-start.18 = (f32[128]{0:T(128)}, f32[128]{0:T(128)S(1)}, u32[]{:S(2)}) copy-start(f32[128]{0:T(128)S(1)} %get-tuple-element.223) | copy-start | bytes 1540
  1072.7 5.9 copy-start.6
  1308.6 3.6 copy-start.2
  1318.4 199.6 %copy-start.13 = (f32[128]{0:T(128)S(1)}, f32[128]{0:T(128)}, u32[]{:S(2)}) copy-start(f32[128]{0:T(128)} %copy-done.12) | copy-start | bytes 1540
  1318.4 199.6 %copy-start.15 = (f32[128]{0:T(128)S(1)}, f32[128]{0:T(128)}, u32[]{:S(2)}) copy-start(f32[128]{0:T(128)} %copy-done.14) | copy-start | bytes 1540
  1321.6 211.6 %copy-start.8 = (f32[2,128,120,1]{1,2,3,0:T(8,128)S(1)}, f32[2,128,120,1]{1,2,3,0:T(8,128)}, u32[]{:S(2)}) copy-start(f32[2,128,120,1]{1,2,3,0:T(8,128)} %copy-done.7) | copy-start | bytes 368644
  1500.8 16.6 %collective-permute-start.4 = (f32[32,360]{1,0:T(8,128)S(1)}, f32[32,360]{1,0:T(8,128)S(1)}, u32[]{:S(2)}, u32[]{:S(2)}) collective-permute-start(f32[32,360]{1,0:T(8,128)S(1)} %fusion), channel_id=1, source_target_pairs={{0,8},{8,16},{16,24},{24,32},{32,40},{40,48},{48,56},{56,64},{64,7... | collective-permute-start | bytes 138248
  1502.7 14.6 collective-permute-start.5
  1504.6 12.7 collective-permute-start.6
  1506.6 10.8 collective-permute-start.7
  1534.1 6.7 collective-permute-start.2
  1538.5 10.3 collective-permute-start.3
  1542.5 8.5 copy-start.4
  1551.0 1.5 copy-start.10
Sparse Core Ops, SparseCore 0:
  25.8 302.0 all-gather.13
  365.3 233.9 all-gather.17
  601.9 234.3 all-gather.15
  838.7 233.9 all-gather.19
  1074.6 233.9 all-gather.21
  1323.2 35.9 reduce-scatter.3
where the time goes:
time: 1560 us
  waiting for transfers between devices  878 us (56%)
  blocking collectives  535 us (34%)
  local copies, waits for them, and re-layouts  51.3 us (3%)
  matrix products  38.5 us (2%)
  starting transfers between devices  29.8 us (2%)
  between operations  15.6 us (1%)
    all_gather x1, waiting for transfers between devices, on_device(): gathered_taps = lax.all_gather(conv_weight, 'tm', axis=0, tiled=True)  255 us
    all_gather x1, waiting for transfers between devices, on_device(): lax.all_gather(key_rows, 'tm', axis=0, tiled=True)  232 us
    all_gather x1, waiting for transfers between devices, on_device(): lax.all_gather(upstream, 'tm', axis=0, tiled=True)  225 us
    unnamed x1, blocking collectives  178 us
    all_gather x1, blocking collectives, on_device(): lax.all_gather(log_total[:, :, 0].T, 'tm', axis=0, tiled=True)  160 us
    all_gather x1, blocking collectives, on_device(): lax.all_gather(delta, 'tm', axis=0, tiled=True)  154 us
    all_gather x1, waiting for transfers between devices, on_device(): lax.all_gather(query_rows, 'tm', axis=0, tiled=True)  78.3 us
    all_gather x1, waiting for transfers between devices, on_device(): lax.all_gather(value_rows, 'tm', axis=0, tiled=True)  72 us
  transfers between devices with their start and end apart: 14, of which 7 were waited for; matrix products, arithmetic and copies ran while one was open for 16% of the time, Pallas kernels for 0%

commit v1 on v0

v1 whole, which is shorter than its diff:
```python
import functools
import math

import jax
import jax.numpy as jnp
from jax import lax
from jax.experimental import pallas as pl
from jax.experimental.pallas import tpu as pltpu
from jax.sharding import PartitionSpec as P

HD = 120
KERNEL = 64
HALF = KERNEL // 2
ROWS = 128
LANES = 128
SCALE = HD ** (-0.5)
SCALE2 = SCALE * math.log2(math.e)
FAR = -(2.0**100)
EPS = 1e-05
INV_ROOT_TWO = 0.7071067811865476
INV_ROOT_TAU = 0.3989422804014327

BF = jnp.bfloat16
F32 = jnp.float32

XY_GROUPS = [[y * 32 + z * 4 + x for y in range(2) for x in range(4)] for z in range(8)]
Z_GROUPS = [[y * 32 + z * 4 + x for z in range(8)] for y in range(2) for x in range(4)]


def exchange_xy(parts):
    return lax.all_to_all(parts, "tm", 0, 0, axis_index_groups=XY_GROUPS)


def exchange_z(parts):
    return lax.all_to_all(parts, "tm", 0, 0, axis_index_groups=Z_GROUPS)


def everyone(array):
    return jnp.broadcast_to(array[None], (8,) + array.shape)


def vmem_call(body, out_shape, scratch=(), scalars=0, inputs=0, flops=0):
    return pl.pallas_call(
        body,
        out_shape=out_shape,
        in_specs=[pl.BlockSpec(memory_space=pltpu.SMEM)] * scalars
        + [pl.BlockSpec(memory_space=pltpu.VMEM)] * inputs,
        out_specs=jax.tree.map(lambda _: pl.BlockSpec(memory_space=pltpu.VMEM), out_shape),
        scratch_shapes=list(scratch),
        compiler_params=pltpu.CompilerParams(vmem_limit_bytes=48 * 1024 * 1024),
        cost_estimate=pl.CostEstimate(flops=flops, bytes_accessed=1 << 20, transcendentals=0),
    )


def conv_body(forward, sc_ref, x_ref, w_ref, out_ref):
    first = sc_ref[0]
    row = lax.broadcasted_iota(jnp.int32, (ROWS, HD), 0)

    def block(b, carry):
        shard = (b // 4) * 32 + sc_ref[1] + b % 4
        pos = shard * ROWS + row
        low = jnp.zeros_like(pos)
        high = jnp.full_like(pos, sc_ref[2])
        for u in range(3):
            end = sc_ref[2 + u]
            inside = pos >= end
            low = jnp.where(inside, end, low)
            high = jnp.where(inside, sc_ref[3 + u], high)
        source = pos - HALF + first
        keep = [
            ((source + 4 * s) >= low) & ((source + 4 * s) < high) for s in range(8)
        ]
        for g in range(2):
            x = x_ref[b, g].astype(F32)
            even = pltpu.roll(x, ROWS + KERNEL - first, 0)
            odd = pltpu.roll(x, ROWS + KERNEL - first - 4, 0)
            total = jnp.zeros((ROWS, HD), F32)
            for s in range(8):
                rolled = odd if s % 2 else even
                start = 8 * (s // 2)
                piece = jnp.where(keep[s], rolled[start : start + ROWS], 0.0).astype(BF)
                if forward:
                    total += jnp.dot(piece, w_ref[s, g], preferred_element_type=F32)
                else:
                    total += lax.dot_general(
                        piece,
                        w_ref[7 - s, g],
                        (((1,), (1,)), ((), ())),
                        preferred_element_type=F32,
                    )
            out_ref[b, g] = total.astype(BF)
        return carry

    lax.fori_loop(0, 8, block, 0)


def conv_partial(forward, scalars, padded, taps):
    return vmem_call(
        functools.partial(conv_body, forward),
        jax.ShapeDtypeStruct((8, 2, ROWS, HD), BF),
        scalars=1,
        inputs=2,
        flops=8 * 2 * 8 * 2 * ROWS * HD * HD,
    )(scalars, padded, taps)


def with_halo(rows):
    devices = 64
    up = [(i, i + 1) for i in range(devices - 1)]
    down = [(i + 1, i) for i in range(devices - 1)]
    before = lax.ppermute(rows[:, ROWS - HALF :], "tm", up)
    after = lax.ppermute(rows[:, :HALF], "tm", down)
    return jnp.concatenate([before, rows, after], axis=1)


CHUNK = 256


def stats_body(qd_ref, kv_ref, out_ref):
    keys = kv_ref[:, :, :LANES].reshape(8 * ROWS, LANES)
    values = kv_ref[:, :, LANES:].reshape(8 * ROWS, LANES)
    out_ref[...] = jnp.zeros_like(out_ref)
    for c in range(8 * ROWS // CHUNK):
        n = CHUNK // ROWS
        q = qd_ref[c * n : (c + 1) * n, :, :LANES].reshape(CHUNK, LANES)
        d = qd_ref[c * n : (c + 1) * n, :, LANES:].reshape(CHUNK, LANES)
        contract = (((1,), (1,)), ((), ()))
        scores = lax.dot_general(keys, q, contract, preferred_element_type=F32)
        dprobs = lax.dot_general(values, d, contract, preferred_element_type=F32)
        peak = jnp.max(scores, axis=0, keepdims=True) * SCALE2
        weight = jnp.exp2(scores * SCALE2 - peak)
        columns = slice(c * CHUNK, (c + 1) * CHUNK)
        out_ref[0:1, columns] = peak
        out_ref[1:2, columns] = jnp.sum(weight, axis=0, keepdims=True)
        out_ref[2:3, columns] = jnp.sum(weight * dprobs, axis=0, keepdims=True)


def grads_body(qd_ref, kv_ref, stats_ref, od_ref, dkv_ref, dk_ref, dv_ref):
    keys = kv_ref[:, :, :LANES].reshape(8 * ROWS, LANES)
    values = kv_ref[:, :, LANES:].reshape(8 * ROWS, LANES)
    peaks = stats_ref[:, 0, :]
    top = jnp.max(peaks, axis=0, keepdims=True)
    factor = jnp.exp2(peaks - top)
    total = jnp.sum(stats_ref[:, 1, :] * factor, axis=0, keepdims=True)
    delta = jnp.sum(stats_ref[:, 2, :] * factor, axis=0, keepdims=True) / total
    lse = top + jnp.log2(total)
    for c in range(8 * ROWS // CHUNK):
        n = CHUNK // ROWS
        q = qd_ref[c * n : (c + 1) * n, :, :LANES].reshape(CHUNK, LANES)
        d = qd_ref[c * n : (c + 1) * n, :, LANES:].reshape(CHUNK, LANES)
        columns = slice(c * CHUNK, (c + 1) * CHUNK)
        contract = (((1,), (1,)), ((), ()))
        scores = lax.dot_general(keys, q, contract, preferred_element_type=F32)
        dprobs = lax.dot_general(values, d, contract, preferred_element_type=F32)
        probs = jnp.exp2(scores * SCALE2 - lse[:, columns])
        dscores = (probs * (dprobs - delta[:, columns])).astype(BF)
        probs = probs.astype(BF)
        dv = jnp.dot(probs, d, preferred_element_type=F32)
        dk = jnp.dot(dscores, q, preferred_element_type=F32)
        if c == 0:
            dv_ref[...] = dv
            dk_ref[...] = dk
        else:
            dv_ref[...] += dv
            dk_ref[...] += dk
        inner = (((0,), (0,)), ((), ()))
        out_t = lax.dot_general(values, probs, inner, preferred_element_type=F32)
        dq_t = lax.dot_general(keys, dscores, inner, preferred_element_type=F32) * SCALE
        for i in range(n):
            od_ref[c * n + i, 0] = out_t[:HD, i * ROWS : (i + 1) * ROWS].astype(BF)
            od_ref[c * n + i, 1] = dq_t[:HD, i * ROWS : (i + 1) * ROWS].astype(BF)
    for i in range(8):
        piece = slice(i * ROWS, (i + 1) * ROWS)
        dkv_ref[i, :, :LANES] = (dk_ref[piece] * SCALE).astype(BF)
        dkv_ref[i, :, LANES:] = dv_ref[piece].astype(BF)


def attention_stats(queries, keys):
    return vmem_call(
        stats_body,
        jax.ShapeDtypeStruct((8, 8 * ROWS), F32),
        inputs=2,
        flops=2 * 2 * (8 * ROWS) ** 2 * LANES,
    )(queries, keys)


def attention_grads(queries, keys, stats):
    return vmem_call(
        grads_body,
        (
            jax.ShapeDtypeStruct((8, 2, HD, ROWS), BF),
            jax.ShapeDtypeStruct((8, ROWS, 2 * LANES), BF),
        ),
        scratch=[pltpu.VMEM((8 * ROWS, LANES), F32)] * 2,
        inputs=3,
        flops=6 * 2 * (8 * ROWS) ** 2 * LANES,
    )(queries, keys, stats)


def gelu_parts(inputs):
    normal_cdf = 0.5 * (1.0 + lax.erf(inputs * INV_ROOT_TWO))
    density = jnp.exp(-0.5 * inputs * inputs) * INV_ROOT_TAU
    return inputs * normal_cdf, normal_cdf + inputs * density


def on_device(frames, conv_weight, w_qkv, lengths, grad_out):
    index = lax.axis_index("tm")
    tap_base = (index // 32) * 32 + index % 4
    z_base = index % 32 - index % 4
    ends = jnp.cumsum(lengths).astype(jnp.int32)
    groups = 2
    width = w_qkv.shape[0]

    def scalars(first):
        return jnp.concatenate([jnp.stack([first, z_base]).astype(jnp.int32), ends])

    frames_g = frames.reshape(ROWS, groups, HD).transpose(1, 0, 2)
    frames_pad = with_halo(frames_g)
    taps = exchange_z(everyone(conv_weight[0]))
    frames_all = exchange_xy(everyone(frames_pad))
    conv = exchange_xy(conv_partial(True, scalars(tap_base), frames_all, taps))
    conv = jnp.sum(conv.astype(F32), axis=0)
    activated, slope = gelu_parts(conv)
    hidden = frames_g.astype(F32) + activated

    hidden_all = lax.all_gather(hidden.astype(BF), "head", axis=0, tiled=True).astype(F32)
    center = jnp.sum(hidden_all, axis=(0, 2)) / width
    square = jnp.sum(hidden_all * hidden_all, axis=(0, 2)) / width
    inv_std = lax.rsqrt(square - center * center + EPS)
    normed = ((hidden_all - center[:, None]) * inv_std[:, None]).astype(BF)
    unit = (hidden - center[:, None]) * inv_std[:, None]
    weights = w_qkv.reshape(16, HD, 3 * HD)
    normed_rows = normed.transpose(1, 0, 2).reshape(ROWS, width)
    projected = jnp.dot(normed_rows, w_qkv, preferred_element_type=F32).astype(BF)

    pos = index * ROWS + jnp.arange(ROWS, dtype=jnp.int32)
    seg = jnp.sum((pos[:, None] >= ends[None, :3]).astype(jnp.int32), axis=1)
    same = seg[:, None] == jnp.arange(8, dtype=jnp.int32)[None]
    q_mark = same.astype(BF)
    k_mark = jnp.where(same, 0.0, FAR).astype(BF)
    nil = jnp.zeros((ROWS, 8), BF)
    queries = jnp.concatenate([projected[:, :HD], q_mark, grad_out, nil], axis=1)
    keys = jnp.concatenate(
        [projected[:, HD : 2 * HD], k_mark, projected[:, 2 * HD :], nil], axis=1
    )
    queries_all = exchange_xy(everyone(queries))
    keys_all = exchange_z(everyone(keys))
    stats = exchange_xy(everyone(attention_stats(queries_all, keys_all)))
    od, dkv = attention_grads(queries_all, keys_all, stats)
    od = jnp.sum(exchange_xy(od).astype(F32), axis=0).astype(BF)
    dkv = jnp.sum(exchange_z(dkv).astype(F32), axis=0).astype(BF)
    attended = od[0].T
    grad_joined = jnp.concatenate([od[1].T, dkv[:, :HD], dkv[:, LANES : LANES + HD]], axis=1)

    share = jnp.einsum("tj,gcj->gtc", grad_joined, weights, preferred_element_type=F32)
    plain = jnp.sum(share, axis=(0, 2))
    along = jnp.sum(share * normed.astype(F32), axis=(0, 2))
    sums = jnp.stack([plain, along], axis=1)
    sums_high = sums.astype(BF)
    sums_low = (sums - sums_high.astype(F32)).astype(BF)
    sums = jnp.concatenate([sums_high, sums_low, jnp.zeros((ROWS, 4), BF)], axis=1)
    parts = jnp.concatenate(
        [share.astype(BF), jnp.broadcast_to(sums[None], (16, ROWS, 8))], axis=2
    ).reshape(8, groups, ROWS, LANES)
    parts = lax.all_to_all(parts, "head", 0, 0)
    parts = jnp.sum(parts.astype(F32), axis=0)
    feature = parts[:, :, :HD]
    plain = parts[0, :, HD] + parts[0, :, HD + 2]
    along = parts[0, :, HD + 1] + parts[0, :, HD + 3]
    hidden_grad = inv_std[:, None] * (
        feature - plain[:, None] / width - unit * (along[:, None] / width)
    )

    error = (slope * hidden_grad).astype(BF)
    error_all = exchange_xy(everyone(with_halo(error)))
    back = exchange_xy(conv_partial(False, scalars(36 - tap_base), error_all, taps))
    frame_grad = hidden_grad + jnp.sum(back.astype(F32), axis=0)
    frame_grad = frame_grad.astype(BF).transpose(1, 0, 2).reshape(ROWS, groups * HD)

    wide = lax.dot_general(
        normed_rows, grad_joined, (((0,), (0,)), ((), ())), preferred_element_type=F32
    ).astype(BF)
    slab = width // 64
    wide = wide.reshape(2, 8, 4, slab, 3 * HD).transpose(0, 2, 1, 3, 4)
    wide = exchange_xy(wide.reshape(8, 8, slab, 3 * HD))
    wide = jnp.sum(wide.astype(F32), axis=0).astype(BF)
    weight_grad = jnp.sum(exchange_z(wide).astype(F32), axis=0)
    return attended, frame_grad, weight_grad


def solution(mesh):
    return jax.shard_map(
        on_device,
        mesh=mesh,
        in_specs=(
            P("tm", "head"),
            P("tm", "head", None, None),
            P(None, "head"),
            P(),
            P("tm", "head"),
        ),
        out_specs=(P("tm", "head"), P("tm", "head"), P("tm", "head")),
        check_vma=False,
    )
```

time: 1560 us -> 257 us (0.16)
  the two profiles are of different devices: /device:TPU:40 before, /device:TPU:8 now
where the time goes in v1:
time: 257 us; the launch traced here: 255 us
  waiting for transfers between devices  92.6 us (36%)
  starting transfers between devices  63.8 us (25%)
  blocking collectives  58.8 us (23%)
  local copies, waits for them, and re-layouts  17.1 us (7%)
  Pallas kernels  14.3 us (6%)
  other arithmetic  4.77 us (2%)
  matrix products  2.89 us (1%)
    all_to_all x6, waiting for transfers between devices, exchange_xy(): return lax.all_to_all(parts, 'tm', 0, 0, axis_index_groups=XY_GROUPS)  46.3 us
    all_to_all x6, starting transfers between devices, exchange_xy(): return lax.all_to_all(parts, 'tm', 0, 0, axis_index_groups=XY_GROUPS)  26.8 us
    all_to_all x2, blocking collectives, exchange_xy(): return lax.all_to_all(parts, 'tm', 0, 0, axis_index_groups=XY_GROUPS)  21.1 us
    all_to_all x1, blocking collectives, exchange_z(): return lax.all_to_all(parts, 'tm', 0, 0, axis_index_groups=Z_GROUPS)  20.7 us
    all_to_all x3, starting transfers between devices, exchange_z(): return lax.all_to_all(parts, 'tm', 0, 0, axis_index_groups=Z_GROUPS)  17.2 us
    all_gather x1, blocking collectives, on_device(): lax.all_gather(hidden.astype(BF), 'head', axis=0, tiled=True).astype(F32)  17 us
    all_to_all x3, waiting for transfers between devices, exchange_z(): return lax.all_to_all(parts, 'tm', 0, 0, axis_index_groups=Z_GROUPS)  15.3 us
    all_to_all x1, waiting for transfers between devices, on_device(): parts = lax.all_to_all(parts, 'head', 0, 0)  11.9 us
  transfers between devices with their start and end apart: 14, of which 12 were waited for; matrix products, arithmetic and copies ran while one was open for 6% of the time, Pallas kernels for 2%

profile of v1, /device:TPU:8, one launch (start us, length us, event | category | flops | bytes accessed | tf_op | source)
XLA Modules:
  0.0 255.4 jit_solution(13322698785557760958)
XLA Ops:
  0.6 1.7 broadcast_in_dim.30
  2.3 10.3 %all-to-all-start.1 = ((bf16[8,2,120,120]{3,2,1,0:T(8,128)(2,1)}), bf16[8,2,120,120]{3,2,1,0:T(8,128)(2,1)S(1)}, u32[]{:S(2)}, u32[]{:S(2)}) async-start(bf16[8,2,120,120]{3,2,1,0:T(8,128)(2,1)} %broadcast_in_dim.30), calls=%async_computation.1 | async-start | bytes 983040 | tf_op jit(solution)/shard_map/all_to_all | solution.py:35
  12.7 0.1 copy.62
  12.8 7.2 %collective-permute-start.1 = (bf16[2,32,120]{2,1,0:T(8,128)(2,1)S(1)}, bf16[2,32,120]{2,1,0:T(8,128)(2,1)S(1)}, u32[]{:S(2)}, u32[]{:S(2)}) collective-permute-start(bf16[2,32,120]{2,1,0:T(8,128)(2,1)S(1)} %get-tuple-element.21), channel_id=1, source_target_pairs={{8,0},{16,8},{24,16},{32,24},{40,32},{48,40},{56,48},{64,56},{72,6... | collective-permute-start | bytes 46088 | tf_op jit(solution)/shard_map/ppermute | solution.py:112
  20.0 1.9 collective-permute-start
  22.0 8.0 %collective-permute-done = bf16[2,32,120]{2,1,0:T(8,128)(2,1)S(1)} collective-permute-done((bf16[2,32,120]{2,1,0:T(8,128)(2,1)S(1)}, bf16[2,32,120]{2,1,0:T(8,128)(2,1)S(1)}, u32[]{:S(2)}, u32[]{:S(2)}) %collective-permute-start) | collective-permute-done | bytes 15392 | tf_op jit(solution)/shard_map/ppermute | solution.py:111
  30.0 1.0 broadcast_in_dim.28
  31.1 5.2 %all-to-all-start = ((bf16[8,2,192,120]{3,2,1,0:T(8,128)(2,1)}), bf16[8,2,192,120]{3,2,1,0:T(8,128)(2,1)S(1)}, u32[]{:S(2)}, u32[]{:S(2)}) async-start(bf16[8,2,192,120]{3,2,1,0:T(8,128)(2,1)} %broadcast_in_dim.28), calls=%async_computation | async-start | bytes 1572864 | tf_op jit(solution)/shard_map/all_to_all | solution.py:31
  36.2 0.2 reduce-window.4
  36.6 11.3 %all-to-all-done.x_ref = bf16[8,2,192,120]{3,2,1,0:T(8,128)(2,1)S(1)} async-done(((bf16[8,2,192,120]{3,2,1,0:T(8,128)(2,1)}), bf16[8,2,192,120]{3,2,1,0:T(8,128)(2,1)S(1)}, u32[]{:S(2)}, u32[]{:S(2)}) %all-to-all-start) | async-done | bytes 737312 | tf_op jit(solution)/shard_map/all_to_all | solution.py:31
  47.9 3.7 %shard_map.76 = bf16[8,2,128,120]{3,2,1,0:T(8,128)(2,1)S(1)} custom-call(s32[6]{0:T(128)S(1)} %get-tuple-element.25.sc_ref, bf16[8,2,192,120]{3,2,1,0:T(8,128)(2,1)S(1)} %all-to-all-done.x_ref, bf16[8,2,120,120]{3,2,1,0:T(8,128)(2,1)S(1)} %all-to-all-done.1.w_ref), custom_call_target="tpu_custom_call" | custom-call | flops 471859200 | bytes 1048576 | tf_op jit(solution)/shard_map/pallas_call | solution.py:98
  51.6 1.0 copy.63
  52.6 4.2 %all-to-all-start.2 = ((bf16[8,2,128,120]{2,3,1,0:T(8,128)(2,1)}), bf16[8,2,128,120]{2,3,1,0:T(8,128)(2,1)S(1)}, u32[]{:S(2)}, u32[]{:S(2)}) async-start(bf16[8,2,128,120]{2,3,1,0:T(8,128)(2,1)} %copy.63), calls=%async_computation.2 | async-start | bytes 983040 | tf_op jit(solution)/shard_map/all_to_all | solution.py:31
  56.9 8.3 %all-to-all-done.2 = bf16[8,2,128,120]{2,3,1,0:T(8,128)(2,1)S(1)} async-done(((bf16[8,2,128,120]{2,3,1,0:T(8,128)(2,1)}), bf16[8,2,128,120]{2,3,1,0:T(8,128)(2,1)S(1)}, u32[]{:S(2)}, u32[]{:S(2)}) %all-to-all-start.2) | async-done | bytes 491552 | tf_op jit(solution)/shard_map/all_to_all | solution.py:31
  65.5 0.1 copy.65
  65.6 17.0 %all_gather.3 = bf16[16,128,120]{1,2,0:T(8,128)(2,1)S(1)} all-gather(bf16[2,128,120]{1,2,0:T(8,128)(2,1)S(1)} %copy.65), channel_id=1, replica_groups=mesh['tm'=64,'head'=8] {'head'}, dimensions={0}, use_global_device_ids=true | all-gather | bytes 552960 | tf_op jit(solution)/shard_map/all_gather | solution.py:226
  82.6 0.3 convert_reduce_fusion
  82.9 0.1 fusion.1
  83.0 0.5 convolution_convert_fusion.1
  83.8 0.8 broadcast_in_dim.32
  84.7 4.4 %all-to-all-start.3 = ((bf16[8,128,256]{2,1,0:T(8,128)(2,1)}), bf16[8,128,256]{2,1,0:T(8,128)(2,1)S(1)}, u32[]{:S(2)}, u32[]{:S(2)}) async-start(bf16[8,128,256]{2,1,0:T(8,128)(2,1)} %broadcast_in_dim.32), calls=%async_computation.3 | async-start | bytes 1048576 | tf_op jit(solution)/shard_map/all_to_all | solution.py:31
  89.2 9.3 %all-to-all-done.3.qd_ref = bf16[8,128,256]{2,1,0:T(8,128)(2,1)S(1)} async-done(((bf16[8,128,256]{2,1,0:T(8,128)(2,1)}), bf16[8,128,256]{2,1,0:T(8,128)(2,1)S(1)}, u32[]{:S(2)}, u32[]{:S(2)}) %all-to-all-start.3) | async-done | bytes 524320 | tf_op jit(solution)/shard_map/all_to_all | solution.py:31
  98.5 20.7 %all_to_all.65.kv_ref = bf16[8,128,256]{2,1,0:T(8,128)(2,1)S(1)} all-to-all(bf16[8,128,256]{2,1,0:T(8,128)(2,1)S(1)} %broadcast_in_dim.35), channel_id=1, replica_groups={{0,32,64,96,128,160,192,224},{8,40,72,104,136,168,200,232},{16,48,80,11..., dimensions={0} | all-to-all | bytes 1048576 | tf_op jit(solution)/shard_map/all_to_all | solution.py:35
  119.3 2.1 shard_map.77
  121.4 10.1 %all_to_all.66.stats_ref = f32[8,8,1024]{2,1,0:T(8,128)S(1)} all-to-all(f32[8,8,1024]{2,1,0:T(8,128)S(1)} %broadcast_in_dim.36), channel_id=1, replica_groups={{0,8,16,24,256,264,272,280},{32,40,48,56,288,296,304,312},{64,72,80,88,..., dimensions={0} | all-to-all | bytes 524288 | tf_op jit(solution)/shard_map/all_to_all | solution.py:31
  131.5 3.6 %shard_map.78 = (bf16[8,2,120,128]{3,2,1,0:T(8,128)(2,1)S(1)}, bf16[8,128,256]{2,1,0:T(8,128)(2,1)}) custom-call(bf16[8,128,256]{2,1,0:T(8,128)(2,1)S(1)} %all-to-all-done.3.qd_ref, bf16[8,128,256]{2,1,0:T(8,128)(2,1)S(1)} %all_to_all.65.kv_ref, f32[8,8,1024]{2,1,0:T(8,128)S(1)} %all_to_all.66.stats_ref), custom_call_target="tpu_custom_call" | custom-call | flops 1610612736 | bytes 1048576 | tf_op jit(solution)/shard_map/pallas_call | solution.py:188
  135.0 11.0 %all_to_all.67 = bf16[8,2,120,128]{3,2,1,0:T(8,128)(2,1)S(1)} all-to-all(bf16[8,2,120,128]{3,2,1,0:T(8,128)(2,1)S(1)} %get-tuple-element.5), channel_id=1, replica_groups={{0,8,16,24,256,264,272,280},{32,40,48,56,288,296,304,312},{64,72,80,88,..., dimensions={0} | all-to-all | bytes 983040 | tf_op jit(solution)/shard_map/all_to_all | solution.py:31
  146.1 3.5 %all-to-all-start.7 = ((bf16[8,128,256]{2,1,0:T(8,128)(2,1)}), bf16[8,128,256]{2,1,0:T(8,128)(2,1)S(1)}, u32[]{:S(2)}, u32[]{:S(2)}) async-start(bf16[8,128,256]{2,1,0:T(8,128)(2,1)} %get-tuple-element.6), calls=%async_computation.7 | async-start | bytes 1048576 | tf_op jit(solution)/shard_map/all_to_all | solution.py:35
  149.6 2.4 copy.78
  152.1 0.6 slice_bitcast_fusion
  152.7 10.7 %all-to-all-done.7 = bf16[8,128,256]{2,1,0:T(8,128)(2,1)S(1)} async-done(((bf16[8,128,256]{2,1,0:T(8,128)(2,1)}), bf16[8,128,256]{2,1,0:T(8,128)(2,1)S(1)}, u32[]{:S(2)}, u32[]{:S(2)}) %all-to-all-start.7) | async-done | bytes 524320 | tf_op jit(solution)/shard_map/all_to_all | solution.py:35
  163.5 0.1 copy.82
  163.6 0.1 copy.81
  163.7 0.6 fusion.3
  164.4 0.3 bitcast_convert_fusion
  164.7 0.9 pad_maximum_fusion
  165.6 4.7 %all-to-all-start.8 = ((bf16[8,2,128,128]{2,3,1,0:T(8,128)(2,1)}), bf16[8,2,128,128]{2,3,1,0:T(8,128)(2,1)}, u32[]{:S(2)}, u32[]{:S(2)}) async-start(bf16[8,2,128,128]{2,3,1,0:T(8,128)(2,1)} %bitcast.19), calls=%async_computation.8 | async-start | bytes 1048576 | tf_op jit(solution)/shard_map/all_to_all | solution.py:265
  170.3 1.7 convolution_convert_fusion
  172.0 2.4 copy.75
  174.4 0.5 reshape.72
  174.9 2.0 copy.76
  176.9 11.9 %all-to-all-done.8 = bf16[8,2,128,128]{2,3,1,0:T(8,128)(2,1)} async-done(((bf16[8,2,128,128]{2,3,1,0:T(8,128)(2,1)}), bf16[8,2,128,128]{2,3,1,0:T(8,128)(2,1)}, u32[]{:S(2)}, u32[]{:S(2)}) %all-to-all-start.8) | async-done | bytes 524320 | tf_op jit(solution)/shard_map/all_to_all | solution.py:265
  188.8 4.3 %all-to-all-start.11 = ((bf16[8,8,30,360]{3,1,2,0:T(8,128)(2,1)}), bf16[8,8,30,360]{3,1,2,0:T(8,128)(2,1)S(1)}, u32[]{:S(2)}, u32[]{:S(2)}) async-start(bf16[8,8,30,360]{3,1,2,0:T(8,128)(2,1)} %bitcast.27), calls=%async_computation.11 | async-start | bytes 2949120 | tf_op jit(solution)/shard_map/all_to_all | solution.py:31
  193.1 1.1 convert_reduce_fusion.1
  194.4 0.1 fusion.9
  194.5 4.0 %collective-permute-start.3 = (bf16[2,32,120]{2,1,0:T(8,128)(2,1)S(1)}, bf16[2,32,120]{2,1,0:T(8,128)(2,1)S(1)}, u32[]{:S(2)}, u32[]{:S(2)}) collective-permute-start(bf16[2,32,120]{2,1,0:T(8,128)(2,1)S(1)} %get-tuple-element.17), channel_id=1, source_target_pairs={{8,0},{16,8},{24,16},{32,24},{40,32},{48,40},{56,48},{64,56},{72,6... | collective-permute-start | bytes 46088 | tf_op jit(solution)/shard_map/ppermute | solution.py:112
  198.6 1.9 collective-permute-start.2
  200.5 10.1 %collective-permute-done.3 = bf16[2,32,120]{2,1,0:T(8,128)(2,1)S(1)} collective-permute-done((bf16[2,32,120]{2,1,0:T(8,128)(2,1)S(1)}, bf16[2,32,120]{2,1,0:T(8,128)(2,1)S(1)}, u32[]{:S(2)}, u32[]{:S(2)}) %collective-permute-start.3) | collective-permute-done | bytes 15392 | tf_op jit(solution)/shard_map/ppermute | solution.py:112
  210.6 1.0 collective-permute-done.2
  211.6 0.2 all-to-all-done.11
  211.8 1.0 broadcast_in_dim.39
  212.8 4.2 %all-to-all-start.9 = ((bf16[8,2,192,120]{3,2,1,0:T(8,128)(2,1)}), bf16[8,2,192,120]{3,2,1,0:T(8,128)(2,1)S(1)}, u32[]{:S(2)}, u32[]{:S(2)}) async-start(bf16[8,2,192,120]{3,2,1,0:T(8,128)(2,1)} %broadcast_in_dim.39), calls=%async_computation.9 | async-start | bytes 1572864 | tf_op jit(solution)/shard_map/all_to_all | solution.py:31
  217.1 0.3 reduce_sum.127
  217.3 0.7 copy.77
  218.0 10.7 %all-to-all-done.9.x_ref = bf16[8,2,192,120]{3,2,1,0:T(8,128)(2,1)S(1)} async-done(((bf16[8,2,192,120]{3,2,1,0:T(8,128)(2,1)}), bf16[8,2,192,120]{3,2,1,0:T(8,128)(2,1)S(1)}, u32[]{:S(2)}, u32[]{:S(2)}) %all-to-all-start.9) | async-done | bytes 737312 | tf_op jit(solution)/shard_map/all_to_all | solution.py:31
  228.7 3.4 %all-to-all-start.12 = ((bf16[8,30,360]{2,1,0:T(8,128)(2,1)}), bf16[8,30,360]{2,1,0:T(8,128)(2,1)S(1)}, u32[]{:S(2)}, u32[]{:S(2)}) async-start(bf16[8,30,360]{2,1,0:T(8,128)(2,1)} %copy.77), calls=%async_computation.12 | async-start | bytes 393216 | tf_op jit(solution)/shard_map/all_to_all | solution.py:35
  232.1 4.9 %shard_map.79 = bf16[8,2,128,120]{3,2,1,0:T(8,128)(2,1)S(1)} custom-call(s32[6]{0:T(128)S(1)} %get-tuple-element.24.sc_ref, bf16[8,2,192,120]{3,2,1,0:T(8,128)(2,1)S(1)} %all-to-all-done.9.x_ref, bf16[8,2,120,120]{3,2,1,0:T(8,128)(2,1)S(1)} %all-to-all-done.1.w_ref), custom_call_target="tpu_custom_call" | custom-call | flops 471859200 | bytes 1048576 | tf_op jit(solution)/shard_map/pallas_call | solution.py:98
  237.0 1.0 copy.72
  238.0 4.6 %all-to-all-done.12 = bf16[8,30,360]{2,1,0:T(8,128)(2,1)S(1)} async-done(((bf16[8,30,360]{2,1,0:T(8,128)(2,1)}), bf16[8,30,360]{2,1,0:T(8,128)(2,1)S(1)}, u32[]{:S(2)}, u32[]{:S(2)}) %all-to-all-start.12) | async-done | bytes 172832 | tf_op jit(solution)/shard_map/all_to_all | solution.py:35
  242.6 4.5 %all-to-all-start.10 = ((bf16[8,2,128,120]{2,3,1,0:T(8,128)(2,1)}), bf16[8,2,128,120]{2,3,1,0:T(8,128)(2,1)S(1)}, u32[]{:S(2)}, u32[]{:S(2)}) async-start(bf16[8,2,128,120]{2,3,1,0:T(8,128)(2,1)} %copy.72), calls=%async_computation.10 | async-start | bytes 983040 | tf_op jit(solution)/shard_map/all_to_all | solution.py:31
  247.1 0.7 convert_reduce_fusion.4
  247.8 6.5 %all-to-all-done.10 = bf16[8,2,128,120]{2,3,1,0:T(8,128)(2,1)S(1)} async-done(((bf16[8,2,128,120]{2,3,1,0:T(8,128)(2,1)}), bf16[8,2,128,120]{2,3,1,0:T(8,128)(2,1)S(1)}, u32[]{:S(2)}, u32[]{:S(2)}) %all-to-all-start.10) | async-done | bytes 491552 | tf_op jit(solution)/shard_map/all_to_all | solution.py:31
  254.5 0.1 fusion.12
  254.6 0.7 copy.74
  (54 shorter events, 1.6 us)
Async XLA Ops:
  0.6 12.0 %copy-start.5 = (bf16[128,240]{0,1:T(8,128)(2,1)S(1)}, bf16[128,240]{0,1:T(8,128)(2,1)}, u32[]{:S(2)}) copy-start(bf16[128,240]{0,1:T(8,128)(2,1)} %param.5) | copy-start | bytes 184324
  2.3 27.7 %all-to-all-start.1 = ((bf16[8,2,120,120]{3,2,1,0:T(8,128)(2,1)}), bf16[8,2,120,120]{3,2,1,0:T(8,128)(2,1)S(1)}, u32[]{:S(2)}, u32[]{:S(2)}) async-start(bf16[8,2,120,120]{3,2,1,0:T(8,128)(2,1)} %broadcast_in_dim.30), calls=%async_computation.1 | async-start | bytes 983040 | tf_op jit(solution)/shard_map/all_to_all | solution.py:35
  12.6 23.6 %copy-start.7 = (s32[4]{0:T(128)S(1)}, s32[4]{0:T(128)}, u32[]{:S(2)}) copy-start(s32[4]{0:T(128)} %param.8) | copy-start | bytes 52
  12.8 52.6 %copy-start.3 = (bf16[128,2,120]{2,0,1:T(8,128)(2,1)}, bf16[128,2,120]{2,0,1:T(8,128)(2,1)S(1)}, u32[]{:S(2)}) copy-start(bf16[128,2,120]{2,0,1:T(8,128)(2,1)S(1)} %copy.62) | copy-start | bytes 184324
  12.8 9.2 %collective-permute-start.1 = (bf16[2,32,120]{2,1,0:T(8,128)(2,1)S(1)}, bf16[2,32,120]{2,1,0:T(8,128)(2,1)S(1)}, u32[]{:S(2)}, u32[]{:S(2)}) collective-permute-start(bf16[2,32,120]{2,1,0:T(8,128)(2,1)S(1)} %get-tuple-element.21), channel_id=1, source_target_pairs={{8,0},{16,8},{24,16},{32,24},{40,32},{48,40},{56,48},{64,56},{72,6... | collective-permute-start | bytes 46088 | tf_op jit(solution)/shard_map/ppermute | solution.py:112
  20.0 10.0 %collective-permute-start = (bf16[2,32,120]{2,1,0:T(8,128)(2,1)S(1)}, bf16[2,32,120]{2,1,0:T(8,128)(2,1)S(1)}, u32[]{:S(2)}, u32[]{:S(2)}) collective-permute-start(bf16[2,32,120]{2,1,0:T(8,128)(2,1)S(1)} %get-tuple-element.20), channel_id=1, source_target_pairs={{0,8},{8,16},{16,24},{24,32},{32,40},{40,48},{48,56},{56,64},{64,7... | collective-permute-start | bytes 46088 | tf_op jit(solution)/shard_map/ppermute | solution.py:111
  31.1 16.8 %all-to-all-start = ((bf16[8,2,192,120]{3,2,1,0:T(8,128)(2,1)}), bf16[8,2,192,120]{3,2,1,0:T(8,128)(2,1)S(1)}, u32[]{:S(2)}, u32[]{:S(2)}) async-start(bf16[8,2,192,120]{3,2,1,0:T(8,128)(2,1)} %broadcast_in_dim.28), calls=%async_computation | async-start | bytes 1572864 | tf_op jit(solution)/shard_map/all_to_all | solution.py:31
  52.6 12.6 %all-to-all-start.2 = ((bf16[8,2,128,120]{2,3,1,0:T(8,128)(2,1)}), bf16[8,2,128,120]{2,3,1,0:T(8,128)(2,1)S(1)}, u32[]{:S(2)}, u32[]{:S(2)}) async-start(bf16[8,2,128,120]{2,3,1,0:T(8,128)(2,1)} %copy.63), calls=%async_computation.2 | async-start | bytes 983040 | tf_op jit(solution)/shard_map/all_to_all | solution.py:31
  65.3 17.7 %copy-start = (bf16[1920,360]{0,1:T(8,128)(2,1)S(1)}, bf16[1920,360]{0,1:T(8,128)(2,1)}, u32[]{:S(2)}) copy-start(bf16[1920,360]{0,1:T(8,128)(2,1)} %param.7) | copy-start | bytes 4147204
  65.4 17.4 %copy-start.1 = (f32[2,128,120]{2,1,0:T(8,128)}, f32[2,128,120]{2,1,0:T(8,128)S(1)}, u32[]{:S(2)}) copy-start(f32[2,128,120]{2,1,0:T(8,128)S(1)} %copy.79) | copy-start | bytes 368644
  82.8 0.8 copy-start.6
  84.7 13.8 %all-to-all-start.3 = ((bf16[8,128,256]{2,1,0:T(8,128)(2,1)}), bf16[8,128,256]{2,1,0:T(8,128)(2,1)S(1)}, u32[]{:S(2)}, u32[]{:S(2)}) async-start(bf16[8,128,256]{2,1,0:T(8,128)(2,1)} %broadcast_in_dim.32), calls=%async_computation.3 | async-start | bytes 1048576 | tf_op jit(solution)/shard_map/all_to_all | solution.py:31
  146.1 17.3 %all-to-all-start.7 = ((bf16[8,128,256]{2,1,0:T(8,128)(2,1)}), bf16[8,128,256]{2,1,0:T(8,128)(2,1)S(1)}, u32[]{:S(2)}, u32[]{:S(2)}) async-start(bf16[8,128,256]{2,1,0:T(8,128)(2,1)} %get-tuple-element.6), calls=%async_computation.7 | async-start | bytes 1048576 | tf_op jit(solution)/shard_map/all_to_all | solution.py:35
  165.6 23.2 %all-to-all-start.8 = ((bf16[8,2,128,128]{2,3,1,0:T(8,128)(2,1)}), bf16[8,2,128,128]{2,3,1,0:T(8,128)(2,1)}, u32[]{:S(2)}, u32[]{:S(2)}) async-start(bf16[8,2,128,128]{2,3,1,0:T(8,128)(2,1)} %bitcast.19), calls=%async_computation.8 | async-start | bytes 1048576 | tf_op jit(solution)/shard_map/all_to_all | solution.py:265
  188.8 5.6 %copy-start.2 = (f32[2,128,120]{2,1,0:T(8,128)S(1)}, f32[2,128,120]{2,1,0:T(8,128)}, u32[]{:S(2)}) copy-start(f32[2,128,120]{2,1,0:T(8,128)} %copy-done.1) | copy-start | bytes 368644
  188.8 5.6 %copy-start.4 = (bf16[128,2,120]{2,0,1:T(8,128)(2,1)S(1)}, bf16[128,2,120]{2,0,1:T(8,128)(2,1)}, u32[]{:S(2)}) copy-start(bf16[128,2,120]{2,0,1:T(8,128)(2,1)} %copy-done.3) | copy-start | bytes 184324
  188.8 23.0 %all-to-all-start.11 = ((bf16[8,8,30,360]{3,1,2,0:T(8,128)(2,1)}), bf16[8,8,30,360]{3,1,2,0:T(8,128)(2,1)S(1)}, u32[]{:S(2)}, u32[]{:S(2)}) async-start(bf16[8,8,30,360]{3,1,2,0:T(8,128)(2,1)} %bitcast.27), calls=%async_computation.11 | async-start | bytes 2949120 | tf_op jit(solution)/shard_map/all_to_all | solution.py:31
  194.5 16.0 %collective-permute-start.3 = (bf16[2,32,120]{2,1,0:T(8,128)(2,1)S(1)}, bf16[2,32,120]{2,1,0:T(8,128)(2,1)S(1)}, u32[]{:S(2)}, u32[]{:S(2)}) collective-permute-start(bf16[2,32,120]{2,1,0:T(8,128)(2,1)S(1)} %get-tuple-element.17), channel_id=1, source_target_pairs={{8,0},{16,8},{24,16},{32,24},{40,32},{48,40},{56,48},{64,56},{72,6... | collective-permute-start | bytes 46088 | tf_op jit(solution)/shard_map/ppermute | solution.py:112
  198.6 13.0 %collective-permute-start.2 = (bf16[2,32,120]{2,1,0:T(8,128)(2,1)S(1)}, bf16[2,32,120]{2,1,0:T(8,128)(2,1)S(1)}, u32[]{:S(2)}, u32[]{:S(2)}) collective-permute-start(bf16[2,32,120]{2,1,0:T(8,128)(2,1)S(1)} %get-tuple-element.16), channel_id=1, source_target_pairs={{0,8},{8,16},{16,24},{24,32},{32,40},{40,48},{48,56},{56,64},{64,7... | collective-permute-start | bytes 46088 | tf_op jit(solution)/shard_map/ppermute | solution.py:111
  212.8 15.9 %all-to-all-start.9 = ((bf16[8,2,192,120]{3,2,1,0:T(8,128)(2,1)}), bf16[8,2,192,120]{3,2,1,0:T(8,128)(2,1)S(1)}, u32[]{:S(2)}, u32[]{:S(2)}) async-start(bf16[8,2,192,120]{3,2,1,0:T(8,128)(2,1)} %broadcast_in_dim.39), calls=%async_computation.9 | async-start | bytes 1572864 | tf_op jit(solution)/shard_map/all_to_all | solution.py:31
  228.7 13.9 %all-to-all-start.12 = ((bf16[8,30,360]{2,1,0:T(8,128)(2,1)}), bf16[8,30,360]{2,1,0:T(8,128)(2,1)S(1)}, u32[]{:S(2)}, u32[]{:S(2)}) async-start(bf16[8,30,360]{2,1,0:T(8,128)(2,1)} %copy.77), calls=%async_computation.12 | async-start | bytes 393216 | tf_op jit(solution)/shard_map/all_to_all | solution.py:35
  242.6 11.7 %all-to-all-start.10 = ((bf16[8,2,128,120]{2,3,1,0:T(8,128)(2,1)}), bf16[8,2,128,120]{2,3,1,0:T(8,128)(2,1)S(1)}, u32[]{:S(2)}, u32[]{:S(2)}) async-start(bf16[8,2,128,120]{2,3,1,0:T(8,128)(2,1)} %copy.72), calls=%async_computation.10 | async-start | bytes 983040 | tf_op jit(solution)/shard_map/all_to_all | solution.py:31

commit v2 on v1

v2 whole, which is shorter than its diff:
```python
import functools
import math

import jax
import jax.numpy as jnp
from jax import lax
from jax.experimental import pallas as pl
from jax.experimental.pallas import tpu as pltpu
from jax.sharding import PartitionSpec as P

HD = 120
KERNEL = 64
HALF = KERNEL // 2
ROWS = 128
LANES = 128
SCALE = HD ** (-0.5)
SCALE2 = SCALE * math.log2(math.e)
FAR = -(2.0**100)
EPS = 1e-05
INV_ROOT_TWO = 0.7071067811865476
INV_ROOT_TAU = 0.3989422804014327

BF = jnp.bfloat16
F32 = jnp.float32

XY_GROUPS = [[y * 32 + z * 4 + x for y in range(2) for x in range(4)] for z in range(8)]
X_GROUPS = [[y * 32 + z * 4 + x for x in range(4)] for y in range(2) for z in range(8)]
Z_GROUPS = [[y * 32 + z * 4 + x for z in range(8)] for y in range(2) for x in range(4)]


def exchange_xy(parts):
    return lax.all_to_all(parts, "tm", 0, 0, axis_index_groups=XY_GROUPS)


def exchange_x(parts):
    return lax.all_to_all(parts, "tm", 0, 0, axis_index_groups=X_GROUPS)


def swap(array, bit):
    return lax.ppermute(array, "tm", [(i, i ^ bit) for i in range(64)])


def exchange_z(parts):
    return lax.all_to_all(parts, "tm", 0, 0, axis_index_groups=Z_GROUPS)


def everyone(array, count=8):
    return jnp.broadcast_to(array[None], (count,) + array.shape)


BITS = (32, 2, 1)
SLOTS = (0, 4, 2, 6, 1, 5, 3, 7)


def doubled(array):
    array = array[None]
    for bit in BITS:
        array = jnp.concatenate([array, swap(array, bit)], axis=0)
    return array


def halved(array):
    for bit in BITS[::-1]:
        half = array.shape[0] // 2
        array = array[:half] + swap(array[half:], bit)
    return array[0]


def vmem_call(body, out_shape, scratch=(), scalars=0, inputs=0, flops=0):
    return pl.pallas_call(
        body,
        out_shape=out_shape,
        in_specs=[pl.BlockSpec(memory_space=pltpu.SMEM)] * scalars
        + [pl.BlockSpec(memory_space=pltpu.VMEM)] * inputs,
        out_specs=jax.tree.map(lambda _: pl.BlockSpec(memory_space=pltpu.VMEM), out_shape),
        scratch_shapes=list(scratch),
        compiler_params=pltpu.CompilerParams(vmem_limit_bytes=48 * 1024 * 1024),
        cost_estimate=pl.CostEstimate(flops=flops, bytes_accessed=1 << 20, transcendentals=0),
    )


def bounds_of(pos, ends):
    low = jnp.zeros_like(pos)
    high = jnp.full_like(pos, ends[0])
    for u in range(3):
        inside = pos >= ends[u]
        low = jnp.where(inside, ends[u], low)
        high = jnp.where(inside, ends[u + 1], high)
    return low, high


PADDED = ROWS + KERNEL


def conv_body(sc_ref, x_ref, w_ref, out_ref):
    first = sc_ref[0]
    ends = [sc_ref[4 + u] for u in range(4)]
    row = lax.broadcasted_iota(jnp.int32, (ROWS, HD), 0)

    def block(b, carry):
        y = (b // 4) ^ sc_ref[2]
        x_at = b % 4
        pos = (y * 32 + sc_ref[1] + x_at) * ROWS + row
        low, high = bounds_of(pos, ends)
        source = pos - HALF + first
        keep = [
            ((source + 4 * s) >= low) & ((source + 4 * s) < high) for s in range(8)
        ]
        for g in range(2):
            x = x_ref[x_at, b // 4, g * PADDED : (g + 1) * PADDED].astype(F32)
            even = pltpu.roll(x, PADDED - first, 0)
            odd = pltpu.roll(x, PADDED - first - 4, 0)
            total = jnp.zeros((ROWS, HD), F32)
            for s in range(8):
                rolled = odd if s % 2 else even
                start = 8 * (s // 2)
                piece = jnp.where(keep[s], rolled[start : start + ROWS], 0.0).astype(BF)
                total += jnp.dot(piece, w_ref[s, g], preferred_element_type=F32)
            out_ref[y * 4 + x_at, g] = total.astype(BF)
        return carry

    lax.fori_loop(0, 8, block, 0)


def conv_partial(scalars, gathered, taps):
    return vmem_call(
        conv_body,
        jax.ShapeDtypeStruct((8, 2, ROWS, HD), BF),
        scalars=1,
        inputs=2,
        flops=8 * 2 * 8 * 2 * ROWS * HD * HD,
    )(scalars, gathered, taps)


def back_body(sc_ref, e_ref, w_ref, out_ref):
    ends = [sc_ref[1 + u] for u in range(4)]
    pos = sc_ref[0] * ROWS + lax.broadcasted_iota(jnp.int32, (ROWS, HD), 0)
    low, high = bounds_of(pos, ends)
    errors = [e_ref[g].astype(F32) for g in range(2)]
    totals = [jnp.zeros((ROWS, HD), F32) for g in range(2)]
    for rest in range(8):
        rolled = [pltpu.roll(e, PADDED - rest, 0) if rest else e for e in errors]
        for start in range(0, KERNEL + 1, 8):
            tap = KERNEL - start - rest
            if not 0 <= tap < KERNEL:
                continue
            source = pos + (HALF - tap)
            keep = (source >= low) & (source < high)
            y, z, x = tap // 32, tap % 32 // 4, tap % 4
            for g in range(2):
                piece = jnp.where(keep, rolled[g][start : start + ROWS], 0.0).astype(BF)
                totals[g] += lax.dot_general(
                    piece,
                    w_ref[y * 4 + x, z, g],
                    (((1,), (1,)), ((), ())),
                    preferred_element_type=F32,
                )
    for g in range(2):
        out_ref[g] = totals[g]


def conv_back(scalars, errors, taps):
    return vmem_call(
        back_body,
        jax.ShapeDtypeStruct((2, ROWS, HD), F32),
        scalars=1,
        inputs=2,
        flops=64 * 2 * 2 * ROWS * HD * HD,
    )(scalars, errors, taps)


def with_halo(rows):
    devices = 64
    up = [(i, i + 1) for i in range(devices - 1)]
    down = [(i + 1, i) for i in range(devices - 1)]
    before = lax.ppermute(rows[:, ROWS - HALF :], "tm", up)
    after = lax.ppermute(rows[:, :HALF], "tm", down)
    return jnp.concatenate([before, rows, after], axis=1)


CHUNK = 256


N = CHUNK // ROWS
ALL = 8 * ROWS
CONTRACT = (((1,), (1,)), ((), ()))


def upstream_rows(sc_ref, f_ref, d_ref):
    for i, e in enumerate(SLOTS):
        d_ref[i * ROWS : (i + 1) * ROWS] = f_ref[sc_ref[1] ^ (e % 4), e // 4, 2 * PADDED :]


def scored(c, q_ref, kv_ref, d_ref):
    keys = kv_ref[:, :, :LANES].reshape(ALL, LANES)
    values = kv_ref[:, :, LANES : LANES + HD].reshape(ALL, HD)
    q = q_ref[c * N : (c + 1) * N].reshape(CHUNK, LANES)
    d = d_ref[c * CHUNK : (c + 1) * CHUNK]
    scores = lax.dot_general(keys, q, CONTRACT, preferred_element_type=F32)
    dprobs = lax.dot_general(values, d, CONTRACT, preferred_element_type=F32)
    return keys, values, q, d, scores * SCALE2, dprobs


def stats_body(sc_ref, q_ref, kv_ref, f_ref, out_ref, d_ref):
    upstream_rows(sc_ref, f_ref, d_ref)
    for c in range(ALL // CHUNK):
        _, _, _, _, scores, dprobs = scored(c, q_ref, kv_ref, d_ref)
        peak = jnp.max(scores, axis=0, keepdims=True)
        weight = jnp.exp2(scores - peak)
        total = jnp.sum(weight, axis=0, keepdims=True)
        along = jnp.sum(weight * dprobs, axis=0, keepdims=True)
        rows = jnp.concatenate([peak, total, along, jnp.zeros((5, CHUNK), F32)], axis=0)
        for i in range(N):
            out_ref[sc_ref[0] ^ SLOTS[c * N + i]] = rows[:, i * ROWS : (i + 1) * ROWS]


def grads_body(
    sc_ref, q_ref, kv_ref, f_ref, stats_ref, od_ref, dkv_ref, d_ref, dk_ref, dv_ref
):
    upstream_rows(sc_ref, f_ref, d_ref)
    for c in range(ALL // CHUNK):
        stats = jnp.concatenate(
            [stats_ref[:, sc_ref[0] ^ SLOTS[c * N + i]] for i in range(N)], axis=2
        )
        peaks = stats[:, 0]
        top = jnp.max(peaks, axis=0, keepdims=True)
        factor = jnp.exp2(peaks - top)
        total = jnp.sum(stats[:, 1] * factor, axis=0, keepdims=True)
        delta = jnp.sum(stats[:, 2] * factor, axis=0, keepdims=True) / total
        lse = top + jnp.log2(total)
        keys, values, q, d, scores, dprobs = scored(c, q_ref, kv_ref, d_ref)
        probs = jnp.exp2(scores - lse)
        dscores = (probs * (dprobs - delta)).astype(BF)
        probs = probs.astype(BF)
        dv = jnp.dot(probs, d, preferred_element_type=F32)
        dk = jnp.dot(dscores, q, preferred_element_type=F32)
        if c == 0:
            dv_ref[...] = dv
            dk_ref[...] = dk
        else:
            dv_ref[...] += dv
            dk_ref[...] += dk
        inner = (((0,), (0,)), ((), ()))
        out_t = lax.dot_general(values, probs, inner, preferred_element_type=F32)
        dq_t = lax.dot_general(keys, dscores, inner, preferred_element_type=F32) * SCALE
        for i in range(N):
            od_ref[0, c * N + i] = out_t[:, i * ROWS : (i + 1) * ROWS].astype(BF)
            od_ref[1, c * N + i] = dq_t[:HD, i * ROWS : (i + 1) * ROWS].astype(BF)
    for i in range(8):
        piece = slice(i * ROWS, (i + 1) * ROWS)
        dkv_ref[i, :, :LANES] = (dk_ref[piece] * SCALE).astype(BF)
        dkv_ref[i, :, LANES : LANES + HD] = dv_ref[piece].astype(BF)
        dkv_ref[i, :, LANES + HD :] = jnp.zeros((ROWS, LANES - HD), BF)


def attention_stats(scalars, queries, keys, gathered):
    return vmem_call(
        stats_body,
        jax.ShapeDtypeStruct((8, 8, ROWS), F32),
        scratch=[pltpu.VMEM((ALL, HD), BF)],
        scalars=1,
        inputs=3,
        flops=2 * 2 * ALL * ALL * LANES,
    )(scalars, queries, keys, gathered)


def attention_grads(scalars, queries, keys, gathered, stats):
    return vmem_call(
        grads_body,
        (
            jax.ShapeDtypeStruct((2, 8, HD, ROWS), BF),
            jax.ShapeDtypeStruct((8, ROWS, 2 * LANES), BF),
        ),
        scratch=[
            pltpu.VMEM((ALL, HD), BF),
            pltpu.VMEM((ALL, LANES), F32),
            pltpu.VMEM((ALL, HD), F32),
        ],
        scalars=1,
        inputs=4,
        flops=6 * 2 * ALL * ALL * LANES,
    )(scalars, queries, keys, gathered, stats)


def gelu_parts(inputs):
    normal_cdf = 0.5 * (1.0 + lax.erf(inputs * INV_ROOT_TWO))
    density = jnp.exp(-0.5 * inputs * inputs) * INV_ROOT_TAU
    return inputs * normal_cdf, normal_cdf + inputs * density


def on_device(frames, conv_weight, w_qkv, lengths, grad_out):
    index = lax.axis_index("tm")
    y, x = index // 32, index % 4
    z_base = index % 32 - x
    place = y * 4 + x
    ends = jnp.cumsum(lengths).astype(jnp.int32)
    groups = 2
    width = w_qkv.shape[0]

    def scalars(*first):
        return jnp.concatenate([jnp.stack(first).astype(jnp.int32), ends])

    frames_g = frames.reshape(ROWS, groups, HD).transpose(1, 0, 2)
    frames_pad = with_halo(frames_g).reshape(groups * PADDED, HD)
    taps = exchange_z(everyone(conv_weight[0]))
    pair = jnp.concatenate([frames_pad, grad_out], axis=0)
    pair = jnp.stack([pair, swap(pair, 32)])
    gathered = exchange_x(everyone(pair, 4))
    conv = conv_partial(scalars(y * 32 + x, z_base, y, x), gathered, taps)
    conv = exchange_xy(conv)
    conv = jnp.sum(conv.astype(F32), axis=0)
    activated, slope = gelu_parts(conv)
    hidden = frames_g.astype(F32) + activated
    all_taps = lax.all_gather(taps, "tm", axis=0, axis_index_groups=XY_GROUPS)

    hidden_all = lax.all_gather(hidden.astype(BF), "head", axis=0, tiled=True).astype(F32)
    center = jnp.sum(hidden_all, axis=(0, 2)) / width
    square = jnp.sum(hidden_all * hidden_all, axis=(0, 2)) / width
    inv_std = lax.rsqrt(square - center * center + EPS)
    normed = ((hidden_all - center[:, None]) * inv_std[:, None]).astype(BF)
    unit = (hidden - center[:, None]) * inv_std[:, None]
    weights = w_qkv.reshape(16, HD, 3 * HD)
    normed_rows = normed.transpose(1, 0, 2).reshape(ROWS, width)
    projected = jnp.dot(normed_rows, w_qkv, preferred_element_type=F32).astype(BF)

    pos = index * ROWS + jnp.arange(ROWS, dtype=jnp.int32)
    seg = jnp.sum((pos[:, None] >= ends[None, :3]).astype(jnp.int32), axis=1)
    same = seg[:, None] == jnp.arange(8, dtype=jnp.int32)[None]
    q_mark = same.astype(BF)
    k_mark = jnp.where(same, 0.0, FAR).astype(BF)
    nil = jnp.zeros((ROWS, 8), BF)
    queries = jnp.concatenate([projected[:, :HD], q_mark], axis=1)
    keys = jnp.concatenate(
        [projected[:, HD : 2 * HD], k_mark, projected[:, 2 * HD :], nil], axis=1
    )
    keys_all = exchange_z(everyone(keys))
    queries_all = doubled(queries)
    where = scalars(place, x)
    stats = attention_stats(where, queries_all, keys_all, gathered)
    stats = exchange_xy(everyone(stats))
    od, dkv = attention_grads(where, queries_all, keys_all, gathered, stats)
    dkv = jnp.sum(exchange_z(dkv).astype(F32), axis=0).astype(BF)
    grad_q = halved(od[1])
    attended = halved(od[0]).T
    grad_joined = jnp.concatenate([grad_q.T, dkv[:, :HD], dkv[:, LANES : LANES + HD]], axis=1)

    share = jnp.einsum("tj,gcj->gtc", grad_joined, weights, preferred_element_type=F32)
    plain = jnp.sum(share, axis=(0, 2))
    along = jnp.sum(share * normed.astype(F32), axis=(0, 2))
    sums = jnp.stack([plain, along], axis=1)
    sums_high = sums.astype(BF)
    sums_low = (sums - sums_high.astype(F32)).astype(BF)
    sums = jnp.concatenate([sums_high, sums_low, jnp.zeros((ROWS, 4), BF)], axis=1)
    parts = jnp.concatenate(
        [share.astype(BF), jnp.broadcast_to(sums[None], (16, ROWS, 8))], axis=2
    ).reshape(8, groups, ROWS, LANES)
    parts = lax.all_to_all(parts, "head", 0, 0)
    parts = jnp.sum(parts.astype(F32), axis=0)
    feature = parts[:, :, :HD]
    plain = parts[0, :, HD] + parts[0, :, HD + 2]
    along = parts[0, :, HD + 1] + parts[0, :, HD + 3]
    hidden_grad = inv_std[:, None] * (
        feature - plain[:, None] / width - unit * (along[:, None] / width)
    )

    error = (slope * hidden_grad).astype(BF)
    back = conv_back(scalars(index), with_halo(error), all_taps)
    frame_grad = hidden_grad + back
    frame_grad = frame_grad.astype(BF).transpose(1, 0, 2).reshape(ROWS, groups * HD)

    wide = lax.dot_general(
        normed_rows, grad_joined, (((0,), (0,)), ((), ())), preferred_element_type=F32
    ).astype(BF)
    slab = width // 64
    wide = wide.reshape(2, 8, 4, slab, 3 * HD).transpose(0, 2, 1, 3, 4)
    wide = exchange_xy(wide.reshape(8, 8, slab, 3 * HD))
    wide = jnp.sum(wide.astype(F32), axis=0).astype(BF)
    weight_grad = jnp.sum(exchange_z(wide).astype(F32), axis=0)
    return attended, frame_grad, weight_grad


def solution(mesh):
    return jax.shard_map(
        on_device,
        mesh=mesh,
        in_specs=(
            P("tm", "head"),
            P("tm", "head", None, None),
            P(None, "head"),
            P(),
            P("tm", "head"),
        ),
        out_specs=(P("tm", "head"), P("tm", "head"), P("tm", "head")),
        check_vma=False,
    )
```

time: 257 us -> 280 us (1.089)
  starting transfers between devices: 63.8 us -> 95.8 us
  blocking collectives: 58.8 us -> 32.7 us
  between operations: 1.05 us -> 14.5 us
    ppermute x0 -> x10, waiting for transfers between devices: none -> 47.4 us  [swap(): return lax.ppermute(array, 'tm', [(i, i ^ bit) for i in range(64)])]
    all_to_all x6 -> x3, waiting for transfers between devices: 46.3 us -> 11.9 us  [exchange_xy(): return lax.all_to_all(parts, 'tm', 0, 0, axis_index_groups=XY_GROUPS)]
    ppermute x0 -> x10, starting transfers between devices: none -> 30.2 us  [swap(): return lax.ppermute(array, 'tm', [(i, i ^ bit) for i in range(64)])]
    all_to_all x3 -> x1, blocking collectives: 41.9 us -> 15.1 us  [exchange_x(): return lax.all_to_all(parts, 'tm', 0, 0, axis_index_groups=X_GROUPS)]
    all_to_all x6 -> x3, starting transfers between devices: 26.8 us -> 14.1 us  [exchange_xy(): return lax.all_to_all(parts, 'tm', 0, 0, axis_index_groups=XY_GROUPS)]
    ppermute x2, waiting for transfers between devices: 10.1 us -> 0.55 us  [with_halo(): after = lax.ppermute(rows[:, :HALF], 'tm', down)]
    ppermute x2, waiting for transfers between devices: 9.03 us -> 0.01 us  [with_halo(): before = lax.ppermute(rows[:, ROWS - HALF:], 'tm', up)]
    ppermute x2, starting transfers between devices: 11.3 us -> 19.2 us  [with_halo(): after = lax.ppermute(rows[:, :HALF], 'tm', down)]
  transfers between devices with their start and end apart: 14 -> 23, of which waited for: 12 -> 14; matrix products, arithmetic and copies ran while one was open for 6% -> 6% of each run, Pallas kernels for 2% -> 2%
where the time goes in v2:
time: 280 us; the launch traced here: 279 us
  starting transfers between devices  95.8 us (34%)
  waiting for transfers between devices  94.4 us (34%)
  blocking collectives  32.7 us (12%)
  local copies, waits for them, and re-layouts  17.8 us (6%)
  between operations  14.5 us (5%)
  Pallas kernels  14 us (5%)
  other arithmetic  6.45 us (2%)
  matrix products  2.89 us (1%)
    ppermute x10, waiting for transfers between devices, swap(): return lax.ppermute(array, 'tm', [(i, i ^ bit) for i in range(64)])  47.4 us
    ppermute x10, starting transfers between devices, swap(): return lax.ppermute(array, 'tm', [(i, i ^ bit) for i in range(64)])  30.2 us
    all_to_all x4, starting transfers between devices, exchange_z(): return lax.all_to_all(parts, 'tm', 0, 0, axis_index_groups=Z_GROUPS)  22.1 us
    all_to_all x4, waiting for transfers between devices, exchange_z(): return lax.all_to_all(parts, 'tm', 0, 0, axis_index_groups=Z_GROUPS)  21.2 us
    ppermute x2, starting transfers between devices, with_halo(): after = lax.ppermute(rows[:, :HALF], 'tm', down)  19.2 us
    all_gather x1, blocking collectives, on_device(): lax.all_gather(hidden.astype(BF), 'head', axis=0, tiled=True).astype(F32)  17.6 us
    all_to_all x1, blocking collectives, exchange_x(): return lax.all_to_all(parts, 'tm', 0, 0, axis_index_groups=X_GROUPS)  15.1 us
    all_to_all x3, starting transfers between devices, exchange_xy(): return lax.all_to_all(parts, 'tm', 0, 0, axis_index_groups=XY_GROUPS)  14.1 us
  transfers between devices with their start and end apart: 23, of which 14 were waited for; matrix products, arithmetic and copies ran while one was open for 6% of the time, Pallas kernels for 2%

profile of v2, /device:TPU:8, one launch (start us, length us, event | category | flops | bytes accessed | tf_op | source)
XLA Modules:
  0.0 278.5 jit_solution(16696580357572008067)
XLA Ops:
  7.2 0.9 copy.62
  8.1 3.4 %collective-permute-start = (bf16[2,32,120]{2,1,0:T(8,128)(2,1)S(1)}, bf16[2,32,120]{2,1,0:T(8,128)(2,1)S(1)}, u32[]{:S(2)}, u32[]{:S(2)}) collective-permute-start(bf16[2,32,120]{2,1,0:T(8,128)(2,1)S(1)} %get-tuple-element.26), channel_id=1, source_target_pairs={{0,8},{8,16},{16,24},{24,32},{32,40},{40,48},{48,56},{56,64},{64,7... | collective-permute-start | bytes 46088 | tf_op jit(solution)/shard_map/ppermute | solution.py:176
  11.5 11.6 %collective-permute-start.1 = (bf16[2,32,120]{2,1,0:T(8,128)(2,1)S(1)}, bf16[2,32,120]{2,1,0:T(8,128)(2,1)S(1)}, u32[]{:S(2)}, u32[]{:S(2)}) collective-permute-start(bf16[2,32,120]{2,1,0:T(8,128)(2,1)S(1)} %get-tuple-element.27), channel_id=1, source_target_pairs={{8,0},{16,8},{24,16},{32,24},{40,32},{48,40},{56,48},{64,56},{72,6... | collective-permute-start | bytes 46088 | tf_op jit(solution)/shard_map/ppermute | solution.py:177
  23.1 0.9 copy.63
  24.0 0.5 collective-permute-done.1
  24.6 1.9 collective-permute-start.2
  26.5 4.9 %collective-permute-done.2 = bf16[512,120]{1,0:T(8,128)(2,1)S(1)} collective-permute-done((bf16[512,120]{1,0:T(8,128)(2,1)S(1)}, bf16[512,120]{1,0:T(8,128)(2,1)S(1)}, u32[]{:S(2)}, u32[]{:S(2)}) %collective-permute-start.2) | collective-permute-done | bytes 122912 | tf_op jit(solution)/shard_map/ppermute | solution.py:40
  31.8 15.1 %all_to_all.45 = bf16[4,2,512,120]{2,3,1,0:T(8,128)(2,1)S(1)} all-to-all(bf16[4,2,512,120]{2,3,1,0:T(8,128)(2,1)S(1)} %broadcast_in_dim.26), channel_id=1, replica_groups={{0,8,16,24},{32,40,48,56},{64,72,80,88},{96,104,112,120},{128,136,144,1..., dimensions={0} | all-to-all | bytes 1966080 | tf_op jit(solution)/shard_map/all_to_all | solution.py:36
  46.9 0.8 broadcast_in_dim.28
  47.7 5.8 %all-to-all-start.1 = ((bf16[8,2,120,120]{3,2,1,0:T(8,128)(2,1)}), bf16[8,2,120,120]{3,2,1,0:T(8,128)(2,1)S(1)}, u32[]{:S(2)}, u32[]{:S(2)}) async-start(bf16[8,2,120,120]{3,2,1,0:T(8,128)(2,1)} %broadcast_in_dim.28), calls=%async_computation.1 | async-start | bytes 983040 | tf_op jit(solution)/shard_map/all_to_all | solution.py:44
  53.8 0.7 copy.65.x_ref.f_ref
  54.4 12.1 %all-to-all-done.1.w_ref = bf16[8,2,120,120]{3,2,1,0:T(8,128)(2,1)S(1)} async-done(((bf16[8,2,120,120]{3,2,1,0:T(8,128)(2,1)}), bf16[8,2,120,120]{3,2,1,0:T(8,128)(2,1)S(1)}, u32[]{:S(2)}, u32[]{:S(2)}) %all-to-all-start.1) | async-done | bytes 460832 | tf_op jit(solution)/shard_map/all_to_all | solution.py:44
  66.5 3.7 %shard_map.76 = bf16[8,2,128,120]{3,2,1,0:T(8,128)(2,1)S(1)} custom-call(s32[8]{0:T(128)S(1)} %concatenate.45.sc_ref, bf16[4,2,512,120]{3,2,1,0:T(8,128)(2,1)S(1)} %copy.65.x_ref.f_ref, bf16[8,2,120,120]{3,2,1,0:T(8,128)(2,1)S(1)} %all-to-all-done.1.w_ref), custom_call_target="tpu_custom_call" | custom-call | flops 471859200 | bytes 1048576 | tf_op jit(solution)/shard_map/pallas_call | solution.py:126
  70.3 1.0 copy.66
  71.3 4.8 %all-to-all-start.2 = ((bf16[8,2,128,120]{2,3,1,0:T(8,128)(2,1)}), bf16[8,2,128,120]{2,3,1,0:T(8,128)(2,1)S(1)}, u32[]{:S(2)}, u32[]{:S(2)}) async-start(bf16[8,2,128,120]{2,3,1,0:T(8,128)(2,1)} %copy.66), calls=%async_computation.2 | async-start | bytes 983040 | tf_op jit(solution)/shard_map/all_to_all | solution.py:32
  76.3 6.8 %all-to-all-done.2 = bf16[8,2,128,120]{2,3,1,0:T(8,128)(2,1)S(1)} async-done(((bf16[8,2,128,120]{2,3,1,0:T(8,128)(2,1)}), bf16[8,2,128,120]{2,3,1,0:T(8,128)(2,1)S(1)}, u32[]{:S(2)}, u32[]{:S(2)}) %all-to-all-start.2) | async-done | bytes 491552 | tf_op jit(solution)/shard_map/all_to_all | solution.py:32
  83.5 17.6 %all_gather.9 = bf16[16,128,120]{1,2,0:T(8,128)(2,1)S(1)} all-gather(bf16[2,128,120]{1,2,0:T(8,128)(2,1)S(1)} %copy.69), channel_id=1, replica_groups=mesh['tm'=64,'head'=8] {'head'}, dimensions={0}, use_global_device_ids=true | all-gather | bytes 552960 | tf_op jit(solution)/shard_map/all_gather | solution.py:316
  101.5 0.6 convolution_convert_fusion.1
  102.2 0.8 broadcast_in_dim.33
  103.1 3.5 %all-to-all-start.3 = ((bf16[8,128,256]{2,1,0:T(8,128)(2,1)}), bf16[8,128,256]{2,1,0:T(8,128)(2,1)S(1)}, u32[]{:S(2)}, u32[]{:S(2)}) async-start(bf16[8,128,256]{2,1,0:T(8,128)(2,1)} %broadcast_in_dim.33), calls=%async_computation.3 | async-start | bytes 1048576 | tf_op jit(solution)/shard_map/all_to_all | solution.py:44
  106.7 2.9 %collective-permute-start.3 = (bf16[1,128,128]{2,1,0:T(8,128)(2,1)S(1)}, bf16[1,128,128]{2,1,0:T(8,128)(2,1)S(1)}, u32[]{:S(2)}, u32[]{:S(2)}) collective-permute-start(bf16[1,128,128]{2,1,0:T(8,128)(2,1)S(1)} %maximum_bitcast_fusion), channel_id=1, source_target_pairs={{0,256},{8,264},{16,272},{24,280},{32,288},{40,296},{48,304},{56,3... | collective-permute-start | bytes 98312 | tf_op jit(solution)/shard_map/ppermute | solution.py:40
  109.6 2.9 %collective-permute-done.3 = bf16[1,128,128]{2,1,0:T(8,128)(2,1)S(1)} collective-permute-done((bf16[1,128,128]{2,1,0:T(8,128)(2,1)S(1)}, bf16[1,128,128]{2,1,0:T(8,128)(2,1)S(1)}, u32[]{:S(2)}, u32[]{:S(2)}) %collective-permute-start.3) | collective-permute-done | bytes 32800 | tf_op jit(solution)/shard_map/ppermute | solution.py:40
  112.6 2.7 collective-permute-start.4
  115.3 4.9 %collective-permute-done.4 = bf16[2,128,128]{2,1,0:T(8,128)(2,1)S(1)} collective-permute-done((bf16[2,128,128]{2,1,0:T(8,128)(2,1)S(1)}, bf16[2,128,128]{2,1,0:T(8,128)(2,1)S(1)}, u32[]{:S(2)}, u32[]{:S(2)}) %collective-permute-start.4) | collective-permute-done | bytes 65568 | tf_op jit(solution)/shard_map/ppermute | solution.py:40
  120.2 3.3 %collective-permute-start.5 = (bf16[4,128,128]{2,1,0:T(8,128)(2,1)S(1)}, bf16[4,128,128]{2,1,0:T(8,128)(2,1)S(1)}, u32[]{:S(2)}, u32[]{:S(2)}) collective-permute-start(bf16[4,128,128]{2,1,0:T(8,128)(2,1)S(1)} %pad_maximum_fusion.4), channel_id=1, source_target_pairs={{0,8},{8,0},{16,24},{24,16},{32,40},{40,32},{48,56},{56,48},{64,72... | collective-permute-start | bytes 393224 | tf_op jit(solution)/shard_map/ppermute | solution.py:40
  123.6 3.5 %collective-permute-done.5 = bf16[4,128,128]{2,1,0:T(8,128)(2,1)S(1)} collective-permute-done((bf16[4,128,128]{2,1,0:T(8,128)(2,1)S(1)}, bf16[4,128,128]{2,1,0:T(8,128)(2,1)S(1)}, u32[]{:S(2)}, u32[]{:S(2)}) %collective-permute-start.5) | collective-permute-done | bytes 131104 | tf_op jit(solution)/shard_map/ppermute | solution.py:40
  127.2 2.4 shard_map.77
  129.6 0.7 broadcast_in_dim.64
  130.3 4.8 %all-to-all-start.4 = ((f32[8,8,8,128]{3,2,1,0:T(8,128)}), f32[8,8,8,128]{3,2,1,0:T(8,128)S(1)}, u32[]{:S(2)}, u32[]{:S(2)}) async-start(f32[8,8,8,128]{3,2,1,0:T(8,128)} %broadcast_in_dim.64), calls=%async_computation.4 | async-start | bytes 524288 | tf_op jit(solution)/shard_map/all_to_all | solution.py:32
  135.1 0.7 all-gather.3.cloned.1.call-update
  135.8 5.1 %all-to-all-done.4.stats_ref = f32[8,8,8,128]{3,2,1,0:T(8,128)S(1)} async-done(((f32[8,8,8,128]{3,2,1,0:T(8,128)}), f32[8,8,8,128]{3,2,1,0:T(8,128)S(1)}, u32[]{:S(2)}, u32[]{:S(2)}) %all-to-all-start.4) | async-done | bytes 262176 | tf_op jit(solution)/shard_map/all_to_all | solution.py:32
  140.9 4.2 %shard_map.78 = (bf16[2,8,120,128]{3,2,1,0:T(8,128)(2,1)S(1)}, bf16[8,128,256]{2,1,0:T(8,128)(2,1)}) custom-call(s32[6]{0:T(128)S(1)} %pad_add_fusion.sc_ref, bf16[8,128,128]{2,1,0:T(8,128)(2,1)S(1)} %pad_maximum_fusion.2.q_ref, bf16[8,128,256]{2,1,0:T(8,128)(2,1)S(1)} %all-to-all-done.3.kv_ref, bf16[4,2,512,120]{3,2,1,0:T(8,128)(2,1)S(1)} %copy.65.x_ref.f_ref, ...), custom_call_target="tpu_custom_call" | custom-call | flops 1610612736 | bytes 1048576 | tf_op jit(solution)/shard_map/pallas_call | solution.py:268
  145.2 7.1 %all-to-all-start.5 = ((bf16[8,128,256]{2,1,0:T(8,128)(2,1)}), bf16[8,128,256]{2,1,0:T(8,128)(2,1)S(1)}, u32[]{:S(2)}, u32[]{:S(2)}) async-start(bf16[8,128,256]{2,1,0:T(8,128)(2,1)} %get-tuple-element.6), calls=%async_computation.5 | async-start | bytes 1048576 | tf_op jit(solution)/shard_map/all_to_all | solution.py:44
  152.3 2.8 collective-permute-start.6
  155.1 3.1 %collective-permute-start.9 = (bf16[4,120,128]{2,1,0:T(8,128)(2,1)S(1)}, bf16[4,120,128]{2,1,0:T(8,128)(2,1)S(1)}, u32[]{:S(2)}, u32[]{:S(2)}) collective-permute-start(bf16[4,120,128]{2,1,0:T(8,128)(2,1)S(1)} %get-tuple-element.13), channel_id=1, source_target_pairs={{0,8},{8,0},{16,24},{24,16},{32,40},{40,32},{48,56},{56,48},{64,72... | collective-permute-start | bytes 368648 | tf_op jit(solution)/shard_map/ppermute | solution.py:40
  158.2 3.8 %collective-permute-done.6 = bf16[4,120,128]{2,1,0:T(8,128)(2,1)S(1)} collective-permute-done((bf16[4,120,128]{2,1,0:T(8,128)(2,1)S(1)}, bf16[4,120,128]{2,1,0:T(8,128)(2,1)S(1)}, u32[]{:S(2)}, u32[]{:S(2)}) %collective-permute-start.6) | collective-permute-done | bytes 122912 | tf_op jit(solution)/shard_map/ppermute | solution.py:40
  162.0 4.5 %collective-permute-done.9 = bf16[4,120,128]{2,1,0:T(8,128)(2,1)S(1)} collective-permute-done((bf16[4,120,128]{2,1,0:T(8,128)(2,1)S(1)}, bf16[4,120,128]{2,1,0:T(8,128)(2,1)S(1)}, u32[]{:S(2)}, u32[]{:S(2)}) %collective-permute-start.9) | collective-permute-done | bytes 122912 | tf_op jit(solution)/shard_map/ppermute | solution.py:40
  166.5 0.7 bitcast_add_fusion
  167.2 2.6 collective-permute-start.10
  169.8 6.8 %collective-permute-done.10 = bf16[2,120,128]{2,1,0:T(8,128)(2,1)S(1)} collective-permute-done((bf16[2,120,128]{2,1,0:T(8,128)(2,1)S(1)}, bf16[2,120,128]{2,1,0:T(8,128)(2,1)S(1)}, u32[]{:S(2)}, u32[]{:S(2)}) %collective-permute-start.10) | collective-permute-done | bytes 61472 | tf_op jit(solution)/shard_map/ppermute | solution.py:40
  176.6 3.7 %collective-permute-start.11 = (bf16[1,120,128]{2,1,0:T(8,128)(2,1)S(1)}, bf16[1,120,128]{2,1,0:T(8,128)(2,1)S(1)}, u32[]{:S(2)}, u32[]{:S(2)}) collective-permute-start(bf16[1,120,128]{2,1,0:T(8,128)(2,1)S(1)} %slice.143), channel_id=1, source_target_pairs={{0,256},{8,264},{16,272},{24,280},{32,288},{40,296},{48,304},{56,3... | collective-permute-start | bytes 92168 | tf_op jit(solution)/shard_map/ppermute | solution.py:40
  180.3 2.4 copy.85
  183.1 0.6 fusion.3
  184.2 0.9 pad_maximum_fusion
  185.0 4.3 %all-to-all-start.6 = ((bf16[8,2,128,128]{2,3,1,0:T(8,128)(2,1)}), bf16[8,2,128,128]{2,3,1,0:T(8,128)(2,1)}, u32[]{:S(2)}, u32[]{:S(2)}) async-start(bf16[8,2,128,128]{2,3,1,0:T(8,128)(2,1)} %bitcast.30), calls=%async_computation.6 | async-start | bytes 1048576 | tf_op jit(solution)/shard_map/all_to_all | solution.py:357
  189.4 1.7 convolution_convert_fusion
  191.0 2.4 copy.81
  193.9 2.0 copy.82
  195.9 12.6 %all-to-all-done.6 = bf16[8,2,128,128]{2,3,1,0:T(8,128)(2,1)} async-done(((bf16[8,2,128,128]{2,3,1,0:T(8,128)(2,1)}), bf16[8,2,128,128]{2,3,1,0:T(8,128)(2,1)}, u32[]{:S(2)}, u32[]{:S(2)}) %all-to-all-start.6) | async-done | bytes 524320 | tf_op jit(solution)/shard_map/all_to_all | solution.py:357
  208.5 4.6 %all-to-all-start.7 = ((bf16[8,8,30,360]{3,1,2,0:T(8,128)(2,1)}), bf16[8,8,30,360]{3,1,2,0:T(8,128)(2,1)S(1)}, u32[]{:S(2)}, u32[]{:S(2)}) async-start(bf16[8,8,30,360]{3,1,2,0:T(8,128)(2,1)} %bitcast.39), calls=%async_computation.7 | async-start | bytes 2949120 | tf_op jit(solution)/shard_map/all_to_all | solution.py:32
  213.1 4.9 %collective-permute-start.7 = (bf16[2,120,128]{2,1,0:T(8,128)(2,1)S(1)}, bf16[2,120,128]{2,1,0:T(8,128)(2,1)S(1)}, u32[]{:S(2)}, u32[]{:S(2)}) collective-permute-start(bf16[2,120,128]{2,1,0:T(8,128)(2,1)S(1)} %slice.137), channel_id=1, source_target_pairs={{0,16},{8,24},{16,0},{24,8},{32,48},{40,56},{48,32},{56,40},{64,80... | collective-permute-start | bytes 184328 | tf_op jit(solution)/shard_map/ppermute | solution.py:40
  218.1 15.9 %collective-permute-done.7 = bf16[2,120,128]{2,1,0:T(8,128)(2,1)S(1)} collective-permute-done((bf16[2,120,128]{2,1,0:T(8,128)(2,1)S(1)}, bf16[2,120,128]{2,1,0:T(8,128)(2,1)S(1)}, u32[]{:S(2)}, u32[]{:S(2)}) %collective-permute-start.7) | collective-permute-done | bytes 61472 | tf_op jit(solution)/shard_map/ppermute | solution.py:40
  234.1 2.4 collective-permute-start.8
  236.5 1.1 convert_reduce_fusion.1
  237.9 2.4 collective-permute-start.12
  240.4 7.6 %collective-permute-start.13 = (bf16[2,32,120]{2,1,0:T(8,128)(2,1)S(1)}, bf16[2,32,120]{2,1,0:T(8,128)(2,1)S(1)}, u32[]{:S(2)}, u32[]{:S(2)}) collective-permute-start(bf16[2,32,120]{2,1,0:T(8,128)(2,1)S(1)} %get-tuple-element.23), channel_id=1, source_target_pairs={{8,0},{16,8},{24,16},{32,24},{40,32},{48,40},{56,48},{64,56},{72,6... | collective-permute-start | bytes 46088 | tf_op jit(solution)/shard_map/ppermute | solution.py:177
  248.3 0.7 copy.83
  249.0 5.7 %all-to-all-start.8 = ((bf16[8,30,360]{2,1,0:T(8,128)(2,1)}), bf16[8,30,360]{2,1,0:T(8,128)(2,1)S(1)}, u32[]{:S(2)}, u32[]{:S(2)}) async-start(bf16[8,30,360]{2,1,0:T(8,128)(2,1)} %copy.83), calls=%async_computation.8 | async-start | bytes 393216 | tf_op jit(solution)/shard_map/all_to_all | solution.py:44
  254.7 0.6 fusion.16
  255.3 9.1 %all-to-all-done.8 = bf16[8,30,360]{2,1,0:T(8,128)(2,1)S(1)} async-done(((bf16[8,30,360]{2,1,0:T(8,128)(2,1)}), bf16[8,30,360]{2,1,0:T(8,128)(2,1)S(1)}, u32[]{:S(2)}, u32[]{:S(2)}) %all-to-all-start.8) | async-done | bytes 172832 | tf_op jit(solution)/shard_map/all_to_all | solution.py:44
  264.4 0.7 convert_reduce_fusion.3
  265.1 2.1 copy-done.1
  267.2 3.6 %shard_map.79 = f32[2,128,120]{2,1,0:T(8,128)S(1)} custom-call(s32[5]{0:T(128)S(1)} %pad_add_fusion.1.sc_ref, bf16[2,192,120]{2,1,0:T(8,128)(2,1)S(1)} %pad_maximum_fusion.6.e_ref, bf16[8,8,2,120,120]{4,3,2,1,0:T(8,128)(2,1)S(1)} %bitcast.69), custom_call_target="tpu_custom_call" | custom-call | flops 471859200 | bytes 1048576 | tf_op jit(solution)/shard_map/pallas_call | solution.py:163
  270.9 0.7 copy.80
  (79 shorter events, 4.2 us)
Async XLA Ops:
  8.1 15.8 %collective-permute-start = (bf16[2,32,120]{2,1,0:T(8,128)(2,1)S(1)}, bf16[2,32,120]{2,1,0:T(8,128)(2,1)S(1)}, u32[]{:S(2)}, u32[]{:S(2)}) collective-permute-start(bf16[2,32,120]{2,1,0:T(8,128)(2,1)S(1)} %get-tuple-element.26), channel_id=1, source_target_pairs={{0,8},{8,16},{16,24},{24,32},{32,40},{40,48},{48,56},{56,64},{64,7... | collective-permute-start | bytes 46088 | tf_op jit(solution)/shard_map/ppermute | solution.py:176
  11.5 13.0 %collective-permute-start.1 = (bf16[2,32,120]{2,1,0:T(8,128)(2,1)S(1)}, bf16[2,32,120]{2,1,0:T(8,128)(2,1)S(1)}, u32[]{:S(2)}, u32[]{:S(2)}) collective-permute-start(bf16[2,32,120]{2,1,0:T(8,128)(2,1)S(1)} %get-tuple-element.27), channel_id=1, source_target_pairs={{8,0},{16,8},{24,16},{32,24},{40,32},{48,40},{56,48},{64,56},{72,6... | collective-permute-start | bytes 46088 | tf_op jit(solution)/shard_map/ppermute | solution.py:177
  24.6 6.9 %collective-permute-start.2 = (bf16[512,120]{1,0:T(8,128)(2,1)S(1)}, bf16[512,120]{1,0:T(8,128)(2,1)S(1)}, u32[]{:S(2)}, u32[]{:S(2)}) collective-permute-start(bf16[512,120]{1,0:T(8,128)(2,1)S(1)} %get-tuple-element.18), channel_id=1, source_target_pairs={{0,256},{8,264},{16,272},{24,280},{32,288},{40,296},{48,304},{56,3... | collective-permute-start | bytes 368648 | tf_op jit(solution)/shard_map/ppermute | solution.py:40
  31.7 15.2 %copy-start.4 = (bf16[1,2,120,120]{3,2,1,0:T(8,128)(2,1)S(1)}, bf16[1,2,120,120]{3,2,1,0:T(8,128)(2,1)}, u32[]{:S(2)}) copy-start(bf16[1,2,120,120]{3,2,1,0:T(8,128)(2,1)} %param.6) | copy-start | bytes 172804
  31.7 21.8 %copy-start.5 = (s32[4]{0:T(128)S(1)}, s32[4]{0:T(128)}, u32[]{:S(2)}) copy-start(s32[4]{0:T(128)} %param.8) | copy-start | bytes 52
  47.7 18.8 %all-to-all-start.1 = ((bf16[8,2,120,120]{3,2,1,0:T(8,128)(2,1)}), bf16[8,2,120,120]{3,2,1,0:T(8,128)(2,1)S(1)}, u32[]{:S(2)}, u32[]{:S(2)}) async-start(bf16[8,2,120,120]{3,2,1,0:T(8,128)(2,1)} %broadcast_in_dim.28), calls=%async_computation.1 | async-start | bytes 983040 | tf_op jit(solution)/shard_map/all_to_all | solution.py:44
  66.5 4.7 %copy-start = (bf16[8,2,120,120]{3,2,1,0:T(8,128)(2,1)}, bf16[8,2,120,120]{3,2,1,0:T(8,128)(2,1)S(1)}, u32[]{:S(2)}) copy-start(bf16[8,2,120,120]{3,2,1,0:T(8,128)(2,1)S(1)} %all-to-all-done.1.w_ref) | copy-start | bytes 1382404
  71.3 11.8 %all-to-all-start.2 = ((bf16[8,2,128,120]{2,3,1,0:T(8,128)(2,1)}), bf16[8,2,128,120]{2,3,1,0:T(8,128)(2,1)S(1)}, u32[]{:S(2)}, u32[]{:S(2)}) async-start(bf16[8,2,128,120]{2,3,1,0:T(8,128)(2,1)} %copy.66), calls=%async_computation.2 | async-start | bytes 983040 | tf_op jit(solution)/shard_map/all_to_all | solution.py:32
  83.2 18.3 %copy-start.2 = (bf16[1920,360]{0,1:T(8,128)(2,1)S(1)}, bf16[1920,360]{0,1:T(8,128)(2,1)}, u32[]{:S(2)}) copy-start(bf16[1920,360]{0,1:T(8,128)(2,1)} %param.7) | copy-start | bytes 4147204
  103.1 24.1 %all-to-all-start.3 = ((bf16[8,128,256]{2,1,0:T(8,128)(2,1)}), bf16[8,128,256]{2,1,0:T(8,128)(2,1)S(1)}, u32[]{:S(2)}, u32[]{:S(2)}) async-start(bf16[8,128,256]{2,1,0:T(8,128)(2,1)} %broadcast_in_dim.33), calls=%async_computation.3 | async-start | bytes 1048576 | tf_op jit(solution)/shard_map/all_to_all | solution.py:44
  106.7 5.8 %collective-permute-start.3 = (bf16[1,128,128]{2,1,0:T(8,128)(2,1)S(1)}, bf16[1,128,128]{2,1,0:T(8,128)(2,1)S(1)}, u32[]{:S(2)}, u32[]{:S(2)}) collective-permute-start(bf16[1,128,128]{2,1,0:T(8,128)(2,1)S(1)} %maximum_bitcast_fusion), channel_id=1, source_target_pairs={{0,256},{8,264},{16,272},{24,280},{32,288},{40,296},{48,304},{56,3... | collective-permute-start | bytes 98312 | tf_op jit(solution)/shard_map/ppermute | solution.py:40
  112.6 7.7 %collective-permute-start.4 = (bf16[2,128,128]{2,1,0:T(8,128)(2,1)S(1)}, bf16[2,128,128]{2,1,0:T(8,128)(2,1)S(1)}, u32[]{:S(2)}, u32[]{:S(2)}) collective-permute-start(bf16[2,128,128]{2,1,0:T(8,128)(2,1)S(1)} %pad_maximum_fusion.8), channel_id=1, source_target_pairs={{0,16},{8,24},{16,0},{24,8},{32,48},{40,56},{48,32},{56,40},{64,80... | collective-permute-start | bytes 196616 | tf_op jit(solution)/shard_map/ppermute | solution.py:40
  120.2 6.9 %collective-permute-start.5 = (bf16[4,128,128]{2,1,0:T(8,128)(2,1)S(1)}, bf16[4,128,128]{2,1,0:T(8,128)(2,1)S(1)}, u32[]{:S(2)}, u32[]{:S(2)}) collective-permute-start(bf16[4,128,128]{2,1,0:T(8,128)(2,1)S(1)} %pad_maximum_fusion.4), channel_id=1, source_target_pairs={{0,8},{8,0},{16,24},{24,16},{32,40},{40,32},{48,56},{56,48},{64,72... | collective-permute-start | bytes 393224 | tf_op jit(solution)/shard_map/ppermute | solution.py:40
  130.3 10.6 %all-to-all-start.4 = ((f32[8,8,8,128]{3,2,1,0:T(8,128)}), f32[8,8,8,128]{3,2,1,0:T(8,128)S(1)}, u32[]{:S(2)}, u32[]{:S(2)}) async-start(f32[8,8,8,128]{3,2,1,0:T(8,128)} %broadcast_in_dim.64), calls=%async_computation.4 | async-start | bytes 524288 | tf_op jit(solution)/shard_map/all_to_all | solution.py:32
  135.1 130.0 %all-gather.3.cloned.1.call-start = ((), (), s32[]{:S(2)}) async-start(), calls=%async_computation.9 | async-start | bytes 4423680 | tf_op jit(solution)/shard_map/all_gather | solution.py:314
  145.2 37.6 %all-to-all-start.5 = ((bf16[8,128,256]{2,1,0:T(8,128)(2,1)}), bf16[8,128,256]{2,1,0:T(8,128)(2,1)S(1)}, u32[]{:S(2)}, u32[]{:S(2)}) async-start(bf16[8,128,256]{2,1,0:T(8,128)(2,1)} %get-tuple-element.6), calls=%async_computation.5 | async-start | bytes 1048576 | tf_op jit(solution)/shard_map/all_to_all | solution.py:44
  152.3 9.7 %collective-permute-start.6 = (bf16[4,120,128]{2,1,0:T(8,128)(2,1)S(1)}, bf16[4,120,128]{2,1,0:T(8,128)(2,1)S(1)}, u32[]{:S(2)}, u32[]{:S(2)}) collective-permute-start(bf16[4,120,128]{2,1,0:T(8,128)(2,1)S(1)} %get-tuple-element.14), channel_id=1, source_target_pairs={{0,8},{8,0},{16,24},{24,16},{32,40},{40,32},{48,56},{56,48},{64,72... | collective-permute-start | bytes 368648 | tf_op jit(solution)/shard_map/ppermute | solution.py:40
  155.1 11.4 %collective-permute-start.9 = (bf16[4,120,128]{2,1,0:T(8,128)(2,1)S(1)}, bf16[4,120,128]{2,1,0:T(8,128)(2,1)S(1)}, u32[]{:S(2)}, u32[]{:S(2)}) collective-permute-start(bf16[4,120,128]{2,1,0:T(8,128)(2,1)S(1)} %get-tuple-element.13), channel_id=1, source_target_pairs={{0,8},{8,0},{16,24},{24,16},{32,40},{40,32},{48,56},{56,48},{64,72... | collective-permute-start | bytes 368648 | tf_op jit(solution)/shard_map/ppermute | solution.py:40
  167.2 9.3 %collective-permute-start.10 = (bf16[2,120,128]{2,1,0:T(8,128)(2,1)S(1)}, bf16[2,120,128]{2,1,0:T(8,128)(2,1)S(1)}, u32[]{:S(2)}, u32[]{:S(2)}) collective-permute-start(bf16[2,120,128]{2,1,0:T(8,128)(2,1)S(1)} %slice.141), channel_id=1, source_target_pairs={{0,16},{8,24},{16,0},{24,8},{32,48},{40,56},{48,32},{56,40},{64,80... | collective-permute-start | bytes 184328 | tf_op jit(solution)/shard_map/ppermute | solution.py:40
  176.6 6.2 %collective-permute-start.11 = (bf16[1,120,128]{2,1,0:T(8,128)(2,1)S(1)}, bf16[1,120,128]{2,1,0:T(8,128)(2,1)S(1)}, u32[]{:S(2)}, u32[]{:S(2)}) collective-permute-start(bf16[1,120,128]{2,1,0:T(8,128)(2,1)S(1)} %slice.143), channel_id=1, source_target_pairs={{0,256},{8,264},{16,272},{24,280},{32,288},{40,296},{48,304},{56,3... | collective-permute-start | bytes 92168 | tf_op jit(solution)/shard_map/ppermute | solution.py:40
  185.0 23.5 %all-to-all-start.6 = ((bf16[8,2,128,128]{2,3,1,0:T(8,128)(2,1)}), bf16[8,2,128,128]{2,3,1,0:T(8,128)(2,1)}, u32[]{:S(2)}, u32[]{:S(2)}) async-start(bf16[8,2,128,128]{2,3,1,0:T(8,128)(2,1)} %bitcast.30), calls=%async_computation.6 | async-start | bytes 1048576 | tf_op jit(solution)/shard_map/all_to_all | solution.py:357
  208.5 4.6 %copy-start.3 = (bf16[4,120,128]{2,1,0:T(8,128)(2,1)S(1)}, bf16[4,120,128]{2,1,0:T(8,128)(2,1)}, u32[]{:S(2)}) copy-start(bf16[4,120,128]{2,1,0:T(8,128)(2,1)} %get-tuple-element.12) | copy-start | bytes 368644
  208.5 39.5 %all-to-all-start.7 = ((bf16[8,8,30,360]{3,1,2,0:T(8,128)(2,1)}), bf16[8,8,30,360]{3,1,2,0:T(8,128)(2,1)S(1)}, u32[]{:S(2)}, u32[]{:S(2)}) async-start(bf16[8,8,30,360]{3,1,2,0:T(8,128)(2,1)} %bitcast.39), calls=%async_computation.7 | async-start | bytes 2949120 | tf_op jit(solution)/shard_map/all_to_all | solution.py:32
  213.1 20.9 %collective-permute-start.7 = (bf16[2,120,128]{2,1,0:T(8,128)(2,1)S(1)}, bf16[2,120,128]{2,1,0:T(8,128)(2,1)S(1)}, u32[]{:S(2)}, u32[]{:S(2)}) collective-permute-start(bf16[2,120,128]{2,1,0:T(8,128)(2,1)S(1)} %slice.137), channel_id=1, source_target_pairs={{0,16},{8,24},{16,0},{24,8},{32,48},{40,56},{48,32},{56,40},{64,80... | collective-permute-start | bytes 184328 | tf_op jit(solution)/shard_map/ppermute | solution.py:40
  234.1 20.6 %collective-permute-start.8 = (bf16[1,120,128]{2,1,0:T(8,128)(2,1)S(1)}, bf16[1,120,128]{2,1,0:T(8,128)(2,1)S(1)}, u32[]{:S(2)}, u32[]{:S(2)}) collective-permute-start(bf16[1,120,128]{2,1,0:T(8,128)(2,1)S(1)} %slice.139), channel_id=1, source_target_pairs={{0,256},{8,264},{16,272},{24,280},{32,288},{40,296},{48,304},{56,3... | collective-permute-start | bytes 92168 | tf_op jit(solution)/shard_map/ppermute | solution.py:40
  237.9 17.4 %collective-permute-start.12 = (bf16[2,32,120]{2,1,0:T(8,128)(2,1)S(1)}, bf16[2,32,120]{2,1,0:T(8,128)(2,1)S(1)}, u32[]{:S(2)}, u32[]{:S(2)}) collective-permute-start(bf16[2,32,120]{2,1,0:T(8,128)(2,1)S(1)} %get-tuple-element.22), channel_id=1, source_target_pairs={{0,8},{8,16},{16,24},{24,32},{32,40},{40,48},{48,56},{56,64},{64,7... | collective-permute-start | bytes 46088 | tf_op jit(solution)/shard_map/ppermute | solution.py:176
  240.4 14.9 %collective-permute-start.13 = (bf16[2,32,120]{2,1,0:T(8,128)(2,1)S(1)}, bf16[2,32,120]{2,1,0:T(8,128)(2,1)S(1)}, u32[]{:S(2)}, u32[]{:S(2)}) collective-permute-start(bf16[2,32,120]{2,1,0:T(8,128)(2,1)S(1)} %get-tuple-element.23), channel_id=1, source_target_pairs={{8,0},{16,8},{24,16},{32,24},{40,32},{48,40},{56,48},{64,56},{72,6... | collective-permute-start | bytes 46088 | tf_op jit(solution)/shard_map/ppermute | solution.py:177
  249.0 15.5 %all-to-all-start.8 = ((bf16[8,30,360]{2,1,0:T(8,128)(2,1)}), bf16[8,30,360]{2,1,0:T(8,128)(2,1)S(1)}, u32[]{:S(2)}, u32[]{:S(2)}) async-start(bf16[8,30,360]{2,1,0:T(8,128)(2,1)} %copy.83), calls=%async_computation.8 | async-start | bytes 393216 | tf_op jit(solution)/shard_map/all_to_all | solution.py:44
  265.1 2.1 copy-start.1
Sparse Core Ops, SparseCore 0:
  138.0 64.3 all-gather.2

commit v3 on v2

--- a/solution.py
+++ b/solution.py
@@ -48,6 +48,10 @@
     return jnp.broadcast_to(array[None], (count,) + array.shape)
 
 
+def after(array, earlier):
+    return array + 0 * earlier.reshape(-1)[0].astype(array.dtype)
+
+
 BITS = (32, 2, 1)
 SLOTS = (0, 4, 2, 6, 1, 5, 3, 7)
 
@@ -90,83 +94,60 @@
 
 
 PADDED = ROWS + KERNEL
-
-
-def conv_body(sc_ref, x_ref, w_ref, out_ref):
-    first = sc_ref[0]
-    ends = [sc_ref[4 + u] for u in range(4)]
+TAPS = KERNEL // 2
+SPAN = ROWS + TAPS
+
+
+def conv_body(forward, sc_ref, x_ref, w_ref, own_ref, other_ref):
+    ends = [sc_ref[2 + u] for u in range(4)]
+    first = TAPS * (sc_ref[0] if forward else 1 - sc_ref[0])
     row = lax.broadcasted_iota(jnp.int32, (ROWS, HD), 0)
-
-    def block(b, carry):
-        y = (b // 4) ^ sc_ref[2]
-        x_at = b % 4
-        pos = (y * 32 + sc_ref[1] + x_at) * ROWS + row
+    for b in range(2):
+        shard = sc_ref[1] if b == 0 else sc_ref[1] ^ 32
+        pos = shard * ROWS + row
         low, high = bounds_of(pos, ends)
-        source = pos - HALF + first
-        keep = [
-            ((source + 4 * s) >= low) & ((source + 4 * s) < high) for s in range(8)
+        source = pos + (first - HALF)
+        spans = [
+            x_ref[b, g, pl.ds(pl.multiple_of(first, TAPS), SPAN)].astype(F32) for g in range(2)
         ]
+        totals = [jnp.zeros((ROWS, HD), F32) for g in range(2)]
+        for rest in range(8):
+            rolled = [pltpu.roll(e, SPAN - rest, 0) if rest else e for e in spans]
+            for start in range(0, TAPS + 1, 8):
+                tap = start + rest if forward else TAPS - start - rest
+                if not 0 <= tap < TAPS:
+                    continue
+                at = source + (start + rest)
+                keep = (at >= low) & (at < high)
+                for g in range(2):
+                    piece = jnp.where(keep, rolled[g][start : start + ROWS], 0.0).astype(BF)
+                    totals[g] += lax.dot_general(
+                        piece,
+                        w_ref[tap % 4, tap // 4, g],
+                        (((1,), (0 if forward else 1,)), ((), ())),
+                        preferred_element_type=F32,
+                    )
         for g in range(2):
-            x = x_ref[x_at, b // 4, g * PADDED : (g + 1) * PADDED].astype(F32)
-            even = pltpu.roll(x, PADDED - first, 0)
-            odd = pltpu.roll(x, PADDED - first - 4, 0)
-            total = jnp.zeros((ROWS, HD), F32)
-            for s in range(8):
-                rolled = odd if s % 2 else even
-                start = 8 * (s // 2)
-                piece = jnp.where(keep[s], rolled[start : start + ROWS], 0.0).astype(BF)
-                total += jnp.dot(piece, w_ref[s, g], preferred_element_type=F32)
-            out_ref[y * 4 + x_at, g] = total.astype(BF)
-        return carry
-
-    lax.fori_loop(0, 8, block, 0)
-
-
-def conv_partial(scalars, gathered, taps):
-    return vmem_call(
-        conv_body,
-        jax.ShapeDtypeStruct((8, 2, ROWS, HD), BF),
+            if b == 0:
+                own_ref[g] = totals[g]
+            else:
+                other_ref[g] = totals[g].astype(BF)
+
+
+def convolved(forward, scalars, rows, taps):
+    padded = with_halo(rows)
+    pair = jnp.stack([padded, swap(padded, 32)])
+    own, other = vmem_call(
+        functools.partial(conv_body, forward),
+        (
+            jax.ShapeDtypeStruct((2, ROWS, HD), F32),
+            jax.ShapeDtypeStruct((2, ROWS, HD), BF),
+        ),
         scalars=1,
         inputs=2,
-        flops=8 * 2 * 8 * 2 * ROWS * HD * HD,
-    )(scalars, gathered, taps)
-
-
-def back_body(sc_ref, e_ref, w_ref, out_ref):
-    ends = [sc_ref[1 + u] for u in range(4)]
-    pos = sc_ref[0] * ROWS + lax.broadcasted_iota(jnp.int32, (ROWS, HD), 0)
-    low, high = bounds_of(pos, ends)
-    errors = [e_ref[g].astype(F32) for g in range(2)]
-    totals = [jnp.zeros((ROWS, HD), F32) for g in range(2)]
-    for rest in range(8):
-        rolled = [pltpu.roll(e, PADDED - rest, 0) if rest else e for e in errors]
-        for start in range(0, KERNEL + 1, 8):
-            tap = KERNEL - start - rest
-            if not 0 <= tap < KERNEL:
-                continue
-            source = pos + (HALF - tap)
-            keep = (source >= low) & (source < high)
-            y, z, x = tap // 32, tap % 32 // 4, tap % 4
-            for g in range(2):
-                piece = jnp.where(keep, rolled[g][start : start + ROWS], 0.0).astype(BF)
-                totals[g] += lax.dot_general(
-                    piece,
-                    w_ref[y * 4 + x, z, g],
-                    (((1,), (1,)), ((), ())),
-                    preferred_element_type=F32,
-                )
-    for g in range(2):
-        out_ref[g] = totals[g]
-
-
-def conv_back(scalars, errors, taps):
-    return vmem_call(
-        back_body,
-        jax.ShapeDtypeStruct((2, ROWS, HD), F32),
-        scalars=1,
-        inputs=2,
-        flops=64 * 2 * 2 * ROWS * HD * HD,
-    )(scalars, errors, taps)
+        flops=32 * 2 * 2 * 2 * ROWS * HD * HD,
+    )(scalars, pair, taps)
+    return own + swap(other, 32).astype(F32)
 
 
 def with_halo(rows):
@@ -186,47 +167,43 @@
 CONTRACT = (((1,), (1,)), ((), ()))
 
 
-def upstream_rows(sc_ref, f_ref, d_ref):
-    for i, e in enumerate(SLOTS):
-        d_ref[i * ROWS : (i + 1) * ROWS] = f_ref[sc_ref[1] ^ (e % 4), e // 4, 2 * PADDED :]
-
-
 def scored(c, q_ref, kv_ref, d_ref):
     keys = kv_ref[:, :, :LANES].reshape(ALL, LANES)
     values = kv_ref[:, :, LANES : LANES + HD].reshape(ALL, HD)
     q = q_ref[c * N : (c + 1) * N].reshape(CHUNK, LANES)
-    d = d_ref[c * CHUNK : (c + 1) * CHUNK]
+    d = d_ref[c * N : (c + 1) * N].reshape(CHUNK, HD)
     scores = lax.dot_general(keys, q, CONTRACT, preferred_element_type=F32)
     dprobs = lax.dot_general(values, d, CONTRACT, preferred_element_type=F32)
     return keys, values, q, d, scores * SCALE2, dprobs
 
 
-def stats_body(sc_ref, q_ref, kv_ref, f_ref, out_ref, d_ref):
-    upstream_rows(sc_ref, f_ref, d_ref)
+def stats_body(sc_ref, q_ref, kv_ref, d_ref, out_ref):
     for c in range(ALL // CHUNK):
         _, _, _, _, scores, dprobs = scored(c, q_ref, kv_ref, d_ref)
         peak = jnp.max(scores, axis=0, keepdims=True)
         weight = jnp.exp2(scores - peak)
         total = jnp.sum(weight, axis=0, keepdims=True)
         along = jnp.sum(weight * dprobs, axis=0, keepdims=True)
-        rows = jnp.concatenate([peak, total, along, jnp.zeros((5, CHUNK), F32)], axis=0)
         for i in range(N):
-            out_ref[sc_ref[0] ^ SLOTS[c * N + i]] = rows[:, i * ROWS : (i + 1) * ROWS]
-
-
-def grads_body(
-    sc_ref, q_ref, kv_ref, f_ref, stats_ref, od_ref, dkv_ref, d_ref, dk_ref, dv_ref
-):
-    upstream_rows(sc_ref, f_ref, d_ref)
+            columns = slice(i * ROWS, (i + 1) * ROWS)
+            shard = pl.ds(sc_ref[0] ^ SLOTS[c * N + i], 1)
+            for j, value in enumerate((peak, total, along)):
+                out_ref[j, shard] = value[:, columns]
+
+
+def grads_body(sc_ref, q_ref, kv_ref, d_ref, stats_ref, od_ref, dkv_ref, dk_ref, dv_ref):
     for c in range(ALL // CHUNK):
-        stats = jnp.concatenate(
-            [stats_ref[:, sc_ref[0] ^ SLOTS[c * N + i]] for i in range(N)], axis=2
+        peaks, totals, alongs = (
+            jnp.concatenate(
+                [stats_ref[:, j, pl.ds(sc_ref[0] ^ SLOTS[c * N + i], 1)] for i in range(N)],
+                axis=2,
+            )
+            for j in range(3)
         )
-        peaks = stats[:, 0]
-        top = jnp.max(peaks, axis=0, keepdims=True)
-        factor = jnp.exp2(peaks - top)
-        total = jnp.sum(stats[:, 1] * factor, axis=0, keepdims=True)
-        delta = jnp.sum(stats[:, 2] * factor, axis=0, keepdims=True) / total
+        top = jnp.max(peaks, axis=0)
+        factor = jnp.exp2(peaks - top[None])
+        total = jnp.sum(totals * factor, axis=0)
+        delta = jnp.sum(alongs * factor, axis=0) / total
         lse = top + jnp.log2(total)
         keys, values, q, d, scores, dprobs = scored(c, q_ref, kv_ref, d_ref)
         probs = jnp.exp2(scores - lse)
@@ -253,18 +230,17 @@
         dkv_ref[i, :, LANES + HD :] = jnp.zeros((ROWS, LANES - HD), BF)
 
 
-def attention_stats(scalars, queries, keys, gathered):
+def attention_stats(scalars, queries, keys, upstream):
     return vmem_call(
         stats_body,
-        jax.ShapeDtypeStruct((8, 8, ROWS), F32),
-        scratch=[pltpu.VMEM((ALL, HD), BF)],
+        jax.ShapeDtypeStruct((3, 8, ROWS), F32),
         scalars=1,
         inputs=3,
         flops=2 * 2 * ALL * ALL * LANES,
-    )(scalars, queries, keys, gathered)
-
-
-def attention_grads(scalars, queries, keys, gathered, stats):
+    )(scalars, queries, keys, upstream)
+
+
+def attention_grads(scalars, queries, keys, upstream, stats):
     return vmem_call(
         grads_body,
         (
@@ -272,14 +248,13 @@
             jax.ShapeDtypeStruct((8, ROWS, 2 * LANES), BF),
         ),
         scratch=[
-            pltpu.VMEM((ALL, HD), BF),
             pltpu.VMEM((ALL, LANES), F32),
             pltpu.VMEM((ALL, HD), F32),
         ],
         scalars=1,
         inputs=4,
         flops=6 * 2 * ALL * ALL * LANES,
-    )(scalars, queries, keys, gathered, stats)
+    )(scalars, queries, keys, upstream, stats)
 
 
 def gelu_parts(inputs):
@@ -291,8 +266,6 @@
 def on_device(frames, conv_weight, w_qkv, lengths, grad_out):
     index = lax.axis_index("tm")
     y, x = index // 32, index % 4
-    z_base = index % 32 - x
-    place = y * 4 + x
     ends = jnp.cumsum(lengths).astype(jnp.int32)
     groups = 2
     width = w_qkv.shape[0]
@@ -301,17 +274,12 @@
         return jnp.concatenate([jnp.stack(first).astype(jnp.int32), ends])
 
     frames_g = frames.reshape(ROWS, groups, HD).transpose(1, 0, 2)
-    frames_pad = with_halo(frames_g).reshape(groups * PADDED, HD)
-    taps = exchange_z(everyone(conv_weight[0]))
-    pair = jnp.concatenate([frames_pad, grad_out], axis=0)
-    pair = jnp.stack([pair, swap(pair, 32)])
-    gathered = exchange_x(everyone(pair, 4))
-    conv = conv_partial(scalars(y * 32 + x, z_base, y, x), gathered, taps)
-    conv = exchange_xy(conv)
-    conv = jnp.sum(conv.astype(F32), axis=0)
+    taps = exchange_x(everyone(exchange_z(everyone(conv_weight[0])), 4))
+    where = scalars(y, index)
+    conv = convolved(True, where, frames_g, taps)
+    upstream = doubled(grad_out)
     activated, slope = gelu_parts(conv)
     hidden = frames_g.astype(F32) + activated
-    all_taps = lax.all_gather(taps, "tm", axis=0, axis_index_groups=XY_GROUPS)
 
     hidden_all = lax.all_gather(hidden.astype(BF), "head", axis=0, tiled=True).astype(F32)
     center = jnp.sum(hidden_all, axis=(0, 2)) / width
@@ -335,13 +303,13 @@
     )
     keys_all = exchange_z(everyone(keys))
     queries_all = doubled(queries)
-    where = scalars(place, x)
-    stats = attention_stats(where, queries_all, keys_all, gathered)
+    order = scalars(y * 4 + x)
+    stats = attention_stats(order, queries_all, keys_all, upstream)
     stats = exchange_xy(everyone(stats))
-    od, dkv = attention_grads(where, queries_all, keys_all, gathered, stats)
+    od, dkv = attention_grads(order, queries_all, keys_all, upstream, stats)
     dkv = jnp.sum(exchange_z(dkv).astype(F32), axis=0).astype(BF)
     grad_q = halved(od[1])
-    attended = halved(od[0]).T
+    attended = halved(after(od[0], grad_q)).T
     grad_joined = jnp.concatenate([grad_q.T, dkv[:, :HD], dkv[:, LANES : LANES + HD]], axis=1)
 
     share = jnp.einsum("tj,gcj->gtc", grad_joined, weights, preferred_element_type=F32)
@@ -364,8 +332,7 @@
     )
 
     error = (slope * hidden_grad).astype(BF)
-    back = conv_back(scalars(index), with_halo(error), all_taps)
-    frame_grad = hidden_grad + back
+    frame_grad = hidden_grad + convolved(False, where, error, taps)
     frame_grad = frame_grad.astype(BF).transpose(1, 0, 2).reshape(ROWS, groups * HD)
 
     wide = lax.dot_general(

time: 280 us -> 257 us (0.918)
  the two profiles are of different devices: /device:TPU:8 before, /device:TPU:16 now
where the time goes in v3:
time: 257 us; the launch traced here: 255 us
  starting transfers between devices  96.3 us (37%)
  blocking collectives  53.8 us (21%)
  waiting for transfers between devices  49.9 us (19%)
  local copies, waits for them, and re-layouts  22.1 us (9%)
  other arithmetic  14.4 us (6%)
  Pallas kernels  12.5 us (5%)
  matrix products  4.27 us (2%)
    ppermute x16, starting transfers between devices, swap(): return lax.ppermute(array, 'tm', [(i, i ^ bit) for i in range(64)])  51 us
    ppermute x16, waiting for transfers between devices, swap(): return lax.ppermute(array, 'tm', [(i, i ^ bit) for i in range(64)])  27 us
    all_to_all x1, blocking collectives, exchange_z(): return lax.all_to_all(parts, 'tm', 0, 0, axis_index_groups=Z_GROUPS)  26.9 us
    all_to_all x3, starting transfers between devices, exchange_z(): return lax.all_to_all(parts, 'tm', 0, 0, axis_index_groups=Z_GROUPS)  18 us
    all_gather x1, blocking collectives, on_device(): lax.all_gather(hidden.astype(BF), 'head', axis=0, tiled=True).astype(F32)  16.5 us
    ppermute x2, waiting for transfers between devices, with_halo(): after = lax.ppermute(rows[:, :HALF], 'tm', down)  10.8 us
    all_to_all x1, blocking collectives, exchange_xy(): return lax.all_to_all(parts, 'tm', 0, 0, axis_index_groups=XY_GROUPS)  10.4 us
    ppermute x2, starting transfers between devices, with_halo(): before = lax.ppermute(rows[:, ROWS - HALF:], 'tm', up)  9.1 us
  transfers between devices with their start and end apart: 26, of which 14 were waited for; matrix products, arithmetic and copies ran while one was open for 12% of the time, Pallas kernels for 2%

profile of v3, /device:TPU:16, one launch (start us, length us, event | category | flops | bytes accessed | tf_op | source)
XLA Modules:
  0.0 255.3 jit_solution(2997781133465340215)
XLA Ops:
  0.6 0.9 broadcast_in_dim.29
  1.5 26.9 %all_to_all.40 = bf16[8,2,120,120]{3,2,1,0:T(8,128)(2,1)S(1)} all-to-all(bf16[8,2,120,120]{3,2,1,0:T(8,128)(2,1)S(1)} %broadcast_in_dim.29), channel_id=1, replica_groups={{0,32,64,96,128,160,192,224},{8,40,72,104,136,168,200,232},{16,48,80,11..., dimensions={0} | all-to-all | bytes 921600 | tf_op jit(solution)/shard_map/all_to_all | solution.py:44
  28.4 1.5 broadcast_in_dim.30
  30.0 4.4 %all-to-all-start.1 = ((bf16[4,8,2,120,120]{4,3,2,1,0:T(8,128)(2,1)}), bf16[4,8,2,120,120]{4,3,2,1,0:T(8,128)(2,1)S(1)}, u32[]{:S(2)}, u32[]{:S(2)}) async-start(bf16[4,8,2,120,120]{4,3,2,1,0:T(8,128)(2,1)} %broadcast_in_dim.30), calls=%async_computation.1 | async-start | bytes 3932160 | tf_op jit(solution)/shard_map/all_to_all | solution.py:36
  34.6 1.3 collective-permute-start.1
  35.9 4.6 %collective-permute-start = (bf16[2,32,120]{2,1,0:T(8,128)(2,1)S(1)}, bf16[2,32,120]{2,1,0:T(8,128)(2,1)S(1)}, u32[]{:S(2)}, u32[]{:S(2)}) collective-permute-start(bf16[2,32,120]{2,1,0:T(8,128)(2,1)S(1)} %get-tuple-element.34), channel_id=1, source_target_pairs={{0,8},{8,16},{16,24},{24,32},{32,40},{40,48},{48,56},{56,64},{64,7... | collective-permute-start | bytes 46088 | tf_op jit(solution)/shard_map/ppermute | solution.py:157
  41.2 3.5 %collective-permute-start.7 = (bf16[1,128,120]{2,1,0:T(8,128)(2,1)}, bf16[1,128,120]{2,1,0:T(8,128)(2,1)}, u32[]{:S(2)}, u32[]{:S(2)}) collective-permute-start(bf16[1,128,120]{2,1,0:T(8,128)(2,1)} %bitcast.14), channel_id=1, source_target_pairs={{0,256},{8,264},{16,272},{24,280},{32,288},{40,296},{48,304},{56,3... | collective-permute-start | bytes 92168 | tf_op jit(solution)/shard_map/ppermute | solution.py:40
  45.6 10.8 %collective-permute-done.1 = bf16[2,32,120]{2,1,0:T(8,128)(2,1)S(1)} collective-permute-done((bf16[2,32,120]{2,1,0:T(8,128)(2,1)S(1)}, bf16[2,32,120]{2,1,0:T(8,128)(2,1)S(1)}, u32[]{:S(2)}, u32[]{:S(2)}) %collective-permute-start.1) | collective-permute-done | bytes 15392 | tf_op jit(solution)/shard_map/ppermute | solution.py:158
  56.5 3.5 %collective-permute-start.2 = (bf16[2,192,120]{2,1,0:T(8,128)(2,1)S(1)}, bf16[2,192,120]{2,1,0:T(8,128)(2,1)S(1)}, u32[]{:S(2)}, u32[]{:S(2)}) collective-permute-start(bf16[2,192,120]{2,1,0:T(8,128)(2,1)S(1)} %get-tuple-element.27), channel_id=1, source_target_pairs={{0,256},{8,264},{16,272},{24,280},{32,288},{40,296},{48,304},{56,3... | collective-permute-start | bytes 276488 | tf_op jit(solution)/shard_map/ppermute | solution.py:40
  60.1 2.9 %collective-permute-done.2 = bf16[2,192,120]{2,1,0:T(8,128)(2,1)S(1)} collective-permute-done((bf16[2,192,120]{2,1,0:T(8,128)(2,1)S(1)}, bf16[2,192,120]{2,1,0:T(8,128)(2,1)S(1)}, u32[]{:S(2)}, u32[]{:S(2)}) %collective-permute-start.2) | collective-permute-done | bytes 92192 | tf_op jit(solution)/shard_map/ppermute | solution.py:40
  63.1 2.2 shard_map.76
  65.3 3.6 %collective-permute-start.3 = (bf16[2,128,120]{2,1,0:T(8,128)(2,1)S(1)}, bf16[2,128,120]{2,1,0:T(8,128)(2,1)}, u32[]{:S(2)}, u32[]{:S(2)}) collective-permute-start(bf16[2,128,120]{2,1,0:T(8,128)(2,1)S(1)} %get-tuple-element.10), channel_id=1, source_target_pairs={{0,256},{8,264},{16,272},{24,280},{32,288},{40,296},{48,304},{56,3... | collective-permute-start | bytes 184328 | tf_op jit(solution)/shard_map/ppermute | solution.py:40
  70.2 1.5 collective-permute-done.3
  71.7 0.9 fusion.25
  73.4 16.5 %all_gather.3 = bf16[16,128,120]{1,2,0:T(8,128)(2,1)S(1)} all-gather(bf16[2,128,120]{1,2,0:T(8,128)(2,1)} %copy.48), channel_id=1, replica_groups=mesh['tm'=64,'head'=8] {'head'}, dimensions={0}, use_global_device_ids=true | all-gather | bytes 552960 | tf_op jit(solution)/shard_map/all_gather | solution.py:284
  90.6 0.8 copy-done.2
  92.2 0.8 broadcast_in_dim.66
  93.1 3.5 %all-to-all-start.2 = ((bf16[8,128,256]{2,1,0:T(8,128)(2,1)}), bf16[8,128,256]{2,1,0:T(8,128)(2,1)S(1)}, u32[]{:S(2)}, u32[]{:S(2)}) async-start(bf16[8,128,256]{2,1,0:T(8,128)(2,1)} %broadcast_in_dim.66), calls=%async_computation.2 | async-start | bytes 1048576 | tf_op jit(solution)/shard_map/all_to_all | solution.py:44
  96.7 2.1 collective-permute-start.4
  98.8 0.8 pad_maximum_fusion.11
  99.6 4.6 %collective-permute-start.8 = (bf16[2,128,120]{2,1,0:T(8,128)(2,1)S(1)}, bf16[2,128,120]{2,1,0:T(8,128)(2,1)S(1)}, u32[]{:S(2)}, u32[]{:S(2)}) collective-permute-start(bf16[2,128,120]{2,1,0:T(8,128)(2,1)S(1)} %pad_maximum_fusion.11), channel_id=1, source_target_pairs={{0,16},{8,24},{16,0},{24,8},{32,48},{40,56},{48,32},{56,40},{64,80... | collective-permute-start | bytes 184328 | tf_op jit(solution)/shard_map/ppermute | solution.py:40
  104.2 2.9 %collective-permute-start.5 = (bf16[2,128,128]{2,1,0:T(8,128)(2,1)S(1)}, bf16[2,128,128]{2,1,0:T(8,128)(2,1)S(1)}, u32[]{:S(2)}, u32[]{:S(2)}) collective-permute-start(bf16[2,128,128]{2,1,0:T(8,128)(2,1)S(1)} %pad_maximum_fusion.10), channel_id=1, source_target_pairs={{0,16},{8,24},{16,0},{24,8},{32,48},{40,56},{48,32},{56,40},{64,80... | collective-permute-start | bytes 196616 | tf_op jit(solution)/shard_map/ppermute | solution.py:40
  107.3 0.8 pad_maximum_fusion.6
  108.1 2.2 collective-permute-start.9
  110.3 1.6 collective-permute-done.5
  111.9 2.2 collective-permute-start.6
  114.9 0.8 pad_maximum_fusion.2.d_ref
  115.8 3.0 %collective-permute-done.6 = bf16[4,128,128]{2,1,0:T(8,128)(2,1)S(1)} collective-permute-done((bf16[4,128,128]{2,1,0:T(8,128)(2,1)S(1)}, bf16[4,128,128]{2,1,0:T(8,128)(2,1)S(1)}, u32[]{:S(2)}, u32[]{:S(2)}) %collective-permute-start.6) | collective-permute-done | bytes 131104 | tf_op jit(solution)/shard_map/ppermute | solution.py:40
  118.8 2.5 shard_map.77
  121.3 10.4 %all_to_all.41.stats_ref = f32[8,3,8,128]{3,2,1,0:T(8,128)S(1)} all-to-all(f32[8,3,8,128]{3,2,1,0:T(8,128)S(1)} %broadcast_in_dim.68), channel_id=1, replica_groups={{0,8,16,24,256,264,272,280},{32,40,48,56,288,296,304,312},{64,72,80,88,..., dimensions={0} | all-to-all | bytes 196608 | tf_op jit(solution)/shard_map/all_to_all | solution.py:32
  131.7 0.9 copy-done.1
  132.7 4.2 %shard_map.78 = (bf16[2,8,120,128]{3,2,1,0:T(8,128)(2,1)S(1)}, bf16[8,128,256]{2,1,0:T(8,128)(2,1)}) custom-call(s32[5]{0:T(128)S(1)} %pad_add_fusion.sc_ref, bf16[8,128,128]{2,1,0:T(8,128)(2,1)S(1)} %copy-done.1, bf16[8,128,256]{2,1,0:T(8,128)(2,1)S(1)} %all-to-all-done.2.kv_ref, bf16[8,128,120]{2,1,0:T(8,128)(2,1)S(1)} %pad_maximum_fusion.2.d_ref, ...), custom_call_target="tpu_custom_call" | custom-call | flops 1610612736 | bytes 1048576 | tf_op jit(solution)/shard_map/pallas_call | solution.py:244
  136.9 7.1 %all-to-all-start.4 = ((bf16[8,128,256]{2,1,0:T(8,128)(2,1)}), bf16[8,128,256]{2,1,0:T(8,128)(2,1)}, u32[]{:S(2)}, u32[]{:S(2)}) async-start(bf16[8,128,256]{2,1,0:T(8,128)(2,1)} %get-tuple-element.12), calls=%async_computation.4 | async-start | bytes 1048576 | tf_op jit(solution)/shard_map/all_to_all | solution.py:44
  144.1 2.5 collective-permute-start.10
  146.5 4.3 %collective-permute-done.10 = bf16[4,120,128]{2,1,0:T(8,128)(2,1)S(1)} collective-permute-done((bf16[4,120,128]{2,1,0:T(8,128)(2,1)S(1)}, bf16[4,120,128]{2,1,0:T(8,128)(2,1)S(1)}, u32[]{:S(2)}, u32[]{:S(2)}) %collective-permute-start.10) | collective-permute-done | bytes 122912 | tf_op jit(solution)/shard_map/ppermute | solution.py:40
  150.9 2.9 %collective-permute-start.11 = (bf16[2,120,128]{2,1,0:T(8,128)(2,1)S(1)}, bf16[2,120,128]{2,1,0:T(8,128)(2,1)S(1)}, u32[]{:S(2)}, u32[]{:S(2)}) collective-permute-start(bf16[2,120,128]{2,1,0:T(8,128)(2,1)S(1)} %slice.142), channel_id=1, source_target_pairs={{0,16},{8,24},{16,0},{24,8},{32,48},{40,56},{48,32},{56,40},{64,80... | collective-permute-start | bytes 184328 | tf_op jit(solution)/shard_map/ppermute | solution.py:40
  153.8 4.7 %collective-permute-done.11 = bf16[2,120,128]{2,1,0:T(8,128)(2,1)S(1)} collective-permute-done((bf16[2,120,128]{2,1,0:T(8,128)(2,1)S(1)}, bf16[2,120,128]{2,1,0:T(8,128)(2,1)S(1)}, u32[]{:S(2)}, u32[]{:S(2)}) %collective-permute-start.11) | collective-permute-done | bytes 61472 | tf_op jit(solution)/shard_map/ppermute | solution.py:40
  158.5 2.9 %collective-permute-start.12 = (bf16[1,120,128]{2,1,0:T(8,128)(2,1)S(1)}, bf16[1,120,128]{2,1,0:T(8,128)(2,1)S(1)}, u32[]{:S(2)}, u32[]{:S(2)}) collective-permute-start(bf16[1,120,128]{2,1,0:T(8,128)(2,1)S(1)} %slice.144), channel_id=1, source_target_pairs={{0,256},{8,264},{16,272},{24,280},{32,288},{40,296},{48,304},{56,3... | collective-permute-start | bytes 92168 | tf_op jit(solution)/shard_map/ppermute | solution.py:40
  161.4 2.6 %copy.60 = bf16[1920,360]{1,0:T(8,128)(2,1)} copy(bf16[1920,360]{0,1:T(8,128)(2,1)} %param.7) | data formatting | bytes 2764800 | tf_op jit(solution)/shard_map/reshape | solution.py:290
  164.5 1.1 reduce_sum.90
  165.8 2.0 fusion.3
  168.2 0.8 pad_maximum_fusion
  169.1 6.9 %all-to-all-start.5 = ((bf16[8,2,128,128]{2,3,1,0:T(8,128)(2,1)}), bf16[8,2,128,128]{2,3,1,0:T(8,128)(2,1)}, u32[]{:S(2)}, u32[]{:S(2)}) async-start(bf16[8,2,128,128]{2,3,1,0:T(8,128)(2,1)} %bitcast.82), calls=%async_computation.5 | async-start | bytes 1048576 | tf_op jit(solution)/shard_map/all_to_all | solution.py:325
  176.0 1.7 convolution_convert_fusion
  177.7 2.5 copy.56
  180.3 3.5 %reshape.78 = bf16[2,8,4,30,360]{4,3,2,1,0:T(8,128)(2,1)} reshape(bf16[1920,360]{1,0:T(8,128)(2,1)} %copy.56) | data formatting | bytes 2764800 | tf_op jit(solution)/shard_map/reshape | solution.py:342
  183.8 3.4 %copy.57 = bf16[2,4,8,30,360]{4,2,3,1,0:T(8,128)(2,1)} copy(bf16[2,4,8,30,360]{4,3,1,2,0:T(8,128)(2,1)} %bitcast.79) | data formatting | bytes 2764800 | tf_op jit(solution)/shard_map/transpose | solution.py:342
  187.2 4.6 %all-to-all-done.5 = bf16[8,2,128,128]{2,3,1,0:T(8,128)(2,1)} async-done(((bf16[8,2,128,128]{2,3,1,0:T(8,128)(2,1)}), bf16[8,2,128,128]{2,3,1,0:T(8,128)(2,1)}, u32[]{:S(2)}, u32[]{:S(2)}) %all-to-all-start.5) | async-done | bytes 524320 | tf_op jit(solution)/shard_map/all_to_all | solution.py:325
  191.8 4.3 %all-to-all-start.6 = ((bf16[8,8,30,360]{3,1,2,0:T(8,128)(2,1)}), bf16[8,8,30,360]{3,1,2,0:T(8,128)(2,1)}, u32[]{:S(2)}, u32[]{:S(2)}) async-start(bf16[8,8,30,360]{3,1,2,0:T(8,128)(2,1)} %bitcast.81), calls=%async_computation.6 | async-start | bytes 2949120 | tf_op jit(solution)/shard_map/all_to_all | solution.py:32
  197.3 3.8 %collective-permute-start.13 = (bf16[4,120,128]{2,1,0:T(8,128)(2,1)S(1)}, bf16[4,120,128]{2,1,0:T(8,128)(2,1)S(1)}, u32[]{:S(2)}, u32[]{:S(2)}) collective-permute-start(bf16[4,120,128]{2,1,0:T(8,128)(2,1)S(1)} %slice_bitcast_fusion), channel_id=1, source_target_pairs={{0,8},{8,0},{16,24},{24,16},{32,40},{40,32},{48,56},{56,48},{64,72... | collective-permute-start | bytes 368648 | tf_op jit(solution)/shard_map/ppermute | solution.py:40
  201.1 1.1 convert_reduce_fusion.1
  202.4 1.0 fusion.9
  203.4 1.3 collective-permute-start.17
  204.7 4.5 %collective-permute-start.16 = (bf16[2,32,120]{2,1,0:T(8,128)(2,1)S(1)}, bf16[2,32,120]{2,1,0:T(8,128)(2,1)S(1)}, u32[]{:S(2)}, u32[]{:S(2)}) collective-permute-start(bf16[2,32,120]{2,1,0:T(8,128)(2,1)S(1)} %get-tuple-element.30), channel_id=1, source_target_pairs={{0,8},{8,16},{16,24},{24,32},{32,40},{40,48},{48,56},{56,64},{64,7... | collective-permute-start | bytes 46088 | tf_op jit(solution)/shard_map/ppermute | solution.py:157
  209.2 7.6 %collective-permute-done.13 = bf16[4,120,128]{2,1,0:T(8,128)(2,1)S(1)} collective-permute-done((bf16[4,120,128]{2,1,0:T(8,128)(2,1)S(1)}, bf16[4,120,128]{2,1,0:T(8,128)(2,1)S(1)}, u32[]{:S(2)}, u32[]{:S(2)}) %collective-permute-start.13) | collective-permute-done | bytes 122912 | tf_op jit(solution)/shard_map/ppermute | solution.py:40
  216.8 4.6 %collective-permute-start.14 = (bf16[2,120,128]{2,1,0:T(8,128)(2,1)S(1)}, bf16[2,120,128]{2,1,0:T(8,128)(2,1)S(1)}, u32[]{:S(2)}, u32[]{:S(2)}) collective-permute-start(bf16[2,120,128]{2,1,0:T(8,128)(2,1)S(1)} %slice.149), channel_id=1, source_target_pairs={{0,16},{8,24},{16,0},{24,8},{32,48},{40,56},{48,32},{56,40},{64,80... | collective-permute-start | bytes 184328 | tf_op jit(solution)/shard_map/ppermute | solution.py:40
  221.5 3.3 %collective-permute-start.18 = (bf16[2,192,120]{2,1,0:T(8,128)(2,1)S(1)}, bf16[2,192,120]{2,1,0:T(8,128)(2,1)S(1)}, u32[]{:S(2)}, u32[]{:S(2)}) collective-permute-start(bf16[2,192,120]{2,1,0:T(8,128)(2,1)S(1)} %get-tuple-element.22), channel_id=1, source_target_pairs={{0,256},{8,264},{16,272},{24,280},{32,288},{40,296},{48,304},{56,3... | collective-permute-start | bytes 276488 | tf_op jit(solution)/shard_map/ppermute | solution.py:40
  224.8 3.1 %collective-permute-start.15 = (bf16[1,120,128]{2,1,0:T(8,128)(2,1)S(1)}, bf16[1,120,128]{2,1,0:T(8,128)(2,1)S(1)}, u32[]{:S(2)}, u32[]{:S(2)}) collective-permute-start(bf16[1,120,128]{2,1,0:T(8,128)(2,1)S(1)} %slice.151), channel_id=1, source_target_pairs={{0,256},{8,264},{16,272},{24,280},{32,288},{40,296},{48,304},{56,3... | collective-permute-start | bytes 92168 | tf_op jit(solution)/shard_map/ppermute | solution.py:40
  228.0 3.6 %shard_map.79 = (f32[2,128,120]{2,1,0:T(8,128)S(1)}, bf16[2,128,120]{2,1,0:T(8,128)(2,1)S(1)}) custom-call(s32[6]{0:T(128)S(1)} %pad_add_fusion.1.sc_ref, bf16[2,2,192,120]{3,2,1,0:T(8,128)(2,1)S(1)} %pad_maximum_fusion.4.x_ref, bf16[4,8,2,120,120]{4,3,2,1,0:T(8,128)(2,1)S(1)} %all-to-all-done.1.w_ref), custom_call_target="tpu_custom_call" | custom-call | flops 471859200 | bytes 1048576 | tf_op jit(solution)/shard_map/pallas_call | solution.py:140
  231.7 3.5 %collective-permute-start.19 = (bf16[2,128,120]{2,1,0:T(8,128)(2,1)S(1)}, bf16[2,128,120]{2,1,0:T(8,128)(2,1)S(1)}, u32[]{:S(2)}, u32[]{:S(2)}) collective-permute-start(bf16[2,128,120]{2,1,0:T(8,128)(2,1)S(1)} %get-tuple-element.14), channel_id=1, source_target_pairs={{0,256},{8,264},{16,272},{24,280},{32,288},{40,296},{48,304},{56,3... | collective-permute-start | bytes 184328 | tf_op jit(solution)/shard_map/ppermute | solution.py:40
  235.1 1.6 reduce_sum.94
  237.5 7.4 %all-to-all-start.7 = ((bf16[8,30,360]{2,1,0:T(8,128)(2,1)}), bf16[8,30,360]{2,1,0:T(8,128)(2,1)S(1)}, u32[]{:S(2)}, u32[]{:S(2)}) async-start(bf16[8,30,360]{2,1,0:T(8,128)(2,1)} %copy.58), calls=%async_computation.7 | async-start | bytes 393216 | tf_op jit(solution)/shard_map/all_to_all | solution.py:44
  245.5 1.0 fusion.13
  247.2 7.4 %all-to-all-done.7 = bf16[8,30,360]{2,1,0:T(8,128)(2,1)S(1)} async-done(((bf16[8,30,360]{2,1,0:T(8,128)(2,1)}), bf16[8,30,360]{2,1,0:T(8,128)(2,1)S(1)}, u32[]{:S(2)}, u32[]{:S(2)}) %all-to-all-start.7) | async-done | bytes 172832 | tf_op jit(solution)/shard_map/all_to_all | solution.py:44
  (108 shorter events, 11.5 us)
Async XLA Ops:
  30.0 4.4 %copy-start.9 = (bf16[128,240]{0,1:T(8,128)(2,1)S(1)}, bf16[128,240]{0,1:T(8,128)(2,1)}, u32[]{:S(2)}) copy-start(bf16[128,240]{0,1:T(8,128)(2,1)} %param.5) | copy-start | bytes 184324
  30.0 10.4 %copy-start.10 = (bf16[128,120]{0,1:T(8,128)(2,1)S(1)}, bf16[128,120]{0,1:T(8,128)(2,1)}, u32[]{:S(2)}) copy-start(bf16[128,120]{0,1:T(8,128)(2,1)} %param.9) | copy-start | bytes 92164
  30.0 14.7 %copy-start.16 = (s32[4]{0:T(128)S(1)}, s32[4]{0:T(128)}, u32[]{:S(2)}) copy-start(s32[4]{0:T(128)} %param.8) | copy-start | bytes 52
  30.0 33.1 %all-to-all-start.1 = ((bf16[4,8,2,120,120]{4,3,2,1,0:T(8,128)(2,1)}), bf16[4,8,2,120,120]{4,3,2,1,0:T(8,128)(2,1)S(1)}, u32[]{:S(2)}, u32[]{:S(2)}) async-start(bf16[4,8,2,120,120]{4,3,2,1,0:T(8,128)(2,1)} %broadcast_in_dim.30), calls=%async_computation.1 | async-start | bytes 3932160 | tf_op jit(solution)/shard_map/all_to_all | solution.py:36
  34.5 28.5 %copy-start.5 = (bf16[128,2,120]{2,0,1:T(8,128)(2,1)}, bf16[128,2,120]{2,0,1:T(8,128)(2,1)S(1)}, u32[]{:S(2)}) copy-start(bf16[128,2,120]{2,0,1:T(8,128)(2,1)S(1)} %copy.47) | copy-start | bytes 184324
  34.6 21.9 %collective-permute-start.1 = (bf16[2,32,120]{2,1,0:T(8,128)(2,1)S(1)}, bf16[2,32,120]{2,1,0:T(8,128)(2,1)S(1)}, u32[]{:S(2)}, u32[]{:S(2)}) collective-permute-start(bf16[2,32,120]{2,1,0:T(8,128)(2,1)S(1)} %get-tuple-element.35), channel_id=1, source_target_pairs={{8,0},{16,8},{24,16},{32,24},{40,32},{48,40},{56,48},{64,56},{72,6... | collective-permute-start | bytes 46088 | tf_op jit(solution)/shard_map/ppermute | solution.py:158
  35.9 20.6 %collective-permute-start = (bf16[2,32,120]{2,1,0:T(8,128)(2,1)S(1)}, bf16[2,32,120]{2,1,0:T(8,128)(2,1)S(1)}, u32[]{:S(2)}, u32[]{:S(2)}) collective-permute-start(bf16[2,32,120]{2,1,0:T(8,128)(2,1)S(1)} %get-tuple-element.34), channel_id=1, source_target_pairs={{0,8},{8,16},{16,24},{24,32},{32,40},{40,48},{48,56},{56,64},{64,7... | collective-permute-start | bytes 46088 | tf_op jit(solution)/shard_map/ppermute | solution.py:157
  41.2 57.6 %collective-permute-start.7 = (bf16[1,128,120]{2,1,0:T(8,128)(2,1)}, bf16[1,128,120]{2,1,0:T(8,128)(2,1)}, u32[]{:S(2)}, u32[]{:S(2)}) collective-permute-start(bf16[1,128,120]{2,1,0:T(8,128)(2,1)} %bitcast.14), channel_id=1, source_target_pairs={{0,256},{8,264},{16,272},{24,280},{32,288},{40,296},{48,304},{56,3... | collective-permute-start | bytes 92168 | tf_op jit(solution)/shard_map/ppermute | solution.py:40
  44.8 18.2 %copy-start.14 = (s32[4,1]{0,1:T(1,128)}, s32[4,1]{0,1:T(1,128)S(1)}, u32[]{:S(2)}) copy-start(s32[4,1]{0,1:T(1,128)S(1)} %reduce-window.4) | copy-start | bytes 52
  56.5 6.5 %collective-permute-start.2 = (bf16[2,192,120]{2,1,0:T(8,128)(2,1)S(1)}, bf16[2,192,120]{2,1,0:T(8,128)(2,1)S(1)}, u32[]{:S(2)}, u32[]{:S(2)}) collective-permute-start(bf16[2,192,120]{2,1,0:T(8,128)(2,1)S(1)} %get-tuple-element.27), channel_id=1, source_target_pairs={{0,256},{8,264},{16,272},{24,280},{32,288},{40,296},{48,304},{56,3... | collective-permute-start | bytes 276488 | tf_op jit(solution)/shard_map/ppermute | solution.py:40
  65.3 26.1 %copy-start.4 = (bf16[1920,360]{0,1:T(8,128)(2,1)S(1)}, bf16[1920,360]{0,1:T(8,128)(2,1)}, u32[]{:S(2)}) copy-start(bf16[1920,360]{0,1:T(8,128)(2,1)} %param.7) | copy-start | bytes 4147204
  65.3 6.4 %collective-permute-start.3 = (bf16[2,128,120]{2,1,0:T(8,128)(2,1)S(1)}, bf16[2,128,120]{2,1,0:T(8,128)(2,1)}, u32[]{:S(2)}, u32[]{:S(2)}) collective-permute-start(bf16[2,128,120]{2,1,0:T(8,128)(2,1)S(1)} %get-tuple-element.10), channel_id=1, source_target_pairs={{0,256},{8,264},{16,272},{24,280},{32,288},{40,296},{48,304},{56,3... | collective-permute-start | bytes 184328 | tf_op jit(solution)/shard_map/ppermute | solution.py:40
  90.1 0.5 copy-start.11
  90.1 2.0 copy-start.8
  90.1 2.0 copy-start.13
  90.6 0.8 copy-start.2
  92.0 4.6 %copy-start.7 = (bf16[128,8]{1,0:T(8,128)(2,1)S(1)}, bf16[128,8]{1,0:T(8,128)(2,1)}, u32[]{:S(2)}) copy-start(bf16[128,8]{1,0:T(8,128)(2,1)} %fusion.14) | copy-start | bytes 6148
  92.0 22.0 %copy-start.15 = (s32[4,1]{0,1:T(1,128)S(1)}, s32[4,1]{0,1:T(1,128)}, u32[]{:S(2)}) copy-start(s32[4,1]{0,1:T(1,128)} %copy-done.14) | copy-start | bytes 52
  93.1 25.7 %all-to-all-start.2 = ((bf16[8,128,256]{2,1,0:T(8,128)(2,1)}), bf16[8,128,256]{2,1,0:T(8,128)(2,1)S(1)}, u32[]{:S(2)}, u32[]{:S(2)}) async-start(bf16[8,128,256]{2,1,0:T(8,128)(2,1)} %broadcast_in_dim.66), calls=%async_computation.2 | async-start | bytes 1048576 | tf_op jit(solution)/shard_map/all_to_all | solution.py:44
  96.7 7.5 %collective-permute-start.4 = (bf16[1,128,128]{2,1,0:T(8,128)(2,1)S(1)}, bf16[1,128,128]{2,1,0:T(8,128)(2,1)S(1)}, u32[]{:S(2)}, u32[]{:S(2)}) collective-permute-start(bf16[1,128,128]{2,1,0:T(8,128)(2,1)S(1)} %maximum_bitcast_fusion), channel_id=1, source_target_pairs={{0,256},{8,264},{16,272},{24,280},{32,288},{40,296},{48,304},{56,3... | collective-permute-start | bytes 98312 | tf_op jit(solution)/shard_map/ppermute | solution.py:40
  99.6 7.7 %collective-permute-start.8 = (bf16[2,128,120]{2,1,0:T(8,128)(2,1)S(1)}, bf16[2,128,120]{2,1,0:T(8,128)(2,1)S(1)}, u32[]{:S(2)}, u32[]{:S(2)}) collective-permute-start(bf16[2,128,120]{2,1,0:T(8,128)(2,1)S(1)} %pad_maximum_fusion.11), channel_id=1, source_target_pairs={{0,16},{8,24},{16,0},{24,8},{32,48},{40,56},{48,32},{56,40},{64,80... | collective-permute-start | bytes 184328 | tf_op jit(solution)/shard_map/ppermute | solution.py:40
  104.2 7.7 %collective-permute-start.5 = (bf16[2,128,128]{2,1,0:T(8,128)(2,1)S(1)}, bf16[2,128,128]{2,1,0:T(8,128)(2,1)S(1)}, u32[]{:S(2)}, u32[]{:S(2)}) collective-permute-start(bf16[2,128,128]{2,1,0:T(8,128)(2,1)S(1)} %pad_maximum_fusion.10), channel_id=1, source_target_pairs={{0,16},{8,24},{16,0},{24,8},{32,48},{40,56},{48,32},{56,40},{64,80... | collective-permute-start | bytes 196616 | tf_op jit(solution)/shard_map/ppermute | solution.py:40
  108.1 6.9 %collective-permute-start.9 = (bf16[4,128,120]{2,1,0:T(8,128)(2,1)S(1)}, bf16[4,128,120]{2,1,0:T(8,128)(2,1)S(1)}, u32[]{:S(2)}, u32[]{:S(2)}) collective-permute-start(bf16[4,128,120]{2,1,0:T(8,128)(2,1)S(1)} %pad_maximum_fusion.6), channel_id=1, source_target_pairs={{0,8},{8,0},{16,24},{24,16},{32,40},{40,32},{48,56},{56,48},{64,72... | collective-permute-start | bytes 368648 | tf_op jit(solution)/shard_map/ppermute | solution.py:40
  111.9 6.9 %collective-permute-start.6 = (bf16[4,128,128]{2,1,0:T(8,128)(2,1)S(1)}, bf16[4,128,128]{2,1,0:T(8,128)(2,1)S(1)}, u32[]{:S(2)}, u32[]{:S(2)}) collective-permute-start(bf16[4,128,128]{2,1,0:T(8,128)(2,1)S(1)} %pad_maximum_fusion.5), channel_id=1, source_target_pairs={{0,8},{8,0},{16,24},{24,16},{32,40},{40,32},{48,56},{56,48},{64,72... | collective-permute-start | bytes 393224 | tf_op jit(solution)/shard_map/ppermute | solution.py:40
  118.8 2.5 copy-start
  131.7 1.0 copy-start.1
  136.9 27.5 %all-to-all-start.4 = ((bf16[8,128,256]{2,1,0:T(8,128)(2,1)}), bf16[8,128,256]{2,1,0:T(8,128)(2,1)}, u32[]{:S(2)}, u32[]{:S(2)}) async-start(bf16[8,128,256]{2,1,0:T(8,128)(2,1)} %get-tuple-element.12), calls=%async_computation.4 | async-start | bytes 1048576 | tf_op jit(solution)/shard_map/all_to_all | solution.py:44
  144.1 6.8 %collective-permute-start.10 = (bf16[4,120,128]{2,1,0:T(8,128)(2,1)S(1)}, bf16[4,120,128]{2,1,0:T(8,128)(2,1)S(1)}, u32[]{:S(2)}, u32[]{:S(2)}) collective-permute-start(bf16[4,120,128]{2,1,0:T(8,128)(2,1)S(1)} %slice_bitcast_fusion.2), channel_id=1, source_target_pairs={{0,8},{8,0},{16,24},{24,16},{32,40},{40,32},{48,56},{56,48},{64,72... | collective-permute-start | bytes 368648 | tf_op jit(solution)/shard_map/ppermute | solution.py:40
  150.9 7.6 %collective-permute-start.11 = (bf16[2,120,128]{2,1,0:T(8,128)(2,1)S(1)}, bf16[2,120,128]{2,1,0:T(8,128)(2,1)S(1)}, u32[]{:S(2)}, u32[]{:S(2)}) collective-permute-start(bf16[2,120,128]{2,1,0:T(8,128)(2,1)S(1)} %slice.142), channel_id=1, source_target_pairs={{0,16},{8,24},{16,0},{24,8},{32,48},{40,56},{48,32},{56,40},{64,80... | collective-permute-start | bytes 184328 | tf_op jit(solution)/shard_map/ppermute | solution.py:40
  158.5 7.3 %copy-start.3 = (bf16[16,128,120]{1,2,0:T(8,128)(2,1)S(1)}, bf16[16,128,120]{1,2,0:T(8,128)(2,1)}, u32[]{:S(2)}) copy-start(bf16[16,128,120]{1,2,0:T(8,128)(2,1)} %copy-done.2) | copy-start | bytes 1474564
  158.5 5.9 %collective-permute-start.12 = (bf16[1,120,128]{2,1,0:T(8,128)(2,1)S(1)}, bf16[1,120,128]{2,1,0:T(8,128)(2,1)S(1)}, u32[]{:S(2)}, u32[]{:S(2)}) collective-permute-start(bf16[1,120,128]{2,1,0:T(8,128)(2,1)S(1)} %slice.144), channel_id=1, source_target_pairs={{0,256},{8,264},{16,272},{24,280},{32,288},{40,296},{48,304},{56,3... | collective-permute-start | bytes 92168 | tf_op jit(solution)/shard_map/ppermute | solution.py:40
  169.1 22.7 %all-to-all-start.5 = ((bf16[8,2,128,128]{2,3,1,0:T(8,128)(2,1)}), bf16[8,2,128,128]{2,3,1,0:T(8,128)(2,1)}, u32[]{:S(2)}, u32[]{:S(2)}) async-start(bf16[8,2,128,128]{2,3,1,0:T(8,128)(2,1)} %bitcast.82), calls=%async_computation.5 | async-start | bytes 1048576 | tf_op jit(solution)/shard_map/all_to_all | solution.py:325
  191.8 43.4 %all-to-all-start.6 = ((bf16[8,8,30,360]{3,1,2,0:T(8,128)(2,1)}), bf16[8,8,30,360]{3,1,2,0:T(8,128)(2,1)}, u32[]{:S(2)}, u32[]{:S(2)}) async-start(bf16[8,8,30,360]{3,1,2,0:T(8,128)(2,1)} %bitcast.81), calls=%async_computation.6 | async-start | bytes 2949120 | tf_op jit(solution)/shard_map/all_to_all | solution.py:32
  196.1 6.3 %copy-start.6 = (bf16[128,2,120]{2,0,1:T(8,128)(2,1)S(1)}, bf16[128,2,120]{2,0,1:T(8,128)(2,1)}, u32[]{:S(2)}) copy-start(bf16[128,2,120]{2,0,1:T(8,128)(2,1)} %copy-done.5) | copy-start | bytes 184324
  196.1 6.3 %copy-start.12 = (f32[128]{0:T(128)S(1)}, f32[128]{0:T(128)}, u32[]{:S(2)}) copy-start(f32[128]{0:T(128)} %copy-done.11) | copy-start | bytes 1540
  197.3 19.5 %collective-permute-start.13 = (bf16[4,120,128]{2,1,0:T(8,128)(2,1)S(1)}, bf16[4,120,128]{2,1,0:T(8,128)(2,1)S(1)}, u32[]{:S(2)}, u32[]{:S(2)}) collective-permute-start(bf16[4,120,128]{2,1,0:T(8,128)(2,1)S(1)} %slice_bitcast_fusion), channel_id=1, source_target_pairs={{0,8},{8,0},{16,24},{24,16},{32,40},{40,32},{48,56},{56,48},{64,72... | collective-permute-start | bytes 368648 | tf_op jit(solution)/shard_map/ppermute | solution.py:40
  203.4 18.1 %collective-permute-start.17 = (bf16[2,32,120]{2,1,0:T(8,128)(2,1)S(1)}, bf16[2,32,120]{2,1,0:T(8,128)(2,1)S(1)}, u32[]{:S(2)}, u32[]{:S(2)}) collective-permute-start(bf16[2,32,120]{2,1,0:T(8,128)(2,1)S(1)} %get-tuple-element.31), channel_id=1, source_target_pairs={{8,0},{16,8},{24,16},{32,24},{40,32},{48,40},{56,48},{64,56},{72,6... | collective-permute-start | bytes 46088 | tf_op jit(solution)/shard_map/ppermute | solution.py:158
  204.7 16.8 %collective-permute-start.16 = (bf16[2,32,120]{2,1,0:T(8,128)(2,1)S(1)}, bf16[2,32,120]{2,1,0:T(8,128)(2,1)S(1)}, u32[]{:S(2)}, u32[]{:S(2)}) collective-permute-start(bf16[2,32,120]{2,1,0:T(8,128)(2,1)S(1)} %get-tuple-element.30), channel_id=1, source_target_pairs={{0,8},{8,16},{16,24},{24,32},{32,40},{40,48},{48,56},{56,64},{64,7... | collective-permute-start | bytes 46088 | tf_op jit(solution)/shard_map/ppermute | solution.py:157
  216.8 8.0 %collective-permute-start.14 = (bf16[2,120,128]{2,1,0:T(8,128)(2,1)S(1)}, bf16[2,120,128]{2,1,0:T(8,128)(2,1)S(1)}, u32[]{:S(2)}, u32[]{:S(2)}) collective-permute-start(bf16[2,120,128]{2,1,0:T(8,128)(2,1)S(1)} %slice.149), channel_id=1, source_target_pairs={{0,16},{8,24},{16,0},{24,8},{32,48},{40,56},{48,32},{56,40},{64,80... | collective-permute-start | bytes 184328 | tf_op jit(solution)/shard_map/ppermute | solution.py:40
  221.5 6.5 %collective-permute-start.18 = (bf16[2,192,120]{2,1,0:T(8,128)(2,1)S(1)}, bf16[2,192,120]{2,1,0:T(8,128)(2,1)S(1)}, u32[]{:S(2)}, u32[]{:S(2)}) collective-permute-start(bf16[2,192,120]{2,1,0:T(8,128)(2,1)S(1)} %get-tuple-element.22), channel_id=1, source_target_pairs={{0,256},{8,264},{16,272},{24,280},{32,288},{40,296},{48,304},{56,3... | collective-permute-start | bytes 276488 | tf_op jit(solution)/shard_map/ppermute | solution.py:40
  224.8 20.1 %collective-permute-start.15 = (bf16[1,120,128]{2,1,0:T(8,128)(2,1)S(1)}, bf16[1,120,128]{2,1,0:T(8,128)(2,1)S(1)}, u32[]{:S(2)}, u32[]{:S(2)}) collective-permute-start(bf16[1,120,128]{2,1,0:T(8,128)(2,1)S(1)} %slice.151), channel_id=1, source_target_pairs={{0,256},{8,264},{16,272},{24,280},{32,288},{40,296},{48,304},{56,3... | collective-permute-start | bytes 92168 | tf_op jit(solution)/shard_map/ppermute | solution.py:40
  231.7 13.9 %collective-permute-start.19 = (bf16[2,128,120]{2,1,0:T(8,128)(2,1)S(1)}, bf16[2,128,120]{2,1,0:T(8,128)(2,1)S(1)}, u32[]{:S(2)}, u32[]{:S(2)}) collective-permute-start(bf16[2,128,120]{2,1,0:T(8,128)(2,1)S(1)} %get-tuple-element.14), channel_id=1, source_target_pairs={{0,256},{8,264},{16,272},{24,280},{32,288},{40,296},{48,304},{56,3... | collective-permute-start | bytes 184328 | tf_op jit(solution)/shard_map/ppermute | solution.py:40
  237.5 17.2 %all-to-all-start.7 = ((bf16[8,30,360]{2,1,0:T(8,128)(2,1)}), bf16[8,30,360]{2,1,0:T(8,128)(2,1)S(1)}, u32[]{:S(2)}, u32[]{:S(2)}) async-start(bf16[8,30,360]{2,1,0:T(8,128)(2,1)} %copy.58), calls=%async_computation.7 | async-start | bytes 393216 | tf_op jit(solution)/shard_map/all_to_all | solution.py:44

commit v4 on v3

--- a/solution.py
+++ b/solution.py
@@ -134,9 +134,11 @@
                 other_ref[g] = totals[g].astype(BF)
 
 
-def convolved(forward, scalars, rows, taps):
-    padded = with_halo(rows)
-    pair = jnp.stack([padded, swap(padded, 32)])
+def paired(padded):
+    return jnp.stack([padded, swap(padded, 32)])
+
+
+def convolved(forward, scalars, pair, taps):
     own, other = vmem_call(
         functools.partial(conv_body, forward),
         (
@@ -257,6 +259,74 @@
     )(scalars, queries, keys, upstream, stats)
 
 
+GROUPS = 16
+SLAB = 32
+
+
+def share_body(dq_ref, dkv_ref, normed_ref, w_ref, parts_ref, grad_ref):
+    dkv = dkv_ref[0].astype(F32)
+    for i in range(1, 8):
+        dkv += dkv_ref[i].astype(F32)
+    grad_ref[:, :HD] = dq_ref[...].astype(F32).T.astype(BF)
+    grad_ref[:, HD : 2 * HD] = dkv[:, :HD].astype(BF)
+    grad_ref[:, 2 * HD :] = dkv[:, LANES : LANES + HD].astype(BF)
+    grad = grad_ref[...]
+    plain = jnp.zeros((ROWS, HD), F32)
+    along = jnp.zeros((ROWS, HD), F32)
+    for g in range(GROUPS):
+        share = lax.dot_general(
+            grad, w_ref[g * HD : (g + 1) * HD], CONTRACT, preferred_element_type=F32
+        )
+        plain += share
+        along += share * normed_ref[g].astype(F32)
+        parts_ref[g, :, :HD] = share.astype(BF)
+    plain = jnp.sum(plain, axis=1, keepdims=True)
+    along = jnp.sum(along, axis=1, keepdims=True)
+    lane = lax.broadcasted_iota(jnp.int32, (ROWS, LANES - HD), 1)
+    plain_high = plain.astype(BF).astype(F32)
+    along_high = along.astype(BF).astype(F32)
+    sums = jnp.where(lane == 0, plain_high, 0.0)
+    sums = jnp.where(lane == 1, along_high, sums)
+    sums = jnp.where(lane == 2, plain - plain_high, sums)
+    sums = jnp.where(lane == 3, along - along_high, sums).astype(BF)
+    for g in range(GROUPS):
+        parts_ref[g, :, HD:] = sums
+
+
+def shares(dq, dkv, normed, w_qkv):
+    return vmem_call(
+        share_body,
+        (
+            jax.ShapeDtypeStruct((GROUPS, ROWS, LANES), BF),
+            jax.ShapeDtypeStruct((ROWS, 3 * HD), BF),
+        ),
+        inputs=4,
+        flops=2 * ROWS * GROUPS * HD * 3 * HD,
+    )(dq, dkv, normed, w_qkv)
+
+
+def slabs_body(normed_ref, grad_ref, out_ref):
+    slab = HD // 4
+    grad = grad_ref[...]
+    for g in range(GROUPS):
+        wide = lax.dot_general(
+            normed_ref[g], grad, (((0,), (0,)), ((), ())), preferred_element_type=F32
+        )
+        for x in range(4):
+            at, row = g // 8 * 4 + x, g % 8 * SLAB
+            out_ref[at, row : row + slab] = wide[x * slab : (x + 1) * slab].astype(BF)
+            out_ref[at, row + slab : row + SLAB] = jnp.zeros((SLAB - slab, 3 * HD), BF)
+
+
+def slabs(normed, grad):
+    return vmem_call(
+        slabs_body,
+        jax.ShapeDtypeStruct((8, 8 * SLAB, 3 * HD), BF),
+        inputs=2,
+        flops=2 * ROWS * GROUPS * HD * 3 * HD,
+    )(normed, grad)
+
+
 def gelu_parts(inputs):
     normal_cdf = 0.5 * (1.0 + lax.erf(inputs * INV_ROOT_TWO))
     density = jnp.exp(-0.5 * inputs * inputs) * INV_ROOT_TAU
@@ -274,20 +344,23 @@
         return jnp.concatenate([jnp.stack(first).astype(jnp.int32), ends])
 
     frames_g = frames.reshape(ROWS, groups, HD).transpose(1, 0, 2)
-    taps = exchange_x(everyone(exchange_z(everyone(conv_weight[0])), 4))
+    pair = paired(with_halo(frames_g))
+    taps = exchange_z(everyone(conv_weight[0]))
+    taps = exchange_x(everyone(after(taps, pair), 4))
     where = scalars(y, index)
-    conv = convolved(True, where, frames_g, taps)
+    conv = convolved(True, where, pair, taps)
     upstream = doubled(grad_out)
     activated, slope = gelu_parts(conv)
     hidden = frames_g.astype(F32) + activated
 
-    hidden_all = lax.all_gather(hidden.astype(BF), "head", axis=0, tiled=True).astype(F32)
+    hidden_all = lax.all_gather(
+        after(hidden.astype(BF), upstream), "head", axis=0, tiled=True
+    ).astype(F32)
     center = jnp.sum(hidden_all, axis=(0, 2)) / width
     square = jnp.sum(hidden_all * hidden_all, axis=(0, 2)) / width
     inv_std = lax.rsqrt(square - center * center + EPS)
     normed = ((hidden_all - center[:, None]) * inv_std[:, None]).astype(BF)
     unit = (hidden - center[:, None]) * inv_std[:, None]
-    weights = w_qkv.reshape(16, HD, 3 * HD)
     normed_rows = normed.transpose(1, 0, 2).reshape(ROWS, width)
     projected = jnp.dot(normed_rows, w_qkv, preferred_element_type=F32).astype(BF)
 
@@ -307,21 +380,12 @@
     stats = attention_stats(order, queries_all, keys_all, upstream)
     stats = exchange_xy(everyone(stats))
     od, dkv = attention_grads(order, queries_all, keys_all, upstream, stats)
-    dkv = jnp.sum(exchange_z(dkv).astype(F32), axis=0).astype(BF)
+    dkv = exchange_z(dkv)
     grad_q = halved(od[1])
     attended = halved(after(od[0], grad_q)).T
-    grad_joined = jnp.concatenate([grad_q.T, dkv[:, :HD], dkv[:, LANES : LANES + HD]], axis=1)
-
-    share = jnp.einsum("tj,gcj->gtc", grad_joined, weights, preferred_element_type=F32)
-    plain = jnp.sum(share, axis=(0, 2))
-    along = jnp.sum(share * normed.astype(F32), axis=(0, 2))
-    sums = jnp.stack([plain, along], axis=1)
-    sums_high = sums.astype(BF)
-    sums_low = (sums - sums_high.astype(F32)).astype(BF)
-    sums = jnp.concatenate([sums_high, sums_low, jnp.zeros((ROWS, 4), BF)], axis=1)
-    parts = jnp.concatenate(
-        [share.astype(BF), jnp.broadcast_to(sums[None], (16, ROWS, 8))], axis=2
-    ).reshape(8, groups, ROWS, LANES)
+
+    parts, grad_joined = shares(grad_q, dkv, normed, w_qkv)
+    parts = parts.reshape(8, groups, ROWS, LANES)
     parts = lax.all_to_all(parts, "head", 0, 0)
     parts = jnp.sum(parts.astype(F32), axis=0)
     feature = parts[:, :, :HD]
@@ -331,18 +395,14 @@
         feature - plain[:, None] / width - unit * (along[:, None] / width)
     )
 
-    error = (slope * hidden_grad).astype(BF)
-    frame_grad = hidden_grad + convolved(False, where, error, taps)
+    error = after((slope * hidden_grad).astype(BF), attended)
+    padded = with_halo(error)
+    wide = exchange_xy(after(slabs(normed, grad_joined), padded))
+    wide = jnp.sum(wide.astype(F32), axis=0).astype(BF).reshape(8, SLAB, 3 * HD)
+    pair = after(paired(padded), wide)
+    frame_grad = hidden_grad + convolved(False, where, pair, taps)
     frame_grad = frame_grad.astype(BF).transpose(1, 0, 2).reshape(ROWS, groups * HD)
-
-    wide = lax.dot_general(
-        normed_rows, grad_joined, (((0,), (0,)), ((), ())), preferred_element_type=F32
-    ).astype(BF)
-    slab = width // 64
-    wide = wide.reshape(2, 8, 4, slab, 3 * HD).transpose(0, 2, 1, 3, 4)
-    wide = exchange_xy(wide.reshape(8, 8, slab, 3 * HD))
-    wide = jnp.sum(wide.astype(F32), axis=0).astype(BF)
-    weight_grad = jnp.sum(exchange_z(wide).astype(F32), axis=0)
+    weight_grad = jnp.sum(exchange_z(wide)[:, : HD // 4].astype(F32), axis=0)
     return attended, frame_grad, weight_grad
 
 

time: 257 us -> 277 us (1.078)
  the two profiles are of different devices: /device:TPU:16 before, /device:TPU:2 now
where the time goes in v4:
time: 277 us; the launch traced here: 275 us
  starting transfers between devices  114 us (41%)
  waiting for transfers between devices  71.9 us (26%)
  local copies, waits for them, and re-layouts  28.1 us (10%)
  blocking collectives  26.7 us (10%)
  Pallas kernels  14.6 us (5%)
  other arithmetic  11.7 us (4%)
  between operations  5.42 us (2%)
    ppermute x16, waiting for transfers between devices, swap(): return lax.ppermute(array, 'tm', [(i, i ^ bit) for i in range(64)])  50.6 us
    ppermute x16, starting transfers between devices, swap(): return lax.ppermute(array, 'tm', [(i, i ^ bit) for i in range(64)])  49.6 us
    all_to_all x4, starting transfers between devices, exchange_z(): return lax.all_to_all(parts, 'tm', 0, 0, axis_index_groups=Z_GROUPS)  32.4 us
    all_gather x1, blocking collectives, on_device(): lax.all_gather(after(hidden.astype(BF), upstream), 'head', axis=0, tiled=...  18 us
    all_to_all x1, waiting for transfers between devices, exchange_xy(): return lax.all_to_all(parts, 'tm', 0, 0, axis_index_groups=XY_GROUPS)  12.7 us
    all_to_all x1, starting transfers between devices, exchange_x(): return lax.all_to_all(parts, 'tm', 0, 0, axis_index_groups=X_GROUPS)  8.76 us
    all_to_all x1, blocking collectives, exchange_xy(): return lax.all_to_all(parts, 'tm', 0, 0, axis_index_groups=XY_GROUPS)  8.67 us
    unnamed x60, local copies, waits for them, and re-layouts  7.41 us
  transfers between devices with their start and end apart: 27, of which 17 were waited for; matrix products, arithmetic and copies ran while one was open for 7% of the time, Pallas kernels for 2%

profile of v4, /device:TPU:2, one launch (start us, length us, event | category | flops | bytes accessed | tf_op | source)
XLA Modules:
  0.0 274.7 jit_solution(1096648155968499609)
XLA Ops:
  0.6 1.7 broadcast_in_dim.25
  2.3 10.3 %all-to-all-start = ((bf16[8,2,120,120]{3,2,1,0:T(8,128)(2,1)}), bf16[8,2,120,120]{3,2,1,0:T(8,128)(2,1)S(1)}, u32[]{:S(2)}, u32[]{:S(2)}) async-start(bf16[8,2,120,120]{3,2,1,0:T(8,128)(2,1)} %broadcast_in_dim.25), calls=%async_computation | async-start | bytes 983040 | tf_op jit(solution)/shard_map/all_to_all | solution.py:44
  12.8 3.4 %collective-permute-start = (bf16[2,32,120]{2,1,0:T(8,128)(2,1)S(1)}, bf16[2,32,120]{2,1,0:T(8,128)(2,1)S(1)}, u32[]{:S(2)}, u32[]{:S(2)}) collective-permute-start(bf16[2,32,120]{2,1,0:T(8,128)(2,1)S(1)} %get-tuple-element.34), channel_id=1, source_target_pairs={{0,8},{8,16},{16,24},{24,32},{32,40},{40,48},{48,56},{56,64},{64,7... | collective-permute-start | bytes 46088 | tf_op jit(solution)/shard_map/ppermute | solution.py:159
  16.2 2.4 collective-permute-start.1
  18.7 3.2 %collective-permute-done.1 = bf16[2,32,120]{2,1,0:T(8,128)(2,1)S(1)} collective-permute-done((bf16[2,32,120]{2,1,0:T(8,128)(2,1)S(1)}, bf16[2,32,120]{2,1,0:T(8,128)(2,1)S(1)}, u32[]{:S(2)}, u32[]{:S(2)}) %collective-permute-start.1) | collective-permute-done | bytes 15392 | tf_op jit(solution)/shard_map/ppermute | solution.py:160
  21.9 3.5 %collective-permute-start.2 = (bf16[2,192,120]{2,1,0:T(8,128)(2,1)S(1)}, bf16[2,192,120]{2,1,0:T(8,128)(2,1)S(1)}, u32[]{:S(2)}, u32[]{:S(2)}) collective-permute-start(bf16[2,192,120]{2,1,0:T(8,128)(2,1)S(1)} %get-tuple-element.29), channel_id=1, source_target_pairs={{0,256},{8,264},{16,272},{24,280},{32,288},{40,296},{48,304},{56,3... | collective-permute-start | bytes 276488 | tf_op jit(solution)/shard_map/ppermute | solution.py:40
  25.4 3.0 %collective-permute-done.2 = bf16[2,192,120]{2,1,0:T(8,128)(2,1)S(1)} collective-permute-done((bf16[2,192,120]{2,1,0:T(8,128)(2,1)S(1)}, bf16[2,192,120]{2,1,0:T(8,128)(2,1)S(1)}, u32[]{:S(2)}, u32[]{:S(2)}) %collective-permute-start.2) | collective-permute-done | bytes 92192 | tf_op jit(solution)/shard_map/ppermute | solution.py:40
  30.1 1.6 broadcast_in_dim.26
  31.7 8.8 %all-to-all-start.1 = ((bf16[4,8,2,120,120]{4,3,2,1,0:T(8,128)(2,1)}), bf16[4,8,2,120,120]{4,3,2,1,0:T(8,128)(2,1)S(1)}, u32[]{:S(2)}, u32[]{:S(2)}) async-start(bf16[4,8,2,120,120]{4,3,2,1,0:T(8,128)(2,1)} %broadcast_in_dim.26), calls=%async_computation.1 | async-start | bytes 3932160 | tf_op jit(solution)/shard_map/all_to_all | solution.py:36
  40.6 3.4 %collective-permute-start.4 = (bf16[1,128,120]{2,1,0:T(8,128)(2,1)S(1)}, bf16[1,128,120]{2,1,0:T(8,128)(2,1)S(1)}, u32[]{:S(2)}, u32[]{:S(2)}) collective-permute-start(bf16[1,128,120]{2,1,0:T(8,128)(2,1)S(1)} %bitcast.66), channel_id=1, source_target_pairs={{0,256},{8,264},{16,272},{24,280},{32,288},{40,296},{48,304},{56,3... | collective-permute-start | bytes 92168 | tf_op jit(solution)/shard_map/ppermute | solution.py:40
  44.3 2.1 collective-permute-done.4
  46.4 4.0 %collective-permute-start.5 = (bf16[2,128,120]{2,1,0:T(8,128)(2,1)S(1)}, bf16[2,128,120]{2,1,0:T(8,128)(2,1)S(1)}, u32[]{:S(2)}, u32[]{:S(2)}) collective-permute-start(bf16[2,128,120]{2,1,0:T(8,128)(2,1)S(1)} %pad_maximum_fusion.7), channel_id=1, source_target_pairs={{0,16},{8,24},{16,0},{24,8},{32,48},{40,56},{48,32},{56,40},{64,80... | collective-permute-start | bytes 184328 | tf_op jit(solution)/shard_map/ppermute | solution.py:40
  50.6 12.1 %collective-permute-done.5 = bf16[2,128,120]{2,1,0:T(8,128)(2,1)S(1)} collective-permute-done((bf16[2,128,120]{2,1,0:T(8,128)(2,1)S(1)}, bf16[2,128,120]{2,1,0:T(8,128)(2,1)S(1)}, u32[]{:S(2)}, u32[]{:S(2)}) %collective-permute-start.5) | collective-permute-done | bytes 61472 | tf_op jit(solution)/shard_map/ppermute | solution.py:40
  62.7 3.4 %collective-permute-start.6 = (bf16[4,128,120]{2,1,0:T(8,128)(2,1)S(1)}, bf16[4,128,120]{2,1,0:T(8,128)(2,1)S(1)}, u32[]{:S(2)}, u32[]{:S(2)}) collective-permute-start(bf16[4,128,120]{2,1,0:T(8,128)(2,1)S(1)} %pad_maximum_fusion.3), channel_id=1, source_target_pairs={{0,8},{8,0},{16,24},{24,16},{32,40},{40,32},{48,56},{56,48},{64,72... | collective-permute-start | bytes 368648 | tf_op jit(solution)/shard_map/ppermute | solution.py:40
  66.2 2.2 shard_map.76
  68.4 3.5 %collective-permute-start.3 = (bf16[2,128,120]{2,1,0:T(8,128)(2,1)S(1)}, bf16[2,128,120]{2,1,0:T(8,128)(2,1)S(1)}, u32[]{:S(2)}, u32[]{:S(2)}) collective-permute-start(bf16[2,128,120]{2,1,0:T(8,128)(2,1)S(1)} %get-tuple-element.12), channel_id=1, source_target_pairs={{0,256},{8,264},{16,272},{24,280},{32,288},{40,296},{48,304},{56,3... | collective-permute-start | bytes 184328 | tf_op jit(solution)/shard_map/ppermute | solution.py:40
  75.2 18.0 %all_gather.3 = bf16[16,128,120]{1,2,0:T(8,128)(2,1)S(1)} all-gather(bf16[2,128,120]{1,2,0:T(8,128)(2,1)S(1)} %copy.65), channel_id=1, replica_groups=mesh['tm'=64,'head'=8] {'head'}, dimensions={0}, use_global_device_ids=true | all-gather | bytes 552960 | tf_op jit(solution)/shard_map/all_gather | solution.py:356
  94.2 1.0 copy.67
  95.2 2.1 convolution_convert_fusion
  98.4 9.8 %all-to-all-start.2 = ((bf16[8,128,256]{2,1,0:T(8,128)(2,1)}), bf16[8,128,256]{2,1,0:T(8,128)(2,1)S(1)}, u32[]{:S(2)}, u32[]{:S(2)}) async-start(bf16[8,128,256]{2,1,0:T(8,128)(2,1)} %broadcast_in_dim.58), calls=%async_computation.2 | async-start | bytes 1048576 | tf_op jit(solution)/shard_map/all_to_all | solution.py:44
  108.3 2.3 collective-permute-start.7
  110.6 3.5 %collective-permute-done.7 = bf16[1,128,128]{2,1,0:T(8,128)(2,1)S(1)} collective-permute-done((bf16[1,128,128]{2,1,0:T(8,128)(2,1)S(1)}, bf16[1,128,128]{2,1,0:T(8,128)(2,1)S(1)}, u32[]{:S(2)}, u32[]{:S(2)}) %collective-permute-start.7) | collective-permute-done | bytes 32800 | tf_op jit(solution)/shard_map/ppermute | solution.py:40
  114.1 1.9 collective-permute-start.8
  116.1 5.7 %collective-permute-done.8 = bf16[2,128,128]{2,1,0:T(8,128)(2,1)S(1)} collective-permute-done((bf16[2,128,128]{2,1,0:T(8,128)(2,1)S(1)}, bf16[2,128,128]{2,1,0:T(8,128)(2,1)S(1)}, u32[]{:S(2)}, u32[]{:S(2)}) %collective-permute-start.8) | collective-permute-done | bytes 65568 | tf_op jit(solution)/shard_map/ppermute | solution.py:40
  121.8 2.5 collective-permute-start.9
  124.4 4.3 %collective-permute-done.9 = bf16[4,128,128]{2,1,0:T(8,128)(2,1)S(1)} collective-permute-done((bf16[4,128,128]{2,1,0:T(8,128)(2,1)S(1)}, bf16[4,128,128]{2,1,0:T(8,128)(2,1)S(1)}, u32[]{:S(2)}, u32[]{:S(2)}) %collective-permute-start.9) | collective-permute-done | bytes 131104 | tf_op jit(solution)/shard_map/ppermute | solution.py:40
  128.7 2.5 shard_map.77
  131.2 8.7 %all_to_all.40.stats_ref = f32[8,3,8,128]{3,2,1,0:T(8,128)S(1)} all-to-all(f32[8,3,8,128]{3,2,1,0:T(8,128)S(1)} %broadcast_in_dim.59), channel_id=1, replica_groups={{0,8,16,24,256,264,272,280},{32,40,48,56,288,296,304,312},{64,72,80,88,..., dimensions={0} | all-to-all | bytes 196608 | tf_op jit(solution)/shard_map/all_to_all | solution.py:32
  139.9 3.6 %shard_map.78 = (bf16[2,8,120,128]{3,2,1,0:T(8,128)(2,1)S(1)}, bf16[8,128,256]{2,1,0:T(8,128)(2,1)S(1)}) custom-call(s32[5]{0:T(128)S(1)} %pad_add_fusion.sc_ref, bf16[8,128,128]{2,1,0:T(8,128)(2,1)S(1)} %pad_maximum_fusion.1.q_ref, bf16[8,128,256]{2,1,0:T(8,128)(2,1)S(1)} %all-to-all-done.2.kv_ref, bf16[8,128,120]{2,1,0:T(8,128)(2,1)S(1)} %pad_maximum_fusion.d_ref, ...), custom_call_target="tpu_custom_call" | custom-call | flops 1610612736 | bytes 1048576 | tf_op jit(solution)/shard_map/pallas_call | solution.py:246
  143.5 3.4 %collective-permute-start.10 = (bf16[4,120,128]{2,1,0:T(8,128)(2,1)S(1)}, bf16[4,120,128]{2,1,0:T(8,128)(2,1)S(1)}, u32[]{:S(2)}, u32[]{:S(2)}) collective-permute-start(bf16[4,120,128]{2,1,0:T(8,128)(2,1)S(1)} %slice_bitcast_fusion.2), channel_id=1, source_target_pairs={{0,8},{8,0},{16,24},{24,16},{32,40},{40,32},{48,56},{56,48},{64,72... | collective-permute-start | bytes 368648 | tf_op jit(solution)/shard_map/ppermute | solution.py:40
  146.9 3.4 %collective-permute-done.10 = bf16[4,120,128]{2,1,0:T(8,128)(2,1)S(1)} collective-permute-done((bf16[4,120,128]{2,1,0:T(8,128)(2,1)S(1)}, bf16[4,120,128]{2,1,0:T(8,128)(2,1)S(1)}, u32[]{:S(2)}, u32[]{:S(2)}) %collective-permute-start.10) | collective-permute-done | bytes 122912 | tf_op jit(solution)/shard_map/ppermute | solution.py:40
  151.0 3.4 %collective-permute-start.11 = (bf16[2,120,128]{2,1,0:T(8,128)(2,1)}, bf16[2,120,128]{2,1,0:T(8,128)(2,1)}, u32[]{:S(2)}, u32[]{:S(2)}) collective-permute-start(bf16[2,120,128]{2,1,0:T(8,128)(2,1)} %slice.160), channel_id=1, source_target_pairs={{0,16},{8,24},{16,0},{24,8},{32,48},{40,56},{48,32},{56,40},{64,80... | collective-permute-start | bytes 184328 | tf_op jit(solution)/shard_map/ppermute | solution.py:40
  154.4 2.4 copy.69.w_ref
  156.7 7.2 %all-to-all-start.4 = ((bf16[8,128,256]{2,1,0:T(8,128)(2,1)}), bf16[8,128,256]{2,1,0:T(8,128)(2,1)}, u32[]{:S(2)}, u32[]{:S(2)}) async-start(bf16[8,128,256]{2,1,0:T(8,128)(2,1)} %copy-done.5), calls=%async_computation.4 | async-start | bytes 1048576 | tf_op jit(solution)/shard_map/all_to_all | solution.py:44
  163.9 0.9 slice_add_fusion.4
  164.9 2.7 collective-permute-start.12
  167.6 2.2 fusion.1.normed_ref
  172.6 4.7 %all-to-all-done.4.dkv_ref = bf16[8,128,256]{2,1,0:T(8,128)(2,1)} async-done(((bf16[8,128,256]{2,1,0:T(8,128)(2,1)}), bf16[8,128,256]{2,1,0:T(8,128)(2,1)}, u32[]{:S(2)}, u32[]{:S(2)}) %all-to-all-start.4) | async-done | bytes 524320 | tf_op jit(solution)/shard_map/all_to_all | solution.py:44
  177.3 1.0 copy-done
  178.4 2.1 shard_map.79
  182.0 5.0 %all-to-all-start.5 = ((bf16[8,2,128,128]{3,2,1,0:T(8,128)(2,1)}), bf16[8,2,128,128]{3,2,1,0:T(8,128)(2,1)S(1)}, u32[]{:S(2)}, u32[]{:S(2)}) async-start(bf16[8,2,128,128]{3,2,1,0:T(8,128)(2,1)} %bitcast.62), calls=%async_computation.5 | async-start | bytes 1048576 | tf_op jit(solution)/shard_map/all_to_all | solution.py:389
  187.9 2.9 %collective-permute-start.13 = (bf16[4,120,128]{2,1,0:T(8,128)(2,1)S(1)}, bf16[4,120,128]{2,1,0:T(8,128)(2,1)S(1)}, u32[]{:S(2)}, u32[]{:S(2)}) collective-permute-start(bf16[4,120,128]{2,1,0:T(8,128)(2,1)S(1)} %slice_bitcast_fusion), channel_id=1, source_target_pairs={{0,8},{8,0},{16,24},{24,16},{32,40},{40,32},{48,56},{56,48},{64,72... | collective-permute-start | bytes 368648 | tf_op jit(solution)/shard_map/ppermute | solution.py:40
  190.8 4.7 %collective-permute-done.13 = bf16[4,120,128]{2,1,0:T(8,128)(2,1)S(1)} collective-permute-done((bf16[4,120,128]{2,1,0:T(8,128)(2,1)S(1)}, bf16[4,120,128]{2,1,0:T(8,128)(2,1)S(1)}, u32[]{:S(2)}, u32[]{:S(2)}) %collective-permute-start.13) | collective-permute-done | bytes 122912 | tf_op jit(solution)/shard_map/ppermute | solution.py:40
  196.4 4.0 %collective-permute-start.14 = (bf16[2,120,128]{2,1,0:T(8,128)(2,1)S(1)}, bf16[2,120,128]{2,1,0:T(8,128)(2,1)S(1)}, u32[]{:S(2)}, u32[]{:S(2)}) collective-permute-start(bf16[2,120,128]{2,1,0:T(8,128)(2,1)S(1)} %slice.167), channel_id=1, source_target_pairs={{0,16},{8,24},{16,0},{24,8},{32,48},{40,56},{48,32},{56,40},{64,80... | collective-permute-start | bytes 184328 | tf_op jit(solution)/shard_map/ppermute | solution.py:40
  200.4 3.6 %collective-permute-done.14 = bf16[2,120,128]{2,1,0:T(8,128)(2,1)S(1)} collective-permute-done((bf16[2,120,128]{2,1,0:T(8,128)(2,1)S(1)}, bf16[2,120,128]{2,1,0:T(8,128)(2,1)S(1)}, u32[]{:S(2)}, u32[]{:S(2)}) %collective-permute-start.14) | collective-permute-done | bytes 61472 | tf_op jit(solution)/shard_map/ppermute | solution.py:40
  204.1 2.7 collective-permute-start.15
  206.8 3.0 %collective-permute-done.15 = bf16[1,120,128]{2,1,0:T(8,128)(2,1)S(1)} collective-permute-done((bf16[1,120,128]{2,1,0:T(8,128)(2,1)S(1)}, bf16[1,120,128]{2,1,0:T(8,128)(2,1)S(1)}, u32[]{:S(2)}, u32[]{:S(2)}) %collective-permute-start.15) | collective-permute-done | bytes 30752 | tf_op jit(solution)/shard_map/ppermute | solution.py:40
  211.8 3.6 %collective-permute-start.16 = (bf16[2,32,120]{2,1,0:T(8,128)(2,1)S(1)}, bf16[2,32,120]{2,1,0:T(8,128)(2,1)S(1)}, u32[]{:S(2)}, u32[]{:S(2)}) collective-permute-start(bf16[2,32,120]{2,1,0:T(8,128)(2,1)S(1)} %get-tuple-element.32), channel_id=1, source_target_pairs={{0,8},{8,16},{16,24},{24,32},{32,40},{40,48},{48,56},{56,64},{64,7... | collective-permute-start | bytes 46088 | tf_op jit(solution)/shard_map/ppermute | solution.py:159
  215.5 2.2 collective-permute-start.17
  217.7 1.0 copy-done.1
  221.8 1.8 reshape.94
  223.6 1.2 slice.178
  225.4 1.3 broadcast_add_fusion
  226.7 2.6 copy.72
  229.3 6.7 %all-to-all-start.6 = ((bf16[8,256,360]{1,2,0:T(8,128)(2,1)}), bf16[8,256,360]{1,2,0:T(8,128)(2,1)S(1)}, u32[]{:S(2)}, u32[]{:S(2)}) async-start(bf16[8,256,360]{1,2,0:T(8,128)(2,1)} %copy.72), calls=%async_computation.6 | async-start | bytes 2949120 | tf_op jit(solution)/shard_map/all_to_all | solution.py:32
  236.0 3.4 %collective-permute-start.18 = (bf16[2,192,120]{2,1,0:T(8,128)(2,1)S(1)}, bf16[2,192,120]{2,1,0:T(8,128)(2,1)}, u32[]{:S(2)}, u32[]{:S(2)}) collective-permute-start(bf16[2,192,120]{2,1,0:T(8,128)(2,1)S(1)} %copy-done.20), channel_id=1, source_target_pairs={{0,256},{8,264},{16,272},{24,280},{32,288},{40,296},{48,304},{56,3... | collective-permute-start | bytes 276488 | tf_op jit(solution)/shard_map/ppermute | solution.py:40
  239.4 12.7 %all-to-all-done.6 = bf16[8,256,360]{1,2,0:T(8,128)(2,1)S(1)} async-done(((bf16[8,256,360]{1,2,0:T(8,128)(2,1)}), bf16[8,256,360]{1,2,0:T(8,128)(2,1)S(1)}, u32[]{:S(2)}, u32[]{:S(2)}) %all-to-all-start.6) | async-done | bytes 1474592 | tf_op jit(solution)/shard_map/all_to_all | solution.py:32
  252.9 1.7 copy.73
  254.7 1.4 reshape_reshape.3
  256.1 5.1 %all-to-all-start.7 = ((bf16[8,32,360]{2,1,0:T(8,128)(2,1)}), bf16[8,32,360]{2,1,0:T(8,128)(2,1)S(1)}, u32[]{:S(2)}, u32[]{:S(2)}) async-start(bf16[8,32,360]{2,1,0:T(8,128)(2,1)} %bitcast.35), calls=%async_computation.7 | async-start | bytes 393216 | tf_op jit(solution)/shard_map/all_to_all | solution.py:44
  262.3 1.0 maximum_add_fusion.x_ref
  263.3 3.6 %shard_map.81 = (f32[2,128,120]{2,1,0:T(8,128)S(1)}, bf16[2,128,120]{2,1,0:T(8,128)(2,1)S(1)}) custom-call(s32[6]{0:T(128)S(1)} %pad_add_fusion.1.sc_ref, bf16[2,2,192,120]{3,2,1,0:T(8,128)(2,1)S(1)} %maximum_add_fusion.x_ref, bf16[4,8,2,120,120]{4,3,2,1,0:T(8,128)(2,1)S(1)} %all-to-all-done.1.w_ref), custom_call_target="tpu_custom_call" | custom-call | flops 471859200 | bytes 1048576 | tf_op jit(solution)/shard_map/pallas_call | solution.py:142
  267.0 2.8 %collective-permute-start.19 = (bf16[2,128,120]{2,1,0:T(8,128)(2,1)S(1)}, bf16[2,128,120]{2,1,0:T(8,128)(2,1)S(1)}, u32[]{:S(2)}, u32[]{:S(2)}) collective-permute-start(bf16[2,128,120]{2,1,0:T(8,128)(2,1)S(1)} %get-tuple-element.18), channel_id=1, source_target_pairs={{0,256},{8,264},{16,272},{24,280},{32,288},{40,296},{48,304},{56,3... | collective-permute-start | bytes 184328 | tf_op jit(solution)/shard_map/ppermute | solution.py:40
  269.8 3.4 %collective-permute-done.19 = bf16[2,128,120]{2,1,0:T(8,128)(2,1)S(1)} collective-permute-done((bf16[2,128,120]{2,1,0:T(8,128)(2,1)S(1)}, bf16[2,128,120]{2,1,0:T(8,128)(2,1)S(1)}, u32[]{:S(2)}, u32[]{:S(2)}) %collective-permute-start.19) | collective-permute-done | bytes 61472 | tf_op jit(solution)/shard_map/ppermute | solution.py:40
  (133 shorter events, 20.1 us)
Async XLA Ops:
  0.6 12.0 %copy-start.22 = (bf16[128,240]{0,1:T(8,128)(2,1)S(1)}, bf16[128,240]{0,1:T(8,128)(2,1)}, u32[]{:S(2)}) copy-start(bf16[128,240]{0,1:T(8,128)(2,1)} %param.5) | copy-start | bytes 184324
  2.3 27.8 %all-to-all-start = ((bf16[8,2,120,120]{3,2,1,0:T(8,128)(2,1)}), bf16[8,2,120,120]{3,2,1,0:T(8,128)(2,1)S(1)}, u32[]{:S(2)}, u32[]{:S(2)}) async-start(bf16[8,2,120,120]{3,2,1,0:T(8,128)(2,1)} %broadcast_in_dim.25), calls=%async_computation | async-start | bytes 983040 | tf_op jit(solution)/shard_map/all_to_all | solution.py:44
  12.8 198.9 %copy-start.14 = (bf16[128,2,120]{2,0,1:T(8,128)(2,1)}, bf16[128,2,120]{2,0,1:T(8,128)(2,1)S(1)}, u32[]{:S(2)}) copy-start(bf16[128,2,120]{2,0,1:T(8,128)(2,1)S(1)} %copy.63) | copy-start | bytes 184324
  12.8 5.9 %collective-permute-start = (bf16[2,32,120]{2,1,0:T(8,128)(2,1)S(1)}, bf16[2,32,120]{2,1,0:T(8,128)(2,1)S(1)}, u32[]{:S(2)}, u32[]{:S(2)}) collective-permute-start(bf16[2,32,120]{2,1,0:T(8,128)(2,1)S(1)} %get-tuple-element.34), channel_id=1, source_target_pairs={{0,8},{8,16},{16,24},{24,32},{32,40},{40,48},{48,56},{56,64},{64,7... | collective-permute-start | bytes 46088 | tf_op jit(solution)/shard_map/ppermute | solution.py:159
  16.2 5.6 %collective-permute-start.1 = (bf16[2,32,120]{2,1,0:T(8,128)(2,1)S(1)}, bf16[2,32,120]{2,1,0:T(8,128)(2,1)S(1)}, u32[]{:S(2)}, u32[]{:S(2)}) collective-permute-start(bf16[2,32,120]{2,1,0:T(8,128)(2,1)S(1)} %get-tuple-element.35), channel_id=1, source_target_pairs={{8,0},{16,8},{24,16},{32,24},{40,32},{48,40},{56,48},{64,56},{72,6... | collective-permute-start | bytes 46088 | tf_op jit(solution)/shard_map/ppermute | solution.py:160
  21.9 6.5 %collective-permute-start.2 = (bf16[2,192,120]{2,1,0:T(8,128)(2,1)S(1)}, bf16[2,192,120]{2,1,0:T(8,128)(2,1)S(1)}, u32[]{:S(2)}, u32[]{:S(2)}) collective-permute-start(bf16[2,192,120]{2,1,0:T(8,128)(2,1)S(1)} %get-tuple-element.29), channel_id=1, source_target_pairs={{0,256},{8,264},{16,272},{24,280},{32,288},{40,296},{48,304},{56,3... | collective-permute-start | bytes 276488 | tf_op jit(solution)/shard_map/ppermute | solution.py:40
  31.7 8.8 %copy-start.23 = (bf16[128,120]{0,1:T(8,128)(2,1)S(1)}, bf16[128,120]{0,1:T(8,128)(2,1)}, u32[]{:S(2)}) copy-start(bf16[128,120]{0,1:T(8,128)(2,1)} %param.9) | copy-start | bytes 92164
  31.7 12.3 %copy-start.28 = (s32[4]{0:T(128)S(1)}, s32[4]{0:T(128)}, u32[]{:S(2)}) copy-start(s32[4]{0:T(128)} %param.8) | copy-start | bytes 52
  31.7 34.5 %all-to-all-start.1 = ((bf16[4,8,2,120,120]{4,3,2,1,0:T(8,128)(2,1)}), bf16[4,8,2,120,120]{4,3,2,1,0:T(8,128)(2,1)S(1)}, u32[]{:S(2)}, u32[]{:S(2)}) async-start(bf16[4,8,2,120,120]{4,3,2,1,0:T(8,128)(2,1)} %broadcast_in_dim.26), calls=%async_computation.1 | async-start | bytes 3932160 | tf_op jit(solution)/shard_map/all_to_all | solution.py:36
  40.6 5.8 %collective-permute-start.4 = (bf16[1,128,120]{2,1,0:T(8,128)(2,1)S(1)}, bf16[1,128,120]{2,1,0:T(8,128)(2,1)S(1)}, u32[]{:S(2)}, u32[]{:S(2)}) collective-permute-start(bf16[1,128,120]{2,1,0:T(8,128)(2,1)S(1)} %bitcast.66), channel_id=1, source_target_pairs={{0,256},{8,264},{16,272},{24,280},{32,288},{40,296},{48,304},{56,3... | collective-permute-start | bytes 92168 | tf_op jit(solution)/shard_map/ppermute | solution.py:40
  44.2 27.8 %copy-start.26 = (s32[4,1]{0,1:T(1,128)}, s32[4,1]{0,1:T(1,128)S(1)}, u32[]{:S(2)}) copy-start(s32[4,1]{0,1:T(1,128)S(1)} %reduce-window.4) | copy-start | bytes 52
  46.4 16.3 %collective-permute-start.5 = (bf16[2,128,120]{2,1,0:T(8,128)(2,1)S(1)}, bf16[2,128,120]{2,1,0:T(8,128)(2,1)S(1)}, u32[]{:S(2)}, u32[]{:S(2)}) collective-permute-start(bf16[2,128,120]{2,1,0:T(8,128)(2,1)S(1)} %pad_maximum_fusion.7), channel_id=1, source_target_pairs={{0,16},{8,24},{16,0},{24,8},{32,48},{40,56},{48,32},{56,40},{64,80... | collective-permute-start | bytes 184328 | tf_op jit(solution)/shard_map/ppermute | solution.py:40
  62.7 9.2 %collective-permute-start.6 = (bf16[4,128,120]{2,1,0:T(8,128)(2,1)S(1)}, bf16[4,128,120]{2,1,0:T(8,128)(2,1)S(1)}, u32[]{:S(2)}, u32[]{:S(2)}) collective-permute-start(bf16[4,128,120]{2,1,0:T(8,128)(2,1)S(1)} %pad_maximum_fusion.3), channel_id=1, source_target_pairs={{0,8},{8,0},{16,24},{24,16},{32,40},{40,32},{48,56},{56,48},{64,72... | collective-permute-start | bytes 368648 | tf_op jit(solution)/shard_map/ppermute | solution.py:40
  68.4 25.4 %copy-start.2 = (f32[2,128,120]{2,1,0:T(8,128)}, f32[2,128,120]{2,1,0:T(8,128)S(1)}, u32[]{:S(2)}) copy-start(f32[2,128,120]{2,1,0:T(8,128)S(1)} %get-tuple-element.11) | copy-start | bytes 368644
  68.4 6.2 %collective-permute-start.3 = (bf16[2,128,120]{2,1,0:T(8,128)(2,1)S(1)}, bf16[2,128,120]{2,1,0:T(8,128)(2,1)S(1)}, u32[]{:S(2)}, u32[]{:S(2)}) collective-permute-start(bf16[2,128,120]{2,1,0:T(8,128)(2,1)S(1)} %get-tuple-element.12), channel_id=1, source_target_pairs={{0,256},{8,264},{16,272},{24,280},{32,288},{40,296},{48,304},{56,3... | collective-permute-start | bytes 184328 | tf_op jit(solution)/shard_map/ppermute | solution.py:40
  74.6 0.6 copy-start.16
  93.5 3.8 %copy-start.11 = (bf16[16,128,120]{2,1,0:T(8,128)(2,1)}, bf16[16,128,120]{2,1,0:T(8,128)(2,1)S(1)}, u32[]{:S(2)}) copy-start(bf16[16,128,120]{2,1,0:T(8,128)(2,1)S(1)} %copy.66) | copy-start | bytes 1474564
  97.3 27.0 %copy-start.27 = (s32[4,1]{0,1:T(1,128)S(1)}, s32[4,1]{0,1:T(1,128)}, u32[]{:S(2)}) copy-start(s32[4,1]{0,1:T(1,128)} %copy-done.26) | copy-start | bytes 52
  98.4 30.4 %all-to-all-start.2 = ((bf16[8,128,256]{2,1,0:T(8,128)(2,1)}), bf16[8,128,256]{2,1,0:T(8,128)(2,1)S(1)}, u32[]{:S(2)}, u32[]{:S(2)}) async-start(bf16[8,128,256]{2,1,0:T(8,128)(2,1)} %broadcast_in_dim.58), calls=%async_computation.2 | async-start | bytes 1048576 | tf_op jit(solution)/shard_map/all_to_all | solution.py:44
  108.3 5.8 %collective-permute-start.7 = (bf16[1,128,128]{2,1,0:T(8,128)(2,1)S(1)}, bf16[1,128,128]{2,1,0:T(8,128)(2,1)S(1)}, u32[]{:S(2)}, u32[]{:S(2)}) collective-permute-start(bf16[1,128,128]{2,1,0:T(8,128)(2,1)S(1)} %maximum_bitcast_fusion), channel_id=1, source_target_pairs={{0,256},{8,264},{16,272},{24,280},{32,288},{40,296},{48,304},{56,3... | collective-permute-start | bytes 98312 | tf_op jit(solution)/shard_map/ppermute | solution.py:40
  114.1 7.7 %collective-permute-start.8 = (bf16[2,128,128]{2,1,0:T(8,128)(2,1)S(1)}, bf16[2,128,128]{2,1,0:T(8,128)(2,1)S(1)}, u32[]{:S(2)}, u32[]{:S(2)}) collective-permute-start(bf16[2,128,128]{2,1,0:T(8,128)(2,1)S(1)} %pad_maximum_fusion.8), channel_id=1, source_target_pairs={{0,16},{8,24},{16,0},{24,8},{32,48},{40,56},{48,32},{56,40},{64,80... | collective-permute-start | bytes 196616 | tf_op jit(solution)/shard_map/ppermute | solution.py:40
  121.8 6.9 %collective-permute-start.9 = (bf16[4,128,128]{2,1,0:T(8,128)(2,1)S(1)}, bf16[4,128,128]{2,1,0:T(8,128)(2,1)S(1)}, u32[]{:S(2)}, u32[]{:S(2)}) collective-permute-start(bf16[4,128,128]{2,1,0:T(8,128)(2,1)S(1)} %pad_maximum_fusion.4), channel_id=1, source_target_pairs={{0,8},{8,0},{16,24},{24,16},{32,40},{40,32},{48,56},{56,48},{64,72... | collective-permute-start | bytes 393224 | tf_op jit(solution)/shard_map/ppermute | solution.py:40
  143.5 7.5 %copy-start.5 = (bf16[8,128,256]{2,1,0:T(8,128)(2,1)}, bf16[8,128,256]{2,1,0:T(8,128)(2,1)S(1)}, u32[]{:S(2)}) copy-start(bf16[8,128,256]{2,1,0:T(8,128)(2,1)S(1)} %get-tuple-element.14) | copy-start | bytes 1572868
  143.5 7.5 %copy-start.7 = (bf16[2,8,120,128]{3,2,1,0:T(8,128)(2,1)}, bf16[2,8,120,128]{3,2,1,0:T(8,128)(2,1)S(1)}, u32[]{:S(2)}) copy-start(bf16[2,8,120,128]{3,2,1,0:T(8,128)(2,1)S(1)} %get-tuple-element.13) | copy-start | bytes 1474564
  143.5 6.8 %collective-permute-start.10 = (bf16[4,120,128]{2,1,0:T(8,128)(2,1)S(1)}, bf16[4,120,128]{2,1,0:T(8,128)(2,1)S(1)}, u32[]{:S(2)}, u32[]{:S(2)}) collective-permute-start(bf16[4,120,128]{2,1,0:T(8,128)(2,1)S(1)} %slice_bitcast_fusion.2), channel_id=1, source_target_pairs={{0,8},{8,0},{16,24},{24,16},{32,40},{40,32},{48,56},{56,48},{64,72... | collective-permute-start | bytes 368648 | tf_op jit(solution)/shard_map/ppermute | solution.py:40
  150.3 0.7 copy-start.19
  151.0 13.0 %collective-permute-start.11 = (bf16[2,120,128]{2,1,0:T(8,128)(2,1)}, bf16[2,120,128]{2,1,0:T(8,128)(2,1)}, u32[]{:S(2)}, u32[]{:S(2)}) collective-permute-start(bf16[2,120,128]{2,1,0:T(8,128)(2,1)} %slice.160), channel_id=1, source_target_pairs={{0,16},{8,24},{16,0},{24,8},{32,48},{40,56},{48,32},{56,40},{64,80... | collective-permute-start | bytes 184328 | tf_op jit(solution)/shard_map/ppermute | solution.py:40
  156.7 20.6 %all-to-all-start.4 = ((bf16[8,128,256]{2,1,0:T(8,128)(2,1)}), bf16[8,128,256]{2,1,0:T(8,128)(2,1)}, u32[]{:S(2)}, u32[]{:S(2)}) async-start(bf16[8,128,256]{2,1,0:T(8,128)(2,1)} %copy-done.5), calls=%async_computation.4 | async-start | bytes 1048576 | tf_op jit(solution)/shard_map/all_to_all | solution.py:44
  163.9 7.9 %copy-start.8 = (bf16[2,8,120,128]{3,2,1,0:T(8,128)(2,1)S(1)}, bf16[2,8,120,128]{3,2,1,0:T(8,128)(2,1)}, u32[]{:S(2)}) copy-start(bf16[2,8,120,128]{3,2,1,0:T(8,128)(2,1)} %copy-done.7) | copy-start | bytes 1474564
  164.9 5.8 %collective-permute-start.12 = (bf16[1,120,128]{2,1,0:T(8,128)(2,1)S(1)}, bf16[1,120,128]{2,1,0:T(8,128)(2,1)S(1)}, u32[]{:S(2)}, u32[]{:S(2)}) collective-permute-start(bf16[1,120,128]{2,1,0:T(8,128)(2,1)S(1)} %slice.162), channel_id=1, source_target_pairs={{0,256},{8,264},{16,272},{24,280},{32,288},{40,296},{48,304},{56,3... | collective-permute-start | bytes 92168 | tf_op jit(solution)/shard_map/ppermute | solution.py:40
  177.3 1.0 copy-start
  180.5 0.8 copy-start.6
  181.3 0.6 copy-start.9
  182.0 29.7 %copy-start.3 = (f32[2,128,120]{2,1,0:T(8,128)S(1)}, f32[2,128,120]{2,1,0:T(8,128)}, u32[]{:S(2)}) copy-start(f32[2,128,120]{2,1,0:T(8,128)} %copy-done.2) | copy-start | bytes 368644
  182.0 29.7 %copy-start.17 = (bf16[2,128,120]{2,1,0:T(8,128)(2,1)S(1)}, bf16[2,128,120]{2,1,0:T(8,128)(2,1)}, u32[]{:S(2)}) copy-start(bf16[2,128,120]{2,1,0:T(8,128)(2,1)} %copy-done.16) | copy-start | bytes 184324
  182.0 29.3 %all-to-all-start.5 = ((bf16[8,2,128,128]{3,2,1,0:T(8,128)(2,1)}), bf16[8,2,128,128]{3,2,1,0:T(8,128)(2,1)S(1)}, u32[]{:S(2)}, u32[]{:S(2)}) async-start(bf16[8,2,128,128]{3,2,1,0:T(8,128)(2,1)} %bitcast.62), calls=%async_computation.5 | async-start | bytes 1048576 | tf_op jit(solution)/shard_map/all_to_all | solution.py:389
  187.9 7.6 %collective-permute-start.13 = (bf16[4,120,128]{2,1,0:T(8,128)(2,1)S(1)}, bf16[4,120,128]{2,1,0:T(8,128)(2,1)S(1)}, u32[]{:S(2)}, u32[]{:S(2)}) collective-permute-start(bf16[4,120,128]{2,1,0:T(8,128)(2,1)S(1)} %slice_bitcast_fusion), channel_id=1, source_target_pairs={{0,8},{8,0},{16,24},{24,16},{32,40},{40,32},{48,56},{56,48},{64,72... | collective-permute-start | bytes 368648 | tf_op jit(solution)/shard_map/ppermute | solution.py:40
  196.4 7.6 %collective-permute-start.14 = (bf16[2,120,128]{2,1,0:T(8,128)(2,1)S(1)}, bf16[2,120,128]{2,1,0:T(8,128)(2,1)S(1)}, u32[]{:S(2)}, u32[]{:S(2)}) collective-permute-start(bf16[2,120,128]{2,1,0:T(8,128)(2,1)S(1)} %slice.167), channel_id=1, source_target_pairs={{0,16},{8,24},{16,0},{24,8},{32,48},{40,56},{48,32},{56,40},{64,80... | collective-permute-start | bytes 184328 | tf_op jit(solution)/shard_map/ppermute | solution.py:40
  204.1 5.8 %collective-permute-start.15 = (bf16[1,120,128]{2,1,0:T(8,128)(2,1)S(1)}, bf16[1,120,128]{2,1,0:T(8,128)(2,1)S(1)}, u32[]{:S(2)}, u32[]{:S(2)}) collective-permute-start(bf16[1,120,128]{2,1,0:T(8,128)(2,1)S(1)} %slice.169), channel_id=1, source_target_pairs={{0,256},{8,264},{16,272},{24,280},{32,288},{40,296},{48,304},{56,3... | collective-permute-start | bytes 92168 | tf_op jit(solution)/shard_map/ppermute | solution.py:40
  209.9 7.8 %copy-start.21 = (bf16[128,120]{0,1:T(8,128)(2,1)}, bf16[128,120]{0,1:T(8,128)(2,1)S(1)}, u32[]{:S(2)}) copy-start(bf16[128,120]{0,1:T(8,128)(2,1)S(1)} %fusion.19) | copy-start | bytes 92164
  211.4 6.3 %copy-start.12 = (f32[2,128,128]{2,1,0:T(8,128)}, f32[2,128,128]{2,1,0:T(8,128)S(1)}, u32[]{:S(2)}) copy-start(f32[2,128,128]{2,1,0:T(8,128)S(1)} %convert_reduce_fusion.1) | copy-start | bytes 393220
  211.6 6.1 %copy-start.24 = (f32[128]{0:T(128)}, f32[128]{0:T(128)S(1)}, u32[]{:S(2)}) copy-start(f32[128]{0:T(128)S(1)} %get-tuple-element.22) | copy-start | bytes 1540
  211.8 8.4 %collective-permute-start.16 = (bf16[2,32,120]{2,1,0:T(8,128)(2,1)S(1)}, bf16[2,32,120]{2,1,0:T(8,128)(2,1)S(1)}, u32[]{:S(2)}, u32[]{:S(2)}) collective-permute-start(bf16[2,32,120]{2,1,0:T(8,128)(2,1)S(1)} %get-tuple-element.32), channel_id=1, source_target_pairs={{0,8},{8,16},{16,24},{24,32},{32,40},{40,48},{48,56},{56,64},{64,7... | collective-permute-start | bytes 46088 | tf_op jit(solution)/shard_map/ppermute | solution.py:159
  215.5 5.6 %collective-permute-start.17 = (bf16[2,32,120]{2,1,0:T(8,128)(2,1)S(1)}, bf16[2,32,120]{2,1,0:T(8,128)(2,1)S(1)}, u32[]{:S(2)}, u32[]{:S(2)}) collective-permute-start(bf16[2,32,120]{2,1,0:T(8,128)(2,1)S(1)} %get-tuple-element.33), channel_id=1, source_target_pairs={{8,0},{16,8},{24,16},{32,24},{40,32},{48,40},{56,48},{64,56},{72,6... | collective-permute-start | bytes 46088 | tf_op jit(solution)/shard_map/ppermute | solution.py:160
  217.7 1.0 copy-start.1
  218.8 0.9 copy-start.10
  229.3 6.7 %copy-start.20 = (bf16[2,192,120]{2,1,0:T(8,128)(2,1)S(1)}, bf16[2,192,120]{2,1,0:T(8,128)(2,1)}, u32[]{:S(2)}) copy-start(bf16[2,192,120]{2,1,0:T(8,128)(2,1)} %get-tuple-element.24) | copy-start | bytes 276484
  229.3 22.7 %all-to-all-start.6 = ((bf16[8,256,360]{1,2,0:T(8,128)(2,1)}), bf16[8,256,360]{1,2,0:T(8,128)(2,1)S(1)}, u32[]{:S(2)}, u32[]{:S(2)}) async-start(bf16[8,256,360]{1,2,0:T(8,128)(2,1)} %copy.72), calls=%async_computation.6 | async-start | bytes 2949120 | tf_op jit(solution)/shard_map/all_to_all | solution.py:32
  236.0 26.3 %collective-permute-start.18 = (bf16[2,192,120]{2,1,0:T(8,128)(2,1)S(1)}, bf16[2,192,120]{2,1,0:T(8,128)(2,1)}, u32[]{:S(2)}, u32[]{:S(2)}) collective-permute-start(bf16[2,192,120]{2,1,0:T(8,128)(2,1)S(1)} %copy-done.20), channel_id=1, source_target_pairs={{0,256},{8,264},{16,272},{24,280},{32,288},{40,296},{48,304},{56,3... | collective-permute-start | bytes 276488 | tf_op jit(solution)/shard_map/ppermute | solution.py:40
  256.0 17.1 %copy-start.4 = (f32[2,128,120]{2,1,0:T(8,128)S(1)}, f32[2,128,120]{2,1,0:T(8,128)}, u32[]{:S(2)}) copy-start(f32[2,128,120]{2,1,0:T(8,128)} %copy-done.2) | copy-start | bytes 368644
  256.1 17.1 %copy-start.13 = (f32[2,128,128]{2,1,0:T(8,128)S(1)}, f32[2,128,128]{2,1,0:T(8,128)}, u32[]{:S(2)}) copy-start(f32[2,128,128]{2,1,0:T(8,128)} %copy-done.12) | copy-start | bytes 393220
  256.1 17.1 %copy-start.15 = (bf16[128,2,120]{2,0,1:T(8,128)(2,1)S(1)}, bf16[128,2,120]{2,0,1:T(8,128)(2,1)}, u32[]{:S(2)}) copy-start(bf16[128,2,120]{2,0,1:T(8,128)(2,1)} %copy-done.14) | copy-start | bytes 184324
  256.1 17.1 %copy-start.18 = (bf16[2,128,120]{2,1,0:T(8,128)(2,1)S(1)}, bf16[2,128,120]{2,1,0:T(8,128)(2,1)}, u32[]{:S(2)}) copy-start(bf16[2,128,120]{2,1,0:T(8,128)(2,1)} %copy-done.16) | copy-start | bytes 184324
  256.1 17.1 %copy-start.25 = (f32[128]{0:T(128)S(1)}, f32[128]{0:T(128)}, u32[]{:S(2)}) copy-start(f32[128]{0:T(128)} %copy-done.24) | copy-start | bytes 1540
  256.1 17.9 %all-to-all-start.7 = ((bf16[8,32,360]{2,1,0:T(8,128)(2,1)}), bf16[8,32,360]{2,1,0:T(8,128)(2,1)S(1)}, u32[]{:S(2)}, u32[]{:S(2)}) async-start(bf16[8,32,360]{2,1,0:T(8,128)(2,1)} %bitcast.35), calls=%async_computation.7 | async-start | bytes 393216 | tf_op jit(solution)/shard_map/all_to_all | solution.py:44
  267.0 6.2 %collective-permute-start.19 = (bf16[2,128,120]{2,1,0:T(8,128)(2,1)S(1)}, bf16[2,128,120]{2,1,0:T(8,128)(2,1)S(1)}, u32[]{:S(2)}, u32[]{:S(2)}) collective-permute-start(bf16[2,128,120]{2,1,0:T(8,128)(2,1)S(1)} %get-tuple-element.18), channel_id=1, source_target_pairs={{0,256},{8,264},{16,272},{24,280},{32,288},{40,296},{48,304},{56,3... | collective-permute-start | bytes 184328 | tf_op jit(solution)/shard_map/ppermute | solution.py:40

commit v5 on v3

--- a/solution.py
+++ b/solution.py
@@ -49,7 +49,7 @@
 
 
 def after(array, earlier):
-    return array + 0 * earlier.reshape(-1)[0].astype(array.dtype)
+    return array + 0 * earlier[(0,) * earlier.ndim].astype(array.dtype)
 
 
 BITS = (32, 2, 1)
@@ -63,11 +63,8 @@
     return array
 
 
-def halved(array):
-    for bit in BITS[::-1]:
-        half = array.shape[0] // 2
-        array = array[:half] + swap(array[half:], bit)
-    return array[0]
+def nothing(array):
+    return (0 * array[(0,) * array.ndim].astype(F32)).astype(jnp.int32)
 
 
 def vmem_call(body, out_shape, scratch=(), scalars=0, inputs=0, flops=0):
@@ -134,9 +131,11 @@
                 other_ref[g] = totals[g].astype(BF)
 
 
-def convolved(forward, scalars, rows, taps):
-    padded = with_halo(rows)
-    pair = jnp.stack([padded, swap(padded, 32)])
+def paired(padded):
+    return jnp.stack([padded, swap(padded, 32)])
+
+
+def convolved(forward, scalars, pair, taps):
     own, other = vmem_call(
         functools.partial(conv_body, forward),
         (
@@ -147,7 +146,7 @@
         inputs=2,
         flops=32 * 2 * 2 * 2 * ROWS * HD * HD,
     )(scalars, pair, taps)
-    return own + swap(other, 32).astype(F32)
+    return own, swap(other, 32)
 
 
 def with_halo(rows):
@@ -167,19 +166,19 @@
 CONTRACT = (((1,), (1,)), ((), ()))
 
 
-def scored(c, q_ref, kv_ref, d_ref):
+def scored(c, q_ref, kv_ref):
     keys = kv_ref[:, :, :LANES].reshape(ALL, LANES)
     values = kv_ref[:, :, LANES : LANES + HD].reshape(ALL, HD)
-    q = q_ref[c * N : (c + 1) * N].reshape(CHUNK, LANES)
-    d = d_ref[c * N : (c + 1) * N].reshape(CHUNK, HD)
+    q = q_ref[c * N : (c + 1) * N, :, :LANES].reshape(CHUNK, LANES)
+    d = q_ref[c * N : (c + 1) * N, :, LANES : LANES + HD].reshape(CHUNK, HD)
     scores = lax.dot_general(keys, q, CONTRACT, preferred_element_type=F32)
     dprobs = lax.dot_general(values, d, CONTRACT, preferred_element_type=F32)
     return keys, values, q, d, scores * SCALE2, dprobs
 
 
-def stats_body(sc_ref, q_ref, kv_ref, d_ref, out_ref):
+def stats_body(sc_ref, q_ref, kv_ref, out_ref):
     for c in range(ALL // CHUNK):
-        _, _, _, _, scores, dprobs = scored(c, q_ref, kv_ref, d_ref)
+        _, _, _, _, scores, dprobs = scored(c, q_ref, kv_ref)
         peak = jnp.max(scores, axis=0, keepdims=True)
         weight = jnp.exp2(scores - peak)
         total = jnp.sum(weight, axis=0, keepdims=True)
@@ -191,7 +190,7 @@
                 out_ref[j, shard] = value[:, columns]
 
 
-def grads_body(sc_ref, q_ref, kv_ref, d_ref, stats_ref, od_ref, dkv_ref, dk_ref, dv_ref):
+def grads_body(sc_ref, q_ref, kv_ref, stats_ref, od_ref, dkv_ref, dk_ref, dv_ref):
     for c in range(ALL // CHUNK):
         peaks, totals, alongs = (
             jnp.concatenate(
@@ -205,7 +204,7 @@
         total = jnp.sum(totals * factor, axis=0)
         delta = jnp.sum(alongs * factor, axis=0) / total
         lse = top + jnp.log2(total)
-        keys, values, q, d, scores, dprobs = scored(c, q_ref, kv_ref, d_ref)
+        keys, values, q, d, scores, dprobs = scored(c, q_ref, kv_ref)
         probs = jnp.exp2(scores - lse)
         dscores = (probs * (dprobs - delta)).astype(BF)
         probs = probs.astype(BF)
@@ -221,8 +220,10 @@
         out_t = lax.dot_general(values, probs, inner, preferred_element_type=F32)
         dq_t = lax.dot_general(keys, dscores, inner, preferred_element_type=F32) * SCALE
         for i in range(N):
-            od_ref[0, c * N + i] = out_t[:, i * ROWS : (i + 1) * ROWS].astype(BF)
-            od_ref[1, c * N + i] = dq_t[:HD, i * ROWS : (i + 1) * ROWS].astype(BF)
+            e = SLOTS[c * N + i]
+            at = (sc_ref[0] % 4) ^ (e % 4)
+            od_ref[e // 4, at, 0] = out_t[:, i * ROWS : (i + 1) * ROWS].astype(BF)
+            od_ref[e // 4, at, 1] = dq_t[:HD, i * ROWS : (i + 1) * ROWS].astype(BF)
     for i in range(8):
         piece = slice(i * ROWS, (i + 1) * ROWS)
         dkv_ref[i, :, :LANES] = (dk_ref[piece] * SCALE).astype(BF)
@@ -230,21 +231,21 @@
         dkv_ref[i, :, LANES + HD :] = jnp.zeros((ROWS, LANES - HD), BF)
 
 
-def attention_stats(scalars, queries, keys, upstream):
+def attention_stats(scalars, queries, keys):
     return vmem_call(
         stats_body,
         jax.ShapeDtypeStruct((3, 8, ROWS), F32),
         scalars=1,
-        inputs=3,
+        inputs=2,
         flops=2 * 2 * ALL * ALL * LANES,
-    )(scalars, queries, keys, upstream)
-
-
-def attention_grads(scalars, queries, keys, upstream, stats):
+    )(scalars, queries, keys)
+
+
+def attention_grads(scalars, queries, keys, stats):
     return vmem_call(
         grads_body,
         (
-            jax.ShapeDtypeStruct((2, 8, HD, ROWS), BF),
+            jax.ShapeDtypeStruct((2, 4, 2, HD, ROWS), BF),
             jax.ShapeDtypeStruct((8, ROWS, 2 * LANES), BF),
         ),
         scratch=[
@@ -252,9 +253,14 @@
             pltpu.VMEM((ALL, HD), F32),
         ],
         scalars=1,
-        inputs=4,
+        inputs=3,
         flops=6 * 2 * ALL * ALL * LANES,
-    )(scalars, queries, keys, upstream, stats)
+    )(scalars, queries, keys, stats)
+
+
+GROUPS = 16
+WIDTH = GROUPS * HD
+SLAB = 32
 
 
 def gelu_parts(inputs):
@@ -263,87 +269,217 @@
     return inputs * normal_cdf, normal_cdf + inputs * density
 
 
+def hidden_body(own_ref, other_ref, frames_ref, hidden_ref, slope_ref, sent_ref):
+    for g in range(2):
+        conv = own_ref[g] + other_ref[g].astype(F32)
+        activated, slope = gelu_parts(conv)
+        hidden = (frames_ref[g].astype(F32) + activated).T
+        hidden_ref[g] = hidden
+        slope_ref[g] = slope.T
+        sent_ref[g] = hidden.astype(BF)
+
+
+def hidden_rows(own, other, frames_g):
+    shape = jax.ShapeDtypeStruct((2, HD, ROWS), F32)
+    return vmem_call(
+        hidden_body, (shape, shape, jax.ShapeDtypeStruct((2, HD, ROWS), BF)), inputs=3
+    )(own, other, frames_g)
+
+
+def project_body(
+    sc_ref, all_ref, hidden_ref, w_ref, up_ref, kv_ref, q_ref, normed_ref, unit_ref, inv_ref
+):
+    total = jnp.zeros((HD, ROWS), F32)
+    square = jnp.zeros((HD, ROWS), F32)
+    for g in range(GROUPS):
+        hidden = all_ref[g].astype(F32)
+        total += hidden
+        square += hidden * hidden
+    center = jnp.sum(total, axis=0, keepdims=True) / WIDTH
+    square = jnp.sum(square, axis=0, keepdims=True) / WIDTH
+    inv_std = lax.rsqrt(square - center * center + EPS)
+    inv_ref[...] = inv_std
+    projected = jnp.zeros((ROWS, 3 * HD), F32)
+    for g in range(GROUPS):
+        normed = ((all_ref[g].astype(F32) - center) * inv_std).astype(BF)
+        normed_ref[g] = normed
+        projected += lax.dot_general(
+            normed,
+            w_ref[g * HD : (g + 1) * HD],
+            (((0,), (0,)), ((), ())),
+            preferred_element_type=F32,
+        )
+    for g in range(2):
+        unit_ref[g] = (hidden_ref[g] - center) * inv_std
+    projected = projected.astype(BF)
+    pos = sc_ref[0] * ROWS + lax.broadcasted_iota(jnp.int32, (ROWS, LANES - HD), 0)
+    lane = lax.broadcasted_iota(jnp.int32, (ROWS, LANES - HD), 1)
+    seg = jnp.zeros_like(pos)
+    for u in range(3):
+        seg += jnp.where(pos >= sc_ref[1 + u], 1, 0)
+    nil = jnp.zeros((ROWS, LANES - HD), BF)
+    q_ref[0, :, :HD] = projected[:, :HD]
+    q_ref[0, :, HD:LANES] = jnp.where(seg == lane, 1.0, 0.0).astype(BF)
+    q_ref[0, :, LANES : LANES + HD] = up_ref[...]
+    q_ref[0, :, LANES + HD :] = nil
+    k_mark = jnp.where(seg == lane, 0.0, FAR).astype(BF)
+    for i in range(8):
+        kv_ref[i, :, :HD] = projected[:, HD : 2 * HD]
+        kv_ref[i, :, HD:LANES] = k_mark
+        kv_ref[i, :, LANES : LANES + HD] = projected[:, 2 * HD :]
+        kv_ref[i, :, LANES + HD :] = nil
+
+
+def project(scalars, all_t, hidden_t, w_qkv, grad_out):
+    return vmem_call(
+        project_body,
+        (
+            jax.ShapeDtypeStruct((8, ROWS, 2 * LANES), BF),
+            jax.ShapeDtypeStruct((1, ROWS, 2 * LANES), BF),
+            jax.ShapeDtypeStruct((GROUPS, HD, ROWS), BF),
+            jax.ShapeDtypeStruct((2, HD, ROWS), F32),
+            jax.ShapeDtypeStruct((1, ROWS), F32),
+        ),
+        scalars=1,
+        inputs=4,
+        flops=2 * ROWS * WIDTH * 3 * HD,
+    )(scalars, all_t, hidden_t, w_qkv, grad_out)
+
+
+def share_body(od_ref, dkv_ref, normed_ref, w_ref, parts_ref, grad_ref, out_ref):
+    out, dq = od_ref[0, 0].astype(F32), od_ref[0, 1].astype(F32)
+    for i in range(1, 4):
+        out += od_ref[i, 0].astype(F32)
+        dq += od_ref[i, 1].astype(F32)
+    dkv = dkv_ref[0].astype(F32)
+    for i in range(1, 8):
+        dkv += dkv_ref[i].astype(F32)
+    out_ref[...] = out.T.astype(BF)
+    grad_ref[:, :HD] = dq.T.astype(BF)
+    grad_ref[:, HD : 2 * HD] = dkv[:, :HD].astype(BF)
+    grad_ref[:, 2 * HD :] = dkv[:, LANES : LANES + HD].astype(BF)
+    grad = grad_ref[...]
+    plain = jnp.zeros((HD, ROWS), F32)
+    along = jnp.zeros((HD, ROWS), F32)
+    for g in range(GROUPS):
+        share = lax.dot_general(
+            w_ref[g * HD : (g + 1) * HD], grad, CONTRACT, preferred_element_type=F32
+        )
+        plain += share
+        along += share * normed_ref[g].astype(F32)
+        parts_ref[g, :HD] = share.astype(BF)
+    plain = jnp.sum(plain, axis=0, keepdims=True)
+    along = jnp.sum(along, axis=0, keepdims=True)
+    plain_high = plain.astype(BF).astype(F32)
+    along_high = along.astype(BF).astype(F32)
+    rows = [plain_high, along_high, plain - plain_high, along - along_high]
+    sums = jnp.concatenate(rows + [jnp.zeros((4, ROWS), F32)], axis=0).astype(BF)
+    for g in range(GROUPS):
+        parts_ref[g, HD:] = sums
+
+
+def shares(od, dkv, normed_t, w_qkv):
+    return vmem_call(
+        share_body,
+        (
+            jax.ShapeDtypeStruct((GROUPS, LANES, ROWS), BF),
+            jax.ShapeDtypeStruct((ROWS, 3 * HD), BF),
+            jax.ShapeDtypeStruct((ROWS, HD), BF),
+        ),
+        inputs=4,
+        flops=2 * ROWS * WIDTH * 3 * HD,
+    )(od, dkv, normed_t, w_qkv)
+
+
+def slabs_body(normed_ref, grad_ref, out_ref):
+    slab = HD // 4
+    grad = grad_ref[...]
+    out_ref[...] = jnp.zeros_like(out_ref)
+    for g in range(GROUPS):
+        wide = jnp.dot(normed_ref[g], grad, preferred_element_type=F32)
+        row = g % 8 * SLAB
+        for x in range(4):
+            piece = wide[x * slab : (x + 1) * slab].astype(BF)
+            out_ref[g // 8 * 4 + x, row : row + slab, : 3 * HD] = piece
+
+
+def slabs(normed_t, grad):
+    return vmem_call(
+        slabs_body,
+        jax.ShapeDtypeStruct((8, 8 * SLAB, 3 * LANES), BF),
+        inputs=2,
+        flops=2 * ROWS * WIDTH * 3 * HD,
+    )(normed_t, grad)
+
+
+def error_body(parts_ref, unit_ref, inv_ref, slope_ref, grad_ref, error_ref):
+    sums = []
+    for g in range(2):
+        total = parts_ref[0, g].astype(F32)
+        for i in range(1, 8):
+            total += parts_ref[i, g].astype(F32)
+        sums.append(total)
+    plain = (sums[0][HD : HD + 1] + sums[0][HD + 2 : HD + 3]) / WIDTH
+    along = (sums[0][HD + 1 : HD + 2] + sums[0][HD + 3 : HD + 4]) / WIDTH
+    for g in range(2):
+        grad = inv_ref[...] * (sums[g][:HD] - plain - unit_ref[g] * along)
+        grad_ref[g] = grad.T
+        error_ref[g] = (slope_ref[g] * grad).T.astype(BF)
+
+
+def errors(parts, unit_t, inv_std, slope_t):
+    return vmem_call(
+        error_body,
+        (
+            jax.ShapeDtypeStruct((2, ROWS, HD), F32),
+            jax.ShapeDtypeStruct((2, ROWS, HD), BF),
+        ),
+        inputs=4,
+    )(parts, unit_t, inv_std, slope_t)
+
+
 def on_device(frames, conv_weight, w_qkv, lengths, grad_out):
     index = lax.axis_index("tm")
     y, x = index // 32, index % 4
     ends = jnp.cumsum(lengths).astype(jnp.int32)
-    groups = 2
-    width = w_qkv.shape[0]
 
     def scalars(*first):
         return jnp.concatenate([jnp.stack(first).astype(jnp.int32), ends])
 
-    frames_g = frames.reshape(ROWS, groups, HD).transpose(1, 0, 2)
-    taps = exchange_x(everyone(exchange_z(everyone(conv_weight[0])), 4))
     where = scalars(y, index)
-    conv = convolved(True, where, frames_g, taps)
-    upstream = doubled(grad_out)
-    activated, slope = gelu_parts(conv)
-    hidden = frames_g.astype(F32) + activated
-
-    hidden_all = lax.all_gather(hidden.astype(BF), "head", axis=0, tiled=True).astype(F32)
-    center = jnp.sum(hidden_all, axis=(0, 2)) / width
-    square = jnp.sum(hidden_all * hidden_all, axis=(0, 2)) / width
-    inv_std = lax.rsqrt(square - center * center + EPS)
-    normed = ((hidden_all - center[:, None]) * inv_std[:, None]).astype(BF)
-    unit = (hidden - center[:, None]) * inv_std[:, None]
-    weights = w_qkv.reshape(16, HD, 3 * HD)
-    normed_rows = normed.transpose(1, 0, 2).reshape(ROWS, width)
-    projected = jnp.dot(normed_rows, w_qkv, preferred_element_type=F32).astype(BF)
-
-    pos = index * ROWS + jnp.arange(ROWS, dtype=jnp.int32)
-    seg = jnp.sum((pos[:, None] >= ends[None, :3]).astype(jnp.int32), axis=1)
-    same = seg[:, None] == jnp.arange(8, dtype=jnp.int32)[None]
-    q_mark = same.astype(BF)
-    k_mark = jnp.where(same, 0.0, FAR).astype(BF)
-    nil = jnp.zeros((ROWS, 8), BF)
-    queries = jnp.concatenate([projected[:, :HD], q_mark], axis=1)
-    keys = jnp.concatenate(
-        [projected[:, HD : 2 * HD], k_mark, projected[:, 2 * HD :], nil], axis=1
+    order = scalars(y * 4 + x)
+
+    frames_g = frames.reshape(ROWS, 2, HD).transpose(1, 0, 2)
+    pair = paired(with_halo(frames_g))
+    taps = exchange_z(everyone(conv_weight[0]))
+    taps = exchange_x(everyone(after(taps, pair), 4))
+    own, other = convolved(True, where, pair, taps)
+    hidden_t, slope_t, sent = hidden_rows(own, other, frames_g)
+
+    all_t = lax.all_gather(sent, "head", axis=0, tiled=True)
+    keys, queries, normed_t, unit_t, inv_std = project(
+        scalars(index), all_t, hidden_t, w_qkv, grad_out
     )
-    keys_all = exchange_z(everyone(keys))
-    queries_all = doubled(queries)
-    order = scalars(y * 4 + x)
-    stats = attention_stats(order, queries_all, keys_all, upstream)
-    stats = exchange_xy(everyone(stats))
-    od, dkv = attention_grads(order, queries_all, keys_all, upstream, stats)
-    dkv = jnp.sum(exchange_z(dkv).astype(F32), axis=0).astype(BF)
-    grad_q = halved(od[1])
-    attended = halved(after(od[0], grad_q)).T
-    grad_joined = jnp.concatenate([grad_q.T, dkv[:, :HD], dkv[:, LANES : LANES + HD]], axis=1)
-
-    share = jnp.einsum("tj,gcj->gtc", grad_joined, weights, preferred_element_type=F32)
-    plain = jnp.sum(share, axis=(0, 2))
-    along = jnp.sum(share * normed.astype(F32), axis=(0, 2))
-    sums = jnp.stack([plain, along], axis=1)
-    sums_high = sums.astype(BF)
-    sums_low = (sums - sums_high.astype(F32)).astype(BF)
-    sums = jnp.concatenate([sums_high, sums_low, jnp.zeros((ROWS, 4), BF)], axis=1)
-    parts = jnp.concatenate(
-        [share.astype(BF), jnp.broadcast_to(sums[None], (16, ROWS, 8))], axis=2
-    ).reshape(8, groups, ROWS, LANES)
-    parts = lax.all_to_all(parts, "head", 0, 0)
-    parts = jnp.sum(parts.astype(F32), axis=0)
-    feature = parts[:, :, :HD]
-    plain = parts[0, :, HD] + parts[0, :, HD + 2]
-    along = parts[0, :, HD + 1] + parts[0, :, HD + 3]
-    hidden_grad = inv_std[:, None] * (
-        feature - plain[:, None] / width - unit * (along[:, None] / width)
-    )
-
-    error = (slope * hidden_grad).astype(BF)
-    frame_grad = hidden_grad + convolved(False, where, error, taps)
-    frame_grad = frame_grad.astype(BF).transpose(1, 0, 2).reshape(ROWS, groups * HD)
-
-    wide = lax.dot_general(
-        normed_rows, grad_joined, (((0,), (0,)), ((), ())), preferred_element_type=F32
-    ).astype(BF)
-    slab = width // 64
-    wide = wide.reshape(2, 8, 4, slab, 3 * HD).transpose(0, 2, 1, 3, 4)
-    wide = exchange_xy(wide.reshape(8, 8, slab, 3 * HD))
+
+    keys = exchange_z(keys)
+    queries = doubled(queries[0])
+    stats = exchange_xy(everyone(attention_stats(order, queries, keys)))
+    od, dkv = attention_grads(order, queries, keys, stats)
+    dkv = exchange_z(dkv)
+    od = exchange_x(after(od[0] + swap(od[1], 32), dkv))
+
+    parts, grad, attended = shares(od, dkv, normed_t, w_qkv)
+    parts = lax.all_to_all(parts.reshape(8, 2, LANES, ROWS), "head", 0, 0)
+    hidden_grad, error = errors(parts, unit_t, inv_std, slope_t)
+    wide = exchange_xy(slabs(normed_t, grad))
     wide = jnp.sum(wide.astype(F32), axis=0).astype(BF)
-    weight_grad = jnp.sum(exchange_z(wide).astype(F32), axis=0)
-    return attended, frame_grad, weight_grad
+
+    pair = paired(with_halo(error))
+    own, other = convolved(False, where + nothing(wide), pair, taps)
+    frame_grad = (hidden_grad + own + other.astype(F32)).astype(BF)
+    wide = exchange_z(wide.reshape(8, SLAB, 3 * LANES))
+    weight_grad = jnp.sum(wide[:, : HD // 4, : 3 * HD].astype(F32), axis=0)
+    return attended, frame_grad.transpose(1, 0, 2).reshape(ROWS, 2 * HD), weight_grad
 
 
 def solution(mesh):

time: 257 us -> 250 us (0.973)
  the two profiles are of different devices: /device:TPU:16 before, /device:TPU:8 now
where the time goes in v5:
time: 250 us; the launch traced here: 249 us
  starting transfers between devices  83 us (33%)
  waiting for transfers between devices  79.7 us (32%)
  blocking collectives  34.9 us (14%)
  local copies, waits for them, and re-layouts  22.7 us (9%)
  Pallas kernels  18.4 us (7%)
  other arithmetic  7.04 us (3%)
  between operations  2.99 us (1%)
    ppermute x8, waiting for transfers between devices, swap(): return lax.ppermute(array, 'tm', [(i, i ^ bit) for i in range(64)])  30.4 us
    all_to_all x4, starting transfers between devices, exchange_z(): return lax.all_to_all(parts, 'tm', 0, 0, axis_index_groups=Z_GROUPS)  26.7 us
    ppermute x8, starting transfers between devices, swap(): return lax.ppermute(array, 'tm', [(i, i ^ bit) for i in range(64)])  20.3 us
    all_gather x1, blocking collectives, on_device(): all_t = lax.all_gather(sent, 'head', axis=0, tiled=True)  16.8 us
    all_to_all x1, waiting for transfers between devices, exchange_x(): return lax.all_to_all(parts, 'tm', 0, 0, axis_index_groups=X_GROUPS)  14.1 us
    unnamed x48, local copies, waits for them, and re-layouts  13.9 us
    ppermute x2, starting transfers between devices, with_halo(): after = lax.ppermute(rows[:, :HALF], 'tm', down)  13.3 us
    all_to_all x1, waiting for transfers between devices, on_device(): parts = lax.all_to_all(parts.reshape(8, 2, LANES, ROWS), 'head', 0, 0)  12.9 us
  transfers between devices with their start and end apart: 19, of which 13 were waited for; matrix products, arithmetic and copies ran while one was open for 4% of the time, Pallas kernels for 2%

profile of v5, /device:TPU:8, one launch (start us, length us, event | category | flops | bytes accessed | tf_op | source)
XLA Modules:
  0.0 248.7 jit_solution(11161887142019675618)
XLA Ops:
  0.6 1.7 broadcast_in_dim.9
  2.3 10.3 %all-to-all-start = ((bf16[8,2,120,120]{3,2,1,0:T(8,128)(2,1)}), bf16[8,2,120,120]{3,2,1,0:T(8,128)(2,1)S(1)}, u32[]{:S(2)}, u32[]{:S(2)}) async-start(bf16[8,2,120,120]{3,2,1,0:T(8,128)(2,1)} %broadcast_in_dim.9), calls=%async_computation | async-start | bytes 983040 | tf_op jit(solution)/shard_map/all_to_all | solution.py:44
  12.8 3.4 %collective-permute-start = (bf16[2,32,120]{2,1,0:T(8,128)(2,1)S(1)}, bf16[2,32,120]{2,1,0:T(8,128)(2,1)S(1)}, u32[]{:S(2)}, u32[]{:S(2)}) collective-permute-start(bf16[2,32,120]{2,1,0:T(8,128)(2,1)S(1)} %get-tuple-element.66), channel_id=1, source_target_pairs={{0,8},{8,16},{16,24},{24,32},{32,40},{40,48},{48,56},{56,64},{64,7... | collective-permute-start | bytes 46088 | tf_op jit(solution)/shard_map/ppermute | solution.py:156
  16.2 6.7 %collective-permute-start.1 = (bf16[2,32,120]{2,1,0:T(8,128)(2,1)S(1)}, bf16[2,32,120]{2,1,0:T(8,128)(2,1)S(1)}, u32[]{:S(2)}, u32[]{:S(2)}) collective-permute-start(bf16[2,32,120]{2,1,0:T(8,128)(2,1)S(1)} %get-tuple-element.67), channel_id=1, source_target_pairs={{8,0},{16,8},{24,16},{32,24},{40,32},{48,40},{56,48},{64,56},{72,6... | collective-permute-start | bytes 46088 | tf_op jit(solution)/shard_map/ppermute | solution.py:157
  22.9 1.4 collective-permute-done.1
  26.2 3.3 %all-to-all-done = bf16[8,2,120,120]{3,2,1,0:T(8,128)(2,1)S(1)} async-done(((bf16[8,2,120,120]{3,2,1,0:T(8,128)(2,1)}), bf16[8,2,120,120]{3,2,1,0:T(8,128)(2,1)S(1)}, u32[]{:S(2)}, u32[]{:S(2)}) %all-to-all-start) | async-done | bytes 460832 | tf_op jit(solution)/shard_map/all_to_all | solution.py:44
  29.5 1.6 broadcast_in_dim.10
  31.1 4.4 %all-to-all-start.1 = ((bf16[4,8,2,120,120]{4,3,2,1,0:T(8,128)(2,1)}), bf16[4,8,2,120,120]{4,3,2,1,0:T(8,128)(2,1)S(1)}, u32[]{:S(2)}, u32[]{:S(2)}) async-start(bf16[4,8,2,120,120]{4,3,2,1,0:T(8,128)(2,1)} %broadcast_in_dim.10), calls=%async_computation.1 | async-start | bytes 3932160 | tf_op jit(solution)/shard_map/all_to_all | solution.py:36
  35.8 2.4 copy.45.w_ref
  38.2 2.4 collective-permute-start.2
  40.6 4.3 %collective-permute-done.2 = bf16[2,192,120]{2,1,0:T(8,128)(2,1)S(1)} collective-permute-done((bf16[2,192,120]{2,1,0:T(8,128)(2,1)}, bf16[2,192,120]{2,1,0:T(8,128)(2,1)S(1)}, u32[]{:S(2)}, u32[]{:S(2)}) %collective-permute-start.2) | collective-permute-done | bytes 92192 | tf_op jit(solution)/shard_map/ppermute | solution.py:40
  44.9 1.6 pad_maximum_fusion.1.x_ref
  46.5 14.1 %all-to-all-done.1.w_ref = bf16[4,8,2,120,120]{4,3,2,1,0:T(8,128)(2,1)S(1)} async-done(((bf16[4,8,2,120,120]{4,3,2,1,0:T(8,128)(2,1)}), bf16[4,8,2,120,120]{4,3,2,1,0:T(8,128)(2,1)S(1)}, u32[]{:S(2)}, u32[]{:S(2)}) %all-to-all-start.1) | async-done | bytes 1843232 | tf_op jit(solution)/shard_map/all_to_all | solution.py:36
  60.6 0.9 copy-done.3
  61.5 2.2 shard_map.76
  63.7 2.4 collective-permute-start.3
  66.2 3.7 %collective-permute-done.3.other_ref = bf16[2,128,120]{2,1,0:T(8,128)(2,1)S(1)} collective-permute-done((bf16[2,128,120]{2,1,0:T(8,128)(2,1)S(1)}, bf16[2,128,120]{2,1,0:T(8,128)(2,1)S(1)}, u32[]{:S(2)}, u32[]{:S(2)}) %collective-permute-start.3) | collective-permute-done | bytes 61472 | tf_op jit(solution)/shard_map/ppermute | solution.py:40
  70.7 16.8 %all_gather.3.all_ref = bf16[16,120,128]{2,1,0:T(8,128)(2,1)S(1)} all-gather(bf16[2,120,128]{2,1,0:T(8,128)(2,1)S(1)} %get-tuple-element.24), channel_id=1, replica_groups=mesh['tm'=64,'head'=8] {'head'}, dimensions={0}, use_global_device_ids=true | all-gather | bytes 552960 | tf_op jit(solution)/shard_map/all_gather | solution.py:459
  87.5 1.5 shard_map.78
  89.0 0.8 copy-done
  89.8 0.8 copy-done.4
  91.3 5.8 %all-to-all-start.2 = ((bf16[8,128,256]{2,1,0:T(8,128)(2,1)}), bf16[8,128,256]{2,1,0:T(8,128)(2,1)}, u32[]{:S(2)}, u32[]{:S(2)}) async-start(bf16[8,128,256]{2,1,0:T(8,128)(2,1)} %copy-done.4), calls=%async_computation.2 | async-start | bytes 1048576 | tf_op jit(solution)/shard_map/all_to_all | solution.py:44
  97.1 3.5 %collective-permute-start.4 = (bf16[1,128,256]{2,1,0:T(8,128)(2,1)S(1)}, bf16[1,128,256]{2,1,0:T(8,128)(2,1)S(1)}, u32[]{:S(2)}, u32[]{:S(2)}) collective-permute-start(bf16[1,128,256]{2,1,0:T(8,128)(2,1)S(1)} %get-tuple-element.26), channel_id=1, source_target_pairs={{0,256},{8,264},{16,272},{24,280},{32,288},{40,296},{48,304},{56,3... | collective-permute-start | bytes 196616 | tf_op jit(solution)/shard_map/ppermute | solution.py:40
  100.7 2.6 %collective-permute-done.4 = bf16[1,128,256]{2,1,0:T(8,128)(2,1)S(1)} collective-permute-done((bf16[1,128,256]{2,1,0:T(8,128)(2,1)S(1)}, bf16[1,128,256]{2,1,0:T(8,128)(2,1)S(1)}, u32[]{:S(2)}, u32[]{:S(2)}) %collective-permute-start.4) | collective-permute-done | bytes 65568 | tf_op jit(solution)/shard_map/ppermute | solution.py:40
  103.3 2.5 collective-permute-start.5
  105.8 5.9 %collective-permute-done.5 = bf16[2,128,256]{2,1,0:T(8,128)(2,1)S(1)} collective-permute-done((bf16[2,128,256]{2,1,0:T(8,128)(2,1)S(1)}, bf16[2,128,256]{2,1,0:T(8,128)(2,1)S(1)}, u32[]{:S(2)}, u32[]{:S(2)}) %collective-permute-start.5) | collective-permute-done | bytes 131104 | tf_op jit(solution)/shard_map/ppermute | solution.py:40
  111.7 2.5 collective-permute-start.6
  114.2 5.8 %collective-permute-done.6 = bf16[4,128,256]{2,1,0:T(8,128)(2,1)S(1)} collective-permute-done((bf16[4,128,256]{2,1,0:T(8,128)(2,1)S(1)}, bf16[4,128,256]{2,1,0:T(8,128)(2,1)S(1)}, u32[]{:S(2)}, u32[]{:S(2)}) %collective-permute-start.6) | collective-permute-done | bytes 262176 | tf_op jit(solution)/shard_map/ppermute | solution.py:40
  120.1 0.8 copy-done.14
  120.9 1.0 copy-done.15
  121.9 3.0 %shard_map.79 = f32[3,8,128]{2,1,0:T(8,128)S(1)} custom-call(s32[5]{0:T(128)S(1)} %get-tuple-element.69.sc_ref, bf16[8,128,256]{2,1,0:T(8,128)(2,1)S(1)} %copy-done.15, bf16[8,128,256]{2,1,0:T(8,128)(2,1)} %all-to-all-done.2.kv_ref), custom_call_target="tpu_custom_call" | custom-call | flops 536870912 | bytes 1048576 | tf_op jit(solution)/shard_map/pallas_call | solution.py:235
  124.9 9.1 %all_to_all.45.stats_ref = f32[8,3,8,128]{3,2,1,0:T(8,128)S(1)} all-to-all(f32[8,3,8,128]{3,2,1,0:T(8,128)S(1)} %broadcast_in_dim.22), channel_id=1, replica_groups={{0,8,16,24,256,264,272,280},{32,40,48,56,288,296,304,312},{64,72,80,88,..., dimensions={0} | all-to-all | bytes 196608 | tf_op jit(solution)/shard_map/all_to_all | solution.py:32
  134.0 4.1 %shard_map.80 = (bf16[2,4,2,120,128]{4,3,2,1,0:T(8,128)(2,1)S(1)}, bf16[8,128,256]{2,1,0:T(8,128)(2,1)S(1)}) custom-call(s32[5]{0:T(128)S(1)} %get-tuple-element.69.sc_ref, bf16[8,128,256]{2,1,0:T(8,128)(2,1)S(1)} %copy-done.15, bf16[8,128,256]{2,1,0:T(8,128)(2,1)} %all-to-all-done.2.kv_ref, f32[8,3,8,128]{3,2,1,0:T(8,128)S(1)} %all_to_all.45.stats_ref), custom_call_target="tpu_custom_call" | custom-call | flops 1610612736 | bytes 1048576 | tf_op jit(solution)/shard_map/pallas_call | solution.py:245
  138.1 0.8 copy-done.5
  138.9 0.8 copy-done.7
  139.7 7.1 %all-to-all-start.4 = ((bf16[8,128,256]{2,1,0:T(8,128)(2,1)}), bf16[8,128,256]{2,1,0:T(8,128)(2,1)}, u32[]{:S(2)}, u32[]{:S(2)}) async-start(bf16[8,128,256]{2,1,0:T(8,128)(2,1)} %copy-done.5), calls=%async_computation.4 | async-start | bytes 1048576 | tf_op jit(solution)/shard_map/all_to_all | solution.py:44
  146.8 1.7 slice_bitcast_fusion
  148.5 3.3 %collective-permute-start.7 = (bf16[4,2,120,128]{3,2,1,0:T(8,128)(2,1)}, bf16[4,2,120,128]{3,2,1,0:T(8,128)(2,1)}, u32[]{:S(2)}, u32[]{:S(2)}) collective-permute-start(bf16[4,2,120,128]{3,2,1,0:T(8,128)(2,1)} %slice_bitcast_fusion), channel_id=1, source_target_pairs={{0,256},{8,264},{16,272},{24,280},{32,288},{40,296},{48,304},{56,3... | collective-permute-start | bytes 737288 | tf_op jit(solution)/shard_map/ppermute | solution.py:40
  151.7 8.5 %all-to-all-done.4.dkv_ref = bf16[8,128,256]{2,1,0:T(8,128)(2,1)} async-done(((bf16[8,128,256]{2,1,0:T(8,128)(2,1)}), bf16[8,128,256]{2,1,0:T(8,128)(2,1)}, u32[]{:S(2)}, u32[]{:S(2)}) %all-to-all-start.4) | async-done | bytes 524320 | tf_op jit(solution)/shard_map/all_to_all | solution.py:44
  160.3 1.2 slice.43
  162.2 1.1 fusion
  163.3 9.0 %all_to_all.46.od_ref = bf16[4,2,120,128]{3,2,1,0:T(8,128)(2,1)S(1)} all-to-all(bf16[4,2,120,128]{3,2,1,0:T(8,128)(2,1)S(1)} %fusion), channel_id=1, replica_groups={{0,8,16,24},{32,40,48,56},{64,72,80,88},{96,104,112,120},{128,136,144,1..., dimensions={0} | all-to-all | bytes 491520 | tf_op jit(solution)/shard_map/all_to_all | solution.py:36
  172.3 2.0 shard_map.81
  174.3 0.8 copy-done.6
  175.7 4.8 %all-to-all-start.6 = ((bf16[8,2,128,128]{3,2,1,0:T(8,128)(2,1)}), bf16[8,2,128,128]{3,2,1,0:T(8,128)(2,1)S(1)}, u32[]{:S(2)}, u32[]{:S(2)}) async-start(bf16[8,2,128,128]{3,2,1,0:T(8,128)(2,1)} %bitcast.31), calls=%async_computation.6 | async-start | bytes 1048576 | tf_op jit(solution)/shard_map/all_to_all | solution.py:472
  180.6 1.0 copy-done.2
  181.6 0.9 copy-done.13
  182.5 1.8 shard_map.83
  184.2 12.9 %all-to-all-done.6.parts_ref = bf16[8,2,128,128]{3,2,1,0:T(8,128)(2,1)S(1)} async-done(((bf16[8,2,128,128]{3,2,1,0:T(8,128)(2,1)}), bf16[8,2,128,128]{3,2,1,0:T(8,128)(2,1)S(1)}, u32[]{:S(2)}, u32[]{:S(2)}) %all-to-all-start.6) | async-done | bytes 524320 | tf_op jit(solution)/shard_map/all_to_all | solution.py:472
  197.1 6.7 %all-to-all-start.7 = ((bf16[8,256,384]{2,1,0:T(8,128)(2,1)}), bf16[8,256,384]{2,1,0:T(8,128)(2,1)}, u32[]{:S(2)}, u32[]{:S(2)}) async-start(bf16[8,256,384]{2,1,0:T(8,128)(2,1)} %shard_map.83), calls=%async_computation.7 | async-start | bytes 3145728 | tf_op jit(solution)/shard_map/all_to_all | solution.py:32
  204.0 3.4 %collective-permute-start.8 = (bf16[2,32,120]{2,1,0:T(8,128)(2,1)S(1)}, bf16[2,32,120]{2,1,0:T(8,128)(2,1)S(1)}, u32[]{:S(2)}, u32[]{:S(2)}) collective-permute-start(bf16[2,32,120]{2,1,0:T(8,128)(2,1)S(1)} %get-tuple-element.65), channel_id=1, source_target_pairs={{0,8},{8,16},{16,24},{24,32},{32,40},{40,48},{48,56},{56,64},{64,7... | collective-permute-start | bytes 46088 | tf_op jit(solution)/shard_map/ppermute | solution.py:156
  207.4 6.7 %collective-permute-start.9 = (bf16[2,32,120]{2,1,0:T(8,128)(2,1)S(1)}, bf16[2,32,120]{2,1,0:T(8,128)(2,1)S(1)}, u32[]{:S(2)}, u32[]{:S(2)}) collective-permute-start(bf16[2,32,120]{2,1,0:T(8,128)(2,1)S(1)} %get-tuple-element.64), channel_id=1, source_target_pairs={{8,0},{16,8},{24,16},{32,24},{40,32},{48,40},{56,48},{64,56},{72,6... | collective-permute-start | bytes 46088 | tf_op jit(solution)/shard_map/ppermute | solution.py:157
  214.1 9.0 %collective-permute-done.8 = bf16[2,32,120]{2,1,0:T(8,128)(2,1)S(1)} collective-permute-done((bf16[2,32,120]{2,1,0:T(8,128)(2,1)S(1)}, bf16[2,32,120]{2,1,0:T(8,128)(2,1)S(1)}, u32[]{:S(2)}, u32[]{:S(2)}) %collective-permute-start.8) | collective-permute-done | bytes 15392 | tf_op jit(solution)/shard_map/ppermute | solution.py:156
  223.2 1.9 collective-permute-start.10
  225.1 4.6 %collective-permute-done.10 = bf16[2,192,120]{2,1,0:T(8,128)(2,1)S(1)} collective-permute-done((bf16[2,192,120]{2,1,0:T(8,128)(2,1)S(1)}, bf16[2,192,120]{2,1,0:T(8,128)(2,1)S(1)}, u32[]{:S(2)}, u32[]{:S(2)}) %collective-permute-start.10) | collective-permute-done | bytes 92192 | tf_op jit(solution)/shard_map/ppermute | solution.py:40
  229.7 2.3 reduce_sum.21
  232.1 1.2 slice.44
  233.9 3.4 %all-to-all-start.8 = ((bf16[8,32,384]{2,1,0:T(8,128)(2,1)}), bf16[8,32,384]{2,1,0:T(8,128)(2,1)S(1)}, u32[]{:S(2)}, u32[]{:S(2)}) async-start(bf16[8,32,384]{2,1,0:T(8,128)(2,1)} %bitcast.20), calls=%async_computation.8 | async-start | bytes 393216 | tf_op jit(solution)/shard_map/all_to_all | solution.py:44
  237.4 3.6 %shard_map.84 = (f32[2,128,120]{2,1,0:T(8,128)S(1)}, bf16[2,128,120]{2,1,0:T(8,128)(2,1)S(1)}) custom-call(s32[6]{0:T(128)S(1)} %broadcast_add_fusion.1.sc_ref, bf16[2,2,192,120]{3,2,1,0:T(8,128)(2,1)S(1)} %pad_maximum_fusion.2.x_ref, bf16[4,8,2,120,120]{4,3,2,1,0:T(8,128)(2,1)S(1)} %all-to-all-done.1.w_ref), custom_call_target="tpu_custom_call" | custom-call | flops 471859200 | bytes 1048576 | tf_op jit(solution)/shard_map/pallas_call | solution.py:139
  241.0 1.9 collective-permute-start.11
  242.9 0.7 copy.50
  243.7 3.5 %collective-permute-done.11 = bf16[2,128,120]{2,1,0:T(8,128)(2,1)S(1)} collective-permute-done((bf16[2,128,120]{2,1,0:T(8,128)(2,1)S(1)}, bf16[2,128,120]{2,1,0:T(8,128)(2,1)S(1)}, u32[]{:S(2)}, u32[]{:S(2)}) %collective-permute-start.11) | collective-permute-done | bytes 61472 | tf_op jit(solution)/shard_map/ppermute | solution.py:40
  247.2 0.7 copy.48
  247.9 0.8 convert_reduce_fusion
  (61 shorter events, 4.4 us)
Async XLA Ops:
  0.6 12.0 %copy-start.17 = (bf16[128,240]{0,1:T(8,128)(2,1)S(1)}, bf16[128,240]{0,1:T(8,128)(2,1)}, u32[]{:S(2)}) copy-start(bf16[128,240]{0,1:T(8,128)(2,1)} %param.5) | copy-start | bytes 184324
  2.3 27.1 %all-to-all-start = ((bf16[8,2,120,120]{3,2,1,0:T(8,128)(2,1)}), bf16[8,2,120,120]{3,2,1,0:T(8,128)(2,1)S(1)}, u32[]{:S(2)}, u32[]{:S(2)}) async-start(bf16[8,2,120,120]{3,2,1,0:T(8,128)(2,1)} %broadcast_in_dim.9), calls=%async_computation | async-start | bytes 983040 | tf_op jit(solution)/shard_map/all_to_all | solution.py:44
  12.8 10.1 %collective-permute-start = (bf16[2,32,120]{2,1,0:T(8,128)(2,1)S(1)}, bf16[2,32,120]{2,1,0:T(8,128)(2,1)S(1)}, u32[]{:S(2)}, u32[]{:S(2)}) collective-permute-start(bf16[2,32,120]{2,1,0:T(8,128)(2,1)S(1)} %get-tuple-element.66), channel_id=1, source_target_pairs={{0,8},{8,16},{16,24},{24,32},{32,40},{40,48},{48,56},{56,64},{64,7... | collective-permute-start | bytes 46088 | tf_op jit(solution)/shard_map/ppermute | solution.py:156
  16.2 8.1 %collective-permute-start.1 = (bf16[2,32,120]{2,1,0:T(8,128)(2,1)S(1)}, bf16[2,32,120]{2,1,0:T(8,128)(2,1)S(1)}, u32[]{:S(2)}, u32[]{:S(2)}) collective-permute-start(bf16[2,32,120]{2,1,0:T(8,128)(2,1)S(1)} %get-tuple-element.67), channel_id=1, source_target_pairs={{8,0},{16,8},{24,16},{32,24},{40,32},{48,40},{56,48},{64,56},{72,6... | collective-permute-start | bytes 46088 | tf_op jit(solution)/shard_map/ppermute | solution.py:157
  25.0 6.1 %copy-start.16 = (bf16[1,2,192,120]{3,2,1,0:T(8,128)(2,1)}, bf16[1,2,192,120]{3,2,1,0:T(8,128)(2,1)S(1)}, u32[]{:S(2)}) copy-start(bf16[1,2,192,120]{3,2,1,0:T(8,128)(2,1)S(1)} %get-tuple-element.62) | copy-start | bytes 276484
  31.1 4.4 %copy-start.19 = (s32[4]{0:T(128)S(1)}, s32[4]{0:T(128)}, u32[]{:S(2)}) copy-start(s32[4]{0:T(128)} %param.8) | copy-start | bytes 52
  31.1 4.6 %copy-start.18 = (bf16[128,120]{0,1:T(8,128)(2,1)S(1)}, bf16[128,120]{0,1:T(8,128)(2,1)}, u32[]{:S(2)}) copy-start(bf16[128,120]{0,1:T(8,128)(2,1)} %param.9) | copy-start | bytes 92164
  31.1 29.5 %all-to-all-start.1 = ((bf16[4,8,2,120,120]{4,3,2,1,0:T(8,128)(2,1)}), bf16[4,8,2,120,120]{4,3,2,1,0:T(8,128)(2,1)S(1)}, u32[]{:S(2)}, u32[]{:S(2)}) async-start(bf16[4,8,2,120,120]{4,3,2,1,0:T(8,128)(2,1)} %broadcast_in_dim.10), calls=%async_computation.1 | async-start | bytes 3932160 | tf_op jit(solution)/shard_map/all_to_all | solution.py:36
  38.2 6.7 %collective-permute-start.2 = (bf16[2,192,120]{2,1,0:T(8,128)(2,1)}, bf16[2,192,120]{2,1,0:T(8,128)(2,1)S(1)}, u32[]{:S(2)}, u32[]{:S(2)}) collective-permute-start(bf16[2,192,120]{2,1,0:T(8,128)(2,1)} %get-tuple-element.63), channel_id=1, source_target_pairs={{0,256},{8,264},{16,272},{24,280},{32,288},{40,296},{48,304},{56,3... | collective-permute-start | bytes 276488 | tf_op jit(solution)/shard_map/ppermute | solution.py:40
  60.6 0.9 copy-start.3
  63.7 6.2 %collective-permute-start.3 = (bf16[2,128,120]{2,1,0:T(8,128)(2,1)S(1)}, bf16[2,128,120]{2,1,0:T(8,128)(2,1)S(1)}, u32[]{:S(2)}, u32[]{:S(2)}) collective-permute-start(bf16[2,128,120]{2,1,0:T(8,128)(2,1)S(1)} %get-tuple-element.23), channel_id=1, source_target_pairs={{0,256},{8,264},{16,272},{24,280},{32,288},{40,296},{48,304},{56,3... | collective-permute-start | bytes 184328 | tf_op jit(solution)/shard_map/ppermute | solution.py:40
  70.0 0.6 copy-start.8
  89.0 0.8 copy-start
  89.8 0.8 copy-start.4
  90.6 0.7 copy-start.10
  91.3 29.6 %all-to-all-start.2 = ((bf16[8,128,256]{2,1,0:T(8,128)(2,1)}), bf16[8,128,256]{2,1,0:T(8,128)(2,1)}, u32[]{:S(2)}, u32[]{:S(2)}) async-start(bf16[8,128,256]{2,1,0:T(8,128)(2,1)} %copy-done.4), calls=%async_computation.2 | async-start | bytes 1048576 | tf_op jit(solution)/shard_map/all_to_all | solution.py:44
  97.1 6.1 %collective-permute-start.4 = (bf16[1,128,256]{2,1,0:T(8,128)(2,1)S(1)}, bf16[1,128,256]{2,1,0:T(8,128)(2,1)S(1)}, u32[]{:S(2)}, u32[]{:S(2)}) collective-permute-start(bf16[1,128,256]{2,1,0:T(8,128)(2,1)S(1)} %get-tuple-element.26), channel_id=1, source_target_pairs={{0,256},{8,264},{16,272},{24,280},{32,288},{40,296},{48,304},{56,3... | collective-permute-start | bytes 196616 | tf_op jit(solution)/shard_map/ppermute | solution.py:40
  103.3 8.4 %collective-permute-start.5 = (bf16[2,128,256]{2,1,0:T(8,128)(2,1)S(1)}, bf16[2,128,256]{2,1,0:T(8,128)(2,1)S(1)}, u32[]{:S(2)}, u32[]{:S(2)}) collective-permute-start(bf16[2,128,256]{2,1,0:T(8,128)(2,1)S(1)} %pad_maximum_fusion.3), channel_id=1, source_target_pairs={{0,16},{8,24},{16,0},{24,8},{32,48},{40,56},{48,32},{56,40},{64,80... | collective-permute-start | bytes 393224 | tf_op jit(solution)/shard_map/ppermute | solution.py:40
  111.7 8.4 %collective-permute-start.6 = (bf16[4,128,256]{2,1,0:T(8,128)(2,1)S(1)}, bf16[4,128,256]{2,1,0:T(8,128)(2,1)S(1)}, u32[]{:S(2)}, u32[]{:S(2)}) collective-permute-start(bf16[4,128,256]{2,1,0:T(8,128)(2,1)S(1)} %pad_maximum_fusion), channel_id=1, source_target_pairs={{0,8},{8,0},{16,24},{24,16},{32,40},{40,32},{48,56},{56,48},{64,72... | collective-permute-start | bytes 786440 | tf_op jit(solution)/shard_map/ppermute | solution.py:40
  120.1 0.8 copy-start.14
  120.9 1.0 copy-start.15
  138.0 0.8 copy-start.5
  138.9 0.8 copy-start.7
  139.7 20.6 %all-to-all-start.4 = ((bf16[8,128,256]{2,1,0:T(8,128)(2,1)}), bf16[8,128,256]{2,1,0:T(8,128)(2,1)}, u32[]{:S(2)}, u32[]{:S(2)}) async-start(bf16[8,128,256]{2,1,0:T(8,128)(2,1)} %copy-done.5), calls=%async_computation.4 | async-start | bytes 1048576 | tf_op jit(solution)/shard_map/all_to_all | solution.py:44
  148.5 13.7 %collective-permute-start.7 = (bf16[4,2,120,128]{3,2,1,0:T(8,128)(2,1)}, bf16[4,2,120,128]{3,2,1,0:T(8,128)(2,1)}, u32[]{:S(2)}, u32[]{:S(2)}) collective-permute-start(bf16[4,2,120,128]{3,2,1,0:T(8,128)(2,1)} %slice_bitcast_fusion), channel_id=1, source_target_pairs={{0,256},{8,264},{16,272},{24,280},{32,288},{40,296},{48,304},{56,3... | collective-permute-start | bytes 737288 | tf_op jit(solution)/shard_map/ppermute | solution.py:40
  160.3 12.0 %copy-start.1 = (bf16[16,120,128]{2,1,0:T(8,128)(2,1)S(1)}, bf16[16,120,128]{2,1,0:T(8,128)(2,1)}, u32[]{:S(2)}) copy-start(bf16[16,120,128]{2,1,0:T(8,128)(2,1)} %copy-done) | copy-start | bytes 1474564
  174.3 0.8 copy-start.6
  175.1 0.6 copy-start.12
  175.7 21.4 %all-to-all-start.6 = ((bf16[8,2,128,128]{3,2,1,0:T(8,128)(2,1)}), bf16[8,2,128,128]{3,2,1,0:T(8,128)(2,1)S(1)}, u32[]{:S(2)}, u32[]{:S(2)}) async-start(bf16[8,2,128,128]{3,2,1,0:T(8,128)(2,1)} %bitcast.31), calls=%async_computation.6 | async-start | bytes 1048576 | tf_op jit(solution)/shard_map/all_to_all | solution.py:472
  180.5 1.0 copy-start.2
  181.6 0.9 copy-start.13
  184.2 19.6 %copy-start.9 = (f32[2,120,128]{2,1,0:T(8,128)S(1)}, f32[2,120,128]{2,1,0:T(8,128)}, u32[]{:S(2)}) copy-start(f32[2,120,128]{2,1,0:T(8,128)} %copy-done.8) | copy-start | bytes 368644
  184.2 19.6 %copy-start.11 = (f32[2,120,128]{2,1,0:T(8,128)S(1)}, f32[2,120,128]{2,1,0:T(8,128)}, u32[]{:S(2)}) copy-start(f32[2,120,128]{2,1,0:T(8,128)} %copy-done.10) | copy-start | bytes 368644
  197.1 32.6 %all-to-all-start.7 = ((bf16[8,256,384]{2,1,0:T(8,128)(2,1)}), bf16[8,256,384]{2,1,0:T(8,128)(2,1)}, u32[]{:S(2)}, u32[]{:S(2)}) async-start(bf16[8,256,384]{2,1,0:T(8,128)(2,1)} %shard_map.83), calls=%async_computation.7 | async-start | bytes 3145728 | tf_op jit(solution)/shard_map/all_to_all | solution.py:32
  204.0 19.1 %collective-permute-start.8 = (bf16[2,32,120]{2,1,0:T(8,128)(2,1)S(1)}, bf16[2,32,120]{2,1,0:T(8,128)(2,1)S(1)}, u32[]{:S(2)}, u32[]{:S(2)}) collective-permute-start(bf16[2,32,120]{2,1,0:T(8,128)(2,1)S(1)} %get-tuple-element.65), channel_id=1, source_target_pairs={{0,8},{8,16},{16,24},{24,32},{32,40},{40,48},{48,56},{56,64},{64,7... | collective-permute-start | bytes 46088 | tf_op jit(solution)/shard_map/ppermute | solution.py:156
  207.4 15.7 %collective-permute-start.9 = (bf16[2,32,120]{2,1,0:T(8,128)(2,1)S(1)}, bf16[2,32,120]{2,1,0:T(8,128)(2,1)S(1)}, u32[]{:S(2)}, u32[]{:S(2)}) collective-permute-start(bf16[2,32,120]{2,1,0:T(8,128)(2,1)S(1)} %get-tuple-element.64), channel_id=1, source_target_pairs={{8,0},{16,8},{24,16},{32,24},{40,32},{48,40},{56,48},{64,56},{72,6... | collective-permute-start | bytes 46088 | tf_op jit(solution)/shard_map/ppermute | solution.py:157
  223.2 6.5 %collective-permute-start.10 = (bf16[2,192,120]{2,1,0:T(8,128)(2,1)S(1)}, bf16[2,192,120]{2,1,0:T(8,128)(2,1)S(1)}, u32[]{:S(2)}, u32[]{:S(2)}) collective-permute-start(bf16[2,192,120]{2,1,0:T(8,128)(2,1)S(1)} %constant_dynamic-update-slice_fusion.4), channel_id=1, source_target_pairs={{0,256},{8,264},{16,272},{24,280},{32,288},{40,296},{48,304},{56,3... | collective-permute-start | bytes 276488 | tf_op jit(solution)/shard_map/ppermute | solution.py:40
  233.9 14.0 %all-to-all-start.8 = ((bf16[8,32,384]{2,1,0:T(8,128)(2,1)}), bf16[8,32,384]{2,1,0:T(8,128)(2,1)S(1)}, u32[]{:S(2)}, u32[]{:S(2)}) async-start(bf16[8,32,384]{2,1,0:T(8,128)(2,1)} %bitcast.20), calls=%async_computation.8 | async-start | bytes 393216 | tf_op jit(solution)/shard_map/all_to_all | solution.py:44
  241.0 6.2 %collective-permute-start.11 = (bf16[2,128,120]{2,1,0:T(8,128)(2,1)S(1)}, bf16[2,128,120]{2,1,0:T(8,128)(2,1)S(1)}, u32[]{:S(2)}, u32[]{:S(2)}) collective-permute-start(bf16[2,128,120]{2,1,0:T(8,128)(2,1)S(1)} %get-tuple-element.40), channel_id=1, source_target_pairs={{0,256},{8,264},{16,272},{24,280},{32,288},{40,296},{48,304},{56,3... | collective-permute-start | bytes 184328 | tf_op jit(solution)/shard_map/ppermute | solution.py:40

commit v6 on v5

--- a/solution.py
+++ b/solution.py
@@ -63,10 +63,6 @@
     return array
 
 
-def nothing(array):
-    return (0 * array[(0,) * array.ndim].astype(F32)).astype(jnp.int32)
-
-
 def vmem_call(body, out_shape, scratch=(), scalars=0, inputs=0, flops=0):
     return pl.pallas_call(
         body,
@@ -98,29 +94,31 @@
 def conv_body(forward, sc_ref, x_ref, w_ref, own_ref, other_ref):
     ends = [sc_ref[2 + u] for u in range(4)]
     first = TAPS * (sc_ref[0] if forward else 1 - sc_ref[0])
-    row = lax.broadcasted_iota(jnp.int32, (ROWS, HD), 0)
+    row = lax.broadcasted_iota(jnp.int32, (ROWS, LANES), 0)
     for b in range(2):
         shard = sc_ref[1] if b == 0 else sc_ref[1] ^ 32
         pos = shard * ROWS + row
         low, high = bounds_of(pos, ends)
         source = pos + (first - HALF)
         spans = [
-            x_ref[b, g, pl.ds(pl.multiple_of(first, TAPS), SPAN)].astype(F32) for g in range(2)
+            x_ref[b, pl.ds(pl.multiple_of(g * PADDED + first, TAPS), SPAN)].astype(F32)
+            for g in range(2)
         ]
-        totals = [jnp.zeros((ROWS, HD), F32) for g in range(2)]
+        totals = [jnp.zeros((ROWS, LANES), F32) for g in range(2)]
         for rest in range(8):
             rolled = [pltpu.roll(e, SPAN - rest, 0) if rest else e for e in spans]
             for start in range(0, TAPS + 1, 8):
                 tap = start + rest if forward else TAPS - start - rest
                 if not 0 <= tap < TAPS:
                     continue
-                at = source + (start + rest)
-                keep = (at >= low) & (at < high)
+                key = source + (start + rest)
+                keep = (key >= low) & (key < high)
                 for g in range(2):
+                    at = (tap // 4 * 2 + g) * LANES
                     piece = jnp.where(keep, rolled[g][start : start + ROWS], 0.0).astype(BF)
                     totals[g] += lax.dot_general(
                         piece,
-                        w_ref[tap % 4, tap // 4, g],
+                        w_ref[tap % 4, at : at + LANES],
                         (((1,), (0 if forward else 1,)), ((), ())),
                         preferred_element_type=F32,
                     )
@@ -131,6 +129,35 @@
                 other_ref[g] = totals[g].astype(BF)
 
 
+def taps_body(w_ref, out_ref):
+    out_ref[0] = jnp.zeros((2 * LANES, LANES), BF)
+    for g in range(2):
+        out_ref[0, g * LANES : g * LANES + HD, :HD] = w_ref[g]
+    for i in range(1, 8):
+        out_ref[i] = out_ref[0]
+
+
+def taps_sent(weight):
+    return vmem_call(
+        taps_body, jax.ShapeDtypeStruct((8, 2 * LANES, LANES), BF), inputs=1
+    )(weight)
+
+
+def joined_body(w_ref, pair_ref, out_ref):
+    for i in range(4):
+        for z in range(8):
+            out_ref[i, z * 2 * LANES : (z + 1) * 2 * LANES] = w_ref[z]
+        for b in range(2):
+            start = 16 * LANES + b * ROWS
+            out_ref[i, start : start + ROWS] = pair_ref[b, 2 * PADDED :]
+
+
+def joined(taps, pair):
+    return vmem_call(
+        joined_body, jax.ShapeDtypeStruct((4, 16 * LANES + 2 * ROWS, LANES), BF), inputs=2
+    )(taps, pair)
+
+
 def paired(padded):
     return jnp.stack([padded, swap(padded, 32)])
 
@@ -139,8 +166,8 @@
     own, other = vmem_call(
         functools.partial(conv_body, forward),
         (
-            jax.ShapeDtypeStruct((2, ROWS, HD), F32),
-            jax.ShapeDtypeStruct((2, ROWS, HD), BF),
+            jax.ShapeDtypeStruct((2, ROWS, LANES), F32),
+            jax.ShapeDtypeStruct((2, ROWS, LANES), BF),
         ),
         scalars=1,
         inputs=2,
@@ -166,19 +193,26 @@
 CONTRACT = (((1,), (1,)), ((), ()))
 
 
-def scored(c, q_ref, kv_ref):
+def upstream_rows(sc_ref, f_ref, d_ref):
+    for i, e in enumerate(SLOTS):
+        row = 16 * LANES + e // 4 * ROWS
+        d_ref[i * ROWS : (i + 1) * ROWS] = f_ref[(sc_ref[0] % 4) ^ (e % 4), row : row + ROWS]
+
+
+def scored(c, q_ref, kv_ref, d_ref):
     keys = kv_ref[:, :, :LANES].reshape(ALL, LANES)
-    values = kv_ref[:, :, LANES : LANES + HD].reshape(ALL, HD)
-    q = q_ref[c * N : (c + 1) * N, :, :LANES].reshape(CHUNK, LANES)
-    d = q_ref[c * N : (c + 1) * N, :, LANES : LANES + HD].reshape(CHUNK, HD)
+    values = kv_ref[:, :, LANES:].reshape(ALL, LANES)
+    q = q_ref[c * N : (c + 1) * N].reshape(CHUNK, LANES)
+    d = d_ref[c * CHUNK : (c + 1) * CHUNK]
     scores = lax.dot_general(keys, q, CONTRACT, preferred_element_type=F32)
     dprobs = lax.dot_general(values, d, CONTRACT, preferred_element_type=F32)
     return keys, values, q, d, scores * SCALE2, dprobs
 
 
-def stats_body(sc_ref, q_ref, kv_ref, out_ref):
+def stats_body(sc_ref, q_ref, kv_ref, f_ref, out_ref, d_ref):
+    upstream_rows(sc_ref, f_ref, d_ref)
     for c in range(ALL // CHUNK):
-        _, _, _, _, scores, dprobs = scored(c, q_ref, kv_ref)
+        _, _, _, _, scores, dprobs = scored(c, q_ref, kv_ref, d_ref)
         peak = jnp.max(scores, axis=0, keepdims=True)
         weight = jnp.exp2(scores - peak)
         total = jnp.sum(weight, axis=0, keepdims=True)
@@ -190,7 +224,10 @@
                 out_ref[j, shard] = value[:, columns]
 
 
-def grads_body(sc_ref, q_ref, kv_ref, stats_ref, od_ref, dkv_ref, dk_ref, dv_ref):
+def grads_body(
+    sc_ref, q_ref, kv_ref, f_ref, stats_ref, od_ref, dkv_ref, d_ref, dk_ref, dv_ref
+):
+    upstream_rows(sc_ref, f_ref, d_ref)
     for c in range(ALL // CHUNK):
         peaks, totals, alongs = (
             jnp.concatenate(
@@ -204,7 +241,7 @@
         total = jnp.sum(totals * factor, axis=0)
         delta = jnp.sum(alongs * factor, axis=0) / total
         lse = top + jnp.log2(total)
-        keys, values, q, d, scores, dprobs = scored(c, q_ref, kv_ref)
+        keys, values, q, d, scores, dprobs = scored(c, q_ref, kv_ref, d_ref)
         probs = jnp.exp2(scores - lse)
         dscores = (probs * (dprobs - delta)).astype(BF)
         probs = probs.astype(BF)
@@ -220,42 +257,42 @@
         out_t = lax.dot_general(values, probs, inner, preferred_element_type=F32)
         dq_t = lax.dot_general(keys, dscores, inner, preferred_element_type=F32) * SCALE
         for i in range(N):
-            e = SLOTS[c * N + i]
-            at = (sc_ref[0] % 4) ^ (e % 4)
-            od_ref[e // 4, at, 0] = out_t[:, i * ROWS : (i + 1) * ROWS].astype(BF)
-            od_ref[e // 4, at, 1] = dq_t[:HD, i * ROWS : (i + 1) * ROWS].astype(BF)
+            at = sc_ref[0] ^ SLOTS[c * N + i]
+            od_ref[at, 0] = out_t[:HD, i * ROWS : (i + 1) * ROWS].astype(BF)
+            od_ref[at, 1] = dq_t[:HD, i * ROWS : (i + 1) * ROWS].astype(BF)
     for i in range(8):
         piece = slice(i * ROWS, (i + 1) * ROWS)
         dkv_ref[i, :, :LANES] = (dk_ref[piece] * SCALE).astype(BF)
-        dkv_ref[i, :, LANES : LANES + HD] = dv_ref[piece].astype(BF)
-        dkv_ref[i, :, LANES + HD :] = jnp.zeros((ROWS, LANES - HD), BF)
-
-
-def attention_stats(scalars, queries, keys):
+        dkv_ref[i, :, LANES:] = dv_ref[piece].astype(BF)
+
+
+def attention_stats(scalars, queries, keys, gathered):
     return vmem_call(
         stats_body,
         jax.ShapeDtypeStruct((3, 8, ROWS), F32),
+        scratch=[pltpu.VMEM((ALL, LANES), BF)],
         scalars=1,
-        inputs=2,
+        inputs=3,
         flops=2 * 2 * ALL * ALL * LANES,
-    )(scalars, queries, keys)
-
-
-def attention_grads(scalars, queries, keys, stats):
+    )(scalars, queries, keys, gathered)
+
+
+def attention_grads(scalars, queries, keys, gathered, stats):
     return vmem_call(
         grads_body,
         (
-            jax.ShapeDtypeStruct((2, 4, 2, HD, ROWS), BF),
+            jax.ShapeDtypeStruct((8, 2, HD, ROWS), BF),
             jax.ShapeDtypeStruct((8, ROWS, 2 * LANES), BF),
         ),
         scratch=[
+            pltpu.VMEM((ALL, LANES), BF),
             pltpu.VMEM((ALL, LANES), F32),
-            pltpu.VMEM((ALL, HD), F32),
+            pltpu.VMEM((ALL, LANES), F32),
         ],
         scalars=1,
-        inputs=3,
+        inputs=4,
         flops=6 * 2 * ALL * ALL * LANES,
-    )(scalars, queries, keys, stats)
+    )(scalars, queries, keys, gathered, stats)
 
 
 GROUPS = 16
@@ -273,9 +310,9 @@
     for g in range(2):
         conv = own_ref[g] + other_ref[g].astype(F32)
         activated, slope = gelu_parts(conv)
-        hidden = (frames_ref[g].astype(F32) + activated).T
+        hidden = (frames_ref[g].astype(F32) + activated).T[:HD]
         hidden_ref[g] = hidden
-        slope_ref[g] = slope.T
+        slope_ref[g] = slope.T[:HD]
         sent_ref[g] = hidden.astype(BF)
 
 
@@ -287,7 +324,7 @@
 
 
 def project_body(
-    sc_ref, all_ref, hidden_ref, w_ref, up_ref, kv_ref, q_ref, normed_ref, unit_ref, inv_ref
+    sc_ref, all_ref, hidden_ref, w_ref, kv_ref, q_ref, normed_ref, unit_ref, inv_ref
 ):
     total = jnp.zeros((HD, ROWS), F32)
     square = jnp.zeros((HD, ROWS), F32)
@@ -318,10 +355,8 @@
     for u in range(3):
         seg += jnp.where(pos >= sc_ref[1 + u], 1, 0)
     nil = jnp.zeros((ROWS, LANES - HD), BF)
-    q_ref[0, :, :HD] = projected[:, :HD]
-    q_ref[0, :, HD:LANES] = jnp.where(seg == lane, 1.0, 0.0).astype(BF)
-    q_ref[0, :, LANES : LANES + HD] = up_ref[...]
-    q_ref[0, :, LANES + HD :] = nil
+    q_ref[:, :HD] = projected[:, :HD]
+    q_ref[:, HD:] = jnp.where(seg == lane, 1.0, 0.0).astype(BF)
     k_mark = jnp.where(seg == lane, 0.0, FAR).astype(BF)
     for i in range(8):
         kv_ref[i, :, :HD] = projected[:, HD : 2 * HD]
@@ -330,25 +365,25 @@
         kv_ref[i, :, LANES + HD :] = nil
 
 
-def project(scalars, all_t, hidden_t, w_qkv, grad_out):
+def project(scalars, all_t, hidden_t, w_qkv):
     return vmem_call(
         project_body,
         (
             jax.ShapeDtypeStruct((8, ROWS, 2 * LANES), BF),
-            jax.ShapeDtypeStruct((1, ROWS, 2 * LANES), BF),
+            jax.ShapeDtypeStruct((ROWS, LANES), BF),
             jax.ShapeDtypeStruct((GROUPS, HD, ROWS), BF),
             jax.ShapeDtypeStruct((2, HD, ROWS), F32),
             jax.ShapeDtypeStruct((1, ROWS), F32),
         ),
         scalars=1,
-        inputs=4,
+        inputs=3,
         flops=2 * ROWS * WIDTH * 3 * HD,
-    )(scalars, all_t, hidden_t, w_qkv, grad_out)
+    )(scalars, all_t, hidden_t, w_qkv)
 
 
 def share_body(od_ref, dkv_ref, normed_ref, w_ref, parts_ref, grad_ref, out_ref):
     out, dq = od_ref[0, 0].astype(F32), od_ref[0, 1].astype(F32)
-    for i in range(1, 4):
+    for i in range(1, 8):
         out += od_ref[i, 0].astype(F32)
         dq += od_ref[i, 1].astype(F32)
     dkv = dkv_ref[0].astype(F32)
@@ -423,16 +458,17 @@
     along = (sums[0][HD + 1 : HD + 2] + sums[0][HD + 3 : HD + 4]) / WIDTH
     for g in range(2):
         grad = inv_ref[...] * (sums[g][:HD] - plain - unit_ref[g] * along)
-        grad_ref[g] = grad.T
-        error_ref[g] = (slope_ref[g] * grad).T.astype(BF)
+        nil = jnp.zeros((LANES - HD, ROWS), F32)
+        grad_ref[g] = jnp.concatenate([grad, nil], axis=0).T
+        error_ref[g] = jnp.concatenate([slope_ref[g] * grad, nil], axis=0).T.astype(BF)
 
 
 def errors(parts, unit_t, inv_std, slope_t):
     return vmem_call(
         error_body,
         (
-            jax.ShapeDtypeStruct((2, ROWS, HD), F32),
-            jax.ShapeDtypeStruct((2, ROWS, HD), BF),
+            jax.ShapeDtypeStruct((2, ROWS, LANES), F32),
+            jax.ShapeDtypeStruct((2, ROWS, LANES), BF),
         ),
         inputs=4,
     )(parts, unit_t, inv_std, slope_t)
@@ -450,23 +486,26 @@
     order = scalars(y * 4 + x)
 
     frames_g = frames.reshape(ROWS, 2, HD).transpose(1, 0, 2)
-    pair = paired(with_halo(frames_g))
-    taps = exchange_z(everyone(conv_weight[0]))
-    taps = exchange_x(everyone(after(taps, pair), 4))
+    frames_g = jnp.pad(frames_g, ((0, 0), (0, 0), (0, LANES - HD)))
+    upstream = jnp.pad(grad_out, ((0, 0), (0, LANES - HD)))
+    rows = with_halo(frames_g).reshape(2 * PADDED, LANES)
+    pair = paired(jnp.concatenate([rows, upstream], axis=0))
+    taps = exchange_z(taps_sent(conv_weight[0]))
+    taps = exchange_x(joined(taps, pair))
     own, other = convolved(True, where, pair, taps)
     hidden_t, slope_t, sent = hidden_rows(own, other, frames_g)
 
     all_t = lax.all_gather(sent, "head", axis=0, tiled=True)
     keys, queries, normed_t, unit_t, inv_std = project(
-        scalars(index), all_t, hidden_t, w_qkv, grad_out
+        scalars(index), all_t, hidden_t, w_qkv
     )
 
     keys = exchange_z(keys)
-    queries = doubled(queries[0])
-    stats = exchange_xy(everyone(attention_stats(order, queries, keys)))
-    od, dkv = attention_grads(order, queries, keys, stats)
+    queries = doubled(queries)
+    stats = exchange_xy(everyone(attention_stats(order, queries, keys, taps)))
+    od, dkv = attention_grads(order, queries, keys, taps, stats)
+    od = exchange_xy(od)
     dkv = exchange_z(dkv)
-    od = exchange_x(after(od[0] + swap(od[1], 32), dkv))
 
     parts, grad, attended = shares(od, dkv, normed_t, w_qkv)
     parts = lax.all_to_all(parts.reshape(8, 2, LANES, ROWS), "head", 0, 0)
@@ -474,9 +513,9 @@
     wide = exchange_xy(slabs(normed_t, grad))
     wide = jnp.sum(wide.astype(F32), axis=0).astype(BF)
 
-    pair = paired(with_halo(error))
-    own, other = convolved(False, where + nothing(wide), pair, taps)
-    frame_grad = (hidden_grad + own + other.astype(F32)).astype(BF)
+    rows = after(with_halo(error).reshape(2 * PADDED, LANES), wide)
+    own, other = convolved(False, where, paired(rows), taps)
+    frame_grad = (hidden_grad + own + other.astype(F32)).astype(BF)[:, :, :HD]
     wide = exchange_z(wide.reshape(8, SLAB, 3 * LANES))
     weight_grad = jnp.sum(wide[:, : HD // 4, : 3 * HD].astype(F32), axis=0)
     return attended, frame_grad.transpose(1, 0, 2).reshape(ROWS, 2 * HD), weight_grad

time: 250 us -> 245 us (0.980)
  blocking collectives: 34.9 us -> 57.2 us
  local copies, waits for them, and re-layouts: 22.7 us -> 13.6 us
  waiting for transfers between devices: 79.7 us -> 73.6 us
  starting transfers between devices: 83 us -> 78.2 us
  other arithmetic: 7.04 us -> 4.34 us
  Pallas kernels: 18.4 us -> 15.7 us
    all_to_all x4 -> x3, waiting for transfers between devices: 11.8 us -> 0.01 us  [exchange_z(): return lax.all_to_all(parts, 'tm', 0, 0, axis_index_groups=Z_GROUPS)]
    all_to_all x1, blocking collectives: 8.99 us -> 20.3 us  [exchange_z(): return lax.all_to_all(parts, 'tm', 0, 0, axis_index_groups=Z_GROUPS)]
    all_to_all x1 -> x2, blocking collectives: 9.07 us -> 20.1 us  [exchange_xy(): return lax.all_to_all(parts, 'tm', 0, 0, axis_index_groups=XY_GROUPS)]
    all_to_all x1, waiting for transfers between devices: 14.1 us -> 23.6 us  [exchange_x(): return lax.all_to_all(parts, 'tm', 0, 0, axis_index_groups=X_GROUPS)]
    ppermute x2, waiting for transfers between devices: 9.04 us -> 0.01 us  [with_halo(): before = lax.ppermute(rows[:, ROWS - HALF:], 'tm', up)]
    all_to_all x1, waiting for transfers between devices: 0.01 us -> 8.85 us  [exchange_xy(): return lax.all_to_all(parts, 'tm', 0, 0, axis_index_groups=XY_GROUPS)]
    ppermute x8 -> x7, waiting for transfers between devices: 30.4 us -> 24.1 us  [swap(): return lax.ppermute(array, 'tm', [(i, i ^ bit) for i in range(64)])]
    broadcast_in_dim x3 -> x1, local copies, waits for them, and re-layouts: 3.29 us -> 0.01 us  [everyone(): return jnp.broadcast_to(array[None], (count,) + array.shape)]
  transfers between devices with their start and end apart: 19 -> 17, of which waited for: 13 -> 11; matrix products, arithmetic and copies ran while one was open for 4% -> 4% of each run, Pallas kernels for 2% -> 2%
where the time goes in v6:
time: 245 us; the launch traced here: 244 us
  starting transfers between devices  78.2 us (32%)
  waiting for transfers between devices  73.6 us (30%)
  blocking collectives  57.2 us (23%)
  Pallas kernels  15.7 us (6%)
  local copies, waits for them, and re-layouts  13.6 us (6%)
  other arithmetic  4.34 us (2%)
    all_to_all x3, starting transfers between devices, exchange_z(): return lax.all_to_all(parts, 'tm', 0, 0, axis_index_groups=Z_GROUPS)  24.3 us
    ppermute x7, waiting for transfers between devices, swap(): return lax.ppermute(array, 'tm', [(i, i ^ bit) for i in range(64)])  24.1 us
    all_to_all x1, waiting for transfers between devices, exchange_x(): return lax.all_to_all(parts, 'tm', 0, 0, axis_index_groups=X_GROUPS)  23.6 us
    all_to_all x1, blocking collectives, exchange_z(): return lax.all_to_all(parts, 'tm', 0, 0, axis_index_groups=Z_GROUPS)  20.3 us
    all_to_all x2, blocking collectives, exchange_xy(): return lax.all_to_all(parts, 'tm', 0, 0, axis_index_groups=XY_GROUPS)  20.1 us
    ppermute x7, starting transfers between devices, swap(): return lax.ppermute(array, 'tm', [(i, i ^ bit) for i in range(64)])  17.6 us
    all_gather x1, blocking collectives, on_device(): all_t = lax.all_gather(sent, 'head', axis=0, tiled=True)  16.8 us
    all_to_all x1, waiting for transfers between devices, on_device(): parts = lax.all_to_all(parts.reshape(8, 2, LANES, ROWS), 'head', 0, 0)  15.8 us
  transfers between devices with their start and end apart: 17, of which 11 were waited for; matrix products, arithmetic and copies ran while one was open for 4% of the time, Pallas kernels for 2%

profile of v6, /device:TPU:8, one launch (start us, length us, event | category | flops | bytes accessed | tf_op | source)
XLA Modules:
  0.0 244.3 jit_solution(3772613620099424642)
XLA Ops:
  0.6 0.8 copy-done.11
  1.5 0.9 shard_map.76
  2.3 10.3 %all-to-all-start = ((bf16[8,256,128]{2,1,0:T(8,128)(2,1)}), bf16[8,256,128]{2,1,0:T(8,128)(2,1)S(1)}, u32[]{:S(2)}, u32[]{:S(2)}) async-start(bf16[8,256,128]{2,1,0:T(8,128)(2,1)} %shard_map.76), calls=%async_computation | async-start | bytes 1048576 | tf_op jit(solution)/shard_map/all_to_all | solution.py:44
  12.7 0.1 copy.44
  12.8 3.4 %collective-permute-start = (bf16[2,32,128]{2,1,0:T(8,128)(2,1)S(1)}, bf16[2,32,128]{2,1,0:T(8,128)(2,1)S(1)}, u32[]{:S(2)}, u32[]{:S(2)}) collective-permute-start(bf16[2,32,128]{2,1,0:T(8,128)(2,1)S(1)} %get-tuple-element.66), channel_id=1, source_target_pairs={{0,8},{8,16},{16,24},{24,32},{32,40},{40,48},{48,56},{56,64},{64,7... | collective-permute-start | bytes 49160 | tf_op jit(solution)/shard_map/ppermute | solution.py:183
  16.2 6.7 %collective-permute-start.1 = (bf16[2,32,128]{2,1,0:T(8,128)(2,1)S(1)}, bf16[2,32,128]{2,1,0:T(8,128)(2,1)S(1)}, u32[]{:S(2)}, u32[]{:S(2)}) collective-permute-start(bf16[2,32,128]{2,1,0:T(8,128)(2,1)S(1)} %get-tuple-element.67), channel_id=1, source_target_pairs={{8,0},{16,8},{24,16},{32,24},{40,32},{48,40},{56,48},{64,56},{72,6... | collective-permute-start | bytes 49160 | tf_op jit(solution)/shard_map/ppermute | solution.py:184
  22.9 0.1 copy.45
  23.0 1.3 collective-permute-done.1
  24.3 1.9 collective-permute-start.2
  26.3 4.9 %collective-permute-done.2 = bf16[512,128]{1,0:T(8,128)(2,1)S(1)} collective-permute-done((bf16[512,128]{1,0:T(8,128)(2,1)S(1)}, bf16[512,128]{1,0:T(8,128)(2,1)S(1)}, u32[]{:S(2)}, u32[]{:S(2)}) %collective-permute-start.2) | collective-permute-done | bytes 131104 | tf_op jit(solution)/shard_map/ppermute | solution.py:40
  31.2 0.2 shard_map.77
  31.4 1.4 copy-done.2
  32.8 6.3 %all-to-all-start.1 = ((bf16[4,2304,128]{2,1,0:T(8,128)(2,1)}), bf16[4,2304,128]{2,1,0:T(8,128)(2,1)S(1)}, u32[]{:S(2)}, u32[]{:S(2)}) async-start(bf16[4,2304,128]{2,1,0:T(8,128)(2,1)} %copy-done.2), calls=%async_computation.1 | async-start | bytes 4718592 | tf_op jit(solution)/shard_map/all_to_all | solution.py:36
  39.1 0.2 reduce-window.9
  39.3 2.5 %copy.46.w_ref = bf16[1920,360]{1,0:T(8,128)(2,1)} copy(bf16[1920,360]{0,1:T(8,128)(2,1)} %param.7) | data formatting | bytes 2764800 | tf_op args[2]
  41.8 0.1 pad_add_fusion.2.sc_ref
  41.9 23.6 %all-to-all-done.1.w_ref.f_ref = bf16[4,2304,128]{2,1,0:T(8,128)(2,1)S(1)} async-done(((bf16[4,2304,128]{2,1,0:T(8,128)(2,1)}), bf16[4,2304,128]{2,1,0:T(8,128)(2,1)S(1)}, u32[]{:S(2)}, u32[]{:S(2)}) %all-to-all-start.1) | async-done | bytes 2359328 | tf_op jit(solution)/shard_map/all_to_all | solution.py:36
  65.5 1.9 shard_map.78
  67.4 2.4 collective-permute-start.3
  69.8 0.1 pad_add_fusion.1
  69.9 3.7 %collective-permute-done.3.other_ref = bf16[2,128,128]{2,1,0:T(8,128)(2,1)S(1)} collective-permute-done((bf16[2,128,128]{2,1,0:T(8,128)(2,1)S(1)}, bf16[2,128,128]{2,1,0:T(8,128)(2,1)S(1)}, u32[]{:S(2)}, u32[]{:S(2)}) %collective-permute-start.3) | collective-permute-done | bytes 65568 | tf_op jit(solution)/shard_map/ppermute | solution.py:40
  73.6 0.1 shard_map.79
  73.7 16.8 %all_gather.3.all_ref = bf16[16,120,128]{2,1,0:T(8,128)(2,1)S(1)} all-gather(bf16[2,120,128]{2,1,0:T(8,128)(2,1)S(1)} %get-tuple-element.24), channel_id=1, replica_groups=mesh['tm'=64,'head'=8] {'head'}, dimensions={0}, use_global_device_ids=true | all-gather | bytes 552960 | tf_op jit(solution)/shard_map/all_gather | solution.py:498
  90.6 1.5 shard_map.80
  92.1 0.8 copy-done.5
  92.9 0.7 copy-done.7
  93.6 10.6 %all-to-all-start.2 = ((bf16[8,128,256]{2,1,0:T(8,128)(2,1)}), bf16[8,128,256]{2,1,0:T(8,128)(2,1)S(1)}, u32[]{:S(2)}, u32[]{:S(2)}) async-start(bf16[8,128,256]{2,1,0:T(8,128)(2,1)} %copy-done.5), calls=%async_computation.2 | async-start | bytes 1048576 | tf_op jit(solution)/shard_map/all_to_all | solution.py:44
  104.1 3.5 %collective-permute-start.4 = (bf16[1,128,128]{2,1,0:T(8,128)(2,1)S(1)}, bf16[1,128,128]{2,1,0:T(8,128)(2,1)S(1)}, u32[]{:S(2)}, u32[]{:S(2)}) collective-permute-start(bf16[1,128,128]{2,1,0:T(8,128)(2,1)S(1)} %bitcast.24), channel_id=1, source_target_pairs={{0,256},{8,264},{16,272},{24,280},{32,288},{40,296},{48,304},{56,3... | collective-permute-start | bytes 98312 | tf_op jit(solution)/shard_map/ppermute | solution.py:40
  107.7 2.3 collective-permute-done.4
  109.9 2.5 %collective-permute-start.5 = (bf16[2,128,128]{2,1,0:T(8,128)(2,1)S(1)}, bf16[2,128,128]{2,1,0:T(8,128)(2,1)S(1)}, u32[]{:S(2)}, u32[]{:S(2)}) collective-permute-start(bf16[2,128,128]{2,1,0:T(8,128)(2,1)S(1)} %pad_maximum_fusion.5), channel_id=1, source_target_pairs={{0,16},{8,24},{16,0},{24,8},{32,48},{40,56},{48,32},{56,40},{64,80... | collective-permute-start | bytes 196616 | tf_op jit(solution)/shard_map/ppermute | solution.py:40
  112.4 5.2 %collective-permute-done.5 = bf16[2,128,128]{2,1,0:T(8,128)(2,1)S(1)} collective-permute-done((bf16[2,128,128]{2,1,0:T(8,128)(2,1)S(1)}, bf16[2,128,128]{2,1,0:T(8,128)(2,1)S(1)}, u32[]{:S(2)}, u32[]{:S(2)}) %collective-permute-start.5) | collective-permute-done | bytes 65568 | tf_op jit(solution)/shard_map/ppermute | solution.py:40
  117.6 2.5 %collective-permute-start.6 = (bf16[4,128,128]{2,1,0:T(8,128)(2,1)S(1)}, bf16[4,128,128]{2,1,0:T(8,128)(2,1)S(1)}, u32[]{:S(2)}, u32[]{:S(2)}) collective-permute-start(bf16[4,128,128]{2,1,0:T(8,128)(2,1)S(1)} %pad_maximum_fusion.3), channel_id=1, source_target_pairs={{0,8},{8,0},{16,24},{24,16},{32,40},{40,32},{48,56},{56,48},{64,72... | collective-permute-start | bytes 393224 | tf_op jit(solution)/shard_map/ppermute | solution.py:40
  120.1 4.4 %collective-permute-done.6 = bf16[4,128,128]{2,1,0:T(8,128)(2,1)S(1)} collective-permute-done((bf16[4,128,128]{2,1,0:T(8,128)(2,1)S(1)}, bf16[4,128,128]{2,1,0:T(8,128)(2,1)S(1)}, u32[]{:S(2)}, u32[]{:S(2)}) %collective-permute-start.6) | collective-permute-done | bytes 131104 | tf_op jit(solution)/shard_map/ppermute | solution.py:40
  124.5 0.7 pad_maximum_fusion.1.q_ref
  125.2 0.9 copy-done.4
  126.2 2.4 shard_map.81
  128.6 9.1 %all_to_all.45.stats_ref = f32[8,3,8,128]{3,2,1,0:T(8,128)S(1)} all-to-all(f32[8,3,8,128]{3,2,1,0:T(8,128)S(1)} %broadcast_in_dim.10), channel_id=1, replica_groups={{0,8,16,24,256,264,272,280},{32,40,48,56,288,296,304,312},{64,72,80,88,..., dimensions={0} | all-to-all | bytes 196608 | tf_op jit(solution)/shard_map/all_to_all | solution.py:32
  137.7 3.5 %shard_map.82 = (bf16[8,2,120,128]{3,2,1,0:T(8,128)(2,1)S(1)}, bf16[8,128,256]{2,1,0:T(8,128)(2,1)S(1)}) custom-call(s32[5]{0:T(128)S(1)} %get-tuple-element.69.sc_ref, bf16[8,128,128]{2,1,0:T(8,128)(2,1)S(1)} %copy-done.4, bf16[8,128,256]{2,1,0:T(8,128)(2,1)S(1)} %all-to-all-done.2.kv_ref, bf16[4,2304,128]{2,1,0:T(8,128)(2,1)S(1)} %all-to-all-done.1.w_ref.f_ref, ...), custom_call_target="tpu_custom_call" | custom-call | flops 1610612736 | bytes 1048576 | tf_op jit(solution)/shard_map/pallas_call | solution.py:281
  141.2 11.0 %all_to_all.46.od_ref = bf16[8,2,120,128]{3,2,1,0:T(8,128)(2,1)S(1)} all-to-all(bf16[8,2,120,128]{3,2,1,0:T(8,128)(2,1)S(1)} %get-tuple-element.28), channel_id=1, replica_groups={{0,8,16,24,256,264,272,280},{32,40,48,56,288,296,304,312},{64,72,80,88,..., dimensions={0} | all-to-all | bytes 983040 | tf_op jit(solution)/shard_map/all_to_all | solution.py:32
  152.2 20.3 %all_to_all.47.dkv_ref = bf16[8,128,256]{2,1,0:T(8,128)(2,1)S(1)} all-to-all(bf16[8,128,256]{2,1,0:T(8,128)(2,1)S(1)} %get-tuple-element.29), channel_id=1, replica_groups={{0,32,64,96,128,160,192,224},{8,40,72,104,136,168,200,232},{16,48,80,11..., dimensions={0} | all-to-all | bytes 1048576 | tf_op jit(solution)/shard_map/all_to_all | solution.py:44
  172.5 1.0 shard_map.83
  173.5 0.8 copy-done.6
  174.3 0.6 copy-done.9
  174.9 4.8 %all-to-all-start.6 = ((bf16[8,2,128,128]{3,2,1,0:T(8,128)(2,1)}), bf16[8,2,128,128]{3,2,1,0:T(8,128)(2,1)S(1)}, u32[]{:S(2)}, u32[]{:S(2)}) async-start(bf16[8,2,128,128]{3,2,1,0:T(8,128)(2,1)} %bitcast.23), calls=%async_computation.6 | async-start | bytes 1048576 | tf_op jit(solution)/shard_map/all_to_all | solution.py:511
  179.7 0.9 copy-done.10
  180.6 0.6 shard_map.85
  181.2 1.1 copy-done.3
  182.4 15.8 %all-to-all-done.6.parts_ref = bf16[8,2,128,128]{3,2,1,0:T(8,128)(2,1)S(1)} async-done(((bf16[8,2,128,128]{3,2,1,0:T(8,128)(2,1)}), bf16[8,2,128,128]{3,2,1,0:T(8,128)(2,1)S(1)}, u32[]{:S(2)}, u32[]{:S(2)}) %all-to-all-start.6) | async-done | bytes 524320 | tf_op jit(solution)/shard_map/all_to_all | solution.py:511
  198.1 4.9 %all-to-all-start.7 = ((bf16[8,256,384]{2,1,0:T(8,128)(2,1)}), bf16[8,256,384]{2,1,0:T(8,128)(2,1)}, u32[]{:S(2)}, u32[]{:S(2)}) async-start(bf16[8,256,384]{2,1,0:T(8,128)(2,1)} %copy-done.3), calls=%async_computation.7 | async-start | bytes 3145728 | tf_op jit(solution)/shard_map/all_to_all | solution.py:32
  203.0 0.2 shard_map.84
  203.2 3.4 %collective-permute-start.7 = (bf16[2,32,128]{2,1,0:T(8,128)(2,1)S(1)}, bf16[2,32,128]{2,1,0:T(8,128)(2,1)S(1)}, u32[]{:S(2)}, u32[]{:S(2)}) collective-permute-start(bf16[2,32,128]{2,1,0:T(8,128)(2,1)S(1)} %get-tuple-element.64), channel_id=1, source_target_pairs={{0,8},{8,16},{16,24},{24,32},{32,40},{40,48},{48,56},{56,64},{64,7... | collective-permute-start | bytes 49160 | tf_op jit(solution)/shard_map/ppermute | solution.py:183
  206.6 6.9 %collective-permute-start.8 = (bf16[2,32,128]{2,1,0:T(8,128)(2,1)S(1)}, bf16[2,32,128]{2,1,0:T(8,128)(2,1)S(1)}, u32[]{:S(2)}, u32[]{:S(2)}) collective-permute-start(bf16[2,32,128]{2,1,0:T(8,128)(2,1)S(1)} %get-tuple-element.65), channel_id=1, source_target_pairs={{8,0},{16,8},{24,16},{32,24},{40,32},{48,40},{56,48},{64,56},{72,6... | collective-permute-start | bytes 49160 | tf_op jit(solution)/shard_map/ppermute | solution.py:184
  213.4 8.9 %all-to-all-done.7 = bf16[8,256,384]{2,1,0:T(8,128)(2,1)} async-done(((bf16[8,256,384]{2,1,0:T(8,128)(2,1)}), bf16[8,256,384]{2,1,0:T(8,128)(2,1)}, u32[]{:S(2)}, u32[]{:S(2)}) %all-to-all-start.7) | async-done | bytes 1572896 | tf_op jit(solution)/shard_map/all_to_all | solution.py:32
  222.3 2.3 reduce_sum.21
  224.6 1.2 slice.28
  226.5 2.1 collective-permute-start.9
  228.6 3.4 %all-to-all-start.8 = ((bf16[8,32,384]{2,1,0:T(8,128)(2,1)}), bf16[8,32,384]{2,1,0:T(8,128)(2,1)S(1)}, u32[]{:S(2)}, u32[]{:S(2)}) async-start(bf16[8,32,384]{2,1,0:T(8,128)(2,1)} %bitcast.19), calls=%async_computation.8 | async-start | bytes 393216 | tf_op jit(solution)/shard_map/all_to_all | solution.py:44
  232.0 1.0 collective-permute-done.9
  233.1 3.5 %shard_map.86 = (f32[2,128,128]{2,1,0:T(8,128)S(1)}, bf16[2,128,128]{2,1,0:T(8,128)(2,1)S(1)}) custom-call(s32[6]{0:T(128)S(1)} %pad_add_fusion.2.sc_ref, bf16[2,384,128]{2,1,0:T(8,128)(2,1)S(1)} %pad_maximum_fusion.2.x_ref, bf16[4,2304,128]{2,1,0:T(8,128)(2,1)S(1)} %all-to-all-done.1.w_ref.f_ref), custom_call_target="tpu_custom_call" | custom-call | flops 471859200 | bytes 1048576 | tf_op jit(solution)/shard_map/pallas_call | solution.py:166
  236.6 2.8 %collective-permute-start.10 = (bf16[2,128,128]{2,1,0:T(8,128)(2,1)S(1)}, bf16[2,128,128]{2,1,0:T(8,128)(2,1)S(1)}, u32[]{:S(2)}, u32[]{:S(2)}) collective-permute-start(bf16[2,128,128]{2,1,0:T(8,128)(2,1)S(1)} %get-tuple-element.40), channel_id=1, source_target_pairs={{0,256},{8,264},{16,272},{24,280},{32,288},{40,296},{48,304},{56,3... | collective-permute-start | bytes 196616 | tf_op jit(solution)/shard_map/ppermute | solution.py:40
  239.4 0.7 copy.50
  240.1 2.7 %collective-permute-done.10 = bf16[2,128,128]{2,1,0:T(8,128)(2,1)S(1)} collective-permute-done((bf16[2,128,128]{2,1,0:T(8,128)(2,1)S(1)}, bf16[2,128,128]{2,1,0:T(8,128)(2,1)S(1)}, u32[]{:S(2)}, u32[]{:S(2)}) %collective-permute-start.10) | collective-permute-done | bytes 65568 | tf_op jit(solution)/shard_map/ppermute | solution.py:40
  242.8 0.7 copy.48
  243.5 0.8 convert_reduce_fusion
  (39 shorter events, 0.2 us)
Async XLA Ops:
  0.6 0.8 copy-start.11
  1.5 11.2 %copy-start.12 = (bf16[128,240]{0,1:T(8,128)(2,1)S(1)}, bf16[128,240]{0,1:T(8,128)(2,1)}, u32[]{:S(2)}) copy-start(bf16[128,240]{0,1:T(8,128)(2,1)} %param.5) | copy-start | bytes 184324
  1.5 21.5 %copy-start.13 = (bf16[128,120]{0,1:T(8,128)(2,1)S(1)}, bf16[128,120]{0,1:T(8,128)(2,1)}, u32[]{:S(2)}) copy-start(bf16[128,120]{0,1:T(8,128)(2,1)} %param.9) | copy-start | bytes 92164
  2.3 28.9 %all-to-all-start = ((bf16[8,256,128]{2,1,0:T(8,128)(2,1)}), bf16[8,256,128]{2,1,0:T(8,128)(2,1)S(1)}, u32[]{:S(2)}, u32[]{:S(2)}) async-start(bf16[8,256,128]{2,1,0:T(8,128)(2,1)} %shard_map.76), calls=%async_computation | async-start | bytes 1048576 | tf_op jit(solution)/shard_map/all_to_all | solution.py:44
  12.8 10.2 %collective-permute-start = (bf16[2,32,128]{2,1,0:T(8,128)(2,1)S(1)}, bf16[2,32,128]{2,1,0:T(8,128)(2,1)S(1)}, u32[]{:S(2)}, u32[]{:S(2)}) collective-permute-start(bf16[2,32,128]{2,1,0:T(8,128)(2,1)S(1)} %get-tuple-element.66), channel_id=1, source_target_pairs={{0,8},{8,16},{16,24},{24,32},{32,40},{40,48},{48,56},{56,64},{64,7... | collective-permute-start | bytes 49160 | tf_op jit(solution)/shard_map/ppermute | solution.py:183
  16.2 8.1 %collective-permute-start.1 = (bf16[2,32,128]{2,1,0:T(8,128)(2,1)S(1)}, bf16[2,32,128]{2,1,0:T(8,128)(2,1)S(1)}, u32[]{:S(2)}, u32[]{:S(2)}) collective-permute-start(bf16[2,32,128]{2,1,0:T(8,128)(2,1)S(1)} %get-tuple-element.67), channel_id=1, source_target_pairs={{8,0},{16,8},{24,16},{32,24},{40,32},{48,40},{56,48},{64,56},{72,6... | collective-permute-start | bytes 49160 | tf_op jit(solution)/shard_map/ppermute | solution.py:184
  24.3 6.9 %collective-permute-start.2 = (bf16[512,128]{1,0:T(8,128)(2,1)S(1)}, bf16[512,128]{1,0:T(8,128)(2,1)S(1)}, u32[]{:S(2)}, u32[]{:S(2)}) collective-permute-start(bf16[512,128]{1,0:T(8,128)(2,1)S(1)} %get-tuple-element.63), channel_id=1, source_target_pairs={{0,256},{8,264},{16,272},{24,280},{32,288},{40,296},{48,304},{56,3... | collective-permute-start | bytes 393224 | tf_op jit(solution)/shard_map/ppermute | solution.py:40
  31.4 1.4 copy-start.2
  32.8 6.3 %copy-start.14 = (s32[4]{0:T(128)S(1)}, s32[4]{0:T(128)}, u32[]{:S(2)}) copy-start(s32[4]{0:T(128)} %param.8) | copy-start | bytes 52
  32.8 32.6 %all-to-all-start.1 = ((bf16[4,2304,128]{2,1,0:T(8,128)(2,1)}), bf16[4,2304,128]{2,1,0:T(8,128)(2,1)S(1)}, u32[]{:S(2)}, u32[]{:S(2)}) async-start(bf16[4,2304,128]{2,1,0:T(8,128)(2,1)} %copy-done.2), calls=%async_computation.1 | async-start | bytes 4718592 | tf_op jit(solution)/shard_map/all_to_all | solution.py:36
  65.5 25.1 %copy-start = (bf16[1920,360]{1,0:T(8,128)(2,1)S(1)}, bf16[1920,360]{1,0:T(8,128)(2,1)}, u32[]{:S(2)}) copy-start(bf16[1920,360]{1,0:T(8,128)(2,1)} %copy.46.w_ref) | copy-start | bytes 4147204
  67.4 6.2 %collective-permute-start.3 = (bf16[2,128,128]{2,1,0:T(8,128)(2,1)S(1)}, bf16[2,128,128]{2,1,0:T(8,128)(2,1)S(1)}, u32[]{:S(2)}, u32[]{:S(2)}) collective-permute-start(bf16[2,128,128]{2,1,0:T(8,128)(2,1)S(1)} %get-tuple-element.23), channel_id=1, source_target_pairs={{0,256},{8,264},{16,272},{24,280},{32,288},{40,296},{48,304},{56,3... | collective-permute-start | bytes 196616 | tf_op jit(solution)/shard_map/ppermute | solution.py:40
  92.1 0.8 copy-start.5
  92.9 0.7 copy-start.7
  93.6 31.6 %all-to-all-start.2 = ((bf16[8,128,256]{2,1,0:T(8,128)(2,1)}), bf16[8,128,256]{2,1,0:T(8,128)(2,1)S(1)}, u32[]{:S(2)}, u32[]{:S(2)}) async-start(bf16[8,128,256]{2,1,0:T(8,128)(2,1)} %copy-done.5), calls=%async_computation.2 | async-start | bytes 1048576 | tf_op jit(solution)/shard_map/all_to_all | solution.py:44
  104.1 5.8 %collective-permute-start.4 = (bf16[1,128,128]{2,1,0:T(8,128)(2,1)S(1)}, bf16[1,128,128]{2,1,0:T(8,128)(2,1)S(1)}, u32[]{:S(2)}, u32[]{:S(2)}) collective-permute-start(bf16[1,128,128]{2,1,0:T(8,128)(2,1)S(1)} %bitcast.24), channel_id=1, source_target_pairs={{0,256},{8,264},{16,272},{24,280},{32,288},{40,296},{48,304},{56,3... | collective-permute-start | bytes 98312 | tf_op jit(solution)/shard_map/ppermute | solution.py:40
  109.9 7.7 %collective-permute-start.5 = (bf16[2,128,128]{2,1,0:T(8,128)(2,1)S(1)}, bf16[2,128,128]{2,1,0:T(8,128)(2,1)S(1)}, u32[]{:S(2)}, u32[]{:S(2)}) collective-permute-start(bf16[2,128,128]{2,1,0:T(8,128)(2,1)S(1)} %pad_maximum_fusion.5), channel_id=1, source_target_pairs={{0,16},{8,24},{16,0},{24,8},{32,48},{40,56},{48,32},{56,40},{64,80... | collective-permute-start | bytes 196616 | tf_op jit(solution)/shard_map/ppermute | solution.py:40
  117.6 6.9 %collective-permute-start.6 = (bf16[4,128,128]{2,1,0:T(8,128)(2,1)S(1)}, bf16[4,128,128]{2,1,0:T(8,128)(2,1)S(1)}, u32[]{:S(2)}, u32[]{:S(2)}) collective-permute-start(bf16[4,128,128]{2,1,0:T(8,128)(2,1)S(1)} %pad_maximum_fusion.3), channel_id=1, source_target_pairs={{0,8},{8,0},{16,24},{24,16},{32,40},{40,32},{48,56},{56,48},{64,72... | collective-permute-start | bytes 393224 | tf_op jit(solution)/shard_map/ppermute | solution.py:40
  125.2 1.0 copy-start.4
  141.1 31.3 %copy-start.1 = (bf16[1920,360]{1,0:T(8,128)(2,1)S(1)}, bf16[1920,360]{1,0:T(8,128)(2,1)}, u32[]{:S(2)}) copy-start(bf16[1920,360]{1,0:T(8,128)(2,1)} %copy.46.w_ref) | copy-start | bytes 4147204
  173.4 0.8 copy-start.6
  174.2 0.6 copy-start.9
  174.9 23.2 %all-to-all-start.6 = ((bf16[8,2,128,128]{3,2,1,0:T(8,128)(2,1)}), bf16[8,2,128,128]{3,2,1,0:T(8,128)(2,1)S(1)}, u32[]{:S(2)}, u32[]{:S(2)}) async-start(bf16[8,2,128,128]{3,2,1,0:T(8,128)(2,1)} %bitcast.23), calls=%async_computation.6 | async-start | bytes 1048576 | tf_op jit(solution)/shard_map/all_to_all | solution.py:511
  179.7 0.9 copy-start.10
  181.2 1.1 copy-start.3
  182.4 20.6 %copy-start.8 = (f32[2,120,128]{2,1,0:T(8,128)S(1)}, f32[2,120,128]{2,1,0:T(8,128)}, u32[]{:S(2)}) copy-start(f32[2,120,128]{2,1,0:T(8,128)} %copy-done.7) | copy-start | bytes 368644
  198.1 24.2 %all-to-all-start.7 = ((bf16[8,256,384]{2,1,0:T(8,128)(2,1)}), bf16[8,256,384]{2,1,0:T(8,128)(2,1)}, u32[]{:S(2)}, u32[]{:S(2)}) async-start(bf16[8,256,384]{2,1,0:T(8,128)(2,1)} %copy-done.3), calls=%async_computation.7 | async-start | bytes 3145728 | tf_op jit(solution)/shard_map/all_to_all | solution.py:32
  203.2 23.3 %collective-permute-start.7 = (bf16[2,32,128]{2,1,0:T(8,128)(2,1)S(1)}, bf16[2,32,128]{2,1,0:T(8,128)(2,1)S(1)}, u32[]{:S(2)}, u32[]{:S(2)}) collective-permute-start(bf16[2,32,128]{2,1,0:T(8,128)(2,1)S(1)} %get-tuple-element.64), channel_id=1, source_target_pairs={{0,8},{8,16},{16,24},{24,32},{32,40},{40,48},{48,56},{56,64},{64,7... | collective-permute-start | bytes 49160 | tf_op jit(solution)/shard_map/ppermute | solution.py:183
  206.6 19.9 %collective-permute-start.8 = (bf16[2,32,128]{2,1,0:T(8,128)(2,1)S(1)}, bf16[2,32,128]{2,1,0:T(8,128)(2,1)S(1)}, u32[]{:S(2)}, u32[]{:S(2)}) collective-permute-start(bf16[2,32,128]{2,1,0:T(8,128)(2,1)S(1)} %get-tuple-element.65), channel_id=1, source_target_pairs={{8,0},{16,8},{24,16},{32,24},{40,32},{48,40},{56,48},{64,56},{72,6... | collective-permute-start | bytes 49160 | tf_op jit(solution)/shard_map/ppermute | solution.py:184
  226.5 6.5 %collective-permute-start.9 = (bf16[384,128]{1,0:T(8,128)(2,1)S(1)}, bf16[384,128]{1,0:T(8,128)(2,1)S(1)}, u32[]{:S(2)}, u32[]{:S(2)}) collective-permute-start(bf16[384,128]{1,0:T(8,128)(2,1)S(1)} %bitcast.32), channel_id=1, source_target_pairs={{0,256},{8,264},{16,272},{24,280},{32,288},{40,296},{48,304},{56,3... | collective-permute-start | bytes 294920 | tf_op jit(solution)/shard_map/ppermute | solution.py:40
  228.6 14.9 %all-to-all-start.8 = ((bf16[8,32,384]{2,1,0:T(8,128)(2,1)}), bf16[8,32,384]{2,1,0:T(8,128)(2,1)S(1)}, u32[]{:S(2)}, u32[]{:S(2)}) async-start(bf16[8,32,384]{2,1,0:T(8,128)(2,1)} %bitcast.19), calls=%async_computation.8 | async-start | bytes 393216 | tf_op jit(solution)/shard_map/all_to_all | solution.py:44
  236.6 6.2 %collective-permute-start.10 = (bf16[2,128,128]{2,1,0:T(8,128)(2,1)S(1)}, bf16[2,128,128]{2,1,0:T(8,128)(2,1)S(1)}, u32[]{:S(2)}, u32[]{:S(2)}) collective-permute-start(bf16[2,128,128]{2,1,0:T(8,128)(2,1)S(1)} %get-tuple-element.40), channel_id=1, source_target_pairs={{0,256},{8,264},{16,272},{24,280},{32,288},{40,296},{48,304},{56,3... | collective-permute-start | bytes 196616 | tf_op jit(solution)/shard_map/ppermute | solution.py:40

commit v7 on v6

--- a/solution.py
+++ b/solution.py
@@ -25,6 +25,8 @@
 
 XY_GROUPS = [[y * 32 + z * 4 + x for y in range(2) for x in range(4)] for z in range(8)]
 X_GROUPS = [[y * 32 + z * 4 + x for x in range(4)] for y in range(2) for z in range(8)]
+CORE_GROUPS = [[h * 2 + c for c in range(2)] for h in range(4)]
+HIGH_GROUPS = [[h * 2 + c for h in range(4)] for c in range(2)]
 Z_GROUPS = [[y * 32 + z * 4 + x for z in range(8)] for y in range(2) for x in range(4)]
 
 
@@ -44,31 +46,17 @@
     return lax.all_to_all(parts, "tm", 0, 0, axis_index_groups=Z_GROUPS)
 
 
-def everyone(array, count=8):
-    return jnp.broadcast_to(array[None], (count,) + array.shape)
-
-
-def after(array, earlier):
-    return array + 0 * earlier[(0,) * earlier.ndim].astype(array.dtype)
-
-
-BITS = (32, 2, 1)
-SLOTS = (0, 4, 2, 6, 1, 5, 3, 7)
-
-
-def doubled(array):
-    array = array[None]
-    for bit in BITS:
-        array = jnp.concatenate([array, swap(array, bit)], axis=0)
-    return array
-
-
-def vmem_call(body, out_shape, scratch=(), scalars=0, inputs=0, flops=0):
+def exchange_head(parts, groups):
+    return lax.all_to_all(parts, "head", 0, 0, axis_index_groups=groups)
+
+
+def vmem_call(body, out_shape, scratch=(), scalars=0, inputs=0, earlier=0, flops=0):
     return pl.pallas_call(
         body,
         out_shape=out_shape,
         in_specs=[pl.BlockSpec(memory_space=pltpu.SMEM)] * scalars
-        + [pl.BlockSpec(memory_space=pltpu.VMEM)] * inputs,
+        + [pl.BlockSpec(memory_space=pltpu.VMEM)] * inputs
+        + [pl.BlockSpec(memory_space=pl.ANY)] * earlier,
         out_specs=jax.tree.map(lambda _: pl.BlockSpec(memory_space=pltpu.VMEM), out_shape),
         scratch_shapes=list(scratch),
         compiler_params=pltpu.CompilerParams(vmem_limit_bytes=48 * 1024 * 1024),
@@ -143,19 +131,16 @@
     )(weight)
 
 
-def joined_body(w_ref, pair_ref, out_ref):
+def joined_body(w_ref, pair_ref, qkv_ref, up_ref, out_ref):
     for i in range(4):
         for z in range(8):
             out_ref[i, z * 2 * LANES : (z + 1) * 2 * LANES] = w_ref[z]
-        for b in range(2):
-            start = 16 * LANES + b * ROWS
-            out_ref[i, start : start + ROWS] = pair_ref[b, 2 * PADDED :]
-
-
-def joined(taps, pair):
-    return vmem_call(
-        joined_body, jax.ShapeDtypeStruct((4, 16 * LANES + 2 * ROWS, LANES), BF), inputs=2
-    )(taps, pair)
+
+
+def joined(taps, pair, w_qkv, grad_out):
+    return vmem_call(
+        joined_body, jax.ShapeDtypeStruct((4, 16 * LANES, LANES), BF), inputs=1, earlier=3
+    )(taps, pair, w_qkv, grad_out)
 
 
 def paired(padded):
@@ -193,46 +178,36 @@
 CONTRACT = (((1,), (1,)), ((), ()))
 
 
-def upstream_rows(sc_ref, f_ref, d_ref):
-    for i, e in enumerate(SLOTS):
-        row = 16 * LANES + e // 4 * ROWS
-        d_ref[i * ROWS : (i + 1) * ROWS] = f_ref[(sc_ref[0] % 4) ^ (e % 4), row : row + ROWS]
-
-
-def scored(c, q_ref, kv_ref, d_ref):
+def scored(c, q_ref, kv_ref):
     keys = kv_ref[:, :, :LANES].reshape(ALL, LANES)
     values = kv_ref[:, :, LANES:].reshape(ALL, LANES)
-    q = q_ref[c * N : (c + 1) * N].reshape(CHUNK, LANES)
-    d = d_ref[c * CHUNK : (c + 1) * CHUNK]
+    q = q_ref[c * N : (c + 1) * N, :, :LANES].reshape(CHUNK, LANES)
+    d = q_ref[c * N : (c + 1) * N, :, LANES:].reshape(CHUNK, LANES)
     scores = lax.dot_general(keys, q, CONTRACT, preferred_element_type=F32)
     dprobs = lax.dot_general(values, d, CONTRACT, preferred_element_type=F32)
     return keys, values, q, d, scores * SCALE2, dprobs
 
 
-def stats_body(sc_ref, q_ref, kv_ref, f_ref, out_ref, d_ref):
-    upstream_rows(sc_ref, f_ref, d_ref)
+def stats_body(q_ref, kv_ref, out_ref):
     for c in range(ALL // CHUNK):
-        _, _, _, _, scores, dprobs = scored(c, q_ref, kv_ref, d_ref)
+        _, _, _, _, scores, dprobs = scored(c, q_ref, kv_ref)
         peak = jnp.max(scores, axis=0, keepdims=True)
         weight = jnp.exp2(scores - peak)
         total = jnp.sum(weight, axis=0, keepdims=True)
         along = jnp.sum(weight * dprobs, axis=0, keepdims=True)
         for i in range(N):
-            columns = slice(i * ROWS, (i + 1) * ROWS)
-            shard = pl.ds(sc_ref[0] ^ SLOTS[c * N + i], 1)
+            shard = c * N + i
             for j, value in enumerate((peak, total, along)):
-                out_ref[j, shard] = value[:, columns]
-
-
-def grads_body(
-    sc_ref, q_ref, kv_ref, f_ref, stats_ref, od_ref, dkv_ref, d_ref, dk_ref, dv_ref
-):
-    upstream_rows(sc_ref, f_ref, d_ref)
+                out_ref[0, j, shard : shard + 1] = value[:, i * ROWS : (i + 1) * ROWS]
+    for i in range(1, 8):
+        out_ref[i] = out_ref[0]
+
+
+def grads_body(q_ref, kv_ref, stats_ref, od_ref, dkv_ref, dk_ref, dv_ref):
     for c in range(ALL // CHUNK):
         peaks, totals, alongs = (
             jnp.concatenate(
-                [stats_ref[:, j, pl.ds(sc_ref[0] ^ SLOTS[c * N + i], 1)] for i in range(N)],
-                axis=2,
+                [stats_ref[:, j, c * N + i : c * N + i + 1] for i in range(N)], axis=2
             )
             for j in range(3)
         )
@@ -241,7 +216,7 @@
         total = jnp.sum(totals * factor, axis=0)
         delta = jnp.sum(alongs * factor, axis=0) / total
         lse = top + jnp.log2(total)
-        keys, values, q, d, scores, dprobs = scored(c, q_ref, kv_ref, d_ref)
+        keys, values, q, d, scores, dprobs = scored(c, q_ref, kv_ref)
         probs = jnp.exp2(scores - lse)
         dscores = (probs * (dprobs - delta)).astype(BF)
         probs = probs.astype(BF)
@@ -257,7 +232,7 @@
         out_t = lax.dot_general(values, probs, inner, preferred_element_type=F32)
         dq_t = lax.dot_general(keys, dscores, inner, preferred_element_type=F32) * SCALE
         for i in range(N):
-            at = sc_ref[0] ^ SLOTS[c * N + i]
+            at = c * N + i
             od_ref[at, 0] = out_t[:HD, i * ROWS : (i + 1) * ROWS].astype(BF)
             od_ref[at, 1] = dq_t[:HD, i * ROWS : (i + 1) * ROWS].astype(BF)
     for i in range(8):
@@ -266,33 +241,26 @@
         dkv_ref[i, :, LANES:] = dv_ref[piece].astype(BF)
 
 
-def attention_stats(scalars, queries, keys, gathered):
+def attention_stats(queries, keys):
     return vmem_call(
         stats_body,
-        jax.ShapeDtypeStruct((3, 8, ROWS), F32),
-        scratch=[pltpu.VMEM((ALL, LANES), BF)],
-        scalars=1,
-        inputs=3,
+        jax.ShapeDtypeStruct((8, 3, 8, ROWS), F32),
+        inputs=2,
         flops=2 * 2 * ALL * ALL * LANES,
-    )(scalars, queries, keys, gathered)
-
-
-def attention_grads(scalars, queries, keys, gathered, stats):
+    )(queries, keys)
+
+
+def attention_grads(queries, keys, stats):
     return vmem_call(
         grads_body,
         (
             jax.ShapeDtypeStruct((8, 2, HD, ROWS), BF),
             jax.ShapeDtypeStruct((8, ROWS, 2 * LANES), BF),
         ),
-        scratch=[
-            pltpu.VMEM((ALL, LANES), BF),
-            pltpu.VMEM((ALL, LANES), F32),
-            pltpu.VMEM((ALL, LANES), F32),
-        ],
-        scalars=1,
-        inputs=4,
+        scratch=[pltpu.VMEM((ALL, LANES), F32)] * 2,
+        inputs=3,
         flops=6 * 2 * ALL * ALL * LANES,
-    )(scalars, queries, keys, gathered, stats)
+    )(queries, keys, stats)
 
 
 GROUPS = 16
@@ -324,7 +292,7 @@
 
 
 def project_body(
-    sc_ref, all_ref, hidden_ref, w_ref, kv_ref, q_ref, normed_ref, unit_ref, inv_ref
+    sc_ref, all_ref, hidden_ref, w_ref, up_ref, kv_ref, q_ref, normed_ref, unit_ref, inv_ref
 ):
     total = jnp.zeros((HD, ROWS), F32)
     square = jnp.zeros((HD, ROWS), F32)
@@ -355,33 +323,43 @@
     for u in range(3):
         seg += jnp.where(pos >= sc_ref[1 + u], 1, 0)
     nil = jnp.zeros((ROWS, LANES - HD), BF)
-    q_ref[:, :HD] = projected[:, :HD]
-    q_ref[:, HD:] = jnp.where(seg == lane, 1.0, 0.0).astype(BF)
     k_mark = jnp.where(seg == lane, 0.0, FAR).astype(BF)
+    q_mark = jnp.where(seg == lane, 1.0, 0.0).astype(BF)
     for i in range(8):
+        q_ref[i, :, :HD] = projected[:, :HD]
+        q_ref[i, :, HD:LANES] = q_mark
+        q_ref[i, :, LANES : LANES + HD] = up_ref[...]
+        q_ref[i, :, LANES + HD :] = nil
         kv_ref[i, :, :HD] = projected[:, HD : 2 * HD]
         kv_ref[i, :, HD:LANES] = k_mark
         kv_ref[i, :, LANES : LANES + HD] = projected[:, 2 * HD :]
         kv_ref[i, :, LANES + HD :] = nil
 
 
-def project(scalars, all_t, hidden_t, w_qkv):
+def project(scalars, all_t, hidden_t, w_qkv, grad_out):
     return vmem_call(
         project_body,
         (
             jax.ShapeDtypeStruct((8, ROWS, 2 * LANES), BF),
-            jax.ShapeDtypeStruct((ROWS, LANES), BF),
+            jax.ShapeDtypeStruct((8, ROWS, 2 * LANES), BF),
             jax.ShapeDtypeStruct((GROUPS, HD, ROWS), BF),
             jax.ShapeDtypeStruct((2, HD, ROWS), F32),
             jax.ShapeDtypeStruct((1, ROWS), F32),
         ),
         scalars=1,
-        inputs=3,
+        inputs=4,
         flops=2 * ROWS * WIDTH * 3 * HD,
-    )(scalars, all_t, hidden_t, w_qkv)
-
-
-def share_body(od_ref, dkv_ref, normed_ref, w_ref, parts_ref, grad_ref, out_ref):
+    )(scalars, all_t, hidden_t, w_qkv, grad_out)
+
+
+def sums_of(plain, along):
+    plain_high = plain.astype(BF).astype(F32)
+    along_high = along.astype(BF).astype(F32)
+    rows = [plain_high, along_high, plain - plain_high, along - along_high]
+    return jnp.concatenate(rows + [jnp.zeros((4, ROWS), F32)], axis=0).astype(BF)
+
+
+def share_body(od_ref, dkv_ref, normed_ref, w_ref, parts_ref, wide_ref, out_ref, grad_ref):
     out, dq = od_ref[0, 0].astype(F32), od_ref[0, 1].astype(F32)
     for i in range(1, 8):
         out += od_ref[i, 0].astype(F32)
@@ -402,56 +380,54 @@
         )
         plain += share
         along += share * normed_ref[g].astype(F32)
-        parts_ref[g, :HD] = share.astype(BF)
+        parts_ref[g // 2 % 2, g // 4, g % 2, :HD] = share.astype(BF)
     plain = jnp.sum(plain, axis=0, keepdims=True)
     along = jnp.sum(along, axis=0, keepdims=True)
-    plain_high = plain.astype(BF).astype(F32)
-    along_high = along.astype(BF).astype(F32)
-    rows = [plain_high, along_high, plain - plain_high, along - along_high]
-    sums = jnp.concatenate(rows + [jnp.zeros((4, ROWS), F32)], axis=0).astype(BF)
+    sums = sums_of(plain, along)
     for g in range(GROUPS):
-        parts_ref[g, HD:] = sums
+        parts_ref[g // 2 % 2, g // 4, g % 2, HD:] = sums
+    slab = HD // 4
+    wide_ref[...] = jnp.zeros_like(wide_ref)
+    for g in range(GROUPS):
+        wide = jnp.dot(normed_ref[g], grad, preferred_element_type=F32)
+        for x in range(4):
+            wide_ref[g * 4 + x, :slab, : 3 * HD] = wide[x * slab : (x + 1) * slab].astype(BF)
 
 
 def shares(od, dkv, normed_t, w_qkv):
     return vmem_call(
         share_body,
         (
-            jax.ShapeDtypeStruct((GROUPS, LANES, ROWS), BF),
-            jax.ShapeDtypeStruct((ROWS, 3 * HD), BF),
+            jax.ShapeDtypeStruct((2, 4, 2, LANES, ROWS), BF),
+            jax.ShapeDtypeStruct((64, SLAB, 3 * LANES), BF),
             jax.ShapeDtypeStruct((ROWS, HD), BF),
         ),
+        scratch=[pltpu.VMEM((ROWS, 3 * HD), BF)],
         inputs=4,
-        flops=2 * ROWS * WIDTH * 3 * HD,
+        flops=4 * ROWS * WIDTH * 3 * HD,
     )(od, dkv, normed_t, w_qkv)
 
 
-def slabs_body(normed_ref, grad_ref, out_ref):
-    slab = HD // 4
-    grad = grad_ref[...]
-    out_ref[...] = jnp.zeros_like(out_ref)
-    for g in range(GROUPS):
-        wide = jnp.dot(normed_ref[g], grad, preferred_element_type=F32)
-        row = g % 8 * SLAB
-        for x in range(4):
-            piece = wide[x * slab : (x + 1) * slab].astype(BF)
-            out_ref[g // 8 * 4 + x, row : row + slab, : 3 * HD] = piece
-
-
-def slabs(normed_t, grad):
-    return vmem_call(
-        slabs_body,
-        jax.ShapeDtypeStruct((8, 8 * SLAB, 3 * LANES), BF),
-        inputs=2,
-        flops=2 * ROWS * WIDTH * 3 * HD,
-    )(normed_t, grad)
+def core_body(parts_ref, out_ref):
+    for h in range(4):
+        for g in range(2):
+            total = parts_ref[0, h, g].astype(F32) + parts_ref[1, h, g].astype(F32)
+            out_ref[h, g, :HD] = total[:HD].astype(BF)
+            if g == 0:
+                plain = total[HD : HD + 1] + total[HD + 2 : HD + 3]
+                along = total[HD + 1 : HD + 2] + total[HD + 3 : HD + 4]
+            out_ref[h, g, HD:] = sums_of(plain, along)
+
+
+def core_sum(parts):
+    return vmem_call(core_body, jax.ShapeDtypeStruct((4, 2, LANES, ROWS), BF), inputs=1)(parts)
 
 
 def error_body(parts_ref, unit_ref, inv_ref, slope_ref, grad_ref, error_ref):
     sums = []
     for g in range(2):
         total = parts_ref[0, g].astype(F32)
-        for i in range(1, 8):
+        for i in range(1, 4):
             total += parts_ref[i, g].astype(F32)
         sums.append(total)
     plain = (sums[0][HD : HD + 1] + sums[0][HD + 2 : HD + 3]) / WIDTH
@@ -476,47 +452,42 @@
 
 def on_device(frames, conv_weight, w_qkv, lengths, grad_out):
     index = lax.axis_index("tm")
-    y, x = index // 32, index % 4
     ends = jnp.cumsum(lengths).astype(jnp.int32)
 
     def scalars(*first):
         return jnp.concatenate([jnp.stack(first).astype(jnp.int32), ends])
 
-    where = scalars(y, index)
-    order = scalars(y * 4 + x)
+    where = scalars(index // 32, index)
 
     frames_g = frames.reshape(ROWS, 2, HD).transpose(1, 0, 2)
     frames_g = jnp.pad(frames_g, ((0, 0), (0, 0), (0, LANES - HD)))
-    upstream = jnp.pad(grad_out, ((0, 0), (0, LANES - HD)))
-    rows = with_halo(frames_g).reshape(2 * PADDED, LANES)
-    pair = paired(jnp.concatenate([rows, upstream], axis=0))
+    pair = paired(with_halo(frames_g).reshape(2 * PADDED, LANES))
     taps = exchange_z(taps_sent(conv_weight[0]))
-    taps = exchange_x(joined(taps, pair))
+    taps = exchange_x(joined(taps, pair, w_qkv, grad_out))
     own, other = convolved(True, where, pair, taps)
     hidden_t, slope_t, sent = hidden_rows(own, other, frames_g)
 
     all_t = lax.all_gather(sent, "head", axis=0, tiled=True)
     keys, queries, normed_t, unit_t, inv_std = project(
-        scalars(index), all_t, hidden_t, w_qkv
+        scalars(index), all_t, hidden_t, w_qkv, grad_out
     )
 
+    queries = exchange_xy(queries)
     keys = exchange_z(keys)
-    queries = doubled(queries)
-    stats = exchange_xy(everyone(attention_stats(order, queries, keys, taps)))
-    od, dkv = attention_grads(order, queries, keys, taps, stats)
+    stats = exchange_xy(attention_stats(queries, keys))
+    od, dkv = attention_grads(queries, keys, stats)
     od = exchange_xy(od)
     dkv = exchange_z(dkv)
 
-    parts, grad, attended = shares(od, dkv, normed_t, w_qkv)
-    parts = lax.all_to_all(parts.reshape(8, 2, LANES, ROWS), "head", 0, 0)
+    parts, wide, attended = shares(od, dkv, normed_t, w_qkv)
+    parts = core_sum(exchange_head(parts, CORE_GROUPS))
+    parts = exchange_head(parts, HIGH_GROUPS)
     hidden_grad, error = errors(parts, unit_t, inv_std, slope_t)
-    wide = exchange_xy(slabs(normed_t, grad))
-    wide = jnp.sum(wide.astype(F32), axis=0).astype(BF)
-
-    rows = after(with_halo(error).reshape(2 * PADDED, LANES), wide)
-    own, other = convolved(False, where, paired(rows), taps)
+
+    wide = lax.all_to_all(wide, "tm", 0, 0)
+    pair = paired(with_halo(error).reshape(2 * PADDED, LANES))
+    own, other = convolved(False, where, pair, taps)
     frame_grad = (hidden_grad + own + other.astype(F32)).astype(BF)[:, :, :HD]
-    wide = exchange_z(wide.reshape(8, SLAB, 3 * LANES))
     weight_grad = jnp.sum(wide[:, : HD // 4, : 3 * HD].astype(F32), axis=0)
     return attended, frame_grad.transpose(1, 0, 2).reshape(ROWS, 2 * HD), weight_grad
 

time: 245 us -> 258 us (1.053)
  the two profiles are of different devices: /device:TPU:8 before, /device:TPU:88 now
where the time goes in v7:
time: 258 us; the launch traced here: 257 us
  blocking collectives  113 us (44%)
  waiting for transfers between devices  71.9 us (28%)
  starting transfers between devices  46 us (18%)
  Pallas kernels  18.2 us (7%)
  local copies, waits for them, and re-layouts  6.23 us (2%)
    all_to_all x2, blocking collectives, exchange_z(): return lax.all_to_all(parts, 'tm', 0, 0, axis_index_groups=Z_GROUPS)  42.4 us
    ppermute x2, waiting for transfers between devices, with_halo(): before = lax.ppermute(rows[:, ROWS - HALF:], 'tm', up)  35.5 us
    all_to_all x3, blocking collectives, exchange_xy(): return lax.all_to_all(parts, 'tm', 0, 0, axis_index_groups=XY_GROUPS)  35 us
    all_to_all x1, waiting for transfers between devices, exchange_x(): return lax.all_to_all(parts, 'tm', 0, 0, axis_index_groups=X_GROUPS)  23.2 us
    all_to_all x2, blocking collectives, exchange_head(): return lax.all_to_all(parts, 'head', 0, 0, axis_index_groups=groups)  20.7 us
    all_gather x1, blocking collectives, on_device(): all_t = lax.all_gather(sent, 'head', axis=0, tiled=True)  14.9 us
    ppermute x4, waiting for transfers between devices, swap(): return lax.ppermute(array, 'tm', [(i, i ^ bit) for i in range(64)])  13.1 us
    all_to_all x1, starting transfers between devices, exchange_z(): return lax.all_to_all(parts, 'tm', 0, 0, axis_index_groups=Z_GROUPS)  9.96 us
  transfers between devices with their start and end apart: 11, of which 7 were waited for; matrix products, arithmetic and copies ran while one was open for 2% of the time, Pallas kernels for 2%

profile of v7, /device:TPU:88, one launch (start us, length us, event | category | flops | bytes accessed | tf_op | source)
XLA Modules:
  0.0 257.3 jit_solution(6029179983889635594)
XLA Ops:
  0.6 0.0 copy-start.1
  0.6 0.8 copy-done.1
  1.5 0.0 copy-start.2
  1.5 0.0 copy-start.3
  1.5 0.9 shard_map.76
  2.3 10.0 %all-to-all-start = ((bf16[8,256,128]{2,1,0:T(8,128)(2,1)}), bf16[8,256,128]{2,1,0:T(8,128)(2,1)S(1)}, u32[]{:S(2)}, u32[]{:S(2)}) async-start(bf16[8,256,128]{2,1,0:T(8,128)(2,1)} %shard_map.76), calls=%async_computation | async-start | bytes 1048576 | tf_op jit(solution)/shard_map/all_to_all | solution.py:46
  12.3 0.0 copy-done.2
  12.3 0.1 copy.22
  12.5 3.4 %collective-permute-start = (bf16[2,32,128]{2,1,0:T(8,128)(2,1)S(1)}, bf16[2,32,128]{2,1,0:T(8,128)(2,1)S(1)}, u32[]{:S(2)}, u32[]{:S(2)}) collective-permute-start(bf16[2,32,128]{2,1,0:T(8,128)(2,1)S(1)} %get-tuple-element.52), channel_id=1, source_target_pairs={{0,8},{8,16},{16,24},{24,32},{32,40},{40,48},{48,56},{56,64},{64,7... | collective-permute-start | bytes 49160 | tf_op jit(solution)/shard_map/ppermute | solution.py:168
  15.9 4.6 %collective-permute-start.1 = (bf16[2,32,128]{2,1,0:T(8,128)(2,1)S(1)}, bf16[2,32,128]{2,1,0:T(8,128)(2,1)S(1)}, u32[]{:S(2)}, u32[]{:S(2)}) collective-permute-start(bf16[2,32,128]{2,1,0:T(8,128)(2,1)S(1)} %get-tuple-element.53), channel_id=1, source_target_pairs={{8,0},{16,8},{24,16},{32,24},{40,32},{48,40},{56,48},{64,56},{72,6... | collective-permute-start | bytes 49160 | tf_op jit(solution)/shard_map/ppermute | solution.py:169
  20.5 4.9 %collective-permute-done = bf16[2,32,128]{2,1,0:T(8,128)(2,1)S(1)} collective-permute-done((bf16[2,32,128]{2,1,0:T(8,128)(2,1)S(1)}, bf16[2,32,128]{2,1,0:T(8,128)(2,1)S(1)}, u32[]{:S(2)}, u32[]{:S(2)}) %collective-permute-start) | collective-permute-done | bytes 16416 | tf_op jit(solution)/shard_map/ppermute | solution.py:168
  25.3 0.0 collective-permute-done.1
  25.3 2.4 collective-permute-start.2
  27.8 0.0 copy-done.3
  27.8 0.1 copy.24.up_ref
  27.9 2.4 copy.23.qkv_ref.w_ref
  30.3 1.6 collective-permute-done.2
  31.9 0.0 all-to-all-done.w_ref
  31.9 0.3 shard_map.77
  32.2 0.0 copy-start
  32.2 1.3 copy-done
  33.5 0.0 copy-start.4
  33.5 4.6 %all-to-all-start.1 = ((bf16[4,2048,128]{2,1,0:T(8,128)(2,1)}), bf16[4,2048,128]{2,1,0:T(8,128)(2,1)}, u32[]{:S(2)}, u32[]{:S(2)}) async-start(bf16[4,2048,128]{2,1,0:T(8,128)(2,1)} %copy-done), calls=%async_computation.1 | async-start | bytes 4194304 | tf_op jit(solution)/shard_map/all_to_all | solution.py:38
  38.1 0.0 copy-done.4
  38.1 0.2 reduce-window.9
  38.3 0.1 pad_add_fusion.1.sc_ref
  38.3 23.2 %all-to-all-done.1.w_ref = bf16[4,2048,128]{2,1,0:T(8,128)(2,1)} async-done(((bf16[4,2048,128]{2,1,0:T(8,128)(2,1)}), bf16[4,2048,128]{2,1,0:T(8,128)(2,1)}, u32[]{:S(2)}, u32[]{:S(2)}) %all-to-all-start.1) | async-done | bytes 2097184 | tf_op jit(solution)/shard_map/all_to_all | solution.py:38
  61.5 3.0 %shard_map.78 = (f32[2,128,128]{2,1,0:T(8,128)S(1)}, bf16[2,128,128]{2,1,0:T(8,128)(2,1)S(1)}) custom-call(s32[6]{0:T(128)S(1)} %pad_add_fusion.1.sc_ref, bf16[2,384,128]{2,1,0:T(8,128)(2,1)S(1)} %pad_maximum_fusion.pair_ref.x_ref, bf16[4,2048,128]{2,1,0:T(8,128)(2,1)} %all-to-all-done.1.w_ref), custom_call_target="tpu_custom_call" | custom-call | flops 471859200 | bytes 1048576 | tf_op jit(solution)/shard_map/pallas_call | solution.py:151
  64.6 2.5 collective-permute-start.3
  67.1 0.1 pad_add_fusion.sc_ref
  67.2 3.6 %collective-permute-done.3.other_ref = bf16[2,128,128]{2,1,0:T(8,128)(2,1)S(1)} collective-permute-done((bf16[2,128,128]{2,1,0:T(8,128)(2,1)S(1)}, bf16[2,128,128]{2,1,0:T(8,128)(2,1)S(1)}, u32[]{:S(2)}, u32[]{:S(2)}) %collective-permute-start.3) | collective-permute-done | bytes 65568 | tf_op jit(solution)/shard_map/ppermute | solution.py:42
  70.7 0.1 shard_map.79
  70.9 14.9 %all_gather.3.all_ref = bf16[16,120,128]{2,1,0:T(8,128)(2,1)S(1)} all-gather(bf16[2,120,128]{2,1,0:T(8,128)(2,1)S(1)} %get-tuple-element.24), channel_id=1, replica_groups=mesh['tm'=64,'head'=8] {'head'}, dimensions={0}, use_global_device_ids=true | all-gather | bytes 552960 | tf_op jit(solution)/shard_map/all_gather | solution.py:470
  85.7 1.6 shard_map.80
  87.4 13.8 %all_to_all.50.q_ref = bf16[8,128,256]{2,1,0:T(8,128)(2,1)S(1)} all-to-all(bf16[8,128,256]{2,1,0:T(8,128)(2,1)S(1)} %get-tuple-element.26), channel_id=1, replica_groups={{0,8,16,24,256,264,272,280},{32,40,48,56,288,296,304,312},{64,72,80,88,..., dimensions={0} | all-to-all | bytes 1048576 | tf_op jit(solution)/shard_map/all_to_all | solution.py:34
  101.2 26.2 %all_to_all.51.kv_ref = bf16[8,128,256]{2,1,0:T(8,128)(2,1)S(1)} all-to-all(bf16[8,128,256]{2,1,0:T(8,128)(2,1)S(1)} %get-tuple-element.27), channel_id=1, replica_groups={{0,32,64,96,128,160,192,224},{8,40,72,104,136,168,200,232},{16,48,80,11..., dimensions={0} | all-to-all | bytes 1048576 | tf_op jit(solution)/shard_map/all_to_all | solution.py:46
  127.5 1.9 shard_map.81
  129.4 10.2 %all_to_all.52.stats_ref = f32[8,3,8,128]{3,2,1,0:T(8,128)S(1)} all-to-all(f32[8,3,8,128]{3,2,1,0:T(8,128)S(1)} %shard_map.81), channel_id=1, replica_groups={{0,8,16,24,256,264,272,280},{32,40,48,56,288,296,304,312},{64,72,80,88,..., dimensions={0} | all-to-all | bytes 196608 | tf_op jit(solution)/shard_map/all_to_all | solution.py:34
  139.6 2.9 %shard_map.82 = (bf16[8,2,120,128]{3,2,1,0:T(8,128)(2,1)S(1)}, bf16[8,128,256]{2,1,0:T(8,128)(2,1)S(1)}) custom-call(bf16[8,128,256]{2,1,0:T(8,128)(2,1)S(1)} %all_to_all.50.q_ref, bf16[8,128,256]{2,1,0:T(8,128)(2,1)S(1)} %all_to_all.51.kv_ref, f32[8,3,8,128]{3,2,1,0:T(8,128)S(1)} %all_to_all.52.stats_ref), custom_call_target="tpu_custom_call" | custom-call | flops 1610612736 | bytes 1048576 | tf_op jit(solution)/shard_map/pallas_call | solution.py:254
  142.5 10.9 %all_to_all.53.od_ref = bf16[8,2,120,128]{3,2,1,0:T(8,128)(2,1)S(1)} all-to-all(bf16[8,2,120,128]{3,2,1,0:T(8,128)(2,1)S(1)} %get-tuple-element.28), channel_id=1, replica_groups={{0,8,16,24,256,264,272,280},{32,40,48,56,288,296,304,312},{64,72,80,88,..., dimensions={0} | all-to-all | bytes 983040 | tf_op jit(solution)/shard_map/all_to_all | solution.py:34
  153.4 16.1 %all_to_all.54.dkv_ref = bf16[8,128,256]{2,1,0:T(8,128)(2,1)S(1)} all-to-all(bf16[8,128,256]{2,1,0:T(8,128)(2,1)S(1)} %get-tuple-element.29), channel_id=1, replica_groups={{0,32,64,96,128,160,192,224},{8,40,72,104,136,168,200,232},{16,48,80,11..., dimensions={0} | all-to-all | bytes 1048576 | tf_op jit(solution)/shard_map/all_to_all | solution.py:46
  169.5 2.6 %shard_map.83 = (bf16[2,4,2,128,128]{4,3,2,1,0:T(8,128)(2,1)S(1)}, bf16[64,32,384]{2,1,0:T(8,128)(2,1)}, bf16[128,120]{1,0:T(8,128)(2,1)S(1)}) custom-call(bf16[8,2,120,128]{3,2,1,0:T(8,128)(2,1)S(1)} %all_to_all.53.od_ref, bf16[8,128,256]{2,1,0:T(8,128)(2,1)S(1)} %all_to_all.54.dkv_ref, bf16[16,120,128]{2,1,0:T(8,128)(2,1)S(1)} %get-tuple-element.30.normed_ref, ...), custom_call_target="tpu_custom_call" | custom-call | flops 353894400 | bytes 1048576 | tf_op jit(solution)/shard_map/pallas_call | solution.py:398
  172.1 4.1 %all_to_all.55.parts_ref = bf16[2,4,2,128,128]{4,3,2,1,0:T(8,128)(2,1)S(1)} all-to-all(bf16[2,4,2,128,128]{4,3,2,1,0:T(8,128)(2,1)S(1)} %get-tuple-element.32), channel_id=1, replica_groups={{0,1},{2,3},{4,5},{6,7},{8,9},{10,11},{12,13},{14,15},{16,17},{18,19},{..., dimensions={0} | all-to-all | bytes 1048576 | tf_op jit(solution)/shard_map/all_to_all | solution.py:50
  176.3 0.1 shard_map.84
  176.3 16.5 %all_to_all.56.parts_ref = bf16[4,2,128,128]{3,2,1,0:T(8,128)(2,1)S(1)} all-to-all(bf16[4,2,128,128]{3,2,1,0:T(8,128)(2,1)S(1)} %shard_map.84), channel_id=1, replica_groups={{0,2,4,6},{1,3,5,7},{8,10,12,14},{9,11,13,15},{16,18,20,22},{17,19,21,2..., dimensions={0} | all-to-all | bytes 524288 | tf_op jit(solution)/shard_map/all_to_all | solution.py:50
  192.9 6.7 %all-to-all-start.9 = ((bf16[64,32,384]{2,1,0:T(8,128)(2,1)}), bf16[64,32,384]{2,1,0:T(8,128)(2,1)S(1)}, u32[]{:S(2)}, u32[]{:S(2)}) async-start(bf16[64,32,384]{2,1,0:T(8,128)(2,1)} %get-tuple-element.40), calls=%async_computation.9 | async-start | bytes 3145728 | tf_op jit(solution)/shard_map/all_to_all | solution.py:487
  199.5 0.1 shard_map.85
  199.7 3.4 %collective-permute-start.4 = (bf16[2,32,128]{2,1,0:T(8,128)(2,1)S(1)}, bf16[2,32,128]{2,1,0:T(8,128)(2,1)S(1)}, u32[]{:S(2)}, u32[]{:S(2)}) collective-permute-start(bf16[2,32,128]{2,1,0:T(8,128)(2,1)S(1)} %get-tuple-element.51), channel_id=1, source_target_pairs={{0,8},{8,16},{16,24},{24,32},{32,40},{40,48},{48,56},{56,64},{64,7... | collective-permute-start | bytes 49160 | tf_op jit(solution)/shard_map/ppermute | solution.py:168
  203.1 4.6 %collective-permute-start.5 = (bf16[2,32,128]{2,1,0:T(8,128)(2,1)S(1)}, bf16[2,32,128]{2,1,0:T(8,128)(2,1)S(1)}, u32[]{:S(2)}, u32[]{:S(2)}) collective-permute-start(bf16[2,32,128]{2,1,0:T(8,128)(2,1)S(1)} %get-tuple-element.50), channel_id=1, source_target_pairs={{8,0},{16,8},{24,16},{32,24},{40,32},{48,40},{56,48},{64,56},{72,6... | collective-permute-start | bytes 49160 | tf_op jit(solution)/shard_map/ppermute | solution.py:169
  207.7 30.6 %collective-permute-done.4 = bf16[2,32,128]{2,1,0:T(8,128)(2,1)S(1)} collective-permute-done((bf16[2,32,128]{2,1,0:T(8,128)(2,1)S(1)}, bf16[2,32,128]{2,1,0:T(8,128)(2,1)S(1)}, u32[]{:S(2)}, u32[]{:S(2)}) %collective-permute-start.4) | collective-permute-done | bytes 16416 | tf_op jit(solution)/shard_map/ppermute | solution.py:168
  238.3 0.0 collective-permute-done.5
  238.4 1.9 collective-permute-start.6
  240.3 4.6 %collective-permute-done.6 = bf16[384,128]{1,0:T(8,128)(2,1)S(1)} collective-permute-done((bf16[384,128]{1,0:T(8,128)(2,1)S(1)}, bf16[384,128]{1,0:T(8,128)(2,1)S(1)}, u32[]{:S(2)}, u32[]{:S(2)}) %collective-permute-start.6) | collective-permute-done | bytes 98336 | tf_op jit(solution)/shard_map/ppermute | solution.py:42
  244.9 4.6 %shard_map.86 = (f32[2,128,128]{2,1,0:T(8,128)S(1)}, bf16[2,128,128]{2,1,0:T(8,128)(2,1)S(1)}) custom-call(s32[6]{0:T(128)S(1)} %pad_add_fusion.1.sc_ref, bf16[2,384,128]{2,1,0:T(8,128)(2,1)S(1)} %pad_maximum_fusion.1.x_ref, bf16[4,2048,128]{2,1,0:T(8,128)(2,1)} %all-to-all-done.1.w_ref), custom_call_target="tpu_custom_call" | custom-call | flops 471859200 | bytes 1048576 | tf_op jit(solution)/shard_map/pallas_call | solution.py:151
  249.5 2.0 collective-permute-start.7
  251.5 0.7 copy.29
  252.2 3.4 %collective-permute-done.7 = bf16[2,128,128]{2,1,0:T(8,128)(2,1)S(1)} collective-permute-done((bf16[2,128,128]{2,1,0:T(8,128)(2,1)S(1)}, bf16[2,128,128]{2,1,0:T(8,128)(2,1)S(1)}, u32[]{:S(2)}, u32[]{:S(2)}) %collective-permute-start.7) | collective-permute-done | bytes 65568 | tf_op jit(solution)/shard_map/ppermute | solution.py:42
  255.7 0.7 copy.28
  256.4 0.0 all-to-all-done.9
  256.4 0.9 convert_reduce_fusion
  (10 shorter events, 0.1 us)
Async XLA Ops:
  0.6 0.8 copy-start.1
  1.5 10.9 %copy-start.2 = (bf16[128,240]{0,1:T(8,128)(2,1)S(1)}, bf16[128,240]{0,1:T(8,128)(2,1)}, u32[]{:S(2)}) copy-start(bf16[128,240]{0,1:T(8,128)(2,1)} %param.5) | copy-start | bytes 184324
  1.5 26.3 %copy-start.3 = (bf16[128,120]{0,1:T(8,128)(2,1)S(1)}, bf16[128,120]{0,1:T(8,128)(2,1)}, u32[]{:S(2)}) copy-start(bf16[128,120]{0,1:T(8,128)(2,1)} %param.9) | copy-start | bytes 92164
  2.3 29.5 %all-to-all-start = ((bf16[8,256,128]{2,1,0:T(8,128)(2,1)}), bf16[8,256,128]{2,1,0:T(8,128)(2,1)S(1)}, u32[]{:S(2)}, u32[]{:S(2)}) async-start(bf16[8,256,128]{2,1,0:T(8,128)(2,1)} %shard_map.76), calls=%async_computation | async-start | bytes 1048576 | tf_op jit(solution)/shard_map/all_to_all | solution.py:46
  12.5 12.9 %collective-permute-start = (bf16[2,32,128]{2,1,0:T(8,128)(2,1)S(1)}, bf16[2,32,128]{2,1,0:T(8,128)(2,1)S(1)}, u32[]{:S(2)}, u32[]{:S(2)}) collective-permute-start(bf16[2,32,128]{2,1,0:T(8,128)(2,1)S(1)} %get-tuple-element.52), channel_id=1, source_target_pairs={{0,8},{8,16},{16,24},{24,32},{32,40},{40,48},{48,56},{56,64},{64,7... | collective-permute-start | bytes 49160 | tf_op jit(solution)/shard_map/ppermute | solution.py:168
  15.9 9.5 %collective-permute-start.1 = (bf16[2,32,128]{2,1,0:T(8,128)(2,1)S(1)}, bf16[2,32,128]{2,1,0:T(8,128)(2,1)S(1)}, u32[]{:S(2)}, u32[]{:S(2)}) collective-permute-start(bf16[2,32,128]{2,1,0:T(8,128)(2,1)S(1)} %get-tuple-element.53), channel_id=1, source_target_pairs={{8,0},{16,8},{24,16},{32,24},{40,32},{48,40},{56,48},{64,56},{72,6... | collective-permute-start | bytes 49160 | tf_op jit(solution)/shard_map/ppermute | solution.py:169
  25.3 6.5 %collective-permute-start.2 = (bf16[384,128]{1,0:T(8,128)(2,1)S(1)}, bf16[384,128]{1,0:T(8,128)(2,1)S(1)}, u32[]{:S(2)}, u32[]{:S(2)}) collective-permute-start(bf16[384,128]{1,0:T(8,128)(2,1)S(1)} %bitcast.19), channel_id=1, source_target_pairs={{0,256},{8,264},{16,272},{24,280},{32,288},{40,296},{48,304},{56,3... | collective-permute-start | bytes 294920 | tf_op jit(solution)/shard_map/ppermute | solution.py:42
  32.2 1.3 copy-start
  33.5 4.6 %copy-start.4 = (s32[4]{0:T(128)S(1)}, s32[4]{0:T(128)}, u32[]{:S(2)}) copy-start(s32[4]{0:T(128)} %param.8) | copy-start | bytes 52
  33.5 28.1 %all-to-all-start.1 = ((bf16[4,2048,128]{2,1,0:T(8,128)(2,1)}), bf16[4,2048,128]{2,1,0:T(8,128)(2,1)}, u32[]{:S(2)}, u32[]{:S(2)}) async-start(bf16[4,2048,128]{2,1,0:T(8,128)(2,1)} %copy-done), calls=%async_computation.1 | async-start | bytes 4194304 | tf_op jit(solution)/shard_map/all_to_all | solution.py:38
  64.6 6.2 %collective-permute-start.3 = (bf16[2,128,128]{2,1,0:T(8,128)(2,1)S(1)}, bf16[2,128,128]{2,1,0:T(8,128)(2,1)S(1)}, u32[]{:S(2)}, u32[]{:S(2)}) collective-permute-start(bf16[2,128,128]{2,1,0:T(8,128)(2,1)S(1)} %get-tuple-element.23), channel_id=1, source_target_pairs={{0,256},{8,264},{16,272},{24,280},{32,288},{40,296},{48,304},{56,3... | collective-permute-start | bytes 196616 | tf_op jit(solution)/shard_map/ppermute | solution.py:42
  192.9 63.5 %all-to-all-start.9 = ((bf16[64,32,384]{2,1,0:T(8,128)(2,1)}), bf16[64,32,384]{2,1,0:T(8,128)(2,1)S(1)}, u32[]{:S(2)}, u32[]{:S(2)}) async-start(bf16[64,32,384]{2,1,0:T(8,128)(2,1)} %get-tuple-element.40), calls=%async_computation.9 | async-start | bytes 3145728 | tf_op jit(solution)/shard_map/all_to_all | solution.py:487
  199.7 38.6 %collective-permute-start.4 = (bf16[2,32,128]{2,1,0:T(8,128)(2,1)S(1)}, bf16[2,32,128]{2,1,0:T(8,128)(2,1)S(1)}, u32[]{:S(2)}, u32[]{:S(2)}) collective-permute-start(bf16[2,32,128]{2,1,0:T(8,128)(2,1)S(1)} %get-tuple-element.51), channel_id=1, source_target_pairs={{0,8},{8,16},{16,24},{24,32},{32,40},{40,48},{48,56},{56,64},{64,7... | collective-permute-start | bytes 49160 | tf_op jit(solution)/shard_map/ppermute | solution.py:168
  203.1 35.2 %collective-permute-start.5 = (bf16[2,32,128]{2,1,0:T(8,128)(2,1)S(1)}, bf16[2,32,128]{2,1,0:T(8,128)(2,1)S(1)}, u32[]{:S(2)}, u32[]{:S(2)}) collective-permute-start(bf16[2,32,128]{2,1,0:T(8,128)(2,1)S(1)} %get-tuple-element.50), channel_id=1, source_target_pairs={{8,0},{16,8},{24,16},{32,24},{40,32},{48,40},{56,48},{64,56},{72,6... | collective-permute-start | bytes 49160 | tf_op jit(solution)/shard_map/ppermute | solution.py:169
  238.4 6.5 %collective-permute-start.6 = (bf16[384,128]{1,0:T(8,128)(2,1)S(1)}, bf16[384,128]{1,0:T(8,128)(2,1)S(1)}, u32[]{:S(2)}, u32[]{:S(2)}) collective-permute-start(bf16[384,128]{1,0:T(8,128)(2,1)S(1)} %bitcast.21), channel_id=1, source_target_pairs={{0,256},{8,264},{16,272},{24,280},{32,288},{40,296},{48,304},{56,3... | collective-permute-start | bytes 294920 | tf_op jit(solution)/shard_map/ppermute | solution.py:42
  249.5 6.2 %collective-permute-start.7 = (bf16[2,128,128]{2,1,0:T(8,128)(2,1)S(1)}, bf16[2,128,128]{2,1,0:T(8,128)(2,1)S(1)}, u32[]{:S(2)}, u32[]{:S(2)}) collective-permute-start(bf16[2,128,128]{2,1,0:T(8,128)(2,1)S(1)} %get-tuple-element.39), channel_id=1, source_target_pairs={{0,256},{8,264},{16,272},{24,280},{32,288},{40,296},{48,304},{56,3... | collective-permute-start | bytes 196616 | tf_op jit(solution)/shard_map/ppermute | solution.py:42

commit v8 on v6

--- a/solution.py
+++ b/solution.py
@@ -25,6 +25,8 @@
 
 XY_GROUPS = [[y * 32 + z * 4 + x for y in range(2) for x in range(4)] for z in range(8)]
 X_GROUPS = [[y * 32 + z * 4 + x for x in range(4)] for y in range(2) for z in range(8)]
+CORE_GROUPS = [[h * 2 + c for c in range(2)] for h in range(4)]
+HIGH_GROUPS = [[h * 2 + c for h in range(4)] for c in range(2)]
 Z_GROUPS = [[y * 32 + z * 4 + x for z in range(8)] for y in range(2) for x in range(4)]
 
 
@@ -44,12 +46,8 @@
     return lax.all_to_all(parts, "tm", 0, 0, axis_index_groups=Z_GROUPS)
 
 
-def everyone(array, count=8):
-    return jnp.broadcast_to(array[None], (count,) + array.shape)
-
-
-def after(array, earlier):
-    return array + 0 * earlier[(0,) * earlier.ndim].astype(array.dtype)
+def exchange_head(parts, groups):
+    return lax.all_to_all(parts, "head", 0, 0, axis_index_groups=groups)
 
 
 BITS = (32, 2, 1)
@@ -63,12 +61,13 @@
     return array
 
 
-def vmem_call(body, out_shape, scratch=(), scalars=0, inputs=0, flops=0):
+def vmem_call(body, out_shape, scratch=(), scalars=0, inputs=0, earlier=0, flops=0):
     return pl.pallas_call(
         body,
         out_shape=out_shape,
         in_specs=[pl.BlockSpec(memory_space=pltpu.SMEM)] * scalars
-        + [pl.BlockSpec(memory_space=pltpu.VMEM)] * inputs,
+        + [pl.BlockSpec(memory_space=pltpu.VMEM)] * inputs
+        + [pl.BlockSpec(memory_space=pl.ANY)] * earlier,
         out_specs=jax.tree.map(lambda _: pl.BlockSpec(memory_space=pltpu.VMEM), out_shape),
         scratch_shapes=list(scratch),
         compiler_params=pltpu.CompilerParams(vmem_limit_bytes=48 * 1024 * 1024),
@@ -91,7 +90,8 @@
 SPAN = ROWS + TAPS
 
 
-def conv_body(forward, sc_ref, x_ref, w_ref, own_ref, other_ref):
+def conv_body(forward, sc_ref, x_ref, w_ref, *refs):
+    own_ref, other_ref = refs[-2:]
     ends = [sc_ref[2 + u] for u in range(4)]
     first = TAPS * (sc_ref[0] if forward else 1 - sc_ref[0])
     row = lax.broadcasted_iota(jnp.int32, (ROWS, LANES), 0)
@@ -143,26 +143,46 @@
     )(weight)
 
 
-def joined_body(w_ref, pair_ref, out_ref):
+def joined_body(w_ref, own_ref, other_ref, qkv_ref, out_ref):
     for i in range(4):
         for z in range(8):
             out_ref[i, z * 2 * LANES : (z + 1) * 2 * LANES] = w_ref[z]
-        for b in range(2):
+        for b, rows_ref in enumerate((own_ref, other_ref)):
             start = 16 * LANES + b * ROWS
-            out_ref[i, start : start + ROWS] = pair_ref[b, 2 * PADDED :]
-
-
-def joined(taps, pair):
-    return vmem_call(
-        joined_body, jax.ShapeDtypeStruct((4, 16 * LANES + 2 * ROWS, LANES), BF), inputs=2
-    )(taps, pair)
-
-
-def paired(padded):
-    return jnp.stack([padded, swap(padded, 32)])
-
-
-def convolved(forward, scalars, pair, taps):
+            out_ref[i, start : start + ROWS] = rows_ref[...]
+
+
+def joined(taps, own, other, w_qkv):
+    return vmem_call(
+        joined_body,
+        jax.ShapeDtypeStruct((4, 16 * LANES + 2 * ROWS, LANES), BF),
+        inputs=3,
+        earlier=1,
+    )(taps, own, other, w_qkv)
+
+
+def paired(rows, more=None):
+    shards = range(64)
+    up = [(i, i + 1) for i in shards[:-1]]
+    down = [(i, i - 1) for i in shards[1:]]
+    last, head = rows[:, ROWS - HALF :], rows[:, :HALF]
+    sent = rows.reshape(2 * ROWS, LANES)
+    if more is not None:
+        sent = jnp.concatenate([sent, more], axis=0)
+    got = swap(sent, 32)
+    sides = [
+        [lax.ppermute(last, "tm", [(i, j ^ bit) for i, j in up]) for bit in (0, 32)],
+        [lax.ppermute(head, "tm", [(i, j ^ bit) for i, j in down]) for bit in (0, 32)],
+    ]
+    other = got[: 2 * ROWS].reshape(2, ROWS, LANES)
+    pair = [
+        jnp.concatenate([sides[0][b], middle, sides[1][b]], axis=1)
+        for b, middle in enumerate((rows, other))
+    ]
+    return jnp.stack(pair).reshape(2, 2 * PADDED, LANES), got[2 * ROWS :]
+
+
+def convolved(forward, scalars, pair, taps, *earlier):
     own, other = vmem_call(
         functools.partial(conv_body, forward),
         (
@@ -171,18 +191,10 @@
         ),
         scalars=1,
         inputs=2,
+        earlier=len(earlier),
         flops=32 * 2 * 2 * 2 * ROWS * HD * HD,
-    )(scalars, pair, taps)
+    )(scalars, pair, taps, *earlier)
     return own, swap(other, 32)
-
-
-def with_halo(rows):
-    devices = 64
-    up = [(i, i + 1) for i in range(devices - 1)]
-    down = [(i + 1, i) for i in range(devices - 1)]
-    before = lax.ppermute(rows[:, ROWS - HALF :], "tm", up)
-    after = lax.ppermute(rows[:, :HALF], "tm", down)
-    return jnp.concatenate([before, rows, after], axis=1)
 
 
 CHUNK = 256
@@ -221,7 +233,9 @@
             columns = slice(i * ROWS, (i + 1) * ROWS)
             shard = pl.ds(sc_ref[0] ^ SLOTS[c * N + i], 1)
             for j, value in enumerate((peak, total, along)):
-                out_ref[j, shard] = value[:, columns]
+                out_ref[0, j, shard] = value[:, columns]
+    for i in range(1, 8):
+        out_ref[i] = out_ref[0]
 
 
 def grads_body(
@@ -269,7 +283,7 @@
 def attention_stats(scalars, queries, keys, gathered):
     return vmem_call(
         stats_body,
-        jax.ShapeDtypeStruct((3, 8, ROWS), F32),
+        jax.ShapeDtypeStruct((8, 3, 8, ROWS), F32),
         scratch=[pltpu.VMEM((ALL, LANES), BF)],
         scalars=1,
         inputs=3,
@@ -381,7 +395,14 @@
     )(scalars, all_t, hidden_t, w_qkv)
 
 
-def share_body(od_ref, dkv_ref, normed_ref, w_ref, parts_ref, grad_ref, out_ref):
+def sums_of(plain, along):
+    plain_high = plain.astype(BF).astype(F32)
+    along_high = along.astype(BF).astype(F32)
+    rows = [plain_high, along_high, plain - plain_high, along - along_high]
+    return jnp.concatenate(rows + [jnp.zeros((4, ROWS), F32)], axis=0).astype(BF)
+
+
+def share_body(od_ref, dkv_ref, normed_ref, w_ref, parts_ref, wide_ref, out_ref, grad_ref):
     out, dq = od_ref[0, 0].astype(F32), od_ref[0, 1].astype(F32)
     for i in range(1, 8):
         out += od_ref[i, 0].astype(F32)
@@ -402,56 +423,71 @@
         )
         plain += share
         along += share * normed_ref[g].astype(F32)
-        parts_ref[g, :HD] = share.astype(BF)
+        parts_ref[g // 2 % 2, g // 4, g % 2, :HD] = share.astype(BF)
     plain = jnp.sum(plain, axis=0, keepdims=True)
     along = jnp.sum(along, axis=0, keepdims=True)
-    plain_high = plain.astype(BF).astype(F32)
-    along_high = along.astype(BF).astype(F32)
-    rows = [plain_high, along_high, plain - plain_high, along - along_high]
-    sums = jnp.concatenate(rows + [jnp.zeros((4, ROWS), F32)], axis=0).astype(BF)
+    sums = sums_of(plain, along)
     for g in range(GROUPS):
-        parts_ref[g, HD:] = sums
+        parts_ref[g // 2 % 2, g // 4, g % 2, HD:] = sums
+    slab = HD // 4
+    wide_ref[...] = jnp.zeros_like(wide_ref)
+    for g in range(GROUPS):
+        wide = jnp.dot(normed_ref[g], grad, preferred_element_type=F32)
+        for x in range(4):
+            piece = wide[x * slab : (x + 1) * slab].astype(BF)
+            row = g % 8 * SLAB
+            wide_ref[g // 8 * 4 + x, row : row + slab, : 3 * HD] = piece
 
 
 def shares(od, dkv, normed_t, w_qkv):
     return vmem_call(
         share_body,
         (
-            jax.ShapeDtypeStruct((GROUPS, LANES, ROWS), BF),
-            jax.ShapeDtypeStruct((ROWS, 3 * HD), BF),
+            jax.ShapeDtypeStruct((2, 4, 2, LANES, ROWS), BF),
+            jax.ShapeDtypeStruct((8, 8 * SLAB, 3 * LANES), BF),
             jax.ShapeDtypeStruct((ROWS, HD), BF),
         ),
+        scratch=[pltpu.VMEM((ROWS, 3 * HD), BF)],
         inputs=4,
-        flops=2 * ROWS * WIDTH * 3 * HD,
+        flops=4 * ROWS * WIDTH * 3 * HD,
     )(od, dkv, normed_t, w_qkv)
 
 
-def slabs_body(normed_ref, grad_ref, out_ref):
-    slab = HD // 4
-    grad = grad_ref[...]
-    out_ref[...] = jnp.zeros_like(out_ref)
-    for g in range(GROUPS):
-        wide = jnp.dot(normed_ref[g], grad, preferred_element_type=F32)
-        row = g % 8 * SLAB
-        for x in range(4):
-            piece = wide[x * slab : (x + 1) * slab].astype(BF)
-            out_ref[g // 8 * 4 + x, row : row + slab, : 3 * HD] = piece
-
-
-def slabs(normed_t, grad):
-    return vmem_call(
-        slabs_body,
-        jax.ShapeDtypeStruct((8, 8 * SLAB, 3 * LANES), BF),
-        inputs=2,
-        flops=2 * ROWS * WIDTH * 3 * HD,
-    )(normed_t, grad)
+def wide_body(wide_ref, out_ref):
+    for z in range(8):
+        rows = slice(z * SLAB, (z + 1) * SLAB)
+        total = wide_ref[0, rows].astype(F32)
+        for i in range(1, 8):
+            total += wide_ref[i, rows].astype(F32)
+        out_ref[z] = total.astype(BF)
+
+
+def wide_sum(wide):
+    return vmem_call(
+        wide_body, jax.ShapeDtypeStruct((8, SLAB, 3 * LANES), BF), inputs=1
+    )(wide)
+
+
+def core_body(parts_ref, out_ref):
+    for h in range(4):
+        for g in range(2):
+            total = parts_ref[0, h, g].astype(F32) + parts_ref[1, h, g].astype(F32)
+            out_ref[h, g, :HD] = total[:HD].astype(BF)
+            if g == 0:
+                plain = total[HD : HD + 1] + total[HD + 2 : HD + 3]
+                along = total[HD + 1 : HD + 2] + total[HD + 3 : HD + 4]
+            out_ref[h, g, HD:] = sums_of(plain, along)
+
+
+def core_sum(parts):
+    return vmem_call(core_body, jax.ShapeDtypeStruct((4, 2, LANES, ROWS), BF), inputs=1)(parts)
 
 
 def error_body(parts_ref, unit_ref, inv_ref, slope_ref, grad_ref, error_ref):
     sums = []
     for g in range(2):
         total = parts_ref[0, g].astype(F32)
-        for i in range(1, 8):
+        for i in range(1, 4):
             total += parts_ref[i, g].astype(F32)
         sums.append(total)
     plain = (sums[0][HD : HD + 1] + sums[0][HD + 2 : HD + 3]) / WIDTH
@@ -476,22 +512,21 @@
 
 def on_device(frames, conv_weight, w_qkv, lengths, grad_out):
     index = lax.axis_index("tm")
-    y, x = index // 32, index % 4
     ends = jnp.cumsum(lengths).astype(jnp.int32)
 
     def scalars(*first):
         return jnp.concatenate([jnp.stack(first).astype(jnp.int32), ends])
 
+    y, x = index // 32, index % 4
     where = scalars(y, index)
     order = scalars(y * 4 + x)
 
     frames_g = frames.reshape(ROWS, 2, HD).transpose(1, 0, 2)
     frames_g = jnp.pad(frames_g, ((0, 0), (0, 0), (0, LANES - HD)))
     upstream = jnp.pad(grad_out, ((0, 0), (0, LANES - HD)))
-    rows = with_halo(frames_g).reshape(2 * PADDED, LANES)
-    pair = paired(jnp.concatenate([rows, upstream], axis=0))
+    pair, other_upstream = paired(frames_g, upstream)
     taps = exchange_z(taps_sent(conv_weight[0]))
-    taps = exchange_x(joined(taps, pair))
+    taps = exchange_x(joined(taps, upstream, other_upstream, w_qkv))
     own, other = convolved(True, where, pair, taps)
     hidden_t, slope_t, sent = hidden_rows(own, other, frames_g)
 
@@ -502,21 +537,21 @@
 
     keys = exchange_z(keys)
     queries = doubled(queries)
-    stats = exchange_xy(everyone(attention_stats(order, queries, keys, taps)))
+    stats = exchange_xy(attention_stats(order, queries, keys, taps))
     od, dkv = attention_grads(order, queries, keys, taps, stats)
     od = exchange_xy(od)
     dkv = exchange_z(dkv)
 
-    parts, grad, attended = shares(od, dkv, normed_t, w_qkv)
-    parts = lax.all_to_all(parts.reshape(8, 2, LANES, ROWS), "head", 0, 0)
+    parts, wide, attended = shares(od, dkv, normed_t, w_qkv)
+    parts = core_sum(exchange_head(parts, CORE_GROUPS))
+    parts = exchange_head(parts, HIGH_GROUPS)
     hidden_grad, error = errors(parts, unit_t, inv_std, slope_t)
-    wide = exchange_xy(slabs(normed_t, grad))
-    wide = jnp.sum(wide.astype(F32), axis=0).astype(BF)
-
-    rows = after(with_halo(error).reshape(2 * PADDED, LANES), wide)
-    own, other = convolved(False, where, paired(rows), taps)
+
+    wide = wide_sum(exchange_xy(wide))
+    pair, _ = paired(error)
+    own, other = convolved(False, where, pair, taps, wide)
     frame_grad = (hidden_grad + own + other.astype(F32)).astype(BF)[:, :, :HD]
-    wide = exchange_z(wide.reshape(8, SLAB, 3 * LANES))
+    wide = exchange_z(wide)
     weight_grad = jnp.sum(wide[:, : HD // 4, : 3 * HD].astype(F32), axis=0)
     return attended, frame_grad.transpose(1, 0, 2).reshape(ROWS, 2 * HD), weight_grad
 

time: 245 us -> 234 us (0.955)
  waiting for transfers between devices: 73.6 us -> 49 us
  blocking collectives: 57.2 us -> 77.3 us
  local copies, waits for them, and re-layouts: 13.6 us -> 7.17 us
  other arithmetic: 4.34 us -> 1.15 us
  Pallas kernels: 15.7 us -> 18.8 us
    all_to_all x1, waiting for transfers between devices: 23.6 us -> 1.12 us  [exchange_x(): return lax.all_to_all(parts, 'tm', 0, 0, axis_index_groups=X_GROUPS)]
    all_to_all x0 -> x2, blocking collectives: none -> 20 us  [exchange_head(): return lax.all_to_all(parts, 'head', 0, 0, axis_index_groups=groups)]
    all_to_all x1 -> x0, waiting for transfers between devices: 15.8 us -> none  [on_device(): parts = lax.all_to_all(parts.reshape(8, 2, LANES, ROWS), 'head', 0, 0)]
    ppermute x4 -> x8, waiting for transfers between devices: 1.27 us -> 16.7 us  [the longest x4 14.5 us: paired(): lax.ppermute(last, 'tm', [(i, j ^ bit) for i, j in up])]
    all_to_all x3, waiting for transfers between devices: 0.01 us -> 10.7 us  [exchange_z(): return lax.all_to_all(parts, 'tm', 0, 0, axis_index_groups=Z_GROUPS)]
    all_to_all x1, waiting for transfers between devices: 8.85 us -> 0.01 us  [exchange_xy(): return lax.all_to_all(parts, 'tm', 0, 0, axis_index_groups=XY_GROUPS)]
    ppermute x4 -> x8, starting transfers between devices: 20.3 us -> 28.6 us  [the longest x4 16.8 us: paired(): lax.ppermute(head, 'tm', [(i, j ^ bit) for i, j in down])]
    unnamed x33 -> x25, local copies, waits for them, and re-layouts: 11.5 us -> 6.26 us
  transfers between devices with their start and end apart: 17 -> 20, of which waited for: 11 -> 12; matrix products, arithmetic and copies ran while one was open for 4% -> 2% of each run, Pallas kernels for 2% -> 2%
where the time goes in v8:
time: 234 us; the launch traced here: 233 us
  starting transfers between devices  78.3 us (33%)
  blocking collectives  77.3 us (33%)
  waiting for transfers between devices  49 us (21%)
  Pallas kernels  18.8 us (8%)
  local copies, waits for them, and re-layouts  7.17 us (3%)
    all_to_all x3, starting transfers between devices, exchange_z(): return lax.all_to_all(parts, 'tm', 0, 0, axis_index_groups=Z_GROUPS)  21.6 us
    ppermute x7, waiting for transfers between devices, swap(): return lax.ppermute(array, 'tm', [(i, i ^ bit) for i in range(64)])  20.4 us
    all_to_all x2, blocking collectives, exchange_xy(): return lax.all_to_all(parts, 'tm', 0, 0, axis_index_groups=XY_GROUPS)  20.3 us
    all_to_all x1, blocking collectives, exchange_z(): return lax.all_to_all(parts, 'tm', 0, 0, axis_index_groups=Z_GROUPS)  20.2 us
    all_to_all x2, blocking collectives, exchange_head(): return lax.all_to_all(parts, 'head', 0, 0, axis_index_groups=groups)  20 us
    ppermute x7, starting transfers between devices, swap(): return lax.ppermute(array, 'tm', [(i, i ^ bit) for i in range(64)])  18 us
    all_gather x1, blocking collectives, on_device(): all_t = lax.all_gather(sent, 'head', axis=0, tiled=True)  16.9 us
    ppermute x4, starting transfers between devices, paired(): lax.ppermute(head, 'tm', [(i, j ^ bit) for i, j in down])  16.8 us
  transfers between devices with their start and end apart: 20, of which 12 were waited for; matrix products, arithmetic and copies ran while one was open for 2% of the time, Pallas kernels for 2%

profile of v8, /device:TPU:8, one launch (start us, length us, event | category | flops | bytes accessed | tf_op | source)
XLA Modules:
  0.0 232.8 jit_solution(12841162250518974291)
XLA Ops:
  0.6 0.8 copy-done.7
  1.5 0.9 shard_map.76
  2.3 10.3 %all-to-all-start = ((bf16[8,256,128]{2,1,0:T(8,128)(2,1)}), bf16[8,256,128]{2,1,0:T(8,128)(2,1)S(1)}, u32[]{:S(2)}, u32[]{:S(2)}) async-start(bf16[8,256,128]{2,1,0:T(8,128)(2,1)} %shard_map.76), calls=%async_computation | async-start | bytes 1048576 | tf_op jit(solution)/shard_map/all_to_all | solution.py:46
  12.7 0.1 copy.21
  12.8 0.1 copy.20
  13.0 2.4 %collective-permute-start.3 = (bf16[384,128]{1,0:T(8,128)(2,1)S(1)}, bf16[384,128]{1,0:T(8,128)(2,1)S(1)}, u32[]{:S(2)}, u32[]{:S(2)}) collective-permute-start(bf16[384,128]{1,0:T(8,128)(2,1)S(1)} %pad_maximum_fusion.5), channel_id=1, source_target_pairs={{0,256},{8,264},{16,272},{24,280},{32,288},{40,296},{48,304},{56,3... | collective-permute-start | bytes 294920 | tf_op jit(solution)/shard_map/ppermute | solution.py:42
  15.3 2.4 %copy.22.qkv_ref.w_ref = bf16[1920,360]{1,0:T(8,128)(2,1)S(1)} copy(bf16[1920,360]{0,1:T(8,128)(2,1)} %param.7) | data formatting | bytes 2764800 | tf_op args[2]
  17.7 1.8 collective-permute-done.3
  19.5 10.7 %all-to-all-done.w_ref = bf16[8,256,128]{2,1,0:T(8,128)(2,1)S(1)} async-done(((bf16[8,256,128]{2,1,0:T(8,128)(2,1)}), bf16[8,256,128]{2,1,0:T(8,128)(2,1)S(1)}, u32[]{:S(2)}, u32[]{:S(2)}) %all-to-all-start) | async-done | bytes 524320 | tf_op jit(solution)/shard_map/all_to_all | solution.py:46
  30.2 0.2 shard_map.77
  30.3 1.4 copy-done.3
  31.8 4.4 %all-to-all-start.1 = ((bf16[4,2304,128]{2,1,0:T(8,128)(2,1)}), bf16[4,2304,128]{2,1,0:T(8,128)(2,1)S(1)}, u32[]{:S(2)}, u32[]{:S(2)}) async-start(bf16[4,2304,128]{2,1,0:T(8,128)(2,1)} %copy-done.3), calls=%async_computation.1 | async-start | bytes 4718592 | tf_op jit(solution)/shard_map/all_to_all | solution.py:38
  36.2 3.8 %collective-permute-start.2 = (bf16[2,32,128]{2,1,0:T(8,128)(2,1)S(1)}, bf16[2,32,128]{2,1,0:T(8,128)(2,1)S(1)}, u32[]{:S(2)}, u32[]{:S(2)}) collective-permute-start(bf16[2,32,128]{2,1,0:T(8,128)(2,1)S(1)} %get-tuple-element.52), channel_id=1, source_target_pairs={{0,264},{8,272},{16,280},{24,288},{32,296},{40,304},{48,312},{56,3... | collective-permute-start | bytes 49160 | tf_op jit(solution)/shard_map/ppermute | solution.py:174
  40.0 3.4 %collective-permute-start = (bf16[2,32,128]{2,1,0:T(8,128)(2,1)S(1)}, bf16[2,32,128]{2,1,0:T(8,128)(2,1)S(1)}, u32[]{:S(2)}, u32[]{:S(2)}) collective-permute-start(bf16[2,32,128]{2,1,0:T(8,128)(2,1)S(1)} %get-tuple-element.52), channel_id=1, source_target_pairs={{0,8},{8,16},{16,24},{24,32},{32,40},{40,48},{48,56},{56,64},{64,7... | collective-permute-start | bytes 49160 | tf_op jit(solution)/shard_map/ppermute | solution.py:174
  43.4 1.9 collective-permute-start.4
  45.3 6.1 %collective-permute-start.1 = (bf16[2,32,128]{2,1,0:T(8,128)(2,1)S(1)}, bf16[2,32,128]{2,1,0:T(8,128)(2,1)S(1)}, u32[]{:S(2)}, u32[]{:S(2)}) collective-permute-start(bf16[2,32,128]{2,1,0:T(8,128)(2,1)S(1)} %get-tuple-element.53), channel_id=1, source_target_pairs={{8,0},{16,8},{24,16},{32,24},{40,32},{48,40},{56,48},{64,56},{72,6... | collective-permute-start | bytes 49160 | tf_op jit(solution)/shard_map/ppermute | solution.py:175
  51.4 0.2 reduce-window.9
  51.6 0.1 pad_add_fusion.2.sc_ref
  51.7 10.9 %collective-permute-done = bf16[2,32,128]{2,1,0:T(8,128)(2,1)S(1)} collective-permute-done((bf16[2,32,128]{2,1,0:T(8,128)(2,1)S(1)}, bf16[2,32,128]{2,1,0:T(8,128)(2,1)S(1)}, u32[]{:S(2)}, u32[]{:S(2)}) %collective-permute-start) | collective-permute-done | bytes 16416 | tf_op jit(solution)/shard_map/ppermute | solution.py:174
  62.5 2.3 collective-permute-done.1
  64.8 0.0 collective-permute-done.2
  64.9 1.1 all-to-all-done.1.w_ref.f_ref
  66.0 1.9 shard_map.78
  68.0 2.4 %collective-permute-start.5 = (bf16[2,128,128]{2,1,0:T(8,128)(2,1)S(1)}, bf16[2,128,128]{2,1,0:T(8,128)(2,1)S(1)}, u32[]{:S(2)}, u32[]{:S(2)}) collective-permute-start(bf16[2,128,128]{2,1,0:T(8,128)(2,1)S(1)} %get-tuple-element.23), channel_id=1, source_target_pairs={{0,256},{8,264},{16,272},{24,280},{32,288},{40,296},{48,304},{56,3... | collective-permute-start | bytes 196616 | tf_op jit(solution)/shard_map/ppermute | solution.py:42
  70.3 0.1 pad_add_fusion.1
  70.4 3.7 %collective-permute-done.5.other_ref = bf16[2,128,128]{2,1,0:T(8,128)(2,1)S(1)} collective-permute-done((bf16[2,128,128]{2,1,0:T(8,128)(2,1)S(1)}, bf16[2,128,128]{2,1,0:T(8,128)(2,1)S(1)}, u32[]{:S(2)}, u32[]{:S(2)}) %collective-permute-start.5) | collective-permute-done | bytes 65568 | tf_op jit(solution)/shard_map/ppermute | solution.py:42
  74.1 0.1 shard_map.79
  74.3 16.9 %all_gather.3.all_ref = bf16[16,120,128]{2,1,0:T(8,128)(2,1)S(1)} all-gather(bf16[2,120,128]{2,1,0:T(8,128)(2,1)S(1)} %get-tuple-element.24), channel_id=1, replica_groups=mesh['tm'=64,'head'=8] {'head'}, dimensions={0}, use_global_device_ids=true | all-gather | bytes 552960 | tf_op jit(solution)/shard_map/all_gather | solution.py:533
  91.1 2.3 %shard_map.80 = (bf16[8,128,256]{2,1,0:T(8,128)(2,1)}, bf16[128,128]{1,0:T(8,128)(2,1)S(1)}, bf16[16,120,128]{2,1,0:T(8,128)(2,1)S(1)}, f32[2,120,128]{2,1,0:T(8,128)S(1)}, f32[1,128]{1,0:T(1,128)S(1)}) custom-call(s32[5]{0:T(128)S(1)} %get-tuple-element.54.sc_ref, bf16[16,120,128]{2,1,0:T(8,128)(2,1)S(1)} %all_gather.3.all_ref, ...), custom_call_target="tpu_custom_call" | custom-call | flops 176947200 | bytes 1048576 | tf_op jit(solution)/shard_map/pallas_call | solution.py:383
  93.5 0.8 copy-done.5
  94.3 3.5 %all-to-all-start.2 = ((bf16[8,128,256]{2,1,0:T(8,128)(2,1)}), bf16[8,128,256]{2,1,0:T(8,128)(2,1)S(1)}, u32[]{:S(2)}, u32[]{:S(2)}) async-start(bf16[8,128,256]{2,1,0:T(8,128)(2,1)} %get-tuple-element.27), calls=%async_computation.2 | async-start | bytes 1048576 | tf_op jit(solution)/shard_map/all_to_all | solution.py:46
  97.8 3.5 %collective-permute-start.6 = (bf16[1,128,128]{2,1,0:T(8,128)(2,1)S(1)}, bf16[1,128,128]{2,1,0:T(8,128)(2,1)S(1)}, u32[]{:S(2)}, u32[]{:S(2)}) collective-permute-start(bf16[1,128,128]{2,1,0:T(8,128)(2,1)S(1)} %bitcast.21), channel_id=1, source_target_pairs={{0,256},{8,264},{16,272},{24,280},{32,288},{40,296},{48,304},{56,3... | collective-permute-start | bytes 98312 | tf_op jit(solution)/shard_map/ppermute | solution.py:42
  101.3 2.3 collective-permute-done.6
  103.6 3.4 %collective-permute-start.7 = (bf16[2,128,128]{2,1,0:T(8,128)(2,1)S(1)}, bf16[2,128,128]{2,1,0:T(8,128)(2,1)S(1)}, u32[]{:S(2)}, u32[]{:S(2)}) collective-permute-start(bf16[2,128,128]{2,1,0:T(8,128)(2,1)S(1)} %pad_maximum_fusion.9), channel_id=1, source_target_pairs={{0,16},{8,24},{16,0},{24,8},{32,48},{40,56},{48,32},{56,40},{64,80... | collective-permute-start | bytes 196616 | tf_op jit(solution)/shard_map/ppermute | solution.py:42
  107.0 4.3 %collective-permute-done.7 = bf16[2,128,128]{2,1,0:T(8,128)(2,1)S(1)} collective-permute-done((bf16[2,128,128]{2,1,0:T(8,128)(2,1)S(1)}, bf16[2,128,128]{2,1,0:T(8,128)(2,1)S(1)}, u32[]{:S(2)}, u32[]{:S(2)}) %collective-permute-start.7) | collective-permute-done | bytes 65568 | tf_op jit(solution)/shard_map/ppermute | solution.py:42
  111.3 2.5 %collective-permute-start.8 = (bf16[4,128,128]{2,1,0:T(8,128)(2,1)S(1)}, bf16[4,128,128]{2,1,0:T(8,128)(2,1)S(1)}, u32[]{:S(2)}, u32[]{:S(2)}) collective-permute-start(bf16[4,128,128]{2,1,0:T(8,128)(2,1)S(1)} %pad_maximum_fusion.3), channel_id=1, source_target_pairs={{0,8},{8,0},{16,24},{24,16},{32,40},{40,32},{48,56},{56,48},{64,72... | collective-permute-start | bytes 393224 | tf_op jit(solution)/shard_map/ppermute | solution.py:42
  113.7 4.4 %collective-permute-done.8 = bf16[4,128,128]{2,1,0:T(8,128)(2,1)S(1)} collective-permute-done((bf16[4,128,128]{2,1,0:T(8,128)(2,1)S(1)}, bf16[4,128,128]{2,1,0:T(8,128)(2,1)S(1)}, u32[]{:S(2)}, u32[]{:S(2)}) %collective-permute-start.8) | collective-permute-done | bytes 131104 | tf_op jit(solution)/shard_map/ppermute | solution.py:42
  118.2 0.0 all-to-all-done.2.kv_ref
  118.2 2.5 %shard_map.81 = f32[8,3,8,128]{3,2,1,0:T(8,128)S(1)} custom-call(s32[5]{0:T(128)S(1)} %get-tuple-element.55.sc_ref, bf16[8,128,128]{2,1,0:T(8,128)(2,1)S(1)} %pad_maximum_fusion.q_ref, bf16[8,128,256]{2,1,0:T(8,128)(2,1)S(1)} %all-to-all-done.2.kv_ref, bf16[4,2304,128]{2,1,0:T(8,128)(2,1)S(1)} %all-to-all-done.1.w_ref.f_ref), custom_call_target="tpu_custom_call" | custom-call | flops 536870912 | bytes 1048576 | tf_op jit(solution)/shard_map/pallas_call | solution.py:284
  120.6 9.2 %all_to_all.50.stats_ref = f32[8,3,8,128]{3,2,1,0:T(8,128)S(1)} all-to-all(f32[8,3,8,128]{3,2,1,0:T(8,128)S(1)} %shard_map.81), channel_id=1, replica_groups={{0,8,16,24,256,264,272,280},{32,40,48,56,288,296,304,312},{64,72,80,88,..., dimensions={0} | all-to-all | bytes 196608 | tf_op jit(solution)/shard_map/all_to_all | solution.py:34
  129.9 3.5 %shard_map.82 = (bf16[8,2,120,128]{3,2,1,0:T(8,128)(2,1)S(1)}, bf16[8,128,256]{2,1,0:T(8,128)(2,1)S(1)}) custom-call(s32[5]{0:T(128)S(1)} %get-tuple-element.55.sc_ref, bf16[8,128,128]{2,1,0:T(8,128)(2,1)S(1)} %pad_maximum_fusion.q_ref, bf16[8,128,256]{2,1,0:T(8,128)(2,1)S(1)} %all-to-all-done.2.kv_ref, ...), custom_call_target="tpu_custom_call" | custom-call | flops 1610612736 | bytes 1048576 | tf_op jit(solution)/shard_map/pallas_call | solution.py:295
  133.4 11.0 %all_to_all.51.od_ref = bf16[8,2,120,128]{3,2,1,0:T(8,128)(2,1)S(1)} all-to-all(bf16[8,2,120,128]{3,2,1,0:T(8,128)(2,1)S(1)} %get-tuple-element.28), channel_id=1, replica_groups={{0,8,16,24,256,264,272,280},{32,40,48,56,288,296,304,312},{64,72,80,88,..., dimensions={0} | all-to-all | bytes 983040 | tf_op jit(solution)/shard_map/all_to_all | solution.py:34
  144.4 20.2 %all_to_all.52.dkv_ref = bf16[8,128,256]{2,1,0:T(8,128)(2,1)S(1)} all-to-all(bf16[8,128,256]{2,1,0:T(8,128)(2,1)S(1)} %get-tuple-element.29), channel_id=1, replica_groups={{0,32,64,96,128,160,192,224},{8,40,72,104,136,168,200,232},{16,48,80,11..., dimensions={0} | all-to-all | bytes 1048576 | tf_op jit(solution)/shard_map/all_to_all | solution.py:46
  164.6 1.4 shard_map.83
  166.1 4.2 %all_to_all.53.parts_ref = bf16[2,4,2,128,128]{4,3,2,1,0:T(8,128)(2,1)S(1)} all-to-all(bf16[2,4,2,128,128]{4,3,2,1,0:T(8,128)(2,1)S(1)} %get-tuple-element.32), channel_id=1, replica_groups={{0,1},{2,3},{4,5},{6,7},{8,9},{10,11},{12,13},{14,15},{16,17},{18,19},{..., dimensions={0} | all-to-all | bytes 1048576 | tf_op jit(solution)/shard_map/all_to_all | solution.py:50
  170.2 0.1 shard_map.84
  170.3 15.8 %all_to_all.54.parts_ref = bf16[4,2,128,128]{3,2,1,0:T(8,128)(2,1)S(1)} all-to-all(bf16[4,2,128,128]{3,2,1,0:T(8,128)(2,1)S(1)} %shard_map.84), channel_id=1, replica_groups={{0,2,4,6},{1,3,5,7},{8,10,12,14},{9,11,13,15},{16,18,20,22},{17,19,21,2..., dimensions={0} | all-to-all | bytes 524288 | tf_op jit(solution)/shard_map/all_to_all | solution.py:50
  186.1 5.6 %all-to-all-start.8 = ((bf16[8,256,384]{2,1,0:T(8,128)(2,1)}), bf16[8,256,384]{2,1,0:T(8,128)(2,1)}, u32[]{:S(2)}, u32[]{:S(2)}) async-start(bf16[8,256,384]{2,1,0:T(8,128)(2,1)} %copy-done.4), calls=%async_computation.8 | async-start | bytes 3145728 | tf_op jit(solution)/shard_map/all_to_all | solution.py:34
  191.7 0.1 shard_map.85
  191.9 3.4 %collective-permute-start.9 = (bf16[2,32,128]{2,1,0:T(8,128)(2,1)S(1)}, bf16[2,32,128]{2,1,0:T(8,128)(2,1)S(1)}, u32[]{:S(2)}, u32[]{:S(2)}) collective-permute-start(bf16[2,32,128]{2,1,0:T(8,128)(2,1)S(1)} %get-tuple-element.50), channel_id=1, source_target_pairs={{0,8},{8,16},{16,24},{24,32},{32,40},{40,48},{48,56},{56,64},{64,7... | collective-permute-start | bytes 49160 | tf_op jit(solution)/shard_map/ppermute | solution.py:174
  195.3 6.9 %collective-permute-start.10 = (bf16[2,32,128]{2,1,0:T(8,128)(2,1)S(1)}, bf16[2,32,128]{2,1,0:T(8,128)(2,1)S(1)}, u32[]{:S(2)}, u32[]{:S(2)}) collective-permute-start(bf16[2,32,128]{2,1,0:T(8,128)(2,1)S(1)} %get-tuple-element.51), channel_id=1, source_target_pairs={{8,0},{16,8},{24,16},{32,24},{40,32},{48,40},{56,48},{64,56},{72,6... | collective-permute-start | bytes 49160 | tf_op jit(solution)/shard_map/ppermute | solution.py:175
  202.1 1.3 collective-permute-start.11
  203.4 1.9 collective-permute-start.13
  205.4 1.9 collective-permute-start.12
  207.3 3.6 %collective-permute-done.9 = bf16[2,32,128]{2,1,0:T(8,128)(2,1)S(1)} collective-permute-done((bf16[2,32,128]{2,1,0:T(8,128)(2,1)S(1)}, bf16[2,32,128]{2,1,0:T(8,128)(2,1)S(1)}, u32[]{:S(2)}, u32[]{:S(2)}) %collective-permute-start.9) | collective-permute-done | bytes 16416 | tf_op jit(solution)/shard_map/ppermute | solution.py:174
  210.9 0.6 collective-permute-done.12
  211.5 2.3 shard_map.86.refs_0_
  213.8 7.8 %all-to-all-start.9 = ((bf16[8,32,384]{2,1,0:T(8,128)(2,1)}), bf16[8,32,384]{2,1,0:T(8,128)(2,1)S(1)}, u32[]{:S(2)}, u32[]{:S(2)}) async-start(bf16[8,32,384]{2,1,0:T(8,128)(2,1)} %shard_map.86.refs_0_), calls=%async_computation.9 | async-start | bytes 393216 | tf_op jit(solution)/shard_map/all_to_all | solution.py:46
  221.7 3.5 %shard_map.87 = (f32[2,128,128]{2,1,0:T(8,128)S(1)}, bf16[2,128,128]{2,1,0:T(8,128)(2,1)S(1)}) custom-call(s32[6]{0:T(128)S(1)} %pad_add_fusion.2.sc_ref, bf16[2,384,128]{2,1,0:T(8,128)(2,1)S(1)} %pad_maximum_fusion.2.x_ref, bf16[4,2304,128]{2,1,0:T(8,128)(2,1)S(1)} %all-to-all-done.1.w_ref.f_ref, bf16[8,32,384]{2,1,0:T(8,128)(2,1)} %shard_map.86.refs_0_), custom_call_target="tpu_custom_call" | custom-call | flops 471859200 | bytes 1048576 | tf_op jit(solution)/shard_map/pallas_call | solution.py:186
  225.2 2.0 collective-permute-start.14
  227.2 0.7 copy.26
  227.9 3.4 %collective-permute-done.14 = bf16[2,128,128]{2,1,0:T(8,128)(2,1)S(1)} collective-permute-done((bf16[2,128,128]{2,1,0:T(8,128)(2,1)S(1)}, bf16[2,128,128]{2,1,0:T(8,128)(2,1)S(1)}, u32[]{:S(2)}, u32[]{:S(2)}) %collective-permute-start.14) | collective-permute-done | bytes 65568 | tf_op jit(solution)/shard_map/ppermute | solution.py:42
  231.4 0.7 copy.25
  232.1 0.7 convert_reduce_fusion
  (42 shorter events, 0.3 us)
Async XLA Ops:
  0.6 0.8 copy-start.7
  1.5 11.2 %copy-start.9 = (bf16[128,120]{0,1:T(8,128)(2,1)S(1)}, bf16[128,120]{0,1:T(8,128)(2,1)}, u32[]{:S(2)}) copy-start(bf16[128,120]{0,1:T(8,128)(2,1)} %param.9) | copy-start | bytes 92164
  1.5 11.3 %copy-start.8 = (bf16[128,240]{0,1:T(8,128)(2,1)S(1)}, bf16[128,240]{0,1:T(8,128)(2,1)}, u32[]{:S(2)}) copy-start(bf16[128,240]{0,1:T(8,128)(2,1)} %param.5) | copy-start | bytes 184324
  2.3 27.8 %all-to-all-start = ((bf16[8,256,128]{2,1,0:T(8,128)(2,1)}), bf16[8,256,128]{2,1,0:T(8,128)(2,1)S(1)}, u32[]{:S(2)}, u32[]{:S(2)}) async-start(bf16[8,256,128]{2,1,0:T(8,128)(2,1)} %shard_map.76), calls=%async_computation | async-start | bytes 1048576 | tf_op jit(solution)/shard_map/all_to_all | solution.py:46
  13.0 6.5 %collective-permute-start.3 = (bf16[384,128]{1,0:T(8,128)(2,1)S(1)}, bf16[384,128]{1,0:T(8,128)(2,1)S(1)}, u32[]{:S(2)}, u32[]{:S(2)}) collective-permute-start(bf16[384,128]{1,0:T(8,128)(2,1)S(1)} %pad_maximum_fusion.5), channel_id=1, source_target_pairs={{0,256},{8,264},{16,272},{24,280},{32,288},{40,296},{48,304},{56,3... | collective-permute-start | bytes 294920 | tf_op jit(solution)/shard_map/ppermute | solution.py:42
  17.7 12.6 %copy-start = (bf16[1920,360]{1,0:T(8,128)(2,1)}, bf16[1920,360]{1,0:T(8,128)(2,1)S(1)}, u32[]{:S(2)}) copy-start(bf16[1920,360]{1,0:T(8,128)(2,1)S(1)} %copy.22.qkv_ref.w_ref) | copy-start | bytes 4147204
  30.3 1.4 copy-start.3
  31.7 19.6 %copy-start.10 = (s32[4]{0:T(128)S(1)}, s32[4]{0:T(128)}, u32[]{:S(2)}) copy-start(s32[4]{0:T(128)} %param.8) | copy-start | bytes 52
  31.8 34.3 %all-to-all-start.1 = ((bf16[4,2304,128]{2,1,0:T(8,128)(2,1)}), bf16[4,2304,128]{2,1,0:T(8,128)(2,1)S(1)}, u32[]{:S(2)}, u32[]{:S(2)}) async-start(bf16[4,2304,128]{2,1,0:T(8,128)(2,1)} %copy-done.3), calls=%async_computation.1 | async-start | bytes 4718592 | tf_op jit(solution)/shard_map/all_to_all | solution.py:38
  36.2 28.7 %collective-permute-start.2 = (bf16[2,32,128]{2,1,0:T(8,128)(2,1)S(1)}, bf16[2,32,128]{2,1,0:T(8,128)(2,1)S(1)}, u32[]{:S(2)}, u32[]{:S(2)}) collective-permute-start(bf16[2,32,128]{2,1,0:T(8,128)(2,1)S(1)} %get-tuple-element.52), channel_id=1, source_target_pairs={{0,264},{8,272},{16,280},{24,288},{32,296},{40,304},{48,312},{56,3... | collective-permute-start | bytes 49160 | tf_op jit(solution)/shard_map/ppermute | solution.py:174
  40.0 22.5 %collective-permute-start = (bf16[2,32,128]{2,1,0:T(8,128)(2,1)S(1)}, bf16[2,32,128]{2,1,0:T(8,128)(2,1)S(1)}, u32[]{:S(2)}, u32[]{:S(2)}) collective-permute-start(bf16[2,32,128]{2,1,0:T(8,128)(2,1)S(1)} %get-tuple-element.52), channel_id=1, source_target_pairs={{0,8},{8,16},{16,24},{24,32},{32,40},{40,48},{48,56},{56,64},{64,7... | collective-permute-start | bytes 49160 | tf_op jit(solution)/shard_map/ppermute | solution.py:174
  43.4 21.5 %collective-permute-start.4 = (bf16[2,32,128]{2,1,0:T(8,128)(2,1)S(1)}, bf16[2,32,128]{2,1,0:T(8,128)(2,1)S(1)}, u32[]{:S(2)}, u32[]{:S(2)}) collective-permute-start(bf16[2,32,128]{2,1,0:T(8,128)(2,1)S(1)} %get-tuple-element.53), channel_id=1, source_target_pairs={{8,256},{16,264},{24,272},{32,280},{40,288},{48,296},{56,304},{64,... | collective-permute-start | bytes 49160 | tf_op jit(solution)/shard_map/ppermute | solution.py:175
  45.3 19.5 %collective-permute-start.1 = (bf16[2,32,128]{2,1,0:T(8,128)(2,1)S(1)}, bf16[2,32,128]{2,1,0:T(8,128)(2,1)S(1)}, u32[]{:S(2)}, u32[]{:S(2)}) collective-permute-start(bf16[2,32,128]{2,1,0:T(8,128)(2,1)S(1)} %get-tuple-element.53), channel_id=1, source_target_pairs={{8,0},{16,8},{24,16},{32,24},{40,32},{48,40},{56,48},{64,56},{72,6... | collective-permute-start | bytes 49160 | tf_op jit(solution)/shard_map/ppermute | solution.py:175
  66.0 25.1 %copy-start.1 = (bf16[1920,360]{1,0:T(8,128)(2,1)S(1)}, bf16[1920,360]{1,0:T(8,128)(2,1)}, u32[]{:S(2)}) copy-start(bf16[1920,360]{1,0:T(8,128)(2,1)} %copy-done) | copy-start | bytes 4147204
  68.0 6.2 %collective-permute-start.5 = (bf16[2,128,128]{2,1,0:T(8,128)(2,1)S(1)}, bf16[2,128,128]{2,1,0:T(8,128)(2,1)S(1)}, u32[]{:S(2)}, u32[]{:S(2)}) collective-permute-start(bf16[2,128,128]{2,1,0:T(8,128)(2,1)S(1)} %get-tuple-element.23), channel_id=1, source_target_pairs={{0,256},{8,264},{16,272},{24,280},{32,288},{40,296},{48,304},{56,3... | collective-permute-start | bytes 196616 | tf_op jit(solution)/shard_map/ppermute | solution.py:42
  93.5 0.8 copy-start.5
  94.3 23.9 %all-to-all-start.2 = ((bf16[8,128,256]{2,1,0:T(8,128)(2,1)}), bf16[8,128,256]{2,1,0:T(8,128)(2,1)S(1)}, u32[]{:S(2)}, u32[]{:S(2)}) async-start(bf16[8,128,256]{2,1,0:T(8,128)(2,1)} %get-tuple-element.27), calls=%async_computation.2 | async-start | bytes 1048576 | tf_op jit(solution)/shard_map/all_to_all | solution.py:46
  97.8 5.8 %collective-permute-start.6 = (bf16[1,128,128]{2,1,0:T(8,128)(2,1)S(1)}, bf16[1,128,128]{2,1,0:T(8,128)(2,1)S(1)}, u32[]{:S(2)}, u32[]{:S(2)}) collective-permute-start(bf16[1,128,128]{2,1,0:T(8,128)(2,1)S(1)} %bitcast.21), channel_id=1, source_target_pairs={{0,256},{8,264},{16,272},{24,280},{32,288},{40,296},{48,304},{56,3... | collective-permute-start | bytes 98312 | tf_op jit(solution)/shard_map/ppermute | solution.py:42
  103.6 7.7 %collective-permute-start.7 = (bf16[2,128,128]{2,1,0:T(8,128)(2,1)S(1)}, bf16[2,128,128]{2,1,0:T(8,128)(2,1)S(1)}, u32[]{:S(2)}, u32[]{:S(2)}) collective-permute-start(bf16[2,128,128]{2,1,0:T(8,128)(2,1)S(1)} %pad_maximum_fusion.9), channel_id=1, source_target_pairs={{0,16},{8,24},{16,0},{24,8},{32,48},{40,56},{48,32},{56,40},{64,80... | collective-permute-start | bytes 196616 | tf_op jit(solution)/shard_map/ppermute | solution.py:42
  111.3 6.9 %collective-permute-start.8 = (bf16[4,128,128]{2,1,0:T(8,128)(2,1)S(1)}, bf16[4,128,128]{2,1,0:T(8,128)(2,1)S(1)}, u32[]{:S(2)}, u32[]{:S(2)}) collective-permute-start(bf16[4,128,128]{2,1,0:T(8,128)(2,1)S(1)} %pad_maximum_fusion.3), channel_id=1, source_target_pairs={{0,8},{8,0},{16,24},{24,16},{32,40},{40,32},{48,56},{56,48},{64,72... | collective-permute-start | bytes 393224 | tf_op jit(solution)/shard_map/ppermute | solution.py:42
  133.4 31.3 %copy-start.2 = (bf16[1920,360]{1,0:T(8,128)(2,1)S(1)}, bf16[1920,360]{1,0:T(8,128)(2,1)}, u32[]{:S(2)}) copy-start(bf16[1920,360]{1,0:T(8,128)(2,1)} %copy-done) | copy-start | bytes 4147204
  133.4 31.3 %copy-start.6 = (bf16[16,120,128]{2,1,0:T(8,128)(2,1)S(1)}, bf16[16,120,128]{2,1,0:T(8,128)(2,1)}, u32[]{:S(2)}) copy-start(bf16[16,120,128]{2,1,0:T(8,128)(2,1)} %copy-done.5) | copy-start | bytes 1474564
  166.1 20.0 %copy-start.4 = (bf16[8,256,384]{2,1,0:T(8,128)(2,1)}, bf16[8,256,384]{2,1,0:T(8,128)(2,1)S(1)}, u32[]{:S(2)}) copy-start(bf16[8,256,384]{2,1,0:T(8,128)(2,1)S(1)} %get-tuple-element.38) | copy-start | bytes 4718596
  186.1 25.5 %all-to-all-start.8 = ((bf16[8,256,384]{2,1,0:T(8,128)(2,1)}), bf16[8,256,384]{2,1,0:T(8,128)(2,1)}, u32[]{:S(2)}, u32[]{:S(2)}) async-start(bf16[8,256,384]{2,1,0:T(8,128)(2,1)} %copy-done.4), calls=%async_computation.8 | async-start | bytes 3145728 | tf_op jit(solution)/shard_map/all_to_all | solution.py:34
  191.9 19.0 %collective-permute-start.9 = (bf16[2,32,128]{2,1,0:T(8,128)(2,1)S(1)}, bf16[2,32,128]{2,1,0:T(8,128)(2,1)S(1)}, u32[]{:S(2)}, u32[]{:S(2)}) collective-permute-start(bf16[2,32,128]{2,1,0:T(8,128)(2,1)S(1)} %get-tuple-element.50), channel_id=1, source_target_pairs={{0,8},{8,16},{16,24},{24,32},{32,40},{40,48},{48,56},{56,64},{64,7... | collective-permute-start | bytes 49160 | tf_op jit(solution)/shard_map/ppermute | solution.py:174
  195.3 15.6 %collective-permute-start.10 = (bf16[2,32,128]{2,1,0:T(8,128)(2,1)S(1)}, bf16[2,32,128]{2,1,0:T(8,128)(2,1)S(1)}, u32[]{:S(2)}, u32[]{:S(2)}) collective-permute-start(bf16[2,32,128]{2,1,0:T(8,128)(2,1)S(1)} %get-tuple-element.51), channel_id=1, source_target_pairs={{8,0},{16,8},{24,16},{32,24},{40,32},{48,40},{56,48},{64,56},{72,6... | collective-permute-start | bytes 49160 | tf_op jit(solution)/shard_map/ppermute | solution.py:175
  202.1 8.7 %collective-permute-start.11 = (bf16[2,32,128]{2,1,0:T(8,128)(2,1)S(1)}, bf16[2,32,128]{2,1,0:T(8,128)(2,1)S(1)}, u32[]{:S(2)}, u32[]{:S(2)}) collective-permute-start(bf16[2,32,128]{2,1,0:T(8,128)(2,1)S(1)} %get-tuple-element.50), channel_id=1, source_target_pairs={{0,264},{8,272},{16,280},{24,288},{32,296},{40,304},{48,312},{56,3... | collective-permute-start | bytes 49160 | tf_op jit(solution)/shard_map/ppermute | solution.py:174
  203.4 7.5 %collective-permute-start.13 = (bf16[2,32,128]{2,1,0:T(8,128)(2,1)S(1)}, bf16[2,32,128]{2,1,0:T(8,128)(2,1)S(1)}, u32[]{:S(2)}, u32[]{:S(2)}) collective-permute-start(bf16[2,32,128]{2,1,0:T(8,128)(2,1)S(1)} %get-tuple-element.51), channel_id=1, source_target_pairs={{8,256},{16,264},{24,272},{32,280},{40,288},{48,296},{56,304},{64,... | collective-permute-start | bytes 49160 | tf_op jit(solution)/shard_map/ppermute | solution.py:175
  205.4 6.2 %collective-permute-start.12 = (bf16[256,128]{1,0:T(8,128)(2,1)S(1)}, bf16[256,128]{1,0:T(8,128)(2,1)S(1)}, u32[]{:S(2)}, u32[]{:S(2)}) collective-permute-start(bf16[256,128]{1,0:T(8,128)(2,1)S(1)} %bitcast.25), channel_id=1, source_target_pairs={{0,256},{8,264},{16,272},{24,280},{32,288},{40,296},{48,304},{56,3... | collective-permute-start | bytes 196616 | tf_op jit(solution)/shard_map/ppermute | solution.py:42
  213.8 18.3 %all-to-all-start.9 = ((bf16[8,32,384]{2,1,0:T(8,128)(2,1)}), bf16[8,32,384]{2,1,0:T(8,128)(2,1)S(1)}, u32[]{:S(2)}, u32[]{:S(2)}) async-start(bf16[8,32,384]{2,1,0:T(8,128)(2,1)} %shard_map.86.refs_0_), calls=%async_computation.9 | async-start | bytes 393216 | tf_op jit(solution)/shard_map/all_to_all | solution.py:46
  225.2 6.2 %collective-permute-start.14 = (bf16[2,128,128]{2,1,0:T(8,128)(2,1)S(1)}, bf16[2,128,128]{2,1,0:T(8,128)(2,1)S(1)}, u32[]{:S(2)}, u32[]{:S(2)}) collective-permute-start(bf16[2,128,128]{2,1,0:T(8,128)(2,1)S(1)} %get-tuple-element.40), channel_id=1, source_target_pairs={{0,256},{8,264},{16,272},{24,280},{32,288},{40,296},{48,304},{56,3... | collective-permute-start | bytes 196616 | tf_op jit(solution)/shard_map/ppermute | solution.py:42

commit v9 on v8

--- a/solution.py
+++ b/solution.py
@@ -90,43 +90,60 @@
 SPAN = ROWS + TAPS
 
 
-def conv_body(forward, sc_ref, x_ref, w_ref, *refs):
-    own_ref, other_ref = refs[-2:]
-    ends = [sc_ref[2 + u] for u in range(4)]
-    first = TAPS * (sc_ref[0] if forward else 1 - sc_ref[0])
+def conv_body(forward, sc_ref, *refs):
+    y, x = sc_ref[0], sc_ref[1]
+    ends = [sc_ref[3 + u] for u in range(4)]
+    if forward:
+        rows, taps, outs = refs[:4], [(refs[4], 0), (refs[5], 0)], refs[6:]
+    else:
+        rows = [refs[0].at[0], refs[0].at[1]]
+        taps = [(refs[1], 0), (refs[2], 0), (refs[3], 0), (refs[3], 16 * LANES)]
+        outs = refs[-2:]
+    first = TAPS * (y if forward else 1 - y)
     row = lax.broadcasted_iota(jnp.int32, (ROWS, LANES), 0)
-    for b in range(2):
-        shard = sc_ref[1] if b == 0 else sc_ref[1] ^ 32
-        pos = shard * ROWS + row
+    for b, rows_ref in enumerate(rows):
+        pos = (sc_ref[2] ^ (0, 32, 2, 34)[b]) * ROWS + row
         low, high = bounds_of(pos, ends)
-        source = pos + (first - HALF)
         spans = [
-            x_ref[b, pl.ds(pl.multiple_of(g * PADDED + first, TAPS), SPAN)].astype(F32)
+            rows_ref[pl.ds(pl.multiple_of(g * PADDED + first, TAPS), SPAN)].astype(F32)
             for g in range(2)
         ]
         totals = [jnp.zeros((ROWS, LANES), F32) for g in range(2)]
-        for rest in range(8):
-            rolled = [pltpu.roll(e, SPAN - rest, 0) if rest else e for e in spans]
-            for start in range(0, TAPS + 1, 8):
-                tap = start + rest if forward else TAPS - start - rest
-                if not 0 <= tap < TAPS:
-                    continue
-                key = source + (start + rest)
-                keep = (key >= low) & (key < high)
-                for g in range(2):
-                    at = (tap // 4 * 2 + g) * LANES
-                    piece = jnp.where(keep, rolled[g][start : start + ROWS], 0.0).astype(BF)
-                    totals[g] += lax.dot_general(
-                        piece,
-                        w_ref[tap % 4, at : at + LANES],
-                        (((1,), (0 if forward else 1,)), ((), ())),
-                        preferred_element_type=F32,
-                    )
+        for m, (w_ref, base) in enumerate(taps):
+            shift = x ^ m if forward else 4 - (x ^ m)
+            source = pos + (first + shift - HALF)
+            for odd in range(2):
+                rolled = [pltpu.roll(e, SPAN - 4 * odd - shift, 0) for e in spans]
+                for step in range(odd, 8, 2):
+                    key = source + 4 * step
+                    keep = (key >= low) & (key < high)
+                    z = step if forward else 7 - step
+                    start = 8 * (step // 2)
+                    for g in range(2):
+                        at = base + (z * 2 + g) * LANES
+                        piece = jnp.where(keep, rolled[g][start : start + ROWS], 0.0).astype(BF)
+                        totals[g] += lax.dot_general(
+                            piece,
+                            w_ref[at : at + LANES],
+                            (((1,), (0 if forward else 1,)), ((), ())),
+                            preferred_element_type=F32,
+                        )
         for g in range(2):
-            if b == 0:
-                own_ref[g] = totals[g]
-            else:
-                other_ref[g] = totals[g].astype(BF)
+            outs[b][g] = totals[g] if b == 0 else totals[g].astype(BF)
+
+
+def convolved(forward, scalars, *arrays, earlier=()):
+    own = jax.ShapeDtypeStruct((2, ROWS, LANES), F32)
+    other = jax.ShapeDtypeStruct((2, ROWS, LANES), BF)
+    own, *others = vmem_call(
+        functools.partial(conv_body, forward),
+        (own, other, other, other) if forward else (own, other),
+        scalars=1,
+        inputs=len(arrays),
+        earlier=len(earlier),
+        flops=32 * 2 * 2 * 2 * ROWS * HD * HD,
+    )(scalars, *arrays, *earlier)
+    return own, *(swap(array, bit) for array, bit in zip(others, (32, 2, 34)))
 
 
 def taps_body(w_ref, out_ref):
@@ -143,58 +160,58 @@
     )(weight)
 
 
-def joined_body(w_ref, own_ref, other_ref, qkv_ref, out_ref):
-    for i in range(4):
-        for z in range(8):
-            out_ref[i, z * 2 * LANES : (z + 1) * 2 * LANES] = w_ref[z]
-        for b, rows_ref in enumerate((own_ref, other_ref)):
-            start = 16 * LANES + b * ROWS
-            out_ref[i, start : start + ROWS] = rows_ref[...]
-
-
-def joined(taps, own, other, w_qkv):
-    return vmem_call(
-        joined_body,
-        jax.ShapeDtypeStruct((4, 16 * LANES + 2 * ROWS, LANES), BF),
-        inputs=3,
+def near_body(w_ref, b0_ref, b1_ref, b2_ref, b3_ref, qkv_ref, out_ref):
+    for z in range(8):
+        out_ref[z * 2 * LANES : (z + 1) * 2 * LANES] = w_ref[z]
+    for b, rows_ref in enumerate((b0_ref, b1_ref, b2_ref, b3_ref)):
+        start = 16 * LANES + b * ROWS
+        out_ref[start : start + ROWS] = rows_ref[2 * PADDED :]
+
+
+def near_taps(taps, blocks, w_qkv):
+    return vmem_call(
+        near_body,
+        jax.ShapeDtypeStruct((16 * LANES + 4 * ROWS, LANES), BF),
+        inputs=5,
         earlier=1,
-    )(taps, own, other, w_qkv)
-
-
-def paired(rows, more=None):
+    )(taps, *blocks, w_qkv)
+
+
+def half_body(near_ref, next_ref, earlier_ref, out_ref):
+    out_ref[: 16 * LANES] = near_ref[: 16 * LANES]
+    out_ref[16 * LANES :] = next_ref[: 16 * LANES]
+
+
+def half_taps(near, following, earlier):
+    return vmem_call(
+        half_body, jax.ShapeDtypeStruct((32 * LANES, LANES), BF), inputs=2, earlier=1
+    )(near, following, earlier)
+
+
+def halos_of(rows, *bits):
     shards = range(64)
     up = [(i, i + 1) for i in shards[:-1]]
     down = [(i, i - 1) for i in shards[1:]]
     last, head = rows[:, ROWS - HALF :], rows[:, :HALF]
-    sent = rows.reshape(2 * ROWS, LANES)
-    if more is not None:
-        sent = jnp.concatenate([sent, more], axis=0)
-    got = swap(sent, 32)
-    sides = [
-        [lax.ppermute(last, "tm", [(i, j ^ bit) for i, j in up]) for bit in (0, 32)],
-        [lax.ppermute(head, "tm", [(i, j ^ bit) for i, j in down]) for bit in (0, 32)],
+    before = [lax.ppermute(last, "tm", [(i, j ^ bit) for i, j in up]) for bit in bits]
+    behind = [lax.ppermute(head, "tm", [(i, j ^ bit) for i, j in down]) for bit in bits]
+    return list(zip(before, behind))
+
+
+def four_blocks(rows, more):
+    ((before, behind),) = halos_of(rows, 0)
+    padded = jnp.concatenate([before, rows, behind], axis=1).reshape(2 * PADDED, LANES)
+    block = jnp.concatenate([padded, more], axis=0)
+    return [block] + [swap(block, bit) for bit in (32, 2, 34)]
+
+
+def paired(rows):
+    other = swap(rows.reshape(2 * ROWS, LANES), 32).reshape(2, ROWS, LANES)
+    pair = [
+        jnp.concatenate([before, middle, behind], axis=1)
+        for (before, behind), middle in zip(halos_of(rows, 0, 32), (rows, other))
     ]
-    other = got[: 2 * ROWS].reshape(2, ROWS, LANES)
-    pair = [
-        jnp.concatenate([sides[0][b], middle, sides[1][b]], axis=1)
-        for b, middle in enumerate((rows, other))
-    ]
-    return jnp.stack(pair).reshape(2, 2 * PADDED, LANES), got[2 * ROWS :]
-
-
-def convolved(forward, scalars, pair, taps, *earlier):
-    own, other = vmem_call(
-        functools.partial(conv_body, forward),
-        (
-            jax.ShapeDtypeStruct((2, ROWS, LANES), F32),
-            jax.ShapeDtypeStruct((2, ROWS, LANES), BF),
-        ),
-        scalars=1,
-        inputs=2,
-        earlier=len(earlier),
-        flops=32 * 2 * 2 * 2 * ROWS * HD * HD,
-    )(scalars, pair, taps, *earlier)
-    return own, swap(other, 32)
+    return jnp.stack(pair).reshape(2, 2 * PADDED, LANES)
 
 
 CHUNK = 256
@@ -205,26 +222,21 @@
 CONTRACT = (((1,), (1,)), ((), ()))
 
 
-def upstream_rows(sc_ref, f_ref, d_ref):
-    for i, e in enumerate(SLOTS):
-        row = 16 * LANES + e // 4 * ROWS
-        d_ref[i * ROWS : (i + 1) * ROWS] = f_ref[(sc_ref[0] % 4) ^ (e % 4), row : row + ROWS]
-
-
-def scored(c, q_ref, kv_ref, d_ref):
+def scored(c, q_ref, kv_ref, near_ref, next_ref):
     keys = kv_ref[:, :, :LANES].reshape(ALL, LANES)
     values = kv_ref[:, :, LANES:].reshape(ALL, LANES)
     q = q_ref[c * N : (c + 1) * N].reshape(CHUNK, LANES)
-    d = d_ref[c * CHUNK : (c + 1) * CHUNK]
+    half = ALL // CHUNK // 2
+    start = 16 * LANES + c % half * CHUNK
+    d = (near_ref if c < half else next_ref)[start : start + CHUNK]
     scores = lax.dot_general(keys, q, CONTRACT, preferred_element_type=F32)
     dprobs = lax.dot_general(values, d, CONTRACT, preferred_element_type=F32)
     return keys, values, q, d, scores * SCALE2, dprobs
 
 
-def stats_body(sc_ref, q_ref, kv_ref, f_ref, out_ref, d_ref):
-    upstream_rows(sc_ref, f_ref, d_ref)
+def stats_body(sc_ref, q_ref, kv_ref, near_ref, next_ref, out_ref):
     for c in range(ALL // CHUNK):
-        _, _, _, _, scores, dprobs = scored(c, q_ref, kv_ref, d_ref)
+        _, _, _, _, scores, dprobs = scored(c, q_ref, kv_ref, near_ref, next_ref)
         peak = jnp.max(scores, axis=0, keepdims=True)
         weight = jnp.exp2(scores - peak)
         total = jnp.sum(weight, axis=0, keepdims=True)
@@ -239,9 +251,8 @@
 
 
 def grads_body(
-    sc_ref, q_ref, kv_ref, f_ref, stats_ref, od_ref, dkv_ref, d_ref, dk_ref, dv_ref
+    sc_ref, q_ref, kv_ref, near_ref, next_ref, stats_ref, od_ref, dkv_ref, dk_ref, dv_ref
 ):
-    upstream_rows(sc_ref, f_ref, d_ref)
     for c in range(ALL // CHUNK):
         peaks, totals, alongs = (
             jnp.concatenate(
@@ -255,7 +266,7 @@
         total = jnp.sum(totals * factor, axis=0)
         delta = jnp.sum(alongs * factor, axis=0) / total
         lse = top + jnp.log2(total)
-        keys, values, q, d, scores, dprobs = scored(c, q_ref, kv_ref, d_ref)
+        keys, values, q, d, scores, dprobs = scored(c, q_ref, kv_ref, near_ref, next_ref)
         probs = jnp.exp2(scores - lse)
         dscores = (probs * (dprobs - delta)).astype(BF)
         probs = probs.astype(BF)
@@ -280,18 +291,17 @@
         dkv_ref[i, :, LANES:] = dv_ref[piece].astype(BF)
 
 
-def attention_stats(scalars, queries, keys, gathered):
+def attention_stats(scalars, queries, keys, near, following):
     return vmem_call(
         stats_body,
         jax.ShapeDtypeStruct((8, 3, 8, ROWS), F32),
-        scratch=[pltpu.VMEM((ALL, LANES), BF)],
         scalars=1,
-        inputs=3,
+        inputs=4,
         flops=2 * 2 * ALL * ALL * LANES,
-    )(scalars, queries, keys, gathered)
-
-
-def attention_grads(scalars, queries, keys, gathered, stats):
+    )(scalars, queries, keys, near, following)
+
+
+def attention_grads(scalars, queries, keys, near, following, stats):
     return vmem_call(
         grads_body,
         (
@@ -299,14 +309,13 @@
             jax.ShapeDtypeStruct((8, ROWS, 2 * LANES), BF),
         ),
         scratch=[
-            pltpu.VMEM((ALL, LANES), BF),
             pltpu.VMEM((ALL, LANES), F32),
             pltpu.VMEM((ALL, LANES), F32),
         ],
         scalars=1,
-        inputs=4,
+        inputs=5,
         flops=6 * 2 * ALL * ALL * LANES,
-    )(scalars, queries, keys, gathered, stats)
+    )(scalars, queries, keys, near, following, stats)
 
 
 GROUPS = 16
@@ -320,9 +329,9 @@
     return inputs * normal_cdf, normal_cdf + inputs * density
 
 
-def hidden_body(own_ref, other_ref, frames_ref, hidden_ref, slope_ref, sent_ref):
+def hidden_body(own_ref, y_ref, x_ref, both_ref, frames_ref, hidden_ref, slope_ref, sent_ref):
     for g in range(2):
-        conv = own_ref[g] + other_ref[g].astype(F32)
+        conv = own_ref[g] + y_ref[g].astype(F32) + x_ref[g].astype(F32) + both_ref[g].astype(F32)
         activated, slope = gelu_parts(conv)
         hidden = (frames_ref[g].astype(F32) + activated).T[:HD]
         hidden_ref[g] = hidden
@@ -330,11 +339,11 @@
         sent_ref[g] = hidden.astype(BF)
 
 
-def hidden_rows(own, other, frames_g):
+def hidden_rows(parts, frames_g):
     shape = jax.ShapeDtypeStruct((2, HD, ROWS), F32)
     return vmem_call(
-        hidden_body, (shape, shape, jax.ShapeDtypeStruct((2, HD, ROWS), BF)), inputs=3
-    )(own, other, frames_g)
+        hidden_body, (shape, shape, jax.ShapeDtypeStruct((2, HD, ROWS), BF)), inputs=5
+    )(*parts, frames_g)
 
 
 def project_body(
@@ -402,7 +411,7 @@
     return jnp.concatenate(rows + [jnp.zeros((4, ROWS), F32)], axis=0).astype(BF)
 
 
-def share_body(od_ref, dkv_ref, normed_ref, w_ref, parts_ref, wide_ref, out_ref, grad_ref):
+def share_body(od_ref, dkv_ref, normed_ref, w_ref, far_ref, parts_ref, wide_ref, out_ref, grad_ref):
     out, dq = od_ref[0, 0].astype(F32), od_ref[0, 1].astype(F32)
     for i in range(1, 8):
         out += od_ref[i, 0].astype(F32)
@@ -439,7 +448,7 @@
             wide_ref[g // 8 * 4 + x, row : row + slab, : 3 * HD] = piece
 
 
-def shares(od, dkv, normed_t, w_qkv):
+def shares(od, dkv, normed_t, w_qkv, earlier):
     return vmem_call(
         share_body,
         (
@@ -449,8 +458,9 @@
         ),
         scratch=[pltpu.VMEM((ROWS, 3 * HD), BF)],
         inputs=4,
+        earlier=1,
         flops=4 * ROWS * WIDTH * 3 * HD,
-    )(od, dkv, normed_t, w_qkv)
+    )(od, dkv, normed_t, w_qkv, earlier)
 
 
 def wide_body(wide_ref, out_ref):
@@ -518,17 +528,17 @@
         return jnp.concatenate([jnp.stack(first).astype(jnp.int32), ends])
 
     y, x = index // 32, index % 4
-    where = scalars(y, index)
+    where = scalars(y, x, index)
     order = scalars(y * 4 + x)
 
     frames_g = frames.reshape(ROWS, 2, HD).transpose(1, 0, 2)
     frames_g = jnp.pad(frames_g, ((0, 0), (0, 0), (0, LANES - HD)))
     upstream = jnp.pad(grad_out, ((0, 0), (0, LANES - HD)))
-    pair, other_upstream = paired(frames_g, upstream)
-    taps = exchange_z(taps_sent(conv_weight[0]))
-    taps = exchange_x(joined(taps, upstream, other_upstream, w_qkv))
-    own, other = convolved(True, where, pair, taps)
-    hidden_t, slope_t, sent = hidden_rows(own, other, frames_g)
+    blocks = four_blocks(frames_g, upstream)
+    near = near_taps(exchange_z(taps_sent(conv_weight[0])), blocks, w_qkv)
+    following = swap(near, 1)
+    parts = convolved(True, where, *blocks, near, following)
+    hidden_t, slope_t, sent = hidden_rows(parts, frames_g)
 
     all_t = lax.all_gather(sent, "head", axis=0, tiled=True)
     keys, queries, normed_t, unit_t, inv_std = project(
@@ -537,19 +547,21 @@
 
     keys = exchange_z(keys)
     queries = doubled(queries)
-    stats = exchange_xy(attention_stats(order, queries, keys, taps))
-    od, dkv = attention_grads(order, queries, keys, taps, stats)
+    stats = exchange_xy(attention_stats(order, queries, keys, near, following))
+    od, dkv = attention_grads(order, queries, keys, near, following, stats)
     od = exchange_xy(od)
+    far = swap(half_taps(near, following, od), 2)
     dkv = exchange_z(dkv)
 
-    parts, wide, attended = shares(od, dkv, normed_t, w_qkv)
+    parts, wide, attended = shares(od, dkv, normed_t, w_qkv, far)
     parts = core_sum(exchange_head(parts, CORE_GROUPS))
     parts = exchange_head(parts, HIGH_GROUPS)
     hidden_grad, error = errors(parts, unit_t, inv_std, slope_t)
 
     wide = wide_sum(exchange_xy(wide))
-    pair, _ = paired(error)
-    own, other = convolved(False, where, pair, taps, wide)
+    own, other = convolved(
+        False, where, paired(error), near, following, far, earlier=(wide,)
+    )
     frame_grad = (hidden_grad + own + other.astype(F32)).astype(BF)[:, :, :HD]
     wide = exchange_z(wide)
     weight_grad = jnp.sum(wide[:, : HD // 4, : 3 * HD].astype(F32), axis=0)

time: 234 us -> 252 us (1.077)
  starting transfers between devices: 78.3 us -> 102 us
  waiting for transfers between devices: 49 us -> 38.7 us
    ppermute x7 -> x13, starting transfers between devices: 18 us -> 43.6 us  [swap(): return lax.ppermute(array, 'tm', [(i, i ^ bit) for i in range(64)])]
    ppermute x7 -> x13, waiting for transfers between devices: 20.4 us -> 31.8 us  [swap(): return lax.ppermute(array, 'tm', [(i, i ^ bit) for i in range(64)])]
    all_to_all x3, waiting for transfers between devices: 10.7 us -> 0.01 us  [exchange_z(): return lax.all_to_all(parts, 'tm', 0, 0, axis_index_groups=Z_GROUPS)]
    ppermute x8 -> x6, waiting for transfers between devices: 16.7 us -> 6.88 us  [the longest x3 5.62 us: halos_of(): lax.ppermute(last, 'tm', [(i, j ^ bit) for i, j in up])]
    all_to_all x3, starting transfers between devices: 21.6 us -> 29.4 us  [exchange_z(): return lax.all_to_all(parts, 'tm', 0, 0, axis_index_groups=Z_GROUPS)]
    ppermute x8 -> x6, starting transfers between devices: 28.6 us -> 23.7 us  [the longest x3 15.5 us: halos_of(): lax.ppermute(head, 'tm', [(i, j ^ bit) for i, j in down])]
    all_to_all x1 -> x0, starting transfers between devices: 4.42 us -> none  [exchange_x(): return lax.all_to_all(parts, 'tm', 0, 0, axis_index_groups=X_GROUPS)]
    pallas_call x4 -> x5, Pallas kernels: 8.09 us -> 10 us  [the longest x2 7.47 us: convolved(): vmem_call(functools.partial(conv_body, forward), (own, other, other, othe...]
  transfers between devices with their start and end apart: 20 -> 23, of which waited for: 12 -> 10; matrix products, arithmetic and copies ran while one was open for 2% -> 2% of each run, Pallas kernels for 2% -> 2%
where the time goes in v9:
time: 252 us; the launch traced here: 251 us
  starting transfers between devices  102 us (40%)
  blocking collectives  78.9 us (31%)
  waiting for transfers between devices  38.7 us (15%)
  Pallas kernels  19.9 us (8%)
  local copies, waits for them, and re-layouts  8.14 us (3%)
    ppermute x13, starting transfers between devices, swap(): return lax.ppermute(array, 'tm', [(i, i ^ bit) for i in range(64)])  43.6 us
    ppermute x13, waiting for transfers between devices, swap(): return lax.ppermute(array, 'tm', [(i, i ^ bit) for i in range(64)])  31.8 us
    all_to_all x3, starting transfers between devices, exchange_z(): return lax.all_to_all(parts, 'tm', 0, 0, axis_index_groups=Z_GROUPS)  29.4 us
    all_to_all x2, blocking collectives, exchange_xy(): return lax.all_to_all(parts, 'tm', 0, 0, axis_index_groups=XY_GROUPS)  21.5 us
    all_to_all x1, blocking collectives, exchange_z(): return lax.all_to_all(parts, 'tm', 0, 0, axis_index_groups=Z_GROUPS)  20.3 us
    all_to_all x2, blocking collectives, exchange_head(): return lax.all_to_all(parts, 'head', 0, 0, axis_index_groups=groups)  20 us
    all_gather x1, blocking collectives, on_device(): all_t = lax.all_gather(sent, 'head', axis=0, tiled=True)  17.1 us
    ppermute x3, starting transfers between devices, halos_of(): lax.ppermute(head, 'tm', [(i, j ^ bit) for i, j in down])  15.5 us
  transfers between devices with their start and end apart: 23, of which 10 were waited for; matrix products, arithmetic and copies ran while one was open for 2% of the time, Pallas kernels for 2%

profile of v9, /device:TPU:8, one launch (start us, length us, event | category | flops | bytes accessed | tf_op | source)
XLA Modules:
  0.0 251.0 jit_solution(13617193644157599519)
XLA Ops:
  0.6 0.8 copy-done.10
  1.5 0.9 shard_map.76
  2.3 10.3 %all-to-all-start = ((bf16[8,256,128]{2,1,0:T(8,128)(2,1)}), bf16[8,256,128]{2,1,0:T(8,128)(2,1)S(1)}, u32[]{:S(2)}, u32[]{:S(2)}) async-start(bf16[8,256,128]{2,1,0:T(8,128)(2,1)} %shard_map.76), calls=%async_computation | async-start | bytes 1048576 | tf_op jit(solution)/shard_map/all_to_all | solution.py:46
  12.7 0.1 copy.20
  12.8 3.4 %collective-permute-start = (bf16[2,32,128]{2,1,0:T(8,128)(2,1)S(1)}, bf16[2,32,128]{2,1,0:T(8,128)(2,1)S(1)}, u32[]{:S(2)}, u32[]{:S(2)}) collective-permute-start(bf16[2,32,128]{2,1,0:T(8,128)(2,1)S(1)} %get-tuple-element.56), channel_id=1, source_target_pairs={{0,8},{8,16},{16,24},{24,32},{32,40},{40,48},{48,56},{56,64},{64,7... | collective-permute-start | bytes 49160 | tf_op jit(solution)/shard_map/ppermute | solution.py:196
  16.2 6.7 %collective-permute-start.1 = (bf16[2,32,128]{2,1,0:T(8,128)(2,1)S(1)}, bf16[2,32,128]{2,1,0:T(8,128)(2,1)S(1)}, u32[]{:S(2)}, u32[]{:S(2)}) collective-permute-start(bf16[2,32,128]{2,1,0:T(8,128)(2,1)S(1)} %get-tuple-element.57), channel_id=1, source_target_pairs={{8,0},{16,8},{24,16},{32,24},{40,32},{48,40},{56,48},{64,56},{72,6... | collective-permute-start | bytes 49160 | tf_op jit(solution)/shard_map/ppermute | solution.py:197
  22.9 0.1 copy.21
  23.0 1.3 collective-permute-done.1
  24.3 2.1 collective-permute-start.4
  26.4 2.7 %collective-permute-start.3 = (bf16[512,128]{1,0:T(8,128)(2,1)S(1)}, bf16[512,128]{1,0:T(8,128)(2,1)S(1)}, u32[]{:S(2)}, u32[]{:S(2)}) collective-permute-start(bf16[512,128]{1,0:T(8,128)(2,1)S(1)} %fusion.1.b0_ref.refs_0_), channel_id=1, source_target_pairs={{0,16},{8,24},{16,0},{24,8},{32,48},{40,56},{48,32},{56,40},{64,80... | collective-permute-start | bytes 393224 | tf_op jit(solution)/shard_map/ppermute | solution.py:42
  29.1 5.9 %collective-permute-start.2 = (bf16[512,128]{1,0:T(8,128)(2,1)S(1)}, bf16[512,128]{1,0:T(8,128)(2,1)S(1)}, u32[]{:S(2)}, u32[]{:S(2)}) collective-permute-start(bf16[512,128]{1,0:T(8,128)(2,1)S(1)} %fusion.1.b0_ref.refs_0_), channel_id=1, source_target_pairs={{0,256},{8,264},{16,272},{24,280},{32,288},{40,296},{48,304},{56,3... | collective-permute-start | bytes 393224 | tf_op jit(solution)/shard_map/ppermute | solution.py:42
  35.1 2.4 copy.22.qkv_ref.w_ref
  37.5 0.5 collective-permute-done.2.b1_ref.refs_1_
  38.1 4.7 %collective-permute-start.5 = (bf16[2560,128]{1,0:T(8,128)(2,1)S(1)}, bf16[2560,128]{1,0:T(8,128)(2,1)S(1)}, u32[]{:S(2)}, u32[]{:S(2)}) collective-permute-start(bf16[2560,128]{1,0:T(8,128)(2,1)S(1)} %shard_map.77.refs_4_.near_ref.refs_1_), channel_id=1, source_target_pairs={{0,8},{8,0},{16,24},{24,16},{32,40},{40,32},{48,56},{56,48},{64,72... | collective-permute-start | bytes 1966088 | tf_op jit(solution)/shard_map/ppermute | solution.py:42
  42.8 0.2 reduce-window.9
  43.0 0.1 pad_add_fusion.2.sc_ref
  43.0 11.4 %collective-permute-done.5.refs_5_.next_ref.refs_2_ = bf16[2560,128]{1,0:T(8,128)(2,1)S(1)} collective-permute-done((bf16[2560,128]{1,0:T(8,128)(2,1)S(1)}, bf16[2560,128]{1,0:T(8,128)(2,1)S(1)}, u32[]{:S(2)}, u32[]{:S(2)}) %collective-permute-start.5) | collective-permute-done | bytes 655392 | tf_op jit(solution)/shard_map/ppermute | solution.py:42
  54.4 3.4 %shard_map.78 = (f32[2,128,128]{2,1,0:T(8,128)S(1)}, bf16[2,128,128]{2,1,0:T(8,128)(2,1)S(1)}, bf16[2,128,128]{2,1,0:T(8,128)(2,1)S(1)}, bf16[2,128,128]{2,1,0:T(8,128)(2,1)S(1)}) custom-call(s32[7]{0:T(128)S(1)} %pad_add_fusion.2.sc_ref, bf16[512,128]{1,0:T(8,128)(2,1)S(1)} %fusion.1.b0_ref.refs_0_, ...), custom_call_target="tpu_custom_call" | custom-call | flops 471859200 | bytes 1048576 | tf_op jit(solution)/shard_map/pallas_call | solution.py:138
  57.8 3.0 %collective-permute-start.6 = (bf16[2,128,128]{2,1,0:T(8,128)(2,1)S(1)}, bf16[2,128,128]{2,1,0:T(8,128)(2,1)S(1)}, u32[]{:S(2)}, u32[]{:S(2)}) collective-permute-start(bf16[2,128,128]{2,1,0:T(8,128)(2,1)S(1)} %get-tuple-element.25), channel_id=1, source_target_pairs={{0,256},{8,264},{16,272},{24,280},{32,288},{40,296},{48,304},{56,3... | collective-permute-start | bytes 196616 | tf_op jit(solution)/shard_map/ppermute | solution.py:42
  60.8 5.8 %collective-permute-start.7 = (bf16[2,128,128]{2,1,0:T(8,128)(2,1)S(1)}, bf16[2,128,128]{2,1,0:T(8,128)(2,1)S(1)}, u32[]{:S(2)}, u32[]{:S(2)}) collective-permute-start(bf16[2,128,128]{2,1,0:T(8,128)(2,1)S(1)} %get-tuple-element.26), channel_id=1, source_target_pairs={{0,16},{8,24},{16,0},{24,8},{32,48},{40,56},{48,32},{56,40},{64,80... | collective-permute-start | bytes 196616 | tf_op jit(solution)/shard_map/ppermute | solution.py:42
  66.6 2.1 collective-permute-start.8
  68.7 0.1 pad_add_fusion.1
  68.8 0.8 collective-permute-done.7.x_ref
  69.5 5.6 %collective-permute-done.8.both_ref = bf16[2,128,128]{2,1,0:T(8,128)(2,1)S(1)} collective-permute-done((bf16[2,128,128]{2,1,0:T(8,128)(2,1)S(1)}, bf16[2,128,128]{2,1,0:T(8,128)(2,1)S(1)}, u32[]{:S(2)}, u32[]{:S(2)}) %collective-permute-start.8) | collective-permute-done | bytes 65568 | tf_op jit(solution)/shard_map/ppermute | solution.py:42
  75.2 0.2 shard_map.79
  75.3 17.1 %all_gather.3.all_ref = bf16[16,120,128]{2,1,0:T(8,128)(2,1)S(1)} all-gather(bf16[2,120,128]{2,1,0:T(8,128)(2,1)S(1)} %get-tuple-element.28), channel_id=1, replica_groups=mesh['tm'=64,'head'=8] {'head'}, dimensions={0}, use_global_device_ids=true | all-gather | bytes 552960 | tf_op jit(solution)/shard_map/all_gather | solution.py:543
  92.5 1.5 shard_map.80
  94.0 0.8 copy-done.5
  94.8 0.8 copy-done.6
  95.6 0.6 copy-done.8
  96.2 8.2 %all-to-all-start.1 = ((bf16[8,128,256]{2,1,0:T(8,128)(2,1)}), bf16[8,128,256]{2,1,0:T(8,128)(2,1)S(1)}, u32[]{:S(2)}, u32[]{:S(2)}) async-start(bf16[8,128,256]{2,1,0:T(8,128)(2,1)} %copy-done.5), calls=%async_computation.1 | async-start | bytes 1048576 | tf_op jit(solution)/shard_map/all_to_all | solution.py:46
  104.5 3.5 %collective-permute-start.9 = (bf16[1,128,128]{2,1,0:T(8,128)(2,1)S(1)}, bf16[1,128,128]{2,1,0:T(8,128)(2,1)S(1)}, u32[]{:S(2)}, u32[]{:S(2)}) collective-permute-start(bf16[1,128,128]{2,1,0:T(8,128)(2,1)S(1)} %bitcast.18), channel_id=1, source_target_pairs={{0,256},{8,264},{16,272},{24,280},{32,288},{40,296},{48,304},{56,3... | collective-permute-start | bytes 98312 | tf_op jit(solution)/shard_map/ppermute | solution.py:42
  108.0 2.2 collective-permute-done.9
  110.3 4.7 %collective-permute-start.10 = (bf16[2,128,128]{2,1,0:T(8,128)(2,1)S(1)}, bf16[2,128,128]{2,1,0:T(8,128)(2,1)S(1)}, u32[]{:S(2)}, u32[]{:S(2)}) collective-permute-start(bf16[2,128,128]{2,1,0:T(8,128)(2,1)S(1)} %pad_maximum_fusion.6), channel_id=1, source_target_pairs={{0,16},{8,24},{16,0},{24,8},{32,48},{40,56},{48,32},{56,40},{64,80... | collective-permute-start | bytes 196616 | tf_op jit(solution)/shard_map/ppermute | solution.py:42
  115.0 2.9 %collective-permute-done.10 = bf16[2,128,128]{2,1,0:T(8,128)(2,1)S(1)} collective-permute-done((bf16[2,128,128]{2,1,0:T(8,128)(2,1)S(1)}, bf16[2,128,128]{2,1,0:T(8,128)(2,1)S(1)}, u32[]{:S(2)}, u32[]{:S(2)}) %collective-permute-start.10) | collective-permute-done | bytes 65568 | tf_op jit(solution)/shard_map/ppermute | solution.py:42
  118.0 1.9 collective-permute-start.11
  119.9 4.9 %collective-permute-done.11 = bf16[4,128,128]{2,1,0:T(8,128)(2,1)S(1)} collective-permute-done((bf16[4,128,128]{2,1,0:T(8,128)(2,1)S(1)}, bf16[4,128,128]{2,1,0:T(8,128)(2,1)S(1)}, u32[]{:S(2)}, u32[]{:S(2)}) %collective-permute-start.11) | collective-permute-done | bytes 131104 | tf_op jit(solution)/shard_map/ppermute | solution.py:42
  124.8 0.7 pad_maximum_fusion.q_ref
  125.6 0.9 copy-done.3
  126.5 2.5 shard_map.81
  129.0 10.6 %all_to_all.45.stats_ref = f32[8,3,8,128]{3,2,1,0:T(8,128)S(1)} all-to-all(f32[8,3,8,128]{3,2,1,0:T(8,128)S(1)} %shard_map.81), channel_id=1, replica_groups={{0,8,16,24,256,264,272,280},{32,40,48,56,288,296,304,312},{64,72,80,88,..., dimensions={0} | all-to-all | bytes 196608 | tf_op jit(solution)/shard_map/all_to_all | solution.py:34
  139.5 3.4 %shard_map.82 = (bf16[8,2,120,128]{3,2,1,0:T(8,128)(2,1)S(1)}, bf16[8,128,256]{2,1,0:T(8,128)(2,1)S(1)}) custom-call(s32[5]{0:T(128)S(1)} %get-tuple-element.59.sc_ref, bf16[8,128,128]{2,1,0:T(8,128)(2,1)S(1)} %copy-done.4, bf16[8,128,256]{2,1,0:T(8,128)(2,1)S(1)} %all-to-all-done.1.kv_ref, bf16[2560,128]{1,0:T(8,128)(2,1)S(1)} %shard_map.77.refs_4_.near_ref.refs_1_, ...), custom_call_target="tpu_custom_call" | custom-call | flops 1610612736 | bytes 1048576 | tf_op jit(solution)/shard_map/pallas_call | solution.py:305
  143.0 10.9 %all_to_all.46.earlier_ref.od_ref = bf16[8,2,120,128]{3,2,1,0:T(8,128)(2,1)S(1)} all-to-all(bf16[8,2,120,128]{3,2,1,0:T(8,128)(2,1)S(1)} %get-tuple-element.32), channel_id=1, replica_groups={{0,8,16,24,256,264,272,280},{32,40,48,56,288,296,304,312},{64,72,80,88,..., dimensions={0} | all-to-all | bytes 983040 | tf_op jit(solution)/shard_map/all_to_all | solution.py:34
  154.0 3.2 %collective-permute-start.12 = (bf16[4096,128]{1,0:T(8,128)(2,1)S(1)}, bf16[4096,128]{1,0:T(8,128)(2,1)S(1)}, u32[]{:S(2)}, u32[]{:S(2)}) collective-permute-start(bf16[4096,128]{1,0:T(8,128)(2,1)S(1)} %shard_map.83), channel_id=1, source_target_pairs={{0,16},{8,24},{16,0},{24,8},{32,48},{40,56},{48,32},{56,40},{64,80... | collective-permute-start | bytes 3145736 | tf_op jit(solution)/shard_map/ppermute | solution.py:42
  157.2 20.3 %all_to_all.47.dkv_ref = bf16[8,128,256]{2,1,0:T(8,128)(2,1)S(1)} all-to-all(bf16[8,128,256]{2,1,0:T(8,128)(2,1)S(1)} %get-tuple-element.33), channel_id=1, replica_groups={{0,32,64,96,128,160,192,224},{8,40,72,104,136,168,200,232},{16,48,80,11..., dimensions={0} | all-to-all | bytes 1048576 | tf_op jit(solution)/shard_map/all_to_all | solution.py:46
  177.5 1.4 shard_map.84
  178.9 4.2 %all_to_all.48.parts_ref = bf16[2,4,2,128,128]{4,3,2,1,0:T(8,128)(2,1)S(1)} all-to-all(bf16[2,4,2,128,128]{4,3,2,1,0:T(8,128)(2,1)S(1)} %get-tuple-element.36), channel_id=1, replica_groups={{0,1},{2,3},{4,5},{6,7},{8,9},{10,11},{12,13},{14,15},{16,17},{18,19},{..., dimensions={0} | all-to-all | bytes 1048576 | tf_op jit(solution)/shard_map/all_to_all | solution.py:50
  183.1 15.8 %all_to_all.49.parts_ref = bf16[4,2,128,128]{3,2,1,0:T(8,128)(2,1)S(1)} all-to-all(bf16[4,2,128,128]{3,2,1,0:T(8,128)(2,1)S(1)} %shard_map.85), channel_id=1, replica_groups={{0,2,4,6},{1,3,5,7},{8,10,12,14},{9,11,13,15},{16,18,20,22},{17,19,21,2..., dimensions={0} | all-to-all | bytes 524288 | tf_op jit(solution)/shard_map/all_to_all | solution.py:50
  198.9 5.7 %all-to-all-start.7 = ((bf16[8,256,384]{2,1,0:T(8,128)(2,1)}), bf16[8,256,384]{2,1,0:T(8,128)(2,1)}, u32[]{:S(2)}, u32[]{:S(2)}) async-start(bf16[8,256,384]{2,1,0:T(8,128)(2,1)} %copy-done.2), calls=%async_computation.7 | async-start | bytes 3145728 | tf_op jit(solution)/shard_map/all_to_all | solution.py:34
  204.7 0.1 shard_map.86
  204.8 3.5 %collective-permute-start.13 = (bf16[2,32,128]{2,1,0:T(8,128)(2,1)S(1)}, bf16[2,32,128]{2,1,0:T(8,128)(2,1)S(1)}, u32[]{:S(2)}, u32[]{:S(2)}) collective-permute-start(bf16[2,32,128]{2,1,0:T(8,128)(2,1)S(1)} %get-tuple-element.54), channel_id=1, source_target_pairs={{0,8},{8,16},{16,24},{24,32},{32,40},{40,48},{48,56},{56,64},{64,7... | collective-permute-start | bytes 49160 | tf_op jit(solution)/shard_map/ppermute | solution.py:196
  208.3 6.7 %collective-permute-start.14 = (bf16[2,32,128]{2,1,0:T(8,128)(2,1)S(1)}, bf16[2,32,128]{2,1,0:T(8,128)(2,1)S(1)}, u32[]{:S(2)}, u32[]{:S(2)}) collective-permute-start(bf16[2,32,128]{2,1,0:T(8,128)(2,1)S(1)} %get-tuple-element.55), channel_id=1, source_target_pairs={{8,0},{16,8},{24,16},{32,24},{40,32},{48,40},{56,48},{64,56},{72,6... | collective-permute-start | bytes 49160 | tf_op jit(solution)/shard_map/ppermute | solution.py:197
  215.0 1.3 collective-permute-start.15
  216.3 2.2 collective-permute-start.17
  218.5 1.9 collective-permute-start.16
  220.5 5.6 %collective-permute-done.13 = bf16[2,32,128]{2,1,0:T(8,128)(2,1)S(1)} collective-permute-done((bf16[2,32,128]{2,1,0:T(8,128)(2,1)S(1)}, bf16[2,32,128]{2,1,0:T(8,128)(2,1)S(1)}, u32[]{:S(2)}, u32[]{:S(2)}) %collective-permute-start.13) | collective-permute-done | bytes 16416 | tf_op jit(solution)/shard_map/ppermute | solution.py:196
  226.1 2.3 shard_map.87.refs_4_
  228.4 10.9 %all-to-all-start.8 = ((bf16[8,32,384]{2,1,0:T(8,128)(2,1)}), bf16[8,32,384]{2,1,0:T(8,128)(2,1)S(1)}, u32[]{:S(2)}, u32[]{:S(2)}) async-start(bf16[8,32,384]{2,1,0:T(8,128)(2,1)} %shard_map.87.refs_4_), calls=%async_computation.8 | async-start | bytes 393216 | tf_op jit(solution)/shard_map/all_to_all | solution.py:46
  239.3 4.1 %shard_map.88 = (f32[2,128,128]{2,1,0:T(8,128)S(1)}, bf16[2,128,128]{2,1,0:T(8,128)(2,1)S(1)}) custom-call(s32[7]{0:T(128)S(1)} %pad_add_fusion.2.sc_ref, bf16[2,384,128]{2,1,0:T(8,128)(2,1)S(1)} %pad_maximum_fusion.1.refs_0_, bf16[2560,128]{1,0:T(8,128)(2,1)S(1)} %shard_map.77.refs_4_.near_ref.refs_1_, ...), custom_call_target="tpu_custom_call" | custom-call | flops 471859200 | bytes 1048576 | tf_op jit(solution)/shard_map/pallas_call | solution.py:138
  243.4 2.0 collective-permute-start.18
  245.4 0.7 copy.26
  246.2 3.4 %collective-permute-done.18 = bf16[2,128,128]{2,1,0:T(8,128)(2,1)S(1)} collective-permute-done((bf16[2,128,128]{2,1,0:T(8,128)(2,1)S(1)}, bf16[2,128,128]{2,1,0:T(8,128)(2,1)S(1)}, u32[]{:S(2)}, u32[]{:S(2)}) %collective-permute-start.18) | collective-permute-done | bytes 65568 | tf_op jit(solution)/shard_map/ppermute | solution.py:42
  249.6 0.7 copy.25
  250.3 0.7 convert_reduce_fusion
  (50 shorter events, 0.4 us)
Async XLA Ops:
  0.6 0.8 copy-start.10
  1.5 11.2 %copy-start.11 = (bf16[128,240]{0,1:T(8,128)(2,1)S(1)}, bf16[128,240]{0,1:T(8,128)(2,1)}, u32[]{:S(2)}) copy-start(bf16[128,240]{0,1:T(8,128)(2,1)} %param.5) | copy-start | bytes 184324
  1.5 21.4 %copy-start.12 = (bf16[128,120]{0,1:T(8,128)(2,1)S(1)}, bf16[128,120]{0,1:T(8,128)(2,1)}, u32[]{:S(2)}) copy-start(bf16[128,120]{0,1:T(8,128)(2,1)} %param.9) | copy-start | bytes 92164
  2.3 35.7 %all-to-all-start = ((bf16[8,256,128]{2,1,0:T(8,128)(2,1)}), bf16[8,256,128]{2,1,0:T(8,128)(2,1)S(1)}, u32[]{:S(2)}, u32[]{:S(2)}) async-start(bf16[8,256,128]{2,1,0:T(8,128)(2,1)} %shard_map.76), calls=%async_computation | async-start | bytes 1048576 | tf_op jit(solution)/shard_map/all_to_all | solution.py:46
  12.8 10.2 %collective-permute-start = (bf16[2,32,128]{2,1,0:T(8,128)(2,1)S(1)}, bf16[2,32,128]{2,1,0:T(8,128)(2,1)S(1)}, u32[]{:S(2)}, u32[]{:S(2)}) collective-permute-start(bf16[2,32,128]{2,1,0:T(8,128)(2,1)S(1)} %get-tuple-element.56), channel_id=1, source_target_pairs={{0,8},{8,16},{16,24},{24,32},{32,40},{40,48},{48,56},{56,64},{64,7... | collective-permute-start | bytes 49160 | tf_op jit(solution)/shard_map/ppermute | solution.py:196
  16.2 8.1 %collective-permute-start.1 = (bf16[2,32,128]{2,1,0:T(8,128)(2,1)S(1)}, bf16[2,32,128]{2,1,0:T(8,128)(2,1)S(1)}, u32[]{:S(2)}, u32[]{:S(2)}) collective-permute-start(bf16[2,32,128]{2,1,0:T(8,128)(2,1)S(1)} %get-tuple-element.57), channel_id=1, source_target_pairs={{8,0},{16,8},{24,16},{32,24},{40,32},{48,40},{56,48},{64,56},{72,6... | collective-permute-start | bytes 49160 | tf_op jit(solution)/shard_map/ppermute | solution.py:197
  24.3 13.1 %collective-permute-start.4 = (bf16[512,128]{1,0:T(8,128)(2,1)S(1)}, bf16[512,128]{1,0:T(8,128)(2,1)S(1)}, u32[]{:S(2)}, u32[]{:S(2)}) collective-permute-start(bf16[512,128]{1,0:T(8,128)(2,1)S(1)} %fusion.1.b0_ref.refs_0_), channel_id=1, source_target_pairs={{0,272},{8,280},{16,256},{24,264},{32,304},{40,312},{48,288},{56,2... | collective-permute-start | bytes 393224 | tf_op jit(solution)/shard_map/ppermute | solution.py:42
  26.4 11.1 %collective-permute-start.3 = (bf16[512,128]{1,0:T(8,128)(2,1)S(1)}, bf16[512,128]{1,0:T(8,128)(2,1)S(1)}, u32[]{:S(2)}, u32[]{:S(2)}) collective-permute-start(bf16[512,128]{1,0:T(8,128)(2,1)S(1)} %fusion.1.b0_ref.refs_0_), channel_id=1, source_target_pairs={{0,16},{8,24},{16,0},{24,8},{32,48},{40,56},{48,32},{56,40},{64,80... | collective-permute-start | bytes 393224 | tf_op jit(solution)/shard_map/ppermute | solution.py:42
  29.1 8.9 %collective-permute-start.2 = (bf16[512,128]{1,0:T(8,128)(2,1)S(1)}, bf16[512,128]{1,0:T(8,128)(2,1)S(1)}, u32[]{:S(2)}, u32[]{:S(2)}) collective-permute-start(bf16[512,128]{1,0:T(8,128)(2,1)S(1)} %fusion.1.b0_ref.refs_0_), channel_id=1, source_target_pairs={{0,256},{8,264},{16,272},{24,280},{32,288},{40,296},{48,304},{56,3... | collective-permute-start | bytes 393224 | tf_op jit(solution)/shard_map/ppermute | solution.py:42
  37.4 5.3 %copy-start.13 = (s32[4]{0:T(128)S(1)}, s32[4]{0:T(128)}, u32[]{:S(2)}) copy-start(s32[4]{0:T(128)} %param.8) | copy-start | bytes 52
  38.1 16.4 %collective-permute-start.5 = (bf16[2560,128]{1,0:T(8,128)(2,1)S(1)}, bf16[2560,128]{1,0:T(8,128)(2,1)S(1)}, u32[]{:S(2)}, u32[]{:S(2)}) collective-permute-start(bf16[2560,128]{1,0:T(8,128)(2,1)S(1)} %shard_map.77.refs_4_.near_ref.refs_1_), channel_id=1, source_target_pairs={{0,8},{8,0},{16,24},{24,16},{32,40},{40,32},{48,56},{56,48},{64,72... | collective-permute-start | bytes 1966088 | tf_op jit(solution)/shard_map/ppermute | solution.py:42
  57.8 10.9 %collective-permute-start.6 = (bf16[2,128,128]{2,1,0:T(8,128)(2,1)S(1)}, bf16[2,128,128]{2,1,0:T(8,128)(2,1)S(1)}, u32[]{:S(2)}, u32[]{:S(2)}) collective-permute-start(bf16[2,128,128]{2,1,0:T(8,128)(2,1)S(1)} %get-tuple-element.25), channel_id=1, source_target_pairs={{0,256},{8,264},{16,272},{24,280},{32,288},{40,296},{48,304},{56,3... | collective-permute-start | bytes 196616 | tf_op jit(solution)/shard_map/ppermute | solution.py:42
  60.8 8.7 %collective-permute-start.7 = (bf16[2,128,128]{2,1,0:T(8,128)(2,1)S(1)}, bf16[2,128,128]{2,1,0:T(8,128)(2,1)S(1)}, u32[]{:S(2)}, u32[]{:S(2)}) collective-permute-start(bf16[2,128,128]{2,1,0:T(8,128)(2,1)S(1)} %get-tuple-element.26), channel_id=1, source_target_pairs={{0,16},{8,24},{16,0},{24,8},{32,48},{40,56},{48,32},{56,40},{64,80... | collective-permute-start | bytes 196616 | tf_op jit(solution)/shard_map/ppermute | solution.py:42
  66.6 8.6 %collective-permute-start.8 = (bf16[2,128,128]{2,1,0:T(8,128)(2,1)S(1)}, bf16[2,128,128]{2,1,0:T(8,128)(2,1)S(1)}, u32[]{:S(2)}, u32[]{:S(2)}) collective-permute-start(bf16[2,128,128]{2,1,0:T(8,128)(2,1)S(1)} %get-tuple-element.27), channel_id=1, source_target_pairs={{0,272},{8,280},{16,256},{24,264},{32,304},{40,312},{48,288},{56,2... | collective-permute-start | bytes 196616 | tf_op jit(solution)/shard_map/ppermute | solution.py:42
  94.0 0.8 copy-start.5
  94.8 0.8 copy-start.6
  95.6 0.7 copy-start.8
  96.2 29.3 %all-to-all-start.1 = ((bf16[8,128,256]{2,1,0:T(8,128)(2,1)}), bf16[8,128,256]{2,1,0:T(8,128)(2,1)S(1)}, u32[]{:S(2)}, u32[]{:S(2)}) async-start(bf16[8,128,256]{2,1,0:T(8,128)(2,1)} %copy-done.5), calls=%async_computation.1 | async-start | bytes 1048576 | tf_op jit(solution)/shard_map/all_to_all | solution.py:46
  104.5 5.8 %collective-permute-start.9 = (bf16[1,128,128]{2,1,0:T(8,128)(2,1)S(1)}, bf16[1,128,128]{2,1,0:T(8,128)(2,1)S(1)}, u32[]{:S(2)}, u32[]{:S(2)}) collective-permute-start(bf16[1,128,128]{2,1,0:T(8,128)(2,1)S(1)} %bitcast.18), channel_id=1, source_target_pairs={{0,256},{8,264},{16,272},{24,280},{32,288},{40,296},{48,304},{56,3... | collective-permute-start | bytes 98312 | tf_op jit(solution)/shard_map/ppermute | solution.py:42
  110.3 7.7 %collective-permute-start.10 = (bf16[2,128,128]{2,1,0:T(8,128)(2,1)S(1)}, bf16[2,128,128]{2,1,0:T(8,128)(2,1)S(1)}, u32[]{:S(2)}, u32[]{:S(2)}) collective-permute-start(bf16[2,128,128]{2,1,0:T(8,128)(2,1)S(1)} %pad_maximum_fusion.6), channel_id=1, source_target_pairs={{0,16},{8,24},{16,0},{24,8},{32,48},{40,56},{48,32},{56,40},{64,80... | collective-permute-start | bytes 196616 | tf_op jit(solution)/shard_map/ppermute | solution.py:42
  118.0 6.9 %collective-permute-start.11 = (bf16[4,128,128]{2,1,0:T(8,128)(2,1)S(1)}, bf16[4,128,128]{2,1,0:T(8,128)(2,1)S(1)}, u32[]{:S(2)}, u32[]{:S(2)}) collective-permute-start(bf16[4,128,128]{2,1,0:T(8,128)(2,1)S(1)} %pad_maximum_fusion.2), channel_id=1, source_target_pairs={{0,8},{8,0},{16,24},{24,16},{32,40},{40,32},{48,56},{56,48},{64,72... | collective-permute-start | bytes 393224 | tf_op jit(solution)/shard_map/ppermute | solution.py:42
  125.5 1.0 copy-start.3
  126.5 13.0 %copy-start.4 = (bf16[8,128,128]{2,1,0:T(8,128)(2,1)S(1)}, bf16[8,128,128]{2,1,0:T(8,128)(2,1)}, u32[]{:S(2)}) copy-start(bf16[8,128,128]{2,1,0:T(8,128)(2,1)} %pad_maximum_fusion.q_ref) | copy-start | bytes 786436
  153.9 23.6 %copy-start.7 = (bf16[16,120,128]{2,1,0:T(8,128)(2,1)S(1)}, bf16[16,120,128]{2,1,0:T(8,128)(2,1)}, u32[]{:S(2)}) copy-start(bf16[16,120,128]{2,1,0:T(8,128)(2,1)} %copy-done.6) | copy-start | bytes 1474564
  154.0 23.5 %collective-permute-start.12 = (bf16[4096,128]{1,0:T(8,128)(2,1)S(1)}, bf16[4096,128]{1,0:T(8,128)(2,1)S(1)}, u32[]{:S(2)}, u32[]{:S(2)}) collective-permute-start(bf16[4096,128]{1,0:T(8,128)(2,1)S(1)} %shard_map.83), channel_id=1, source_target_pairs={{0,16},{8,24},{16,0},{24,8},{32,48},{40,56},{48,32},{56,40},{64,80... | collective-permute-start | bytes 3145736 | tf_op jit(solution)/shard_map/ppermute | solution.py:42
  177.5 1.4 copy-start
  178.9 20.0 %copy-start.2 = (bf16[8,256,384]{2,1,0:T(8,128)(2,1)}, bf16[8,256,384]{2,1,0:T(8,128)(2,1)S(1)}, u32[]{:S(2)}) copy-start(bf16[8,256,384]{2,1,0:T(8,128)(2,1)S(1)} %get-tuple-element.42) | copy-start | bytes 4718596
  198.9 5.7 %copy-start.9 = (f32[2,120,128]{2,1,0:T(8,128)S(1)}, f32[2,120,128]{2,1,0:T(8,128)}, u32[]{:S(2)}) copy-start(f32[2,120,128]{2,1,0:T(8,128)} %copy-done.8) | copy-start | bytes 368644
  198.9 27.2 %all-to-all-start.7 = ((bf16[8,256,384]{2,1,0:T(8,128)(2,1)}), bf16[8,256,384]{2,1,0:T(8,128)(2,1)}, u32[]{:S(2)}, u32[]{:S(2)}) async-start(bf16[8,256,384]{2,1,0:T(8,128)(2,1)} %copy-done.2), calls=%async_computation.7 | async-start | bytes 3145728 | tf_op jit(solution)/shard_map/all_to_all | solution.py:34
  204.8 34.5 %copy-start.1 = (bf16[4096,128]{1,0:T(8,128)(2,1)S(1)}, bf16[4096,128]{1,0:T(8,128)(2,1)}, u32[]{:S(2)}) copy-start(bf16[4096,128]{1,0:T(8,128)(2,1)} %copy-done) | copy-start | bytes 3145732
  204.8 21.2 %collective-permute-start.13 = (bf16[2,32,128]{2,1,0:T(8,128)(2,1)S(1)}, bf16[2,32,128]{2,1,0:T(8,128)(2,1)S(1)}, u32[]{:S(2)}, u32[]{:S(2)}) collective-permute-start(bf16[2,32,128]{2,1,0:T(8,128)(2,1)S(1)} %get-tuple-element.54), channel_id=1, source_target_pairs={{0,8},{8,16},{16,24},{24,32},{32,40},{40,48},{48,56},{56,64},{64,7... | collective-permute-start | bytes 49160 | tf_op jit(solution)/shard_map/ppermute | solution.py:196
  208.3 17.7 %collective-permute-start.14 = (bf16[2,32,128]{2,1,0:T(8,128)(2,1)S(1)}, bf16[2,32,128]{2,1,0:T(8,128)(2,1)S(1)}, u32[]{:S(2)}, u32[]{:S(2)}) collective-permute-start(bf16[2,32,128]{2,1,0:T(8,128)(2,1)S(1)} %get-tuple-element.55), channel_id=1, source_target_pairs={{8,0},{16,8},{24,16},{32,24},{40,32},{48,40},{56,48},{64,56},{72,6... | collective-permute-start | bytes 49160 | tf_op jit(solution)/shard_map/ppermute | solution.py:197
  215.0 11.0 %collective-permute-start.15 = (bf16[2,32,128]{2,1,0:T(8,128)(2,1)S(1)}, bf16[2,32,128]{2,1,0:T(8,128)(2,1)S(1)}, u32[]{:S(2)}, u32[]{:S(2)}) collective-permute-start(bf16[2,32,128]{2,1,0:T(8,128)(2,1)S(1)} %get-tuple-element.54), channel_id=1, source_target_pairs={{0,264},{8,272},{16,280},{24,288},{32,296},{40,304},{48,312},{56,3... | collective-permute-start | bytes 49160 | tf_op jit(solution)/shard_map/ppermute | solution.py:196
  216.3 9.8 %collective-permute-start.17 = (bf16[2,32,128]{2,1,0:T(8,128)(2,1)S(1)}, bf16[2,32,128]{2,1,0:T(8,128)(2,1)S(1)}, u32[]{:S(2)}, u32[]{:S(2)}) collective-permute-start(bf16[2,32,128]{2,1,0:T(8,128)(2,1)S(1)} %get-tuple-element.55), channel_id=1, source_target_pairs={{8,256},{16,264},{24,272},{32,280},{40,288},{48,296},{56,304},{64,... | collective-permute-start | bytes 49160 | tf_op jit(solution)/shard_map/ppermute | solution.py:197
  218.5 7.6 %collective-permute-start.16 = (bf16[256,128]{1,0:T(8,128)(2,1)S(1)}, bf16[256,128]{1,0:T(8,128)(2,1)S(1)}, u32[]{:S(2)}, u32[]{:S(2)}) collective-permute-start(bf16[256,128]{1,0:T(8,128)(2,1)S(1)} %bitcast.22), channel_id=1, source_target_pairs={{0,256},{8,264},{16,272},{24,280},{32,288},{40,296},{48,304},{56,3... | collective-permute-start | bytes 196616 | tf_op jit(solution)/shard_map/ppermute | solution.py:42
  228.4 21.9 %all-to-all-start.8 = ((bf16[8,32,384]{2,1,0:T(8,128)(2,1)}), bf16[8,32,384]{2,1,0:T(8,128)(2,1)S(1)}, u32[]{:S(2)}, u32[]{:S(2)}) async-start(bf16[8,32,384]{2,1,0:T(8,128)(2,1)} %shard_map.87.refs_4_), calls=%async_computation.8 | async-start | bytes 393216 | tf_op jit(solution)/shard_map/all_to_all | solution.py:46
  243.4 6.2 %collective-permute-start.18 = (bf16[2,128,128]{2,1,0:T(8,128)(2,1)S(1)}, bf16[2,128,128]{2,1,0:T(8,128)(2,1)S(1)}, u32[]{:S(2)}, u32[]{:S(2)}) collective-permute-start(bf16[2,128,128]{2,1,0:T(8,128)(2,1)S(1)} %get-tuple-element.44), channel_id=1, source_target_pairs={{0,256},{8,264},{16,272},{24,280},{32,288},{40,296},{48,304},{56,3... | collective-permute-start | bytes 196616 | tf_op jit(solution)/shard_map/ppermute | solution.py:42

commit v10 on v8

--- a/solution.py
+++ b/solution.py
@@ -50,8 +50,8 @@
     return lax.all_to_all(parts, "head", 0, 0, axis_index_groups=groups)
 
 
-BITS = (32, 2, 1)
-SLOTS = (0, 4, 2, 6, 1, 5, 3, 7)
+BITS = (2, 32, 1)
+SLOTS = (0, 2, 4, 6, 1, 3, 5, 7)
 
 
 def doubled(array):
@@ -90,38 +90,52 @@
 SPAN = ROWS + TAPS
 
 
-def conv_body(forward, sc_ref, x_ref, w_ref, *refs):
+PART = 8 * LANES
+LATER = PART + 2 * ROWS
+
+
+def conv_body(forward, sc_ref, x_ref, *refs):
+    near_ref, gy_ref, gx_ref, low_ref, high_ref = refs[:5]
     own_ref, other_ref = refs[-2:]
-    ends = [sc_ref[2 + u] for u in range(4)]
-    first = TAPS * (sc_ref[0] if forward else 1 - sc_ref[0])
+    y, x = sc_ref[0], sc_ref[1]
+    ends = [sc_ref[3 + u] for u in range(4)]
     row = lax.broadcasted_iota(jnp.int32, (ROWS, LANES), 0)
     for b in range(2):
-        shard = sc_ref[1] if b == 0 else sc_ref[1] ^ 32
-        pos = shard * ROWS + row
+        pos = (sc_ref[2] ^ (0, 2)[b]) * ROWS + row
         low, high = bounds_of(pos, ends)
-        source = pos + (first - HALF)
-        spans = [
-            x_ref[b, pl.ds(pl.multiple_of(g * PADDED + first, TAPS), SPAN)].astype(F32)
-            for g in range(2)
-        ]
         totals = [jnp.zeros((ROWS, LANES), F32) for g in range(2)]
-        for rest in range(8):
-            rolled = [pltpu.roll(e, SPAN - rest, 0) if rest else e for e in spans]
-            for start in range(0, TAPS + 1, 8):
-                tap = start + rest if forward else TAPS - start - rest
-                if not 0 <= tap < TAPS:
-                    continue
-                key = source + (start + rest)
-                keep = (key >= low) & (key < high)
-                for g in range(2):
-                    at = (tap // 4 * 2 + g) * LANES
-                    piece = jnp.where(keep, rolled[g][start : start + ROWS], 0.0).astype(BF)
-                    totals[g] += lax.dot_general(
-                        piece,
-                        w_ref[tap % 4, at : at + LANES],
-                        (((1,), (0 if forward else 1,)), ((), ())),
-                        preferred_element_type=F32,
-                    )
+        for my in range(2):
+            first = TAPS * (y ^ my if forward else 1 - (y ^ my))
+            spans = [
+                x_ref[b, pl.ds(pl.multiple_of(g * PADDED + first, TAPS), SPAN)].astype(F32)
+                for g in range(2)
+            ]
+            for mx in range(2):
+                shift = x ^ mx if forward else 4 - (x ^ mx)
+                source = pos + (first + shift - HALF)
+                for odd in range(2):
+                    rolled = [pltpu.roll(e, SPAN - 4 * odd - shift, 0) for e in spans]
+                    for step in range(odd, 8, 2):
+                        key = source + 4 * step
+                        keep = (key >= low) & (key < high)
+                        z = step if forward else 7 - step
+                        start = 8 * (step // 2)
+                        if my and mx:
+                            w_ref, base = (low_ref, 0) if z < 4 else (high_ref, 0)
+                        else:
+                            w_ref = (near_ref, gx_ref)[mx] if not my else gy_ref
+                            base = 0 if z < 4 else LATER
+                        for g in range(2):
+                            at = base + (z % 4 * 2 + g) * LANES
+                            piece = jnp.where(
+                                keep, rolled[g][start : start + ROWS], 0.0
+                            ).astype(BF)
+                            totals[g] += lax.dot_general(
+                                piece,
+                                w_ref[at : at + LANES],
+                                (((1,), (0 if forward else 1,)), ((), ())),
+                                preferred_element_type=F32,
+                            )
         for g in range(2):
             if b == 0:
                 own_ref[g] = totals[g]
@@ -143,19 +157,18 @@
     )(weight)
 
 
-def joined_body(w_ref, own_ref, other_ref, qkv_ref, out_ref):
-    for i in range(4):
-        for z in range(8):
-            out_ref[i, z * 2 * LANES : (z + 1) * 2 * LANES] = w_ref[z]
-        for b, rows_ref in enumerate((own_ref, other_ref)):
-            start = 16 * LANES + b * ROWS
-            out_ref[i, start : start + ROWS] = rows_ref[...]
-
-
-def joined(taps, own, other, w_qkv):
-    return vmem_call(
-        joined_body,
-        jax.ShapeDtypeStruct((4, 16 * LANES + 2 * ROWS, LANES), BF),
+def near_body(w_ref, own_ref, other_ref, qkv_ref, out_ref):
+    for z in range(8):
+        start = z * 2 * LANES if z < 4 else LATER + (z - 4) * 2 * LANES
+        out_ref[start : start + 2 * LANES] = w_ref[z]
+    out_ref[PART : PART + ROWS] = own_ref[...]
+    out_ref[PART + ROWS : LATER] = other_ref[...]
+
+
+def near_taps(taps, own, other, w_qkv):
+    return vmem_call(
+        near_body,
+        jax.ShapeDtypeStruct((LATER + PART, LANES), BF),
         inputs=3,
         earlier=1,
     )(taps, own, other, w_qkv)
@@ -169,10 +182,10 @@
     sent = rows.reshape(2 * ROWS, LANES)
     if more is not None:
         sent = jnp.concatenate([sent, more], axis=0)
-    got = swap(sent, 32)
+    got = swap(sent, 2)
     sides = [
-        [lax.ppermute(last, "tm", [(i, j ^ bit) for i, j in up]) for bit in (0, 32)],
-        [lax.ppermute(head, "tm", [(i, j ^ bit) for i, j in down]) for bit in (0, 32)],
+        [lax.ppermute(last, "tm", [(i, j ^ bit) for i, j in up]) for bit in (0, 2)],
+        [lax.ppermute(head, "tm", [(i, j ^ bit) for i, j in down]) for bit in (0, 2)],
     ]
     other = got[: 2 * ROWS].reshape(2, ROWS, LANES)
     pair = [
@@ -190,11 +203,11 @@
             jax.ShapeDtypeStruct((2, ROWS, LANES), BF),
         ),
         scalars=1,
-        inputs=2,
+        inputs=6,
         earlier=len(earlier),
         flops=32 * 2 * 2 * 2 * ROWS * HD * HD,
-    )(scalars, pair, taps, *earlier)
-    return own, swap(other, 32)
+    )(scalars, pair, *taps, *earlier)
+    return own, swap(other, 2)
 
 
 CHUNK = 256
@@ -205,26 +218,20 @@
 CONTRACT = (((1,), (1,)), ((), ()))
 
 
-def upstream_rows(sc_ref, f_ref, d_ref):
-    for i, e in enumerate(SLOTS):
-        row = 16 * LANES + e // 4 * ROWS
-        d_ref[i * ROWS : (i + 1) * ROWS] = f_ref[(sc_ref[0] % 4) ^ (e % 4), row : row + ROWS]
-
-
-def scored(c, q_ref, kv_ref, d_ref):
+def scored(c, q_ref, kv_ref, up_refs):
     keys = kv_ref[:, :, :LANES].reshape(ALL, LANES)
     values = kv_ref[:, :, LANES:].reshape(ALL, LANES)
     q = q_ref[c * N : (c + 1) * N].reshape(CHUNK, LANES)
-    d = d_ref[c * CHUNK : (c + 1) * CHUNK]
+    d = up_refs[c][PART:LATER]
     scores = lax.dot_general(keys, q, CONTRACT, preferred_element_type=F32)
     dprobs = lax.dot_general(values, d, CONTRACT, preferred_element_type=F32)
     return keys, values, q, d, scores * SCALE2, dprobs
 
 
-def stats_body(sc_ref, q_ref, kv_ref, f_ref, out_ref, d_ref):
-    upstream_rows(sc_ref, f_ref, d_ref)
+def stats_body(sc_ref, q_ref, kv_ref, *refs):
+    *up_refs, out_ref = refs
     for c in range(ALL // CHUNK):
-        _, _, _, _, scores, dprobs = scored(c, q_ref, kv_ref, d_ref)
+        _, _, _, _, scores, dprobs = scored(c, q_ref, kv_ref, up_refs)
         peak = jnp.max(scores, axis=0, keepdims=True)
         weight = jnp.exp2(scores - peak)
         total = jnp.sum(weight, axis=0, keepdims=True)
@@ -238,10 +245,8 @@
         out_ref[i] = out_ref[0]
 
 
-def grads_body(
-    sc_ref, q_ref, kv_ref, f_ref, stats_ref, od_ref, dkv_ref, d_ref, dk_ref, dv_ref
-):
-    upstream_rows(sc_ref, f_ref, d_ref)
+def grads_body(sc_ref, q_ref, kv_ref, *refs):
+    *up_refs, stats_ref, od_ref, dkv_ref, dk_ref, dv_ref = refs
     for c in range(ALL // CHUNK):
         peaks, totals, alongs = (
             jnp.concatenate(
@@ -255,7 +260,7 @@
         total = jnp.sum(totals * factor, axis=0)
         delta = jnp.sum(alongs * factor, axis=0) / total
         lse = top + jnp.log2(total)
-        keys, values, q, d, scores, dprobs = scored(c, q_ref, kv_ref, d_ref)
+        keys, values, q, d, scores, dprobs = scored(c, q_ref, kv_ref, up_refs)
         probs = jnp.exp2(scores - lse)
         dscores = (probs * (dprobs - delta)).astype(BF)
         probs = probs.astype(BF)
@@ -280,18 +285,17 @@
         dkv_ref[i, :, LANES:] = dv_ref[piece].astype(BF)
 
 
-def attention_stats(scalars, queries, keys, gathered):
+def attention_stats(scalars, queries, keys, upstream):
     return vmem_call(
         stats_body,
         jax.ShapeDtypeStruct((8, 3, 8, ROWS), F32),
-        scratch=[pltpu.VMEM((ALL, LANES), BF)],
         scalars=1,
-        inputs=3,
+        inputs=6,
         flops=2 * 2 * ALL * ALL * LANES,
-    )(scalars, queries, keys, gathered)
-
-
-def attention_grads(scalars, queries, keys, gathered, stats):
+    )(scalars, queries, keys, *upstream)
+
+
+def attention_grads(scalars, queries, keys, upstream, stats):
     return vmem_call(
         grads_body,
         (
@@ -299,14 +303,13 @@
             jax.ShapeDtypeStruct((8, ROWS, 2 * LANES), BF),
         ),
         scratch=[
-            pltpu.VMEM((ALL, LANES), BF),
             pltpu.VMEM((ALL, LANES), F32),
             pltpu.VMEM((ALL, LANES), F32),
         ],
         scalars=1,
-        inputs=4,
+        inputs=7,
         flops=6 * 2 * ALL * ALL * LANES,
-    )(scalars, queries, keys, gathered, stats)
+    )(scalars, queries, keys, *upstream, stats)
 
 
 GROUPS = 16
@@ -518,7 +521,7 @@
         return jnp.concatenate([jnp.stack(first).astype(jnp.int32), ends])
 
     y, x = index // 32, index % 4
-    where = scalars(y, index)
+    where = scalars(y, x, index)
     order = scalars(y * 4 + x)
 
     frames_g = frames.reshape(ROWS, 2, HD).transpose(1, 0, 2)
@@ -526,7 +529,11 @@
     upstream = jnp.pad(grad_out, ((0, 0), (0, LANES - HD)))
     pair, other_upstream = paired(frames_g, upstream)
     taps = exchange_z(taps_sent(conv_weight[0]))
-    taps = exchange_x(joined(taps, upstream, other_upstream, w_qkv))
+    near = near_taps(taps, upstream, other_upstream, w_qkv)
+    by_y, by_x = swap(near, 32), swap(near, 1)
+    both = swap(by_x[:LATER], 32), swap(by_y[LATER:], 1)
+    taps = near, by_y, by_x, *both
+    upstream = near, by_y, by_x, both[0]
     own, other = convolved(True, where, pair, taps)
     hidden_t, slope_t, sent = hidden_rows(own, other, frames_g)
 
@@ -537,8 +544,8 @@
 
     keys = exchange_z(keys)
     queries = doubled(queries)
-    stats = exchange_xy(attention_stats(order, queries, keys, taps))
-    od, dkv = attention_grads(order, queries, keys, taps, stats)
+    stats = exchange_xy(attention_stats(order, queries, keys, upstream))
+    od, dkv = attention_grads(order, queries, keys, upstream, stats)
     od = exchange_xy(od)
     dkv = exchange_z(dkv)
 

time: 234 us -> 243 us (1.038)
  starting transfers between devices: 78.3 us -> 89.4 us
  waiting for transfers between devices: 49 us -> 38.4 us
  local copies, waits for them, and re-layouts: 7.17 us -> 10.2 us
    ppermute x7 -> x11, starting transfers between devices: 18 us -> 34.4 us  [swap(): return lax.ppermute(array, 'tm', [(i, i ^ bit) for i in range(64)])]
    ppermute x4, waiting for transfers between devices: 14.5 us -> 1.96 us  [paired(): lax.ppermute(last, 'tm', [(i, j ^ bit) for i, j in up])]
    ppermute x7 -> x11, waiting for transfers between devices: 20.4 us -> 25.2 us  [swap(): return lax.ppermute(array, 'tm', [(i, i ^ bit) for i in range(64)])]
    all_to_all x1 -> x0, starting transfers between devices: 4.42 us -> none  [exchange_x(): return lax.all_to_all(parts, 'tm', 0, 0, axis_index_groups=X_GROUPS)]
    unnamed x25 -> x37, local copies, waits for them, and re-layouts: 6.26 us -> 8.6 us
  transfers between devices with their start and end apart: 20 -> 23, of which waited for: 12 -> 12; matrix products, arithmetic and copies ran while one was open for 2% -> 2% of each run, Pallas kernels for 2% -> 2%
where the time goes in v10:
time: 243 us; the launch traced here: 241 us
  starting transfers between devices  89.4 us (37%)
  blocking collectives  79.6 us (33%)
  waiting for transfers between devices  38.4 us (16%)
  Pallas kernels  20.9 us (9%)
  local copies, waits for them, and re-layouts  10.2 us (4%)
    ppermute x11, starting transfers between devices, swap(): return lax.ppermute(array, 'tm', [(i, i ^ bit) for i in range(64)])  34.4 us
    ppermute x11, waiting for transfers between devices, swap(): return lax.ppermute(array, 'tm', [(i, i ^ bit) for i in range(64)])  25.2 us
    all_to_all x2, blocking collectives, exchange_xy(): return lax.all_to_all(parts, 'tm', 0, 0, axis_index_groups=XY_GROUPS)  22.4 us
    all_to_all x1, blocking collectives, exchange_z(): return lax.all_to_all(parts, 'tm', 0, 0, axis_index_groups=Z_GROUPS)  20.2 us
    all_to_all x2, blocking collectives, exchange_head(): return lax.all_to_all(parts, 'head', 0, 0, axis_index_groups=groups)  19.9 us
    all_to_all x3, starting transfers between devices, exchange_z(): return lax.all_to_all(parts, 'tm', 0, 0, axis_index_groups=Z_GROUPS)  19.2 us
    ppermute x4, starting transfers between devices, paired(): lax.ppermute(head, 'tm', [(i, j ^ bit) for i, j in down])  18.7 us
    all_gather x1, blocking collectives, on_device(): all_t = lax.all_gather(sent, 'head', axis=0, tiled=True)  17.1 us
  transfers between devices with their start and end apart: 23, of which 12 were waited for; matrix products, arithmetic and copies ran while one was open for 2% of the time, Pallas kernels for 2%

profile of v10, /device:TPU:8, one launch (start us, length us, event | category | flops | bytes accessed | tf_op | source)
XLA Modules:
  0.0 241.4 jit_solution(12924384611779742062)
XLA Ops:
  0.6 0.8 copy-done.13
  1.5 0.9 shard_map.76
  2.3 10.3 %all-to-all-start = ((bf16[8,256,128]{2,1,0:T(8,128)(2,1)}), bf16[8,256,128]{2,1,0:T(8,128)(2,1)S(1)}, u32[]{:S(2)}, u32[]{:S(2)}) async-start(bf16[8,256,128]{2,1,0:T(8,128)(2,1)} %shard_map.76), calls=%async_computation | async-start | bytes 1048576 | tf_op jit(solution)/shard_map/all_to_all | solution.py:46
  13.0 4.9 %collective-permute-start.3 = (bf16[384,128]{1,0:T(8,128)(2,1)S(1)}, bf16[384,128]{1,0:T(8,128)(2,1)S(1)}, u32[]{:S(2)}, u32[]{:S(2)}) collective-permute-start(bf16[384,128]{1,0:T(8,128)(2,1)S(1)} %pad_maximum_fusion.5), channel_id=1, source_target_pairs={{0,16},{8,24},{16,0},{24,8},{32,48},{40,56},{48,32},{56,40},{64,80... | collective-permute-start | bytes 294920 | tf_op jit(solution)/shard_map/ppermute | solution.py:42
  17.9 2.4 copy.22.qkv_ref.w_ref
  20.3 0.7 collective-permute-done.3
  21.0 9.1 %all-to-all-done.w_ref = bf16[8,256,128]{2,1,0:T(8,128)(2,1)S(1)} async-done(((bf16[8,256,128]{2,1,0:T(8,128)(2,1)}), bf16[8,256,128]{2,1,0:T(8,128)(2,1)S(1)}, u32[]{:S(2)}, u32[]{:S(2)}) %all-to-all-start) | async-done | bytes 524320 | tf_op jit(solution)/shard_map/all_to_all | solution.py:46
  30.2 3.4 %collective-permute-start.6 = (bf16[2304,128]{1,0:T(8,128)(2,1)S(1)}, bf16[2304,128]{1,0:T(8,128)(2,1)S(1)}, u32[]{:S(2)}, u32[]{:S(2)}) collective-permute-start(bf16[2304,128]{1,0:T(8,128)(2,1)S(1)} %shard_map.77.refs_0_), channel_id=1, source_target_pairs={{0,8},{8,0},{16,24},{24,16},{32,40},{40,32},{48,56},{56,48},{64,72... | collective-permute-start | bytes 1769480 | tf_op jit(solution)/shard_map/ppermute | solution.py:42
  33.6 2.4 collective-permute-start.5
  36.0 0.6 pad_slice_fusion.1
  36.6 4.0 %collective-permute-start.2 = (bf16[2,32,128]{2,1,0:T(8,128)(2,1)}, bf16[2,32,128]{2,1,0:T(8,128)(2,1)S(1)}, u32[]{:S(2)}, u32[]{:S(2)}) collective-permute-start(bf16[2,32,128]{2,1,0:T(8,128)(2,1)} %get-tuple-element.52), channel_id=1, source_target_pairs={{0,24},{8,0},{16,8},{24,48},{32,56},{40,32},{48,40},{56,80},{64,88... | collective-permute-start | bytes 49160 | tf_op jit(solution)/shard_map/ppermute | solution.py:187
  40.6 1.9 collective-permute-start
  42.5 8.1 %collective-permute-start.1 = (bf16[2,32,128]{2,1,0:T(8,128)(2,1)}, bf16[2,32,128]{2,1,0:T(8,128)(2,1)}, u32[]{:S(2)}, u32[]{:S(2)}) collective-permute-start(bf16[2,32,128]{2,1,0:T(8,128)(2,1)} %get-tuple-element.53), channel_id=1, source_target_pairs={{8,0},{16,8},{24,16},{32,24},{40,32},{48,40},{56,48},{64,56},{72,6... | collective-permute-start | bytes 49160 | tf_op jit(solution)/shard_map/ppermute | solution.py:188
  50.7 0.2 reduce-window.9
  51.0 1.9 collective-permute-start.4
  52.9 1.9 collective-permute-start.7
  54.9 1.9 collective-permute-start.8
  56.8 0.7 pad_maximum_fusion.4
  57.6 0.4 collective-permute-done.4
  58.0 5.6 %collective-permute-done.8.refs_4_ = bf16[1024,128]{1,0:T(8,128)(2,1)S(1)} collective-permute-done((bf16[1024,128]{1,0:T(8,128)(2,1)S(1)}, bf16[1024,128]{1,0:T(8,128)(2,1)S(1)}, u32[]{:S(2)}, u32[]{:S(2)}) %collective-permute-start.8) | collective-permute-done | bytes 262176 | tf_op jit(solution)/shard_map/ppermute | solution.py:42
  63.6 3.3 %shard_map.78 = (f32[2,128,128]{2,1,0:T(8,128)S(1)}, bf16[2,128,128]{2,1,0:T(8,128)(2,1)S(1)}) custom-call(s32[7]{0:T(128)S(1)} %pad_add_fusion.2.sc_ref, bf16[2,384,128]{2,1,0:T(8,128)(2,1)S(1)} %pad_maximum_fusion.1.x_ref, bf16[2304,128]{1,0:T(8,128)(2,1)S(1)} %shard_map.77.refs_0_, bf16[2304,128]{1,0:T(8,128)(2,1)S(1)} %collective-permute-done.5.refs_1_, ...), custom_call_target="tpu_custom_call" | custom-call | flops 471859200 | bytes 1048576 | tf_op jit(solution)/shard_map/pallas_call | solution.py:199
  67.0 0.7 copy-done
  67.7 4.6 %collective-permute-start.9 = (bf16[2,128,128]{2,1,0:T(8,128)(2,1)S(1)}, bf16[2,128,128]{2,1,0:T(8,128)(2,1)S(1)}, u32[]{:S(2)}, u32[]{:S(2)}) collective-permute-start(bf16[2,128,128]{2,1,0:T(8,128)(2,1)S(1)} %get-tuple-element.23), channel_id=1, source_target_pairs={{0,16},{8,24},{16,0},{24,8},{32,48},{40,56},{48,32},{56,40},{64,80... | collective-permute-start | bytes 196616 | tf_op jit(solution)/shard_map/ppermute | solution.py:42
  72.3 3.0 %collective-permute-done.9.other_ref = bf16[2,128,128]{2,1,0:T(8,128)(2,1)S(1)} collective-permute-done((bf16[2,128,128]{2,1,0:T(8,128)(2,1)S(1)}, bf16[2,128,128]{2,1,0:T(8,128)(2,1)S(1)}, u32[]{:S(2)}, u32[]{:S(2)}) %collective-permute-start.9) | collective-permute-done | bytes 65568 | tf_op jit(solution)/shard_map/ppermute | solution.py:42
  75.5 0.6 copy-done.9
  76.1 17.1 %all_gather.3.all_ref = bf16[16,120,128]{2,1,0:T(8,128)(2,1)S(1)} all-gather(bf16[2,120,128]{2,1,0:T(8,128)(2,1)S(1)} %get-tuple-element.24), channel_id=1, replica_groups=mesh['tm'=64,'head'=8] {'head'}, dimensions={0}, use_global_device_ids=true | all-gather | bytes 552960 | tf_op jit(solution)/shard_map/all_gather | solution.py:540
  93.3 1.5 shard_map.80
  94.8 0.8 copy-done.6
  95.6 0.8 copy-done.7
  96.4 0.6 copy-done.11
  97.0 4.1 %all-to-all-start.1 = ((bf16[8,128,256]{2,1,0:T(8,128)(2,1)}), bf16[8,128,256]{2,1,0:T(8,128)(2,1)}, u32[]{:S(2)}, u32[]{:S(2)}) async-start(bf16[8,128,256]{2,1,0:T(8,128)(2,1)} %copy-done.6), calls=%async_computation.1 | async-start | bytes 1048576 | tf_op jit(solution)/shard_map/all_to_all | solution.py:46
  101.2 4.6 %collective-permute-start.10 = (bf16[1,128,128]{2,1,0:T(8,128)(2,1)S(1)}, bf16[1,128,128]{2,1,0:T(8,128)(2,1)S(1)}, u32[]{:S(2)}, u32[]{:S(2)}) collective-permute-start(bf16[1,128,128]{2,1,0:T(8,128)(2,1)S(1)} %bitcast.22), channel_id=1, source_target_pairs={{0,16},{8,24},{16,0},{24,8},{32,48},{40,56},{48,32},{56,40},{64,80... | collective-permute-start | bytes 98312 | tf_op jit(solution)/shard_map/ppermute | solution.py:42
  105.8 2.7 %collective-permute-done.10 = bf16[1,128,128]{2,1,0:T(8,128)(2,1)S(1)} collective-permute-done((bf16[1,128,128]{2,1,0:T(8,128)(2,1)S(1)}, bf16[1,128,128]{2,1,0:T(8,128)(2,1)S(1)}, u32[]{:S(2)}, u32[]{:S(2)}) %collective-permute-start.10) | collective-permute-done | bytes 32800 | tf_op jit(solution)/shard_map/ppermute | solution.py:42
  108.5 3.9 %collective-permute-start.11 = (bf16[2,128,128]{2,1,0:T(8,128)(2,1)S(1)}, bf16[2,128,128]{2,1,0:T(8,128)(2,1)S(1)}, u32[]{:S(2)}, u32[]{:S(2)}) collective-permute-start(bf16[2,128,128]{2,1,0:T(8,128)(2,1)S(1)} %pad_maximum_fusion.9), channel_id=1, source_target_pairs={{0,256},{8,264},{16,272},{24,280},{32,288},{40,296},{48,304},{56,3... | collective-permute-start | bytes 196616 | tf_op jit(solution)/shard_map/ppermute | solution.py:42
  112.4 2.3 collective-permute-done.11
  114.7 2.6 %collective-permute-start.12 = (bf16[4,128,128]{2,1,0:T(8,128)(2,1)S(1)}, bf16[4,128,128]{2,1,0:T(8,128)(2,1)S(1)}, u32[]{:S(2)}, u32[]{:S(2)}) collective-permute-start(bf16[4,128,128]{2,1,0:T(8,128)(2,1)S(1)} %pad_maximum_fusion.3), channel_id=1, source_target_pairs={{0,8},{8,0},{16,24},{24,16},{32,40},{40,32},{48,56},{56,48},{64,72... | collective-permute-start | bytes 393224 | tf_op jit(solution)/shard_map/ppermute | solution.py:42
  117.3 4.2 %collective-permute-done.12 = bf16[4,128,128]{2,1,0:T(8,128)(2,1)S(1)} collective-permute-done((bf16[4,128,128]{2,1,0:T(8,128)(2,1)S(1)}, bf16[4,128,128]{2,1,0:T(8,128)(2,1)S(1)}, u32[]{:S(2)}, u32[]{:S(2)}) %collective-permute-start.12) | collective-permute-done | bytes 131104 | tf_op jit(solution)/shard_map/ppermute | solution.py:42
  121.6 1.0 copy-done.1
  122.6 2.9 %shard_map.81 = f32[8,3,8,128]{3,2,1,0:T(8,128)S(1)} custom-call(s32[5]{0:T(128)S(1)} %get-tuple-element.55.sc_ref, bf16[8,128,128]{2,1,0:T(8,128)(2,1)S(1)} %pad_maximum_fusion.q_ref, bf16[8,128,256]{2,1,0:T(8,128)(2,1)} %all-to-all-done.1.kv_ref, bf16[2304,128]{1,0:T(8,128)(2,1)S(1)} %shard_map.77.refs_0_, ...), custom_call_target="tpu_custom_call" | custom-call | flops 536870912 | bytes 1048576 | tf_op jit(solution)/shard_map/pallas_call | solution.py:289
  125.5 11.3 %all_to_all.45.refs_4_ = f32[8,3,8,128]{3,2,1,0:T(8,128)S(1)} all-to-all(f32[8,3,8,128]{3,2,1,0:T(8,128)S(1)} %shard_map.81), channel_id=1, replica_groups={{0,8,16,24,256,264,272,280},{32,40,48,56,288,296,304,312},{64,72,80,88,..., dimensions={0} | all-to-all | bytes 196608 | tf_op jit(solution)/shard_map/all_to_all | solution.py:34
  136.8 4.0 %shard_map.82 = (bf16[8,2,120,128]{3,2,1,0:T(8,128)(2,1)S(1)}, bf16[8,128,256]{2,1,0:T(8,128)(2,1)S(1)}) custom-call(s32[5]{0:T(128)S(1)} %get-tuple-element.55.sc_ref, bf16[8,128,128]{2,1,0:T(8,128)(2,1)S(1)} %pad_maximum_fusion.q_ref, bf16[8,128,256]{2,1,0:T(8,128)(2,1)} %all-to-all-done.1.kv_ref, bf16[2304,128]{1,0:T(8,128)(2,1)S(1)} %shard_map.77.refs_0_, ...), custom_call_target="tpu_custom_call" | custom-call | flops 1610612736 | bytes 1048576 | tf_op jit(solution)/shard_map/pallas_call | solution.py:299
  140.8 11.0 %all_to_all.46.od_ref = bf16[8,2,120,128]{3,2,1,0:T(8,128)(2,1)S(1)} all-to-all(bf16[8,2,120,128]{3,2,1,0:T(8,128)(2,1)S(1)} %get-tuple-element.28), channel_id=1, replica_groups={{0,8,16,24,256,264,272,280},{32,40,48,56,288,296,304,312},{64,72,80,88,..., dimensions={0} | all-to-all | bytes 983040 | tf_op jit(solution)/shard_map/all_to_all | solution.py:34
  151.9 20.2 %all_to_all.47.dkv_ref = bf16[8,128,256]{2,1,0:T(8,128)(2,1)S(1)} all-to-all(bf16[8,128,256]{2,1,0:T(8,128)(2,1)S(1)} %get-tuple-element.29), channel_id=1, replica_groups={{0,32,64,96,128,160,192,224},{8,40,72,104,136,168,200,232},{16,48,80,11..., dimensions={0} | all-to-all | bytes 1048576 | tf_op jit(solution)/shard_map/all_to_all | solution.py:46
  172.0 1.4 shard_map.83
  173.5 4.2 %all_to_all.48.parts_ref = bf16[2,4,2,128,128]{4,3,2,1,0:T(8,128)(2,1)S(1)} all-to-all(bf16[2,4,2,128,128]{4,3,2,1,0:T(8,128)(2,1)S(1)} %get-tuple-element.32), channel_id=1, replica_groups={{0,1},{2,3},{4,5},{6,7},{8,9},{10,11},{12,13},{14,15},{16,17},{18,19},{..., dimensions={0} | all-to-all | bytes 1048576 | tf_op jit(solution)/shard_map/all_to_all | solution.py:50
  177.7 15.8 %all_to_all.49.parts_ref = bf16[4,2,128,128]{3,2,1,0:T(8,128)(2,1)S(1)} all-to-all(bf16[4,2,128,128]{3,2,1,0:T(8,128)(2,1)S(1)} %shard_map.84), channel_id=1, replica_groups={{0,2,4,6},{1,3,5,7},{8,10,12,14},{9,11,13,15},{16,18,20,22},{17,19,21,2..., dimensions={0} | all-to-all | bytes 524288 | tf_op jit(solution)/shard_map/all_to_all | solution.py:50
  193.4 5.8 %all-to-all-start.7 = ((bf16[8,256,384]{2,1,0:T(8,128)(2,1)}), bf16[8,256,384]{2,1,0:T(8,128)(2,1)}, u32[]{:S(2)}, u32[]{:S(2)}) async-start(bf16[8,256,384]{2,1,0:T(8,128)(2,1)} %copy-done.3), calls=%async_computation.7 | async-start | bytes 3145728 | tf_op jit(solution)/shard_map/all_to_all | solution.py:34
  199.2 0.1 shard_map.85
  199.4 3.5 %collective-permute-start.13 = (bf16[2,32,128]{2,1,0:T(8,128)(2,1)S(1)}, bf16[2,32,128]{2,1,0:T(8,128)(2,1)S(1)}, u32[]{:S(2)}, u32[]{:S(2)}) collective-permute-start(bf16[2,32,128]{2,1,0:T(8,128)(2,1)S(1)} %get-tuple-element.50), channel_id=1, source_target_pairs={{0,8},{8,16},{16,24},{24,32},{32,40},{40,48},{48,56},{56,64},{64,7... | collective-permute-start | bytes 49160 | tf_op jit(solution)/shard_map/ppermute | solution.py:187
  202.9 6.7 %collective-permute-start.14 = (bf16[2,32,128]{2,1,0:T(8,128)(2,1)S(1)}, bf16[2,32,128]{2,1,0:T(8,128)(2,1)S(1)}, u32[]{:S(2)}, u32[]{:S(2)}) collective-permute-start(bf16[2,32,128]{2,1,0:T(8,128)(2,1)S(1)} %get-tuple-element.51), channel_id=1, source_target_pairs={{8,0},{16,8},{24,16},{32,24},{40,32},{48,40},{56,48},{64,56},{72,6... | collective-permute-start | bytes 49160 | tf_op jit(solution)/shard_map/ppermute | solution.py:188
  209.6 1.9 collective-permute-start.15
  211.5 1.9 collective-permute-start.17
  213.5 2.3 collective-permute-start.16
  215.8 2.0 collective-permute-done.13
  217.8 1.6 collective-permute-done.17
  219.4 1.7 collective-permute-done.16
  221.2 2.3 shard_map.86.refs_5_
  223.4 4.7 %all-to-all-start.8 = ((bf16[8,32,384]{2,1,0:T(8,128)(2,1)}), bf16[8,32,384]{2,1,0:T(8,128)(2,1)S(1)}, u32[]{:S(2)}, u32[]{:S(2)}) async-start(bf16[8,32,384]{2,1,0:T(8,128)(2,1)} %shard_map.86.refs_5_), calls=%async_computation.8 | async-start | bytes 393216 | tf_op jit(solution)/shard_map/all_to_all | solution.py:46
  228.2 4.1 %shard_map.87 = (f32[2,128,128]{2,1,0:T(8,128)S(1)}, bf16[2,128,128]{2,1,0:T(8,128)(2,1)S(1)}) custom-call(s32[7]{0:T(128)S(1)} %pad_add_fusion.2.sc_ref, bf16[2,384,128]{2,1,0:T(8,128)(2,1)S(1)} %pad_maximum_fusion.2.x_ref, bf16[2304,128]{1,0:T(8,128)(2,1)S(1)} %shard_map.77.refs_0_, bf16[2304,128]{1,0:T(8,128)(2,1)S(1)} %collective-permute-done.5.refs_1_, ...), custom_call_target="tpu_custom_call" | custom-call | flops 471859200 | bytes 1048576 | tf_op jit(solution)/shard_map/pallas_call | solution.py:199
  232.4 1.9 collective-permute-start.18
  234.3 0.7 copy.26
  235.0 5.0 %collective-permute-done.18 = bf16[2,128,128]{2,1,0:T(8,128)(2,1)S(1)} collective-permute-done((bf16[2,128,128]{2,1,0:T(8,128)(2,1)S(1)}, bf16[2,128,128]{2,1,0:T(8,128)(2,1)S(1)}, u32[]{:S(2)}, u32[]{:S(2)}) %collective-permute-start.18) | collective-permute-done | bytes 65568 | tf_op jit(solution)/shard_map/ppermute | solution.py:42
  240.1 0.7 copy.25
  240.8 0.7 convert_reduce_fusion
  (62 shorter events, 1.0 us)
Async XLA Ops:
  0.6 0.8 copy-start.13
  1.5 11.2 %copy-start.15 = (bf16[128,120]{0,1:T(8,128)(2,1)S(1)}, bf16[128,120]{0,1:T(8,128)(2,1)}, u32[]{:S(2)}) copy-start(bf16[128,120]{0,1:T(8,128)(2,1)} %param.9) | copy-start | bytes 92164
  1.5 11.3 %copy-start.14 = (bf16[128,240]{0,1:T(8,128)(2,1)S(1)}, bf16[128,240]{0,1:T(8,128)(2,1)}, u32[]{:S(2)}) copy-start(bf16[128,240]{0,1:T(8,128)(2,1)} %param.5) | copy-start | bytes 184324
  2.3 27.8 %all-to-all-start = ((bf16[8,256,128]{2,1,0:T(8,128)(2,1)}), bf16[8,256,128]{2,1,0:T(8,128)(2,1)S(1)}, u32[]{:S(2)}, u32[]{:S(2)}) async-start(bf16[8,256,128]{2,1,0:T(8,128)(2,1)} %shard_map.76), calls=%async_computation | async-start | bytes 1048576 | tf_op jit(solution)/shard_map/all_to_all | solution.py:46
  13.0 8.0 %collective-permute-start.3 = (bf16[384,128]{1,0:T(8,128)(2,1)S(1)}, bf16[384,128]{1,0:T(8,128)(2,1)S(1)}, u32[]{:S(2)}, u32[]{:S(2)}) collective-permute-start(bf16[384,128]{1,0:T(8,128)(2,1)S(1)} %pad_maximum_fusion.5), channel_id=1, source_target_pairs={{0,16},{8,24},{16,0},{24,8},{32,48},{40,56},{48,32},{56,40},{64,80... | collective-permute-start | bytes 294920 | tf_op jit(solution)/shard_map/ppermute | solution.py:42
  20.3 30.4 %copy-start.16 = (s32[4]{0:T(128)S(1)}, s32[4]{0:T(128)}, u32[]{:S(2)}) copy-start(s32[4]{0:T(128)} %param.8) | copy-start | bytes 52
  30.2 20.8 %collective-permute-start.6 = (bf16[2304,128]{1,0:T(8,128)(2,1)S(1)}, bf16[2304,128]{1,0:T(8,128)(2,1)S(1)}, u32[]{:S(2)}, u32[]{:S(2)}) collective-permute-start(bf16[2304,128]{1,0:T(8,128)(2,1)S(1)} %shard_map.77.refs_0_), channel_id=1, source_target_pairs={{0,8},{8,0},{16,24},{24,16},{32,40},{40,32},{48,56},{56,48},{64,72... | collective-permute-start | bytes 1769480 | tf_op jit(solution)/shard_map/ppermute | solution.py:42
  33.6 19.3 %collective-permute-start.5 = (bf16[2304,128]{1,0:T(8,128)(2,1)S(1)}, bf16[2304,128]{1,0:T(8,128)(2,1)S(1)}, u32[]{:S(2)}, u32[]{:S(2)}) collective-permute-start(bf16[2304,128]{1,0:T(8,128)(2,1)S(1)} %shard_map.77.refs_0_), channel_id=1, source_target_pairs={{0,256},{8,264},{16,272},{24,280},{32,288},{40,296},{48,304},{56,3... | collective-permute-start | bytes 1769480 | tf_op jit(solution)/shard_map/ppermute | solution.py:42
  36.6 21.0 %collective-permute-start.2 = (bf16[2,32,128]{2,1,0:T(8,128)(2,1)}, bf16[2,32,128]{2,1,0:T(8,128)(2,1)S(1)}, u32[]{:S(2)}, u32[]{:S(2)}) collective-permute-start(bf16[2,32,128]{2,1,0:T(8,128)(2,1)} %get-tuple-element.52), channel_id=1, source_target_pairs={{0,24},{8,0},{16,8},{24,48},{32,56},{40,32},{48,40},{56,80},{64,88... | collective-permute-start | bytes 49160 | tf_op jit(solution)/shard_map/ppermute | solution.py:187
  40.6 14.3 %collective-permute-start = (bf16[2,32,128]{2,1,0:T(8,128)(2,1)}, bf16[2,32,128]{2,1,0:T(8,128)(2,1)S(1)}, u32[]{:S(2)}, u32[]{:S(2)}) collective-permute-start(bf16[2,32,128]{2,1,0:T(8,128)(2,1)} %get-tuple-element.52), channel_id=1, source_target_pairs={{0,8},{8,16},{16,24},{24,32},{32,40},{40,48},{48,56},{56,64},{64,7... | collective-permute-start | bytes 49160 | tf_op jit(solution)/shard_map/ppermute | solution.py:187
  42.5 14.3 %collective-permute-start.1 = (bf16[2,32,128]{2,1,0:T(8,128)(2,1)}, bf16[2,32,128]{2,1,0:T(8,128)(2,1)}, u32[]{:S(2)}, u32[]{:S(2)}) collective-permute-start(bf16[2,32,128]{2,1,0:T(8,128)(2,1)} %get-tuple-element.53), channel_id=1, source_target_pairs={{8,0},{16,8},{24,16},{32,24},{40,32},{48,40},{56,48},{64,56},{72,6... | collective-permute-start | bytes 49160 | tf_op jit(solution)/shard_map/ppermute | solution.py:188
  51.0 7.0 %collective-permute-start.4 = (bf16[2,32,128]{2,1,0:T(8,128)(2,1)}, bf16[2,32,128]{2,1,0:T(8,128)(2,1)S(1)}, u32[]{:S(2)}, u32[]{:S(2)}) collective-permute-start(bf16[2,32,128]{2,1,0:T(8,128)(2,1)} %get-tuple-element.53), channel_id=1, source_target_pairs={{8,16},{16,24},{24,0},{32,8},{40,48},{48,56},{56,32},{64,40},{72,8... | collective-permute-start | bytes 49160 | tf_op jit(solution)/shard_map/ppermute | solution.py:188
  52.9 10.7 %collective-permute-start.7 = (bf16[1280,128]{1,0:T(8,128)(2,1)S(1)}, bf16[1280,128]{1,0:T(8,128)(2,1)S(1)}, u32[]{:S(2)}, u32[]{:S(2)}) collective-permute-start(bf16[1280,128]{1,0:T(8,128)(2,1)S(1)} %slice.42), channel_id=1, source_target_pairs={{0,256},{8,264},{16,272},{24,280},{32,288},{40,296},{48,304},{56,3... | collective-permute-start | bytes 983048 | tf_op jit(solution)/shard_map/ppermute | solution.py:42
  54.9 8.7 %collective-permute-start.8 = (bf16[1024,128]{1,0:T(8,128)(2,1)S(1)}, bf16[1024,128]{1,0:T(8,128)(2,1)S(1)}, u32[]{:S(2)}, u32[]{:S(2)}) collective-permute-start(bf16[1024,128]{1,0:T(8,128)(2,1)S(1)} %slice.43), channel_id=1, source_target_pairs={{0,8},{8,0},{16,24},{24,16},{32,40},{40,32},{48,56},{56,48},{64,72... | collective-permute-start | bytes 786440 | tf_op jit(solution)/shard_map/ppermute | solution.py:42
  63.6 29.7 %copy-start.4 = (bf16[1024,128]{1,0:T(8,128)(2,1)}, bf16[1024,128]{1,0:T(8,128)(2,1)S(1)}, u32[]{:S(2)}) copy-start(bf16[1024,128]{1,0:T(8,128)(2,1)S(1)} %collective-permute-done.8.refs_4_) | copy-start | bytes 786436
  67.0 0.7 copy-start
  67.7 7.7 %collective-permute-start.9 = (bf16[2,128,128]{2,1,0:T(8,128)(2,1)S(1)}, bf16[2,128,128]{2,1,0:T(8,128)(2,1)S(1)}, u32[]{:S(2)}, u32[]{:S(2)}) collective-permute-start(bf16[2,128,128]{2,1,0:T(8,128)(2,1)S(1)} %get-tuple-element.23), channel_id=1, source_target_pairs={{0,16},{8,24},{16,0},{24,8},{32,48},{40,56},{48,32},{56,40},{64,80... | collective-permute-start | bytes 196616 | tf_op jit(solution)/shard_map/ppermute | solution.py:42
  75.5 0.6 copy-start.9
  94.8 0.8 copy-start.6
  95.6 0.8 copy-start.7
  96.4 0.7 copy-start.11
  97.0 24.6 %all-to-all-start.1 = ((bf16[8,128,256]{2,1,0:T(8,128)(2,1)}), bf16[8,128,256]{2,1,0:T(8,128)(2,1)}, u32[]{:S(2)}, u32[]{:S(2)}) async-start(bf16[8,128,256]{2,1,0:T(8,128)(2,1)} %copy-done.6), calls=%async_computation.1 | async-start | bytes 1048576 | tf_op jit(solution)/shard_map/all_to_all | solution.py:46
  101.2 7.3 %collective-permute-start.10 = (bf16[1,128,128]{2,1,0:T(8,128)(2,1)S(1)}, bf16[1,128,128]{2,1,0:T(8,128)(2,1)S(1)}, u32[]{:S(2)}, u32[]{:S(2)}) collective-permute-start(bf16[1,128,128]{2,1,0:T(8,128)(2,1)S(1)} %bitcast.22), channel_id=1, source_target_pairs={{0,16},{8,24},{16,0},{24,8},{32,48},{40,56},{48,32},{56,40},{64,80... | collective-permute-start | bytes 98312 | tf_op jit(solution)/shard_map/ppermute | solution.py:42
  108.5 6.2 %collective-permute-start.11 = (bf16[2,128,128]{2,1,0:T(8,128)(2,1)S(1)}, bf16[2,128,128]{2,1,0:T(8,128)(2,1)S(1)}, u32[]{:S(2)}, u32[]{:S(2)}) collective-permute-start(bf16[2,128,128]{2,1,0:T(8,128)(2,1)S(1)} %pad_maximum_fusion.9), channel_id=1, source_target_pairs={{0,256},{8,264},{16,272},{24,280},{32,288},{40,296},{48,304},{56,3... | collective-permute-start | bytes 196616 | tf_op jit(solution)/shard_map/ppermute | solution.py:42
  114.7 6.9 %collective-permute-start.12 = (bf16[4,128,128]{2,1,0:T(8,128)(2,1)S(1)}, bf16[4,128,128]{2,1,0:T(8,128)(2,1)S(1)}, u32[]{:S(2)}, u32[]{:S(2)}) collective-permute-start(bf16[4,128,128]{2,1,0:T(8,128)(2,1)S(1)} %pad_maximum_fusion.3), channel_id=1, source_target_pairs={{0,8},{8,0},{16,24},{24,16},{32,40},{40,32},{48,56},{56,48},{64,72... | collective-permute-start | bytes 393224 | tf_op jit(solution)/shard_map/ppermute | solution.py:42
  121.6 1.0 copy-start.1
  140.8 31.2 %copy-start.8 = (bf16[16,120,128]{2,1,0:T(8,128)(2,1)S(1)}, bf16[16,120,128]{2,1,0:T(8,128)(2,1)}, u32[]{:S(2)}) copy-start(bf16[16,120,128]{2,1,0:T(8,128)(2,1)} %copy-done.7) | copy-start | bytes 1474564
  173.4 20.0 %copy-start.3 = (bf16[8,256,384]{2,1,0:T(8,128)(2,1)}, bf16[8,256,384]{2,1,0:T(8,128)(2,1)S(1)}, u32[]{:S(2)}) copy-start(bf16[8,256,384]{2,1,0:T(8,128)(2,1)S(1)} %get-tuple-element.38) | copy-start | bytes 4718596
  193.4 5.8 %copy-start.10 = (f32[2,120,128]{2,1,0:T(8,128)S(1)}, f32[2,120,128]{2,1,0:T(8,128)}, u32[]{:S(2)}) copy-start(f32[2,120,128]{2,1,0:T(8,128)} %copy-done.9) | copy-start | bytes 368644
  193.4 5.8 %copy-start.12 = (f32[2,120,128]{2,1,0:T(8,128)S(1)}, f32[2,120,128]{2,1,0:T(8,128)}, u32[]{:S(2)}) copy-start(f32[2,120,128]{2,1,0:T(8,128)} %copy-done.11) | copy-start | bytes 368644
  193.4 27.7 %all-to-all-start.7 = ((bf16[8,256,384]{2,1,0:T(8,128)(2,1)}), bf16[8,256,384]{2,1,0:T(8,128)(2,1)}, u32[]{:S(2)}, u32[]{:S(2)}) async-start(bf16[8,256,384]{2,1,0:T(8,128)(2,1)} %copy-done.3), calls=%async_computation.7 | async-start | bytes 3145728 | tf_op jit(solution)/shard_map/all_to_all | solution.py:34
  199.4 28.8 %copy-start.2 = (bf16[1280,128]{1,0:T(8,128)(2,1)S(1)}, bf16[1280,128]{1,0:T(8,128)(2,1)}, u32[]{:S(2)}) copy-start(bf16[1280,128]{1,0:T(8,128)(2,1)} %copy-done) | copy-start | bytes 983044
  199.4 28.8 %copy-start.5 = (bf16[1024,128]{1,0:T(8,128)(2,1)S(1)}, bf16[1024,128]{1,0:T(8,128)(2,1)}, u32[]{:S(2)}) copy-start(bf16[1024,128]{1,0:T(8,128)(2,1)} %copy-done.4) | copy-start | bytes 786436
  199.4 18.3 %collective-permute-start.13 = (bf16[2,32,128]{2,1,0:T(8,128)(2,1)S(1)}, bf16[2,32,128]{2,1,0:T(8,128)(2,1)S(1)}, u32[]{:S(2)}, u32[]{:S(2)}) collective-permute-start(bf16[2,32,128]{2,1,0:T(8,128)(2,1)S(1)} %get-tuple-element.50), channel_id=1, source_target_pairs={{0,8},{8,16},{16,24},{24,32},{32,40},{40,48},{48,56},{56,64},{64,7... | collective-permute-start | bytes 49160 | tf_op jit(solution)/shard_map/ppermute | solution.py:187
  202.9 14.8 %collective-permute-start.14 = (bf16[2,32,128]{2,1,0:T(8,128)(2,1)S(1)}, bf16[2,32,128]{2,1,0:T(8,128)(2,1)S(1)}, u32[]{:S(2)}, u32[]{:S(2)}) collective-permute-start(bf16[2,32,128]{2,1,0:T(8,128)(2,1)S(1)} %get-tuple-element.51), channel_id=1, source_target_pairs={{8,0},{16,8},{24,16},{32,24},{40,32},{48,40},{56,48},{64,56},{72,6... | collective-permute-start | bytes 49160 | tf_op jit(solution)/shard_map/ppermute | solution.py:188
  209.6 8.2 %collective-permute-start.15 = (bf16[2,32,128]{2,1,0:T(8,128)(2,1)S(1)}, bf16[2,32,128]{2,1,0:T(8,128)(2,1)S(1)}, u32[]{:S(2)}, u32[]{:S(2)}) collective-permute-start(bf16[2,32,128]{2,1,0:T(8,128)(2,1)S(1)} %get-tuple-element.50), channel_id=1, source_target_pairs={{0,24},{8,0},{16,8},{24,48},{32,56},{40,32},{48,40},{56,80},{64,88... | collective-permute-start | bytes 49160 | tf_op jit(solution)/shard_map/ppermute | solution.py:187
  211.5 7.9 %collective-permute-start.17 = (bf16[2,32,128]{2,1,0:T(8,128)(2,1)S(1)}, bf16[2,32,128]{2,1,0:T(8,128)(2,1)S(1)}, u32[]{:S(2)}, u32[]{:S(2)}) collective-permute-start(bf16[2,32,128]{2,1,0:T(8,128)(2,1)S(1)} %get-tuple-element.51), channel_id=1, source_target_pairs={{8,16},{16,24},{24,0},{32,8},{40,48},{48,56},{56,32},{64,40},{72,8... | collective-permute-start | bytes 49160 | tf_op jit(solution)/shard_map/ppermute | solution.py:188
  213.5 7.7 %collective-permute-start.16 = (bf16[256,128]{1,0:T(8,128)(2,1)S(1)}, bf16[256,128]{1,0:T(8,128)(2,1)S(1)}, u32[]{:S(2)}, u32[]{:S(2)}) collective-permute-start(bf16[256,128]{1,0:T(8,128)(2,1)S(1)} %bitcast.26), channel_id=1, source_target_pairs={{0,16},{8,24},{16,0},{24,8},{32,48},{40,56},{48,32},{56,40},{64,80... | collective-permute-start | bytes 196616 | tf_op jit(solution)/shard_map/ppermute | solution.py:42
  223.4 17.4 %all-to-all-start.8 = ((bf16[8,32,384]{2,1,0:T(8,128)(2,1)}), bf16[8,32,384]{2,1,0:T(8,128)(2,1)S(1)}, u32[]{:S(2)}, u32[]{:S(2)}) async-start(bf16[8,32,384]{2,1,0:T(8,128)(2,1)} %shard_map.86.refs_5_), calls=%async_computation.8 | async-start | bytes 393216 | tf_op jit(solution)/shard_map/all_to_all | solution.py:46
  232.4 7.7 %collective-permute-start.18 = (bf16[2,128,128]{2,1,0:T(8,128)(2,1)S(1)}, bf16[2,128,128]{2,1,0:T(8,128)(2,1)S(1)}, u32[]{:S(2)}, u32[]{:S(2)}) collective-permute-start(bf16[2,128,128]{2,1,0:T(8,128)(2,1)S(1)} %get-tuple-element.40), channel_id=1, source_target_pairs={{0,16},{8,24},{16,0},{24,8},{32,48},{40,56},{48,32},{56,40},{64,80... | collective-permute-start | bytes 196616 | tf_op jit(solution)/shard_map/ppermute | solution.py:42

commit v11 on v8

--- a/solution.py
+++ b/solution.py
@@ -50,8 +50,8 @@
     return lax.all_to_all(parts, "head", 0, 0, axis_index_groups=groups)
 
 
-BITS = (32, 2, 1)
-SLOTS = (0, 4, 2, 6, 1, 5, 3, 7)
+BITS = (1, 2, 32)
+SLOTS = (0, 1, 2, 3, 4, 5, 6, 7)
 
 
 def doubled(array):
@@ -539,8 +539,8 @@
     queries = doubled(queries)
     stats = exchange_xy(attention_stats(order, queries, keys, taps))
     od, dkv = attention_grads(order, queries, keys, taps, stats)
+    dkv = exchange_z(dkv)
     od = exchange_xy(od)
-    dkv = exchange_z(dkv)
 
     parts, wide, attended = shares(od, dkv, normed_t, w_qkv)
     parts = core_sum(exchange_head(parts, CORE_GROUPS))

time: 234 us -> 234 us (level)
  no operation moved by 1% of the time
where the time goes in v11:
time: 234 us; the launch traced here: 233 us
  starting transfers between devices  78.3 us (33%)
  blocking collectives  77.3 us (33%)
  waiting for transfers between devices  49 us (21%)
  Pallas kernels  18.9 us (8%)
  local copies, waits for them, and re-layouts  7.17 us (3%)
    all_to_all x3, starting transfers between devices, exchange_z(): return lax.all_to_all(parts, 'tm', 0, 0, axis_index_groups=Z_GROUPS)  21.6 us
    ppermute x7, waiting for transfers between devices, swap(): return lax.ppermute(array, 'tm', [(i, i ^ bit) for i in range(64)])  20.5 us
    all_to_all x2, blocking collectives, exchange_xy(): return lax.all_to_all(parts, 'tm', 0, 0, axis_index_groups=XY_GROUPS)  20.3 us
    all_to_all x1, blocking collectives, exchange_z(): return lax.all_to_all(parts, 'tm', 0, 0, axis_index_groups=Z_GROUPS)  20.2 us
    all_to_all x2, blocking collectives, exchange_head(): return lax.all_to_all(parts, 'head', 0, 0, axis_index_groups=groups)  20 us
    ppermute x7, starting transfers between devices, swap(): return lax.ppermute(array, 'tm', [(i, i ^ bit) for i in range(64)])  18 us
    all_gather x1, blocking collectives, on_device(): all_t = lax.all_gather(sent, 'head', axis=0, tiled=True)  16.9 us
    ppermute x4, starting transfers between devices, paired(): lax.ppermute(head, 'tm', [(i, j ^ bit) for i, j in down])  16.6 us
  transfers between devices with their start and end apart: 20, of which 12 were waited for; matrix products, arithmetic and copies ran while one was open for 2% of the time, Pallas kernels for 2%

profile of v11, /device:TPU:8, one launch (start us, length us, event | category | flops | bytes accessed | tf_op | source)
XLA Modules:
  0.0 232.8 jit_solution(11091824881908249508)
XLA Ops:
  0.6 0.8 copy-done.7
  1.5 0.9 shard_map.76
  2.3 10.3 %all-to-all-start = ((bf16[8,256,128]{2,1,0:T(8,128)(2,1)}), bf16[8,256,128]{2,1,0:T(8,128)(2,1)S(1)}, u32[]{:S(2)}, u32[]{:S(2)}) async-start(bf16[8,256,128]{2,1,0:T(8,128)(2,1)} %shard_map.76), calls=%async_computation | async-start | bytes 1048576 | tf_op jit(solution)/shard_map/all_to_all | solution.py:46
  12.7 0.1 copy.21
  12.8 0.1 copy.20
  13.0 2.4 %collective-permute-start.3 = (bf16[384,128]{1,0:T(8,128)(2,1)S(1)}, bf16[384,128]{1,0:T(8,128)(2,1)S(1)}, u32[]{:S(2)}, u32[]{:S(2)}) collective-permute-start(bf16[384,128]{1,0:T(8,128)(2,1)S(1)} %pad_maximum_fusion.5), channel_id=1, source_target_pairs={{0,256},{8,264},{16,272},{24,280},{32,288},{40,296},{48,304},{56,3... | collective-permute-start | bytes 294920 | tf_op jit(solution)/shard_map/ppermute | solution.py:42
  15.3 2.4 %copy.22.qkv_ref.w_ref = bf16[1920,360]{1,0:T(8,128)(2,1)S(1)} copy(bf16[1920,360]{0,1:T(8,128)(2,1)} %param.7) | data formatting | bytes 2764800 | tf_op args[2]
  17.7 1.8 collective-permute-done.3
  19.5 10.7 %all-to-all-done.w_ref = bf16[8,256,128]{2,1,0:T(8,128)(2,1)S(1)} async-done(((bf16[8,256,128]{2,1,0:T(8,128)(2,1)}), bf16[8,256,128]{2,1,0:T(8,128)(2,1)S(1)}, u32[]{:S(2)}, u32[]{:S(2)}) %all-to-all-start) | async-done | bytes 524320 | tf_op jit(solution)/shard_map/all_to_all | solution.py:46
  30.2 0.2 shard_map.77
  30.3 1.4 copy-done.3
  31.8 4.4 %all-to-all-start.1 = ((bf16[4,2304,128]{2,1,0:T(8,128)(2,1)}), bf16[4,2304,128]{2,1,0:T(8,128)(2,1)S(1)}, u32[]{:S(2)}, u32[]{:S(2)}) async-start(bf16[4,2304,128]{2,1,0:T(8,128)(2,1)} %copy-done.3), calls=%async_computation.1 | async-start | bytes 4718592 | tf_op jit(solution)/shard_map/all_to_all | solution.py:38
  36.2 3.8 %collective-permute-start.2 = (bf16[2,32,128]{2,1,0:T(8,128)(2,1)S(1)}, bf16[2,32,128]{2,1,0:T(8,128)(2,1)S(1)}, u32[]{:S(2)}, u32[]{:S(2)}) collective-permute-start(bf16[2,32,128]{2,1,0:T(8,128)(2,1)S(1)} %get-tuple-element.52), channel_id=1, source_target_pairs={{0,264},{8,272},{16,280},{24,288},{32,296},{40,304},{48,312},{56,3... | collective-permute-start | bytes 49160 | tf_op jit(solution)/shard_map/ppermute | solution.py:174
  40.0 3.4 %collective-permute-start = (bf16[2,32,128]{2,1,0:T(8,128)(2,1)S(1)}, bf16[2,32,128]{2,1,0:T(8,128)(2,1)S(1)}, u32[]{:S(2)}, u32[]{:S(2)}) collective-permute-start(bf16[2,32,128]{2,1,0:T(8,128)(2,1)S(1)} %get-tuple-element.52), channel_id=1, source_target_pairs={{0,8},{8,16},{16,24},{24,32},{32,40},{40,48},{48,56},{56,64},{64,7... | collective-permute-start | bytes 49160 | tf_op jit(solution)/shard_map/ppermute | solution.py:174
  43.4 1.9 collective-permute-start.4
  45.3 6.1 %collective-permute-start.1 = (bf16[2,32,128]{2,1,0:T(8,128)(2,1)S(1)}, bf16[2,32,128]{2,1,0:T(8,128)(2,1)S(1)}, u32[]{:S(2)}, u32[]{:S(2)}) collective-permute-start(bf16[2,32,128]{2,1,0:T(8,128)(2,1)S(1)} %get-tuple-element.53), channel_id=1, source_target_pairs={{8,0},{16,8},{24,16},{32,24},{40,32},{48,40},{56,48},{64,56},{72,6... | collective-permute-start | bytes 49160 | tf_op jit(solution)/shard_map/ppermute | solution.py:175
  51.4 0.2 reduce-window.9
  51.6 0.1 pad_add_fusion.2.sc_ref
  51.7 10.9 %collective-permute-done = bf16[2,32,128]{2,1,0:T(8,128)(2,1)S(1)} collective-permute-done((bf16[2,32,128]{2,1,0:T(8,128)(2,1)S(1)}, bf16[2,32,128]{2,1,0:T(8,128)(2,1)S(1)}, u32[]{:S(2)}, u32[]{:S(2)}) %collective-permute-start) | collective-permute-done | bytes 16416 | tf_op jit(solution)/shard_map/ppermute | solution.py:174
  62.5 2.3 collective-permute-done.1
  64.8 0.0 collective-permute-done.2
  64.9 1.1 all-to-all-done.1.w_ref.f_ref
  66.0 1.9 shard_map.78
  68.0 2.4 %collective-permute-start.5 = (bf16[2,128,128]{2,1,0:T(8,128)(2,1)S(1)}, bf16[2,128,128]{2,1,0:T(8,128)(2,1)S(1)}, u32[]{:S(2)}, u32[]{:S(2)}) collective-permute-start(bf16[2,128,128]{2,1,0:T(8,128)(2,1)S(1)} %get-tuple-element.23), channel_id=1, source_target_pairs={{0,256},{8,264},{16,272},{24,280},{32,288},{40,296},{48,304},{56,3... | collective-permute-start | bytes 196616 | tf_op jit(solution)/shard_map/ppermute | solution.py:42
  70.3 0.1 pad_add_fusion.1
  70.4 3.7 %collective-permute-done.5.other_ref = bf16[2,128,128]{2,1,0:T(8,128)(2,1)S(1)} collective-permute-done((bf16[2,128,128]{2,1,0:T(8,128)(2,1)S(1)}, bf16[2,128,128]{2,1,0:T(8,128)(2,1)S(1)}, u32[]{:S(2)}, u32[]{:S(2)}) %collective-permute-start.5) | collective-permute-done | bytes 65568 | tf_op jit(solution)/shard_map/ppermute | solution.py:42
  74.1 0.1 shard_map.79
  74.3 16.9 %all_gather.3.all_ref = bf16[16,120,128]{2,1,0:T(8,128)(2,1)S(1)} all-gather(bf16[2,120,128]{2,1,0:T(8,128)(2,1)S(1)} %get-tuple-element.24), channel_id=1, replica_groups=mesh['tm'=64,'head'=8] {'head'}, dimensions={0}, use_global_device_ids=true | all-gather | bytes 552960 | tf_op jit(solution)/shard_map/all_gather | solution.py:533
  91.1 2.3 %shard_map.80 = (bf16[8,128,256]{2,1,0:T(8,128)(2,1)}, bf16[128,128]{1,0:T(8,128)(2,1)S(1)}, bf16[16,120,128]{2,1,0:T(8,128)(2,1)S(1)}, f32[2,120,128]{2,1,0:T(8,128)S(1)}, f32[1,128]{1,0:T(1,128)S(1)}) custom-call(s32[5]{0:T(128)S(1)} %get-tuple-element.54.sc_ref, bf16[16,120,128]{2,1,0:T(8,128)(2,1)S(1)} %all_gather.3.all_ref, ...), custom_call_target="tpu_custom_call" | custom-call | flops 176947200 | bytes 1048576 | tf_op jit(solution)/shard_map/pallas_call | solution.py:383
  93.5 0.8 copy-done.5
  94.3 3.5 %all-to-all-start.2 = ((bf16[8,128,256]{2,1,0:T(8,128)(2,1)}), bf16[8,128,256]{2,1,0:T(8,128)(2,1)S(1)}, u32[]{:S(2)}, u32[]{:S(2)}) async-start(bf16[8,128,256]{2,1,0:T(8,128)(2,1)} %get-tuple-element.27), calls=%async_computation.2 | async-start | bytes 1048576 | tf_op jit(solution)/shard_map/all_to_all | solution.py:46
  97.8 2.5 %collective-permute-start.6 = (bf16[1,128,128]{2,1,0:T(8,128)(2,1)S(1)}, bf16[1,128,128]{2,1,0:T(8,128)(2,1)S(1)}, u32[]{:S(2)}, u32[]{:S(2)}) collective-permute-start(bf16[1,128,128]{2,1,0:T(8,128)(2,1)S(1)} %bitcast.21), channel_id=1, source_target_pairs={{0,8},{8,0},{16,24},{24,16},{32,40},{40,32},{48,56},{56,48},{64,72... | collective-permute-start | bytes 98312 | tf_op jit(solution)/shard_map/ppermute | solution.py:42
  100.2 3.3 %collective-permute-done.6 = bf16[1,128,128]{2,1,0:T(8,128)(2,1)S(1)} collective-permute-done((bf16[1,128,128]{2,1,0:T(8,128)(2,1)S(1)}, bf16[1,128,128]{2,1,0:T(8,128)(2,1)S(1)}, u32[]{:S(2)}, u32[]{:S(2)}) %collective-permute-start.6) | collective-permute-done | bytes 32800 | tf_op jit(solution)/shard_map/ppermute | solution.py:42
  103.6 3.4 %collective-permute-start.7 = (bf16[2,128,128]{2,1,0:T(8,128)(2,1)S(1)}, bf16[2,128,128]{2,1,0:T(8,128)(2,1)S(1)}, u32[]{:S(2)}, u32[]{:S(2)}) collective-permute-start(bf16[2,128,128]{2,1,0:T(8,128)(2,1)S(1)} %pad_maximum_fusion.9), channel_id=1, source_target_pairs={{0,16},{8,24},{16,0},{24,8},{32,48},{40,56},{48,32},{56,40},{64,80... | collective-permute-start | bytes 196616 | tf_op jit(solution)/shard_map/ppermute | solution.py:42
  107.0 4.3 %collective-permute-done.7 = bf16[2,128,128]{2,1,0:T(8,128)(2,1)S(1)} collective-permute-done((bf16[2,128,128]{2,1,0:T(8,128)(2,1)S(1)}, bf16[2,128,128]{2,1,0:T(8,128)(2,1)S(1)}, u32[]{:S(2)}, u32[]{:S(2)}) %collective-permute-start.7) | collective-permute-done | bytes 65568 | tf_op jit(solution)/shard_map/ppermute | solution.py:42
  111.3 3.5 %collective-permute-start.8 = (bf16[4,128,128]{2,1,0:T(8,128)(2,1)S(1)}, bf16[4,128,128]{2,1,0:T(8,128)(2,1)S(1)}, u32[]{:S(2)}, u32[]{:S(2)}) collective-permute-start(bf16[4,128,128]{2,1,0:T(8,128)(2,1)S(1)} %pad_maximum_fusion.3), channel_id=1, source_target_pairs={{0,256},{8,264},{16,272},{24,280},{32,288},{40,296},{48,304},{56,3... | collective-permute-start | bytes 393224 | tf_op jit(solution)/shard_map/ppermute | solution.py:42
  114.8 3.3 %collective-permute-done.8 = bf16[4,128,128]{2,1,0:T(8,128)(2,1)S(1)} collective-permute-done((bf16[4,128,128]{2,1,0:T(8,128)(2,1)S(1)}, bf16[4,128,128]{2,1,0:T(8,128)(2,1)S(1)}, u32[]{:S(2)}, u32[]{:S(2)}) %collective-permute-start.8) | collective-permute-done | bytes 131104 | tf_op jit(solution)/shard_map/ppermute | solution.py:42
  118.2 0.0 all-to-all-done.2.kv_ref
  118.2 2.5 %shard_map.81 = f32[8,3,8,128]{3,2,1,0:T(8,128)S(1)} custom-call(s32[5]{0:T(128)S(1)} %get-tuple-element.55.sc_ref, bf16[8,128,128]{2,1,0:T(8,128)(2,1)S(1)} %pad_maximum_fusion.q_ref, bf16[8,128,256]{2,1,0:T(8,128)(2,1)S(1)} %all-to-all-done.2.kv_ref, bf16[4,2304,128]{2,1,0:T(8,128)(2,1)S(1)} %all-to-all-done.1.w_ref.f_ref), custom_call_target="tpu_custom_call" | custom-call | flops 536870912 | bytes 1048576 | tf_op jit(solution)/shard_map/pallas_call | solution.py:284
  120.6 9.2 %all_to_all.50.stats_ref = f32[8,3,8,128]{3,2,1,0:T(8,128)S(1)} all-to-all(f32[8,3,8,128]{3,2,1,0:T(8,128)S(1)} %shard_map.81), channel_id=1, replica_groups={{0,8,16,24,256,264,272,280},{32,40,48,56,288,296,304,312},{64,72,80,88,..., dimensions={0} | all-to-all | bytes 196608 | tf_op jit(solution)/shard_map/all_to_all | solution.py:34
  129.9 3.5 %shard_map.82 = (bf16[8,2,120,128]{3,2,1,0:T(8,128)(2,1)S(1)}, bf16[8,128,256]{2,1,0:T(8,128)(2,1)S(1)}) custom-call(s32[5]{0:T(128)S(1)} %get-tuple-element.55.sc_ref, bf16[8,128,128]{2,1,0:T(8,128)(2,1)S(1)} %pad_maximum_fusion.q_ref, bf16[8,128,256]{2,1,0:T(8,128)(2,1)S(1)} %all-to-all-done.2.kv_ref, ...), custom_call_target="tpu_custom_call" | custom-call | flops 1610612736 | bytes 1048576 | tf_op jit(solution)/shard_map/pallas_call | solution.py:295
  133.4 11.0 %all_to_all.51.od_ref = bf16[8,2,120,128]{3,2,1,0:T(8,128)(2,1)S(1)} all-to-all(bf16[8,2,120,128]{3,2,1,0:T(8,128)(2,1)S(1)} %get-tuple-element.28), channel_id=1, replica_groups={{0,8,16,24,256,264,272,280},{32,40,48,56,288,296,304,312},{64,72,80,88,..., dimensions={0} | all-to-all | bytes 983040 | tf_op jit(solution)/shard_map/all_to_all | solution.py:34
  144.4 20.2 %all_to_all.52.dkv_ref = bf16[8,128,256]{2,1,0:T(8,128)(2,1)S(1)} all-to-all(bf16[8,128,256]{2,1,0:T(8,128)(2,1)S(1)} %get-tuple-element.29), channel_id=1, replica_groups={{0,32,64,96,128,160,192,224},{8,40,72,104,136,168,200,232},{16,48,80,11..., dimensions={0} | all-to-all | bytes 1048576 | tf_op jit(solution)/shard_map/all_to_all | solution.py:46
  164.6 1.4 shard_map.83
  166.1 4.2 %all_to_all.53.parts_ref = bf16[2,4,2,128,128]{4,3,2,1,0:T(8,128)(2,1)S(1)} all-to-all(bf16[2,4,2,128,128]{4,3,2,1,0:T(8,128)(2,1)S(1)} %get-tuple-element.32), channel_id=1, replica_groups={{0,1},{2,3},{4,5},{6,7},{8,9},{10,11},{12,13},{14,15},{16,17},{18,19},{..., dimensions={0} | all-to-all | bytes 1048576 | tf_op jit(solution)/shard_map/all_to_all | solution.py:50
  170.2 0.1 shard_map.84
  170.3 15.8 %all_to_all.54.parts_ref = bf16[4,2,128,128]{3,2,1,0:T(8,128)(2,1)S(1)} all-to-all(bf16[4,2,128,128]{3,2,1,0:T(8,128)(2,1)S(1)} %shard_map.84), channel_id=1, replica_groups={{0,2,4,6},{1,3,5,7},{8,10,12,14},{9,11,13,15},{16,18,20,22},{17,19,21,2..., dimensions={0} | all-to-all | bytes 524288 | tf_op jit(solution)/shard_map/all_to_all | solution.py:50
  186.1 5.6 %all-to-all-start.8 = ((bf16[8,256,384]{2,1,0:T(8,128)(2,1)}), bf16[8,256,384]{2,1,0:T(8,128)(2,1)}, u32[]{:S(2)}, u32[]{:S(2)}) async-start(bf16[8,256,384]{2,1,0:T(8,128)(2,1)} %copy-done.4), calls=%async_computation.8 | async-start | bytes 3145728 | tf_op jit(solution)/shard_map/all_to_all | solution.py:34
  191.7 0.1 shard_map.85
  191.9 3.6 %collective-permute-start.9 = (bf16[2,32,128]{2,1,0:T(8,128)(2,1)S(1)}, bf16[2,32,128]{2,1,0:T(8,128)(2,1)S(1)}, u32[]{:S(2)}, u32[]{:S(2)}) collective-permute-start(bf16[2,32,128]{2,1,0:T(8,128)(2,1)S(1)} %get-tuple-element.50), channel_id=1, source_target_pairs={{0,8},{8,16},{16,24},{24,32},{32,40},{40,48},{48,56},{56,64},{64,7... | collective-permute-start | bytes 49160 | tf_op jit(solution)/shard_map/ppermute | solution.py:174
  195.5 6.7 %collective-permute-start.10 = (bf16[2,32,128]{2,1,0:T(8,128)(2,1)S(1)}, bf16[2,32,128]{2,1,0:T(8,128)(2,1)S(1)}, u32[]{:S(2)}, u32[]{:S(2)}) collective-permute-start(bf16[2,32,128]{2,1,0:T(8,128)(2,1)S(1)} %get-tuple-element.51), channel_id=1, source_target_pairs={{8,0},{16,8},{24,16},{32,24},{40,32},{48,40},{56,48},{64,56},{72,6... | collective-permute-start | bytes 49160 | tf_op jit(solution)/shard_map/ppermute | solution.py:175
  202.2 1.3 collective-permute-start.11
  203.5 1.9 collective-permute-start.13
  205.4 1.9 collective-permute-start.12
  207.3 3.6 %collective-permute-done.9 = bf16[2,32,128]{2,1,0:T(8,128)(2,1)S(1)} collective-permute-done((bf16[2,32,128]{2,1,0:T(8,128)(2,1)S(1)}, bf16[2,32,128]{2,1,0:T(8,128)(2,1)S(1)}, u32[]{:S(2)}, u32[]{:S(2)}) %collective-permute-start.9) | collective-permute-done | bytes 16416 | tf_op jit(solution)/shard_map/ppermute | solution.py:174
  210.9 0.6 collective-permute-done.12
  211.6 2.3 shard_map.86.refs_0_
  213.8 7.8 %all-to-all-start.9 = ((bf16[8,32,384]{2,1,0:T(8,128)(2,1)}), bf16[8,32,384]{2,1,0:T(8,128)(2,1)S(1)}, u32[]{:S(2)}, u32[]{:S(2)}) async-start(bf16[8,32,384]{2,1,0:T(8,128)(2,1)} %shard_map.86.refs_0_), calls=%async_computation.9 | async-start | bytes 393216 | tf_op jit(solution)/shard_map/all_to_all | solution.py:46
  221.7 3.5 %shard_map.87 = (f32[2,128,128]{2,1,0:T(8,128)S(1)}, bf16[2,128,128]{2,1,0:T(8,128)(2,1)S(1)}) custom-call(s32[6]{0:T(128)S(1)} %pad_add_fusion.2.sc_ref, bf16[2,384,128]{2,1,0:T(8,128)(2,1)S(1)} %pad_maximum_fusion.2.x_ref, bf16[4,2304,128]{2,1,0:T(8,128)(2,1)S(1)} %all-to-all-done.1.w_ref.f_ref, bf16[8,32,384]{2,1,0:T(8,128)(2,1)} %shard_map.86.refs_0_), custom_call_target="tpu_custom_call" | custom-call | flops 471859200 | bytes 1048576 | tf_op jit(solution)/shard_map/pallas_call | solution.py:186
  225.2 2.0 collective-permute-start.14
  227.2 0.7 copy.26
  227.9 3.4 %collective-permute-done.14 = bf16[2,128,128]{2,1,0:T(8,128)(2,1)S(1)} collective-permute-done((bf16[2,128,128]{2,1,0:T(8,128)(2,1)S(1)}, bf16[2,128,128]{2,1,0:T(8,128)(2,1)S(1)}, u32[]{:S(2)}, u32[]{:S(2)}) %collective-permute-start.14) | collective-permute-done | bytes 65568 | tf_op jit(solution)/shard_map/ppermute | solution.py:42
  231.4 0.7 copy.25
  232.1 0.7 convert_reduce_fusion
  (42 shorter events, 0.3 us)
Async XLA Ops:
  0.6 0.8 copy-start.7
  1.5 11.2 %copy-start.9 = (bf16[128,120]{0,1:T(8,128)(2,1)S(1)}, bf16[128,120]{0,1:T(8,128)(2,1)}, u32[]{:S(2)}) copy-start(bf16[128,120]{0,1:T(8,128)(2,1)} %param.9) | copy-start | bytes 92164
  1.5 11.3 %copy-start.8 = (bf16[128,240]{0,1:T(8,128)(2,1)S(1)}, bf16[128,240]{0,1:T(8,128)(2,1)}, u32[]{:S(2)}) copy-start(bf16[128,240]{0,1:T(8,128)(2,1)} %param.5) | copy-start | bytes 184324
  2.3 27.8 %all-to-all-start = ((bf16[8,256,128]{2,1,0:T(8,128)(2,1)}), bf16[8,256,128]{2,1,0:T(8,128)(2,1)S(1)}, u32[]{:S(2)}, u32[]{:S(2)}) async-start(bf16[8,256,128]{2,1,0:T(8,128)(2,1)} %shard_map.76), calls=%async_computation | async-start | bytes 1048576 | tf_op jit(solution)/shard_map/all_to_all | solution.py:46
  13.0 6.5 %collective-permute-start.3 = (bf16[384,128]{1,0:T(8,128)(2,1)S(1)}, bf16[384,128]{1,0:T(8,128)(2,1)S(1)}, u32[]{:S(2)}, u32[]{:S(2)}) collective-permute-start(bf16[384,128]{1,0:T(8,128)(2,1)S(1)} %pad_maximum_fusion.5), channel_id=1, source_target_pairs={{0,256},{8,264},{16,272},{24,280},{32,288},{40,296},{48,304},{56,3... | collective-permute-start | bytes 294920 | tf_op jit(solution)/shard_map/ppermute | solution.py:42
  17.7 12.6 %copy-start = (bf16[1920,360]{1,0:T(8,128)(2,1)}, bf16[1920,360]{1,0:T(8,128)(2,1)S(1)}, u32[]{:S(2)}) copy-start(bf16[1920,360]{1,0:T(8,128)(2,1)S(1)} %copy.22.qkv_ref.w_ref) | copy-start | bytes 4147204
  30.3 1.4 copy-start.3
  31.7 19.6 %copy-start.10 = (s32[4]{0:T(128)S(1)}, s32[4]{0:T(128)}, u32[]{:S(2)}) copy-start(s32[4]{0:T(128)} %param.8) | copy-start | bytes 52
  31.8 34.3 %all-to-all-start.1 = ((bf16[4,2304,128]{2,1,0:T(8,128)(2,1)}), bf16[4,2304,128]{2,1,0:T(8,128)(2,1)S(1)}, u32[]{:S(2)}, u32[]{:S(2)}) async-start(bf16[4,2304,128]{2,1,0:T(8,128)(2,1)} %copy-done.3), calls=%async_computation.1 | async-start | bytes 4718592 | tf_op jit(solution)/shard_map/all_to_all | solution.py:38
  36.2 28.7 %collective-permute-start.2 = (bf16[2,32,128]{2,1,0:T(8,128)(2,1)S(1)}, bf16[2,32,128]{2,1,0:T(8,128)(2,1)S(1)}, u32[]{:S(2)}, u32[]{:S(2)}) collective-permute-start(bf16[2,32,128]{2,1,0:T(8,128)(2,1)S(1)} %get-tuple-element.52), channel_id=1, source_target_pairs={{0,264},{8,272},{16,280},{24,288},{32,296},{40,304},{48,312},{56,3... | collective-permute-start | bytes 49160 | tf_op jit(solution)/shard_map/ppermute | solution.py:174
  40.0 22.5 %collective-permute-start = (bf16[2,32,128]{2,1,0:T(8,128)(2,1)S(1)}, bf16[2,32,128]{2,1,0:T(8,128)(2,1)S(1)}, u32[]{:S(2)}, u32[]{:S(2)}) collective-permute-start(bf16[2,32,128]{2,1,0:T(8,128)(2,1)S(1)} %get-tuple-element.52), channel_id=1, source_target_pairs={{0,8},{8,16},{16,24},{24,32},{32,40},{40,48},{48,56},{56,64},{64,7... | collective-permute-start | bytes 49160 | tf_op jit(solution)/shard_map/ppermute | solution.py:174
  43.4 21.5 %collective-permute-start.4 = (bf16[2,32,128]{2,1,0:T(8,128)(2,1)S(1)}, bf16[2,32,128]{2,1,0:T(8,128)(2,1)S(1)}, u32[]{:S(2)}, u32[]{:S(2)}) collective-permute-start(bf16[2,32,128]{2,1,0:T(8,128)(2,1)S(1)} %get-tuple-element.53), channel_id=1, source_target_pairs={{8,256},{16,264},{24,272},{32,280},{40,288},{48,296},{56,304},{64,... | collective-permute-start | bytes 49160 | tf_op jit(solution)/shard_map/ppermute | solution.py:175
  45.3 19.5 %collective-permute-start.1 = (bf16[2,32,128]{2,1,0:T(8,128)(2,1)S(1)}, bf16[2,32,128]{2,1,0:T(8,128)(2,1)S(1)}, u32[]{:S(2)}, u32[]{:S(2)}) collective-permute-start(bf16[2,32,128]{2,1,0:T(8,128)(2,1)S(1)} %get-tuple-element.53), channel_id=1, source_target_pairs={{8,0},{16,8},{24,16},{32,24},{40,32},{48,40},{56,48},{64,56},{72,6... | collective-permute-start | bytes 49160 | tf_op jit(solution)/shard_map/ppermute | solution.py:175
  66.0 25.1 %copy-start.1 = (bf16[1920,360]{1,0:T(8,128)(2,1)S(1)}, bf16[1920,360]{1,0:T(8,128)(2,1)}, u32[]{:S(2)}) copy-start(bf16[1920,360]{1,0:T(8,128)(2,1)} %copy-done) | copy-start | bytes 4147204
  68.0 6.2 %collective-permute-start.5 = (bf16[2,128,128]{2,1,0:T(8,128)(2,1)S(1)}, bf16[2,128,128]{2,1,0:T(8,128)(2,1)S(1)}, u32[]{:S(2)}, u32[]{:S(2)}) collective-permute-start(bf16[2,128,128]{2,1,0:T(8,128)(2,1)S(1)} %get-tuple-element.23), channel_id=1, source_target_pairs={{0,256},{8,264},{16,272},{24,280},{32,288},{40,296},{48,304},{56,3... | collective-permute-start | bytes 196616 | tf_op jit(solution)/shard_map/ppermute | solution.py:42
  93.5 0.8 copy-start.5
  94.3 23.9 %all-to-all-start.2 = ((bf16[8,128,256]{2,1,0:T(8,128)(2,1)}), bf16[8,128,256]{2,1,0:T(8,128)(2,1)S(1)}, u32[]{:S(2)}, u32[]{:S(2)}) async-start(bf16[8,128,256]{2,1,0:T(8,128)(2,1)} %get-tuple-element.27), calls=%async_computation.2 | async-start | bytes 1048576 | tf_op jit(solution)/shard_map/all_to_all | solution.py:46
  97.8 5.8 %collective-permute-start.6 = (bf16[1,128,128]{2,1,0:T(8,128)(2,1)S(1)}, bf16[1,128,128]{2,1,0:T(8,128)(2,1)S(1)}, u32[]{:S(2)}, u32[]{:S(2)}) collective-permute-start(bf16[1,128,128]{2,1,0:T(8,128)(2,1)S(1)} %bitcast.21), channel_id=1, source_target_pairs={{0,8},{8,0},{16,24},{24,16},{32,40},{40,32},{48,56},{56,48},{64,72... | collective-permute-start | bytes 98312 | tf_op jit(solution)/shard_map/ppermute | solution.py:42
  103.6 7.7 %collective-permute-start.7 = (bf16[2,128,128]{2,1,0:T(8,128)(2,1)S(1)}, bf16[2,128,128]{2,1,0:T(8,128)(2,1)S(1)}, u32[]{:S(2)}, u32[]{:S(2)}) collective-permute-start(bf16[2,128,128]{2,1,0:T(8,128)(2,1)S(1)} %pad_maximum_fusion.9), channel_id=1, source_target_pairs={{0,16},{8,24},{16,0},{24,8},{32,48},{40,56},{48,32},{56,40},{64,80... | collective-permute-start | bytes 196616 | tf_op jit(solution)/shard_map/ppermute | solution.py:42
  111.3 6.9 %collective-permute-start.8 = (bf16[4,128,128]{2,1,0:T(8,128)(2,1)S(1)}, bf16[4,128,128]{2,1,0:T(8,128)(2,1)S(1)}, u32[]{:S(2)}, u32[]{:S(2)}) collective-permute-start(bf16[4,128,128]{2,1,0:T(8,128)(2,1)S(1)} %pad_maximum_fusion.3), channel_id=1, source_target_pairs={{0,256},{8,264},{16,272},{24,280},{32,288},{40,296},{48,304},{56,3... | collective-permute-start | bytes 393224 | tf_op jit(solution)/shard_map/ppermute | solution.py:42
  133.4 31.3 %copy-start.2 = (bf16[1920,360]{1,0:T(8,128)(2,1)S(1)}, bf16[1920,360]{1,0:T(8,128)(2,1)}, u32[]{:S(2)}) copy-start(bf16[1920,360]{1,0:T(8,128)(2,1)} %copy-done) | copy-start | bytes 4147204
  133.4 31.3 %copy-start.6 = (bf16[16,120,128]{2,1,0:T(8,128)(2,1)S(1)}, bf16[16,120,128]{2,1,0:T(8,128)(2,1)}, u32[]{:S(2)}) copy-start(bf16[16,120,128]{2,1,0:T(8,128)(2,1)} %copy-done.5) | copy-start | bytes 1474564
  166.1 20.0 %copy-start.4 = (bf16[8,256,384]{2,1,0:T(8,128)(2,1)}, bf16[8,256,384]{2,1,0:T(8,128)(2,1)S(1)}, u32[]{:S(2)}) copy-start(bf16[8,256,384]{2,1,0:T(8,128)(2,1)S(1)} %get-tuple-element.38) | copy-start | bytes 4718596
  186.1 25.5 %all-to-all-start.8 = ((bf16[8,256,384]{2,1,0:T(8,128)(2,1)}), bf16[8,256,384]{2,1,0:T(8,128)(2,1)}, u32[]{:S(2)}, u32[]{:S(2)}) async-start(bf16[8,256,384]{2,1,0:T(8,128)(2,1)} %copy-done.4), calls=%async_computation.8 | async-start | bytes 3145728 | tf_op jit(solution)/shard_map/all_to_all | solution.py:34
  191.9 19.0 %collective-permute-start.9 = (bf16[2,32,128]{2,1,0:T(8,128)(2,1)S(1)}, bf16[2,32,128]{2,1,0:T(8,128)(2,1)S(1)}, u32[]{:S(2)}, u32[]{:S(2)}) collective-permute-start(bf16[2,32,128]{2,1,0:T(8,128)(2,1)S(1)} %get-tuple-element.50), channel_id=1, source_target_pairs={{0,8},{8,16},{16,24},{24,32},{32,40},{40,48},{48,56},{56,64},{64,7... | collective-permute-start | bytes 49160 | tf_op jit(solution)/shard_map/ppermute | solution.py:174
  195.5 15.4 %collective-permute-start.10 = (bf16[2,32,128]{2,1,0:T(8,128)(2,1)S(1)}, bf16[2,32,128]{2,1,0:T(8,128)(2,1)S(1)}, u32[]{:S(2)}, u32[]{:S(2)}) collective-permute-start(bf16[2,32,128]{2,1,0:T(8,128)(2,1)S(1)} %get-tuple-element.51), channel_id=1, source_target_pairs={{8,0},{16,8},{24,16},{32,24},{40,32},{48,40},{56,48},{64,56},{72,6... | collective-permute-start | bytes 49160 | tf_op jit(solution)/shard_map/ppermute | solution.py:175
  202.2 8.7 %collective-permute-start.11 = (bf16[2,32,128]{2,1,0:T(8,128)(2,1)S(1)}, bf16[2,32,128]{2,1,0:T(8,128)(2,1)S(1)}, u32[]{:S(2)}, u32[]{:S(2)}) collective-permute-start(bf16[2,32,128]{2,1,0:T(8,128)(2,1)S(1)} %get-tuple-element.50), channel_id=1, source_target_pairs={{0,264},{8,272},{16,280},{24,288},{32,296},{40,304},{48,312},{56,3... | collective-permute-start | bytes 49160 | tf_op jit(solution)/shard_map/ppermute | solution.py:174
  203.5 7.4 %collective-permute-start.13 = (bf16[2,32,128]{2,1,0:T(8,128)(2,1)S(1)}, bf16[2,32,128]{2,1,0:T(8,128)(2,1)S(1)}, u32[]{:S(2)}, u32[]{:S(2)}) collective-permute-start(bf16[2,32,128]{2,1,0:T(8,128)(2,1)S(1)} %get-tuple-element.51), channel_id=1, source_target_pairs={{8,256},{16,264},{24,272},{32,280},{40,288},{48,296},{56,304},{64,... | collective-permute-start | bytes 49160 | tf_op jit(solution)/shard_map/ppermute | solution.py:175
  205.4 6.2 %collective-permute-start.12 = (bf16[256,128]{1,0:T(8,128)(2,1)S(1)}, bf16[256,128]{1,0:T(8,128)(2,1)S(1)}, u32[]{:S(2)}, u32[]{:S(2)}) collective-permute-start(bf16[256,128]{1,0:T(8,128)(2,1)S(1)} %bitcast.25), channel_id=1, source_target_pairs={{0,256},{8,264},{16,272},{24,280},{32,288},{40,296},{48,304},{56,3... | collective-permute-start | bytes 196616 | tf_op jit(solution)/shard_map/ppermute | solution.py:42
  213.8 18.3 %all-to-all-start.9 = ((bf16[8,32,384]{2,1,0:T(8,128)(2,1)}), bf16[8,32,384]{2,1,0:T(8,128)(2,1)S(1)}, u32[]{:S(2)}, u32[]{:S(2)}) async-start(bf16[8,32,384]{2,1,0:T(8,128)(2,1)} %shard_map.86.refs_0_), calls=%async_computation.9 | async-start | bytes 393216 | tf_op jit(solution)/shard_map/all_to_all | solution.py:46
  225.2 6.2 %collective-permute-start.14 = (bf16[2,128,128]{2,1,0:T(8,128)(2,1)S(1)}, bf16[2,128,128]{2,1,0:T(8,128)(2,1)S(1)}, u32[]{:S(2)}, u32[]{:S(2)}) collective-permute-start(bf16[2,128,128]{2,1,0:T(8,128)(2,1)S(1)} %get-tuple-element.40), channel_id=1, source_target_pairs={{0,256},{8,264},{16,272},{24,280},{32,288},{40,296},{48,304},{56,3... | collective-permute-start | bytes 196616 | tf_op jit(solution)/shard_map/ppermute | solution.py:42
